TPU v7x, 32 devices: a whole 2x2x4 slice. The times are simulated.
32 devices in a mesh: sx: 2 (over core), sy: 2 (over x), fsdp: 8 (over z, y).
Axes of the slice: x: 2, y: 2, z: 4, core: 2. Of those that a mesh axis runs over, the one named last changes fastest.
Arguments:
- x_code: bfloat16 [8, 16, 32, 1536], P('fsdp', 'sx', 'sy'), may hold values from -6 to 6
- x_exp: int32 [8, 16, 32, 12], P('fsdp', 'sx', 'sy'), may hold values from -2 to 2
- dw_kernel: float32 [7, 7, 1536], replicated, may hold values from -1.2 to 1.2
- dw_bias: float32 [1536], replicated, may hold values from -4 to 4
- ln_gain: float32 [1536], replicated, may hold values from 0.1 to 1.9
- ln_bias: float32 [1536], replicated, may hold values from -3 to 3
- w_up: bfloat16 [1536, 3072], P('fsdp'), may hold values from -0.15625 to 0.15625
- b_up: float32 [3072], replicated, may hold values from -3 to 3
- w_down: bfloat16 [3072, 1536], P(None, 'fsdp'), may hold values from -0.109375 to 0.109375
- b_down: float32 [1536], replicated, may hold values from -3 to 3
- layer_scale: float32 [1536], replicated, may hold values from 0.3 to 1.5
- cotangent: bfloat16 [8, 16, 32, 1536], P('fsdp', 'sx', 'sy'), may hold values from -6 to 6
Outputs:
- block_out: bfloat16 [8, 16, 32, 1536], P('fsdp', 'sx', 'sy')
- grad_input: bfloat16 [8, 16, 32, 1536], P('fsdp', 'sx', 'sy')
- grad_kernel: float32 [7, 7, 1536], replicated
- grad_gain: float32 [1536], replicated
- grad_scale: float32 [1536], replicated
All inputs are finite; a program needn't handle non-finite values.
Results may differ from a plain program's by a relative error of at most 0.006.
Values may be sent and summed in bfloat16 or wider, within the bound.
No kernel may reach another device: no remote copies, remote signals or barrier semaphores. Data moves between devices by JAX's collectives and lax.ppermute only.
A program may use at most 192 MiB of HBM per device.

v0:
```python
import jax
import jax.numpy as jnp
from jax import lax
from jax.sharding import PartitionSpec as P

CG = 128
KW = 7


def with_halo(shard, sides, width):
    for axis, dim in sides:
        devices, length = (lax.axis_size(axis), shard.shape[dim])
        up = [(i, (i + 1) % devices) for i in range(devices - 1)]
        down = [(j, i) for i, j in up]
        last = lax.slice_in_dim(shard, length - width, length, axis=dim)
        initial = lax.slice_in_dim(shard, 0, width, axis=dim)
        before = lax.ppermute(last, axis, up)
        after = lax.ppermute(initial, axis, down)
        shard = jnp.concatenate([before, shard, after], axis=dim)
    return shard


def gelu_tanh(v):
    return jax.nn.gelu(v, approximate=True)


def on_device(
    x_code,
    x_exp,
    dw_kernel,
    dw_bias,
    ln_gain,
    ln_bias,
    w_up,
    b_up,
    w_down,
    b_down,
    layer_scale,
    cotangent,
):
    code = x_code[0]
    rows, cols, chans = code.shape
    factor = jnp.exp2(x_exp[0].astype(jnp.float32))
    grouped = code.astype(jnp.float32).reshape(rows, cols, chans // CG, CG) * factor[..., None]
    scaled = grouped.reshape(rows, cols, chans).astype(jnp.bfloat16)
    up_full, down_full = (
        lax.all_gather(w_up, "fsdp", axis=0, tiled=True),
        lax.all_gather(w_down, "fsdp", axis=1, tiled=True),
    )
    padded_x = with_halo(scaled[None], (("sx", 1), ("sy", 2)), 3)[0].astype(jnp.float32)
    conv = jnp.zeros((rows, cols, chans), jnp.float32) + dw_bias
    for i in range(KW):
        for j in range(KW):
            conv = conv + dw_kernel[i, j] * padded_x[i : i + rows, j : j + cols]
    mean_val = jnp.mean(conv, axis=-1, keepdims=True)
    centred = conv - mean_val
    rstd = lax.rsqrt(jnp.mean(centred * centred, axis=-1, keepdims=True) + 1e-06)
    normed = centred * rstd
    ln_out = (normed * ln_gain + ln_bias).astype(jnp.bfloat16).reshape(rows * cols, chans)
    pre = jnp.dot(ln_out, up_full, preferred_element_type=jnp.float32) + b_up
    act, gelu_back = jax.vjp(gelu_tanh, pre)
    mlp = jnp.dot(act.astype(jnp.bfloat16), down_full, preferred_element_type=jnp.float32) + b_down
    mlp = mlp.reshape(rows, cols, chans)
    block_out = (scaled.astype(jnp.float32) + layer_scale * mlp).astype(jnp.bfloat16)
    grad_f = cotangent[0].astype(jnp.float32)
    scale_term = jnp.sum(grad_f * mlp, axis=(0, 1))
    d_mlp = (layer_scale * grad_f).astype(jnp.bfloat16).reshape(rows * cols, chans)
    d_act = lax.dot_general(
        d_mlp, down_full, (((1,), (1,)), ((), ())), preferred_element_type=jnp.float32
    )
    d_pre = gelu_back(d_act)[0].astype(jnp.bfloat16)
    d_ln = lax.dot_general(
        d_pre, up_full, (((1,), (1,)), ((), ())), preferred_element_type=jnp.float32
    )
    d_ln = d_ln.reshape(rows, cols, chans)
    gain_term = jnp.sum(d_ln * normed, axis=(0, 1))
    d_norm = d_ln * ln_gain
    d_conv = rstd * (
        d_norm
        - jnp.mean(d_norm, axis=-1, keepdims=True)
        - normed * jnp.mean(d_norm * normed, axis=-1, keepdims=True)
    )
    kernel_rows = []
    for i in range(KW):
        kernel_cols = []
        for j in range(KW):
            kernel_cols.append(jnp.sum(d_conv * padded_x[i : i + rows, j : j + cols], axis=(0, 1)))
        kernel_rows.append(jnp.stack(kernel_cols))
    kernel_term = jnp.stack(kernel_rows)
    padded_grad = with_halo(d_conv[None].astype(jnp.bfloat16), (("sx", 1), ("sy", 2)), 3).astype(
        jnp.float32
    )[0]
    back_conv = grad_f
    for i in range(KW):
        for j in range(KW):
            back_conv = (
                back_conv
                + dw_kernel[i, j] * padded_grad[6 - i : 6 - i + rows, 6 - j : 6 - j + cols]
            )
    grad_input = back_conv.astype(jnp.bfloat16)
    grad_kernel, grad_gain, grad_scale = lax.psum(
        (kernel_term, gain_term, scale_term), ("sx", "sy", "fsdp")
    )
    return (block_out[None], grad_input[None], grad_kernel, grad_gain, grad_scale)


def solution(mesh):
    placed = (
        P("fsdp", "sx", "sy", None),
        P("fsdp", "sx", "sy", None),
        P(),
        P(),
        P(),
        P(),
        P("fsdp", None),
        P(),
        P(None, "fsdp"),
        P(),
        P(),
        P("fsdp", "sx", "sy", None),
    )
    return jax.shard_map(
        on_device,
        mesh=mesh,
        in_specs=placed,
        out_specs=(P("fsdp", "sx", "sy", None), P("fsdp", "sx", "sy", None), P(), P(), P()),
        check_vma=False,
    )
```

profile of v0, /device:TPU:0, one launch (start us, length us, event | category | flops | bytes accessed | tf_op | source)
XLA Modules:
  0.0 466.3 jit_solution(9054006674799197369)
XLA Ops:
  7.2 0.0 all-gather.3.cloned.1.call-start
  7.2 0.7 all-gather.3.cloned.1.call-update
  7.9 0.0 all-gather.5.cloned.1.call-start
  8.0 0.7 all-gather.5.cloned.1.call-update
  8.7 0.0 all-reduce.3.cloned.1.call-start
  8.7 0.1 copy.18
  8.9 0.3 mul.1066
  9.2 0.0 copy-start.5
  9.2 0.1 mul.1067
  9.3 0.3 copy-done.4
  9.7 0.1 multiply_convert_fusion.2
  9.8 2.4 collective-permute-start
  12.1 1.3 collective-permute-start.1
  13.4 0.3 slice_reduce_fusion.48
  13.9 0.9 slice_reduce_fusion.47
  15.0 0.4 collective-permute-done.1
  15.4 0.1 pad_maximum_fusion.3
  15.5 4.2 collective-permute-start.2
  19.8 1.3 collective-permute-start.3
  21.1 0.8 slice_reduce_fusion.46
  21.9 2.4 collective-permute-done.2
  24.3 4.1 collective-permute-done.3
  28.4 0.4 fusion.7
  29.2 9.4 %fusion.84 = (f32[8,16]{1,0:T(8,128)S(1)}, f32[8,16,1536]{2,1,0:T(8,128)S(1)}) fusion(f32[14,22,1536]{2,1,0:T(8,128)S(1)} %fusion.7, f32[1536]{0:T(1024)} %get-tuple-element.103, f32[1536]{0:T(1024)} %get-tuple-element.104, f32[1536]{0:T(1024)S(1)} %get-tuple-element.57, f32[1536]{0:T(1024)S(1)} %get-tuple-element.58, f32[1536]{0:T(1024)S(1)} %get-tuple-element.59, ...), kind=kLoop, calls=%fused_computation.267 | loop fusion | flops 19464064 | bytes 39629312 | tf_op jit(solution)/shard_map/reduce_sum | solution.py:55
  38.6 0.2 multiply_reduce_fusion.52
  38.9 1.7 add_convert_fusion.1
  40.5 110.5 %all-gather.3.cloned.1.call-done = bf16[1536,3072]{1,0:T(8,128)(2,1)} async-done(((bf16[192,3072]{1,0:T(8,128)(2,1)}), bf16[1536,3072]{1,0:T(8,128)(2,1)}) %all-gather.3.cloned.1.call-update) | async-done | bytes 9437200 | tf_op jit(solution)/shard_map/all_gather | solution.py:47
  151.0 6.4 %convolution_add_fusion = f32[128,3072]{1,0:T(8,128)} fusion(bf16[128,1536]{1,0:T(8,128)(2,1)} %bitcast.55, bf16[1536,3072]{1,0:T(8,128)(2,1)} %all-gather.3.cloned.1.call-done, f32[3072]{0:T(1024)S(1)} %copy-done.51), kind=kOutput, calls=%fused_computation | convolution fusion | flops 1208352768 | bytes 11415552 | tf_op jit(solution)/shard_map/dot_general | solution.py:60
  157.4 132.0 %all-gather.5.cloned.1.call-done = bf16[3072,1536]{0,1:T(8,128)(2,1)} async-done(((bf16[3072,192]{0,1:T(8,128)(2,1)}), bf16[3072,1536]{0,1:T(8,128)(2,1)}) %all-gather.5.cloned.1.call-update) | async-done | bytes 9437200 | tf_op jit(solution)/shard_map/all_gather | solution.py:48
  289.5 8.9 %fusion.61 = (f32[1536]{0:T(1024)}, bf16[128,1536]{1,0:T(8,128)(2,1)}, f32[128,1536]{1,0:T(8,128)}) fusion(bf16[1,8,16,1536]{3,2,1,0:T(8,128)(2,1)} %param.23, f32[1536]{0:T(1024)S(1)} %copy-done.52, f32[1536]{0:T(1024)S(1)} %copy-done.55, bf16[3072,1536]{0,1:T(8,128)(2,1)} %all-gather.5.cloned.1.call-done, f32[128,3072]{1,0:T(8,128)} %convolution_add_fusion), kind=kOutput, calls=%fused_computation.119 | convolution fusion | flops 1212676608 | bytes 12601344 | tf_op jit(solution)/shard_map/dot_general | solution.py:62
  298.4 13.3 %multiply_reduce_fusion.51 = (f32[128]{0:T(128)S(1)}, f32[128,1536]{1,0:T(8,128)}) fusion(f32[1536]{0:T(1024)S(1)} %copy-done.8, bf16[1536,3072]{1,0:T(8,128)(2,1)} %all-gather.3.cloned.1.call-done, f32[128,3072]{1,0:T(8,128)} %convolution_add_fusion, bf16[128,1536]{1,0:T(8,128)(2,1)} %get-tuple-element.118, ...), kind=kOutput, calls=%fused_computation.172 | convolution fusion | flops 2424176640 | bytes 21633536 | tf_op jit(solution)/shard_map/dot_general | solution.py:72
  311.7 0.1 div.17
  311.8 2.4 multiply_reduce_fusion
  314.2 2.6 multiply_reduce_fusion.1
  316.8 1.4 multiply_reduce_fusion.37
  318.3 0.0 copy-start.53
  318.3 2.0 multiply_reduce_fusion.19
  320.3 0.9 add_convert_fusion
  321.7 0.1 stack.199
  321.8 1.3 collective-permute-start.4
  323.2 1.3 collective-permute-start.5
  324.5 0.1 stack.208
  324.6 0.1 stack.217
  324.7 0.1 stack.226
  324.7 0.1 stack.235
  324.8 0.1 stack.244
  325.0 0.1 stack.253
  325.1 0.0 copy-start.54
  325.1 1.3 collective-permute-done.5
  326.4 0.1 fusion.83
  326.5 0.1 fusion.85
  326.7 3.4 collective-permute-start.6
  330.1 1.3 collective-permute-start.7
  331.4 0.0 copy-start.2
  331.4 0.7 copy-done.2
  332.1 0.0 all-reduce.3.cloned.1.call-update
  332.1 0.0 copy-start.3
  332.2 39.8 %all-reduce = (f32[1536]{0:T(1024)}, f32[1536]{0:T(1024)}) all-reduce(f32[1536]{0:T(1024)S(1)} %copy-done.50, f32[1536]{0:T(1024)S(1)} %copy-done.54), channel_id=1, replica_groups=mesh['sx'=2,'sy'=2,'fsdp'=8] {'sx','sy','fsdp'}, use_global_device_ids=true, to_apply=%region_55.0 | all-reduce | flops 3072 | bytes 24576 | tf_op jit(solution)/shard_map/psum | solution.py:101
  372.1 0.6 copy-done.6
  372.7 0.1 copy-done.7
  372.8 1.4 maximum_convert_fusion
  374.3 7.7 %fusion.72 = bf16[1,8,16,1536]{3,2,1,0:T(8,128)(2,1)} fusion(f32[14,22,1536]{2,1,0:T(8,128)S(1)} %maximum_convert_fusion, f32[1536]{0:T(1024)} %get-tuple-element.103, f32[1536]{0:T(1024)} %get-tuple-element.104, f32[1536]{0:T(1024)S(1)} %get-tuple-element.57, f32[1536]{0:T(1024)S(1)} %copy-done.10, f32[1536]{0:T(1024)S(1)} %copy-done.12, ...), kind=kLoop, calls=%fused_computation.191 | loop fusion | flops 19660800 | bytes 39622656 | tf_op jit(solution)/shard_map/broadcast_in_dim | solution.py:104
  381.9 76.1 %all-reduce.3.cloned.1.call-done = f32[7,7,1536]{2,1,0:T(8,128)} async-done(((f32[7,7,1536]{2,1,0:T(8,128)}), f32[7,7,1536]{2,1,0:T(8,128)}) %all-reduce.3.cloned.1.call-update) | async-done | bytes 301072 | tf_op jit(solution)/shard_map/psum | solution.py:101
  458.1 1.7 copy.26
  (170 shorter events, 0.7 us)
Async XLA Ops:
  7.2 1.6 copy-start.49
  7.2 143.8 %all-gather.3.cloned.1.call-start = ((), (), s32[]{:S(2)}) async-start(), calls=%async_computation | async-start | bytes 10616832 | tf_op jit(solution)/shard_map/all_gather | solution.py:47
  7.9 281.5 %all-gather.5.cloned.1.call-start = ((), (), s32[]{:S(2)}) async-start(), calls=%async_computation.1 | async-start | bytes 10616832 | tf_op jit(solution)/shard_map/all_gather | solution.py:48
  8.7 1.0 copy-start.4
  8.7 449.4 %all-reduce.3.cloned.1.call-start = ((), (), s32[]{:S(2)}) async-start(), calls=%async_computation.2 | async-start | bytes 688128 | tf_op jit(solution)/shard_map/psum | solution.py:101
  9.2 4.2 copy-start.5
  9.8 5.2 %collective-permute-start = (bf16[1,3,16,1536]{3,2,1,0:T(8,128)(2,1)S(1)}, bf16[1,3,16,1536]{3,2,1,0:T(8,128)(2,1)S(1)}, u32[]{:S(2)}, u32[]{:S(2)}) collective-permute-start(bf16[1,3,16,1536]{3,2,1,0:T(8,128)(2,1)S(1)} %get-tuple-element.121), channel_id=1, source_target_pairs={{0,16},{1,17},{2,18},{3,19},{4,20},{5,21},{6,22},{7,23},{8,24},{9,... | collective-permute-start | bytes 442376 | tf_op jit(solution)/shard_map/ppermute | solution.py:17
  12.1 3.3 collective-permute-start.1
  13.8 15.0 %copy-start.9 = (f32[1536]{0:T(1024)}, f32[1536]{0:T(1024)S(1)}, u32[]{:S(2)}) copy-start(f32[1536]{0:T(1024)S(1)} %get-tuple-element.58) | copy-start | bytes 18436
  13.8 15.0 %copy-start.11 = (f32[1536]{0:T(1024)}, f32[1536]{0:T(1024)S(1)}, u32[]{:S(2)}) copy-start(f32[1536]{0:T(1024)S(1)} %get-tuple-element.59) | copy-start | bytes 18436
  13.8 15.0 %copy-start.13 = (f32[1536]{0:T(1024)}, f32[1536]{0:T(1024)S(1)}, u32[]{:S(2)}) copy-start(f32[1536]{0:T(1024)S(1)} %get-tuple-element.60) | copy-start | bytes 18436
  13.8 15.0 %copy-start.15 = (f32[1536]{0:T(1024)}, f32[1536]{0:T(1024)S(1)}, u32[]{:S(2)}) copy-start(f32[1536]{0:T(1024)S(1)} %get-tuple-element.61) | copy-start | bytes 18436
  13.8 15.0 %copy-start.17 = (f32[1536]{0:T(1024)}, f32[1536]{0:T(1024)S(1)}, u32[]{:S(2)}) copy-start(f32[1536]{0:T(1024)S(1)} %get-tuple-element.62) | copy-start | bytes 18436
  13.8 15.0 %copy-start.19 = (f32[1536]{0:T(1024)}, f32[1536]{0:T(1024)S(1)}, u32[]{:S(2)}) copy-start(f32[1536]{0:T(1024)S(1)} %get-tuple-element.63) | copy-start | bytes 18436
  13.8 15.0 %copy-start.21 = (f32[1536]{0:T(1024)}, f32[1536]{0:T(1024)S(1)}, u32[]{:S(2)}) copy-start(f32[1536]{0:T(1024)S(1)} %get-tuple-element.64) | copy-start | bytes 18436
  13.8 15.0 %copy-start.22 = (f32[1536]{0:T(1024)}, f32[1536]{0:T(1024)S(1)}, u32[]{:S(2)}) copy-start(f32[1536]{0:T(1024)S(1)} %get-tuple-element.65) | copy-start | bytes 18436
  13.8 15.0 %copy-start.23 = (f32[1536]{0:T(1024)}, f32[1536]{0:T(1024)S(1)}, u32[]{:S(2)}) copy-start(f32[1536]{0:T(1024)S(1)} %get-tuple-element.66) | copy-start | bytes 18436
  13.9 15.0 %copy-start.24 = (f32[1536]{0:T(1024)}, f32[1536]{0:T(1024)S(1)}, u32[]{:S(2)}) copy-start(f32[1536]{0:T(1024)S(1)} %get-tuple-element.67) | copy-start | bytes 18436
  13.9 15.0 %copy-start.25 = (f32[1536]{0:T(1024)}, f32[1536]{0:T(1024)S(1)}, u32[]{:S(2)}) copy-start(f32[1536]{0:T(1024)S(1)} %get-tuple-element.68) | copy-start | bytes 18436
  13.9 15.0 %copy-start.26 = (f32[1536]{0:T(1024)}, f32[1536]{0:T(1024)S(1)}, u32[]{:S(2)}) copy-start(f32[1536]{0:T(1024)S(1)} %get-tuple-element.69) | copy-start | bytes 18436
  13.9 15.0 %copy-start.27 = (f32[1536]{0:T(1024)}, f32[1536]{0:T(1024)S(1)}, u32[]{:S(2)}) copy-start(f32[1536]{0:T(1024)S(1)} %get-tuple-element.70) | copy-start | bytes 18436
  13.9 15.0 %copy-start.28 = (f32[1536]{0:T(1024)}, f32[1536]{0:T(1024)S(1)}, u32[]{:S(2)}) copy-start(f32[1536]{0:T(1024)S(1)} %get-tuple-element.71) | copy-start | bytes 18436
  13.9 15.0 %copy-start.29 = (f32[1536]{0:T(1024)}, f32[1536]{0:T(1024)S(1)}, u32[]{:S(2)}) copy-start(f32[1536]{0:T(1024)S(1)} %get-tuple-element.72) | copy-start | bytes 18436
  13.9 15.0 %copy-start.30 = (f32[1536]{0:T(1024)}, f32[1536]{0:T(1024)S(1)}, u32[]{:S(2)}) copy-start(f32[1536]{0:T(1024)S(1)} %get-tuple-element.73) | copy-start | bytes 18436
  13.9 15.0 %copy-start.31 = (f32[1536]{0:T(1024)}, f32[1536]{0:T(1024)S(1)}, u32[]{:S(2)}) copy-start(f32[1536]{0:T(1024)S(1)} %get-tuple-element.74) | copy-start | bytes 18436
  14.8 14.1 %copy-start.32 = (f32[1536]{0:T(1024)}, f32[1536]{0:T(1024)S(1)}, u32[]{:S(2)}) copy-start(f32[1536]{0:T(1024)S(1)} %get-tuple-element.75) | copy-start | bytes 18436
  14.8 14.1 %copy-start.33 = (f32[1536]{0:T(1024)}, f32[1536]{0:T(1024)S(1)}, u32[]{:S(2)}) copy-start(f32[1536]{0:T(1024)S(1)} %get-tuple-element.76) | copy-start | bytes 18436
  14.9 14.2 %copy-start.34 = (f32[1536]{0:T(1024)}, f32[1536]{0:T(1024)S(1)}, u32[]{:S(2)}) copy-start(f32[1536]{0:T(1024)S(1)} %get-tuple-element.77) | copy-start | bytes 18436
  14.9 14.2 %copy-start.35 = (f32[1536]{0:T(1024)}, f32[1536]{0:T(1024)S(1)}, u32[]{:S(2)}) copy-start(f32[1536]{0:T(1024)S(1)} %get-tuple-element.78) | copy-start | bytes 18436
  14.9 14.2 %copy-start.36 = (f32[1536]{0:T(1024)}, f32[1536]{0:T(1024)S(1)}, u32[]{:S(2)}) copy-start(f32[1536]{0:T(1024)S(1)} %get-tuple-element.79) | copy-start | bytes 18436
  14.9 14.2 %copy-start.37 = (f32[1536]{0:T(1024)}, f32[1536]{0:T(1024)S(1)}, u32[]{:S(2)}) copy-start(f32[1536]{0:T(1024)S(1)} %get-tuple-element.80) | copy-start | bytes 18436
  14.9 14.2 %copy-start.38 = (f32[1536]{0:T(1024)}, f32[1536]{0:T(1024)S(1)}, u32[]{:S(2)}) copy-start(f32[1536]{0:T(1024)S(1)} %get-tuple-element.81) | copy-start | bytes 18436
  14.9 14.2 %copy-start.39 = (f32[1536]{0:T(1024)}, f32[1536]{0:T(1024)S(1)}, u32[]{:S(2)}) copy-start(f32[1536]{0:T(1024)S(1)} %get-tuple-element.82) | copy-start | bytes 18436
  14.9 14.2 %copy-start.40 = (f32[1536]{0:T(1024)}, f32[1536]{0:T(1024)S(1)}, u32[]{:S(2)}) copy-start(f32[1536]{0:T(1024)S(1)} %get-tuple-element.83) | copy-start | bytes 18436
  14.9 14.2 %copy-start.41 = (f32[1536]{0:T(1024)}, f32[1536]{0:T(1024)S(1)}, u32[]{:S(2)}) copy-start(f32[1536]{0:T(1024)S(1)} %get-tuple-element.84) | copy-start | bytes 18436
  14.9 14.2 %copy-start.42 = (f32[1536]{0:T(1024)}, f32[1536]{0:T(1024)S(1)}, u32[]{:S(2)}) copy-start(f32[1536]{0:T(1024)S(1)} %get-tuple-element.85) | copy-start | bytes 18436
  14.9 14.2 %copy-start.43 = (f32[1536]{0:T(1024)}, f32[1536]{0:T(1024)S(1)}, u32[]{:S(2)}) copy-start(f32[1536]{0:T(1024)S(1)} %get-tuple-element.86) | copy-start | bytes 18436
  14.9 14.2 %copy-start.44 = (f32[1536]{0:T(1024)}, f32[1536]{0:T(1024)S(1)}, u32[]{:S(2)}) copy-start(f32[1536]{0:T(1024)S(1)} %get-tuple-element.87) | copy-start | bytes 18436
  14.9 14.2 %copy-start.45 = (f32[1536]{0:T(1024)}, f32[1536]{0:T(1024)S(1)}, u32[]{:S(2)}) copy-start(f32[1536]{0:T(1024)S(1)} %get-tuple-element.88) | copy-start | bytes 18436
  14.9 14.2 %copy-start.46 = (f32[1536]{0:T(1024)}, f32[1536]{0:T(1024)S(1)}, u32[]{:S(2)}) copy-start(f32[1536]{0:T(1024)S(1)} %get-tuple-element.89) | copy-start | bytes 18436
  15.0 14.2 %copy-start.47 = (f32[1536]{0:T(1024)}, f32[1536]{0:T(1024)S(1)}, u32[]{:S(2)}) copy-start(f32[1536]{0:T(1024)S(1)} %get-tuple-element.90) | copy-start | bytes 18436
  15.0 14.2 %copy-start.48 = (f32[1536]{0:T(1024)}, f32[1536]{0:T(1024)S(1)}, u32[]{:S(2)}) copy-start(f32[1536]{0:T(1024)S(1)} %get-tuple-element.91) | copy-start | bytes 18436
  15.5 8.8 %collective-permute-start.2 = (bf16[1,14,3,1536]{3,2,1,0:T(4,128)(2,1)S(1)}, bf16[1,14,3,1536]{3,2,1,0:T(4,128)(2,1)S(1)}, u32[]{:S(2)}, u32[]{:S(2)}) collective-permute-start(bf16[1,14,3,1536]{3,2,1,0:T(4,128)(2,1)S(1)} %get-tuple-element.115), channel_id=1, source_target_pairs={{0,8},{1,9},{2,10},{3,11},{4,12},{5,13},{6,14},{7,15},{16,24},{17,... | collective-permute-start | bytes 387080 | tf_op jit(solution)/shard_map/ppermute | solution.py:17
  19.8 8.6 %collective-permute-start.3 = (bf16[1,14,3,1536]{3,2,1,0:T(4,128)(2,1)S(1)}, bf16[1,14,3,1536]{3,2,1,0:T(4,128)(2,1)S(1)}, u32[]{:S(2)}, u32[]{:S(2)}) collective-permute-start(bf16[1,14,3,1536]{3,2,1,0:T(4,128)(2,1)S(1)} %get-tuple-element.116), channel_id=1, source_target_pairs={{8,0},{9,1},{10,2},{11,3},{12,4},{13,5},{14,6},{15,7},{24,16},{25,... | collective-permute-start | bytes 387080 | tf_op jit(solution)/shard_map/ppermute | solution.py:18
  29.2 9.7 %copy-start.8 = (f32[1536]{0:T(1024)S(1)}, f32[1536]{0:T(1024)}, u32[]{:S(2)}) copy-start(f32[1536]{0:T(1024)} %param.16) | copy-start | bytes 18436
  38.6 112.4 %copy-start.51 = (f32[3072]{0:T(1024)S(1)}, f32[3072]{0:T(1024)}, u32[]{:S(2)}) copy-start(f32[3072]{0:T(1024)} %param.19) | copy-start | bytes 36868
  151.0 138.5 %copy-start.52 = (f32[1536]{0:T(1024)S(1)}, f32[1536]{0:T(1024)}, u32[]{:S(2)}) copy-start(f32[1536]{0:T(1024)} %param.22) | copy-start | bytes 18436
  151.0 138.5 %copy-start.55 = (f32[1536]{0:T(1024)S(1)}, f32[1536]{0:T(1024)}, u32[]{:S(2)}) copy-start(f32[1536]{0:T(1024)} %param.21) | copy-start | bytes 18436
  311.8 2.4 copy-start
  318.3 2.0 copy-start.1
  318.3 2.0 copy-start.53
  321.8 3.3 collective-permute-start.4
  323.2 3.3 collective-permute-start.5
  325.1 7.1 %copy-start.50 = (f32[1536]{0:T(1024)S(1)}, f32[1536]{0:T(1024)}, u32[]{:S(2)}) copy-start(f32[1536]{0:T(1024)} %get-tuple-element.54) | copy-start | bytes 18436
  325.1 7.1 %copy-start.54 = (f32[1536]{0:T(1024)S(1)}, f32[1536]{0:T(1024)}, u32[]{:S(2)}) copy-start(f32[1536]{0:T(1024)} %get-tuple-element.117) | copy-start | bytes 18436
  326.7 45.4 %collective-permute-start.6 = (bf16[1,14,3,1536]{3,2,1,0:T(4,128)(2,1)S(1)}, bf16[1,14,3,1536]{3,2,1,0:T(4,128)(2,1)S(1)}, u32[]{:S(2)}, u32[]{:S(2)}) collective-permute-start(bf16[1,14,3,1536]{3,2,1,0:T(4,128)(2,1)S(1)} %get-tuple-element.111), channel_id=1, source_target_pairs={{0,8},{1,9},{2,10},{3,11},{4,12},{5,13},{6,14},{7,15},{16,24},{17,... | collective-permute-start | bytes 387080 | tf_op jit(solution)/shard_map/ppermute | solution.py:17
  330.1 42.0 %collective-permute-start.7 = (bf16[1,14,3,1536]{3,2,1,0:T(4,128)(2,1)S(1)}, bf16[1,14,3,1536]{3,2,1,0:T(4,128)(2,1)S(1)}, u32[]{:S(2)}, u32[]{:S(2)}) collective-permute-start(bf16[1,14,3,1536]{3,2,1,0:T(4,128)(2,1)S(1)} %get-tuple-element.112), channel_id=1, source_target_pairs={{8,0},{9,1},{10,2},{11,3},{12,4},{13,5},{14,6},{15,7},{24,16},{25,... | collective-permute-start | bytes 387080 | tf_op jit(solution)/shard_map/ppermute | solution.py:18
  332.1 42.0 %copy-start.3 = (bf16[1,8,16,1536]{3,2,1,0:T(8,128)(2,1)S(1)}, bf16[1,8,16,1536]{3,2,1,0:T(8,128)(2,1)}, u32[]{:S(2)}) copy-start(bf16[1,8,16,1536]{3,2,1,0:T(8,128)(2,1)} %param.23) | copy-start | bytes 1179652
  332.2 42.0 %copy-start.10 = (f32[1536]{0:T(1024)S(1)}, f32[1536]{0:T(1024)}, u32[]{:S(2)}) copy-start(f32[1536]{0:T(1024)} %copy-done.9) | copy-start | bytes 18436
  332.2 42.0 %copy-start.12 = (f32[1536]{0:T(1024)S(1)}, f32[1536]{0:T(1024)}, u32[]{:S(2)}) copy-start(f32[1536]{0:T(1024)} %copy-done.11) | copy-start | bytes 18436
  332.2 42.0 %copy-start.14 = (f32[1536]{0:T(1024)S(1)}, f32[1536]{0:T(1024)}, u32[]{:S(2)}) copy-start(f32[1536]{0:T(1024)} %copy-done.13) | copy-start | bytes 18436
  332.2 42.0 %copy-start.16 = (f32[1536]{0:T(1024)S(1)}, f32[1536]{0:T(1024)}, u32[]{:S(2)}) copy-start(f32[1536]{0:T(1024)} %copy-done.15) | copy-start | bytes 18436
  332.2 42.0 %copy-start.18 = (f32[1536]{0:T(1024)S(1)}, f32[1536]{0:T(1024)}, u32[]{:S(2)}) copy-start(f32[1536]{0:T(1024)} %copy-done.17) | copy-start | bytes 18436
  332.2 42.0 %copy-start.20 = (f32[1536]{0:T(1024)S(1)}, f32[1536]{0:T(1024)}, u32[]{:S(2)}) copy-start(f32[1536]{0:T(1024)} %copy-done.19) | copy-start | bytes 18436
  (3 other events, 2.1 us)
Sparse Core Ops, SparseCore 0:
  10.2 140.7 all-gather.2
  153.2 136.2 all-gather.4
  332.3 125.7 all-reduce.2
where the time goes:
time: 467 us; the launch traced here: 466 us
  waiting for transfers between devices  328 us (70%)
  blocking collectives  39.8 us (9%)
  other arithmetic  30.4 us (7%)
  matrix products  28.6 us (6%)
  starting transfers between devices  16.6 us (4%)
  between operations  15.2 us (3%)
  local copies, waits for them, and re-layouts  7.43 us (2%)
    all_gather x1, waiting for transfers between devices, on_device(): lax.all_gather(w_down, 'fsdp', axis=1, tiled=True)  132 us
    all_gather x1, waiting for transfers between devices, on_device(): lax.all_gather(w_up, 'fsdp', axis=0, tiled=True)  110 us
    psum x1, waiting for transfers between devices, on_device(): lax.psum((kernel_term, gain_term, scale_term), ('sx', 'sy', 'fsdp'))  76.1 us
    psum x1, blocking collectives, on_device(): lax.psum((kernel_term, gain_term, scale_term), ('sx', 'sy', 'fsdp'))  39.8 us
    dot_general x1, matrix products, on_device(): lax.dot_general(d_pre, up_full, (((1,), (1,)), ((), ())), preferred_eleme...  13.3 us
    ppermute x4, starting transfers between devices, with_halo(): before = lax.ppermute(last, axis, up)  11.3 us
    reduce_sum x1, other arithmetic, on_device(): mean_val = jnp.mean(conv, axis=-1, keepdims=True)  9.45 us
  transfers between devices with their start and end apart: 11, of which 7 were waited for; matrix products, arithmetic and copies ran while one was open for 7% of the time, Pallas kernels for 0%

commit v1 on v0

v1 whole, which is shorter than its diff:
```python
import jax
import jax.numpy as jnp
from jax import lax
from jax.sharding import PartitionSpec as P

CG = 128
KW = 7
BF = jnp.bfloat16
F32 = jnp.float32


def with_halo(shard, sides, width):
    for axis, dim in sides:
        devices, length = (lax.axis_size(axis), shard.shape[dim])
        up = [(i, (i + 1) % devices) for i in range(devices - 1)]
        down = [(j, i) for i, j in up]
        last = lax.slice_in_dim(shard, length - width, length, axis=dim)
        initial = lax.slice_in_dim(shard, 0, width, axis=dim)
        before = lax.ppermute(last, axis, up)
        after = lax.ppermute(initial, axis, down)
        shard = jnp.concatenate([before, shard, after], axis=dim)
    return shard


def ring_order(n):
    if n == 8:
        return [0, 2, 4, 6, 7, 5, 3, 1]
    return list(range(n))


def ring_gather(block):
    n, rows = lax.axis_size("fsdp"), block.shape[0]
    order = ring_order(n)
    place = [0] * n
    for k, d in enumerate(order):
        place[d] = k
    forth = [(order[k], order[(k + 1) % n]) for k in range(n)]
    back = [(d, s) for s, d in forth]
    me = jnp.asarray(place)[lax.axis_index("fsdp")]
    order = jnp.asarray(order)
    whole = jnp.zeros((n * rows,) + block.shape[1:], block.dtype)

    def put(whole, piece, k, offset=0):
        owner = order[(me + k) % n]
        return lax.dynamic_update_slice_in_dim(whole, piece, owner * rows + offset, 0)

    whole = put(whole, block, 0)
    one = two = block
    for k in range(1, (n + 1) // 2):
        one = lax.ppermute(one, "fsdp", forth)
        two = lax.ppermute(two, "fsdp", back)
        whole = put(whole, one, -k)
        whole = put(whole, two, k)
    if n % 2 == 0:
        half = rows // 2
        one = lax.ppermute(one[:half], "fsdp", forth)
        two = lax.ppermute(two[half:], "fsdp", back)
        whole = put(whole, one, -(n // 2))
        whole = put(whole, two, n // 2, half)
    return whole


def shift(a, axis, k):
    n = lax.axis_size(axis)
    return lax.ppermute(a, axis, [((i + k) % n, i) for i in range(n)])


def gather_tile(a):
    a = jnp.concatenate([a] + [shift(a, "sy", k) for k in range(1, lax.axis_size("sy"))], 0)
    return jnp.concatenate([a] + [shift(a, "sx", k) for k in range(1, lax.axis_size("sx"))], 0)


def scatter_tile(a):
    for axis in ("sx", "sy"):
        n = lax.axis_size(axis)
        a = a.reshape((n, a.shape[0] // n) + a.shape[1:])
        total = a[0].astype(F32)
        for k in range(1, n):
            total = total + shift(a[k].astype(BF), axis, -k).astype(F32)
        a = total
    return a[0]


def swap(a, axis, mask):
    return lax.ppermute(a, axis, [(i, i ^ mask) for i in range(lax.axis_size(axis))])


def sum_everywhere(a):
    half = a.shape[0] // 2
    core = lax.axis_index("sx") % 2
    mine = lax.dynamic_slice_in_dim(a, core * half, half, 0)
    other = lax.dynamic_slice_in_dim(a, (1 - core) * half, half, 0)
    total = mine + swap(other, "sx", 1)
    for axis in ("sx", "sy", "fsdp"):
        mask = 2 if axis == "sx" else 1
        while mask < lax.axis_size(axis):
            rounded = total.astype(BF)
            total = rounded.astype(F32) + swap(rounded, axis, mask).astype(F32)
            mask *= 2
    other = swap(total, "sx", 1)
    first = jnp.where(core == 0, total, other)
    second = jnp.where(core == 0, other, total)
    return jnp.concatenate([first, second], 0)


def gelu_tanh(v):
    return jax.nn.gelu(v, approximate=True)


def on_device(
    x_code,
    x_exp,
    dw_kernel,
    dw_bias,
    ln_gain,
    ln_bias,
    w_up,
    b_up,
    w_down,
    b_down,
    layer_scale,
    cotangent,
):
    code = x_code[0]
    rows, cols, chans = code.shape
    tiles = lax.axis_size("sx") * lax.axis_size("sy")
    quarter = lax.axis_index("sx") * lax.axis_size("sy") + lax.axis_index("sy")
    hidden = w_up.shape[1] // tiles
    up = ring_gather(lax.dynamic_slice_in_dim(w_up, quarter * hidden, hidden, 1))
    down = ring_gather(lax.dynamic_slice_in_dim(w_down, quarter * hidden, hidden, 0).T)
    bias_up = lax.dynamic_slice_in_dim(b_up, quarter * hidden, hidden, 0)

    factor = jnp.exp2(x_exp[0].astype(F32))
    grouped = code.astype(F32).reshape(rows, cols, chans // CG, CG) * factor[..., None]
    scaled = grouped.reshape(rows, cols, chans).astype(BF)
    grad_f = cotangent[0].astype(F32)
    d_mlp = gather_tile((layer_scale * grad_f).astype(BF).reshape(1, rows * cols, chans))
    d_mlp = d_mlp.reshape(tiles * rows * cols, chans)

    padded_x = with_halo(scaled[None], (("sx", 1), ("sy", 2)), 3)[0].astype(F32)
    conv = jnp.zeros((rows, cols, chans), F32) + dw_bias
    for i in range(KW):
        for j in range(KW):
            conv = conv + dw_kernel[i, j] * padded_x[i : i + rows, j : j + cols]
    mean_val = jnp.mean(conv, axis=-1, keepdims=True)
    centred = conv - mean_val
    rstd = lax.rsqrt(jnp.mean(centred * centred, axis=-1, keepdims=True) + 1e-06)
    normed = centred * rstd
    ln_out = (normed * ln_gain + ln_bias).astype(BF).reshape(1, rows * cols, chans)
    ln_all = gather_tile(ln_out).reshape(tiles * rows * cols, chans)

    pre = jnp.dot(ln_all, up, preferred_element_type=F32) + bias_up
    act, gelu_back = jax.vjp(gelu_tanh, pre)
    d_act = jnp.dot(d_mlp, down, preferred_element_type=F32)
    d_pre = gelu_back(d_act)[0].astype(BF)
    d_ln = lax.dot_general(d_pre, up, (((1,), (1,)), ((), ())), preferred_element_type=F32)
    d_ln = scatter_tile(d_ln.reshape(tiles, rows, cols, chans))
    mlp = lax.dot_general(
        act.astype(BF), down, (((1,), (1,)), ((), ())), preferred_element_type=F32
    )
    mlp = scatter_tile(mlp.reshape(tiles, rows, cols, chans)) + b_down
    block_out = (scaled.astype(F32) + layer_scale * mlp).astype(BF)
    scale_term = jnp.sum(grad_f * mlp, axis=(0, 1))

    gain_term = jnp.sum(d_ln * normed, axis=(0, 1))
    d_norm = d_ln * ln_gain
    d_conv = rstd * (
        d_norm
        - jnp.mean(d_norm, axis=-1, keepdims=True)
        - normed * jnp.mean(d_norm * normed, axis=-1, keepdims=True)
    )
    terms = []
    for i in range(KW):
        for j in range(KW):
            terms.append(jnp.sum(d_conv * padded_x[i : i + rows, j : j + cols], axis=(0, 1)))
    terms += [gain_term, scale_term]
    terms += [jnp.zeros_like(gain_term)] * (-len(terms) % 32)
    sums = sum_everywhere(jnp.stack(terms))
    padded_grad = with_halo(d_conv[None].astype(BF), (("sx", 1), ("sy", 2)), 3).astype(F32)[0]
    back_conv = grad_f
    for i in range(KW):
        for j in range(KW):
            back_conv = (
                back_conv
                + dw_kernel[i, j] * padded_grad[6 - i : 6 - i + rows, 6 - j : 6 - j + cols]
            )
    grad_input = back_conv.astype(BF)
    taps = KW * KW
    grad_kernel = sums[:taps].reshape(KW, KW, chans)
    return (block_out[None], grad_input[None], grad_kernel, sums[taps], sums[taps + 1])


def solution(mesh):
    placed = (
        P("fsdp", "sx", "sy", None),
        P("fsdp", "sx", "sy", None),
        P(),
        P(),
        P(),
        P(),
        P("fsdp", None),
        P(),
        P(None, "fsdp"),
        P(),
        P(),
        P("fsdp", "sx", "sy", None),
    )
    return jax.shard_map(
        on_device,
        mesh=mesh,
        in_specs=placed,
        out_specs=(P("fsdp", "sx", "sy", None), P("fsdp", "sx", "sy", None), P(), P(), P()),
        check_vma=False,
    )
```

time: 467 us -> 194 us (0.42)
  waiting for transfers between devices: 328 us -> 39 us
  blocking collectives: 39.8 us -> 0 us
  local copies, waits for them, and re-layouts: 7.43 us -> 41.4 us
  starting transfers between devices: 16.6 us -> 46.2 us
  matrix products: 28.6 us -> 14.9 us
  other arithmetic: 30.4 us -> 35.9 us
    all_gather x2 -> x0, waiting for transfers between devices: 243 us -> none  [the longest x1 132 us: on_device(): lax.all_gather(w_down, 'fsdp', axis=1, tiled=True)]
    psum x1 -> x0, waiting for transfers between devices: 76.1 us -> none  [on_device(): lax.psum((kernel_term, gain_term, scale_term), ('sx', 'sy', 'fsdp'))]
    psum x1 -> x0, blocking collectives: 39.8 us -> none  [on_device(): lax.psum((kernel_term, gain_term, scale_term), ('sx', 'sy', 'fsdp'))]
    ppermute x0 -> x30, starting transfers between devices: none -> 30.5 us  [the longest x6 11.2 us: ring_gather(): one = lax.ppermute(one, 'fsdp', forth)]
    ppermute x0 -> x30, waiting for transfers between devices: none -> 29.4 us  [the longest x8 8.49 us: shift(): return lax.ppermute(a, axis, [((i + k) % n, i) for i in range(n)])]
    dot_general x3, matrix products: 28.6 us -> 14.9 us  [the longest x1 8.7 us: on_device(): lax.dot_general(d_pre, up, (((1,), (1,)), ((), ())), preferred_element_ty...]
    dynamic_update_slice x0 -> x18, local copies, waits for them, and re-layouts: none -> 12.4 us  [put(): lax.dynamic_update_slice_in_dim(whole, piece, owner * rows + offset, 0)]
    another operation x57, local copies, waits for them, and re-layouts: 0.86 us -> 12.5 us  [the longest x55 10.8 us: on_device(): sums = sum_everywhere(jnp.stack(terms))]
  transfers between devices with their start and end apart: 11 -> 38, of which waited for: 7 -> 16; matrix products, arithmetic and copies ran while one was open for 7% -> 32% of each run, Pallas kernels for 0% -> 0%
where the time goes in v1:
time: 194 us; the launch traced here: 193 us
  starting transfers between devices  46.2 us (24%)
  local copies, waits for them, and re-layouts  41.4 us (21%)
  waiting for transfers between devices  39 us (20%)
  other arithmetic  35.9 us (19%)
  between operations  15.2 us (8%)
  matrix products  14.9 us (8%)
    dynamic_update_slice x18, local copies, waits for them, and re-layouts, put(): lax.dynamic_update_slice_in_dim(whole, piece, owner * rows + offset, 0)  12.4 us
    ppermute x6, starting transfers between devices, ring_gather(): one = lax.ppermute(one, 'fsdp', forth)  11.2 us
    another operation x55, local copies, waits for them, and re-layouts, on_device(): sums = sum_everywhere(jnp.stack(terms))  10.8 us
    ppermute x4, starting transfers between devices, with_halo(): before = lax.ppermute(last, axis, up)  10.3 us
    reduce_sum x1, other arithmetic, on_device(): mean_val = jnp.mean(conv, axis=-1, keepdims=True)  9.86 us
    dot_general x1, matrix products, on_device(): lax.dot_general(d_pre, up, (((1,), (1,)), ((), ())), preferred_element_ty...  8.7 us
    ppermute x8, waiting for transfers between devices, shift(): return lax.ppermute(a, axis, [((i + k) % n, i) for i in range(n)])  8.49 us
    broadcast_in_dim x1, other arithmetic, on_device(): grad_input[None]  7.13 us
  transfers between devices with their start and end apart: 38, of which 16 were waited for; matrix products, arithmetic and copies ran while one was open for 32% of the time, Pallas kernels for 0%

profile of v1, /device:TPU:0, one launch (start us, length us, event | category | flops | bytes accessed | tf_op | source)
XLA Modules:
  0.0 192.5 jit_solution(5018079023357596213)
XLA Ops:
  0.6 1.2 dynamic_slice.76
  9.2 1.7 fusion.91
  11.5 1.6 broadcast.102.clone
  13.1 1.9 constant_dynamic-update-slice_fusion.8
  15.0 3.0 %collective-permute-start.14 = (bf16[192,768]{1,0:T(8,128)(2,1)}, bf16[192,768]{1,0:T(8,128)(2,1)}, u32[]{:S(2)}, u32[]{:S(2)}) collective-permute-start(bf16[192,768]{1,0:T(8,128)(2,1)} %get-tuple-element.114), channel_id=1, source_target_pairs={{0,2},{2,4},{4,6},{6,7},{7,5},{5,3},{3,1},{1,0},{8,10},{10,12},{12... | collective-permute-start | bytes 884744 | tf_op jit(solution)/shard_map/ppermute | solution.py:50
  18.8 1.6 collective-permute-start
  20.4 1.3 collective-permute-start.1
  21.8 1.7 constant_dynamic-update-slice_fusion.17
  23.5 1.9 collective-permute-start.6
  26.2 0.9 slice_reduce_fusion.50
  32.1 1.4 dynamic_slice.86
  34.5 3.4 %collective-permute-start.2 = (bf16[1,14,3,1536]{3,2,1,0:T(4,128)(2,1)S(1)}, bf16[1,14,3,1536]{3,2,1,0:T(4,128)(2,1)S(1)}, u32[]{:S(2)}, u32[]{:S(2)}) collective-permute-start(bf16[1,14,3,1536]{3,2,1,0:T(4,128)(2,1)S(1)} %get-tuple-element.120), channel_id=1, source_target_pairs={{0,8},{1,9},{2,10},{3,11},{4,12},{5,13},{6,14},{7,15},{16,24},{17,... | collective-permute-start | bytes 387080 | tf_op jit(solution)/shard_map/ppermute | solution.py:19
  38.0 1.3 collective-permute-start.3
  40.0 2.5 %collective-permute-done.2 = bf16[1,14,3,1536]{3,2,1,0:T(4,128)(2,1)S(1)} collective-permute-done((bf16[1,14,3,1536]{3,2,1,0:T(4,128)(2,1)S(1)}, bf16[1,14,3,1536]{3,2,1,0:T(4,128)(2,1)S(1)}, u32[]{:S(2)}, u32[]{:S(2)}) %collective-permute-start.2) | collective-permute-done | bytes 129056 | tf_op jit(solution)/shard_map/ppermute | solution.py:19
  43.2 3.5 %collective-permute-done.3 = bf16[1,14,3,1536]{3,2,1,0:T(4,128)(2,1)S(1)} collective-permute-done((bf16[1,14,3,1536]{3,2,1,0:T(4,128)(2,1)S(1)}, bf16[1,14,3,1536]{3,2,1,0:T(4,128)(2,1)S(1)}, u32[]{:S(2)}, u32[]{:S(2)}) %collective-permute-start.3) | collective-permute-done | bytes 129056 | tf_op jit(solution)/shard_map/ppermute | solution.py:20
  47.1 9.9 %fusion.87 = (f32[8,16]{1,0:T(8,128)S(1)}, f32[8,16,1536]{2,1,0:T(8,128)S(1)}) fusion(f32[14,22,1536]{2,1,0:T(8,128)S(1)} %fusion.7, f32[1536]{0:T(1024)} %get-tuple-element.104, f32[1536]{0:T(1024)} %get-tuple-element.105, f32[1536]{0:T(1024)} %get-tuple-element.58, f32[1536]{0:T(1024)} %get-tuple-element.59, f32[1536]{0:T(1024)} %get-tuple-element.60, ...), kind=kLoop, calls=%fused_computation.304 | loop fusion | flops 19464064 | bytes 39629312 | tf_op jit(solution)/shard_map/reduce_sum | solution.py:145
  57.2 1.0 add_convert_fusion.1
  58.3 2.1 %collective-permute-start.4 = (bf16[1,128,1536]{2,1,0:T(8,128)(2,1)S(1)}, bf16[1,128,1536]{2,1,0:T(8,128)(2,1)S(1)}, u32[]{:S(2)}, u32[]{:S(2)}) collective-permute-start(bf16[1,128,1536]{2,1,0:T(8,128)(2,1)S(1)} %bitcast.70), channel_id=1, source_target_pairs={{8,0},{0,8},{9,1},{1,9},{10,2},{2,10},{11,3},{3,11},{12,4},{4,12},... | collective-permute-start | bytes 1179656 | tf_op jit(solution)/shard_map/ppermute | solution.py:65
  60.4 1.7 constant_dynamic-update-slice_fusion.5
  62.1 1.6 collective-permute-start.16
  64.9 1.0 constant_dynamic-update-slice_fusion.16
  65.9 1.6 collective-permute-start.8
  67.5 1.0 constant_dynamic-update-slice_fusion.15
  69.0 1.2 pad_maximum_fusion.3
  70.2 2.1 %collective-permute-done.16 = bf16[192,768]{1,0:T(8,128)(2,1)S(1)} collective-permute-done((bf16[192,768]{1,0:T(8,128)(2,1)}, bf16[192,768]{1,0:T(8,128)(2,1)S(1)}, u32[]{:S(2)}, u32[]{:S(2)}) %collective-permute-start.16) | collective-permute-done | bytes 294944 | tf_op jit(solution)/shard_map/ppermute | solution.py:50
  73.0 1.4 collective-permute-done.17
  74.4 1.6 collective-permute-start.18
  76.7 0.9 collective-permute-done.8
  77.6 1.3 collective-permute-start.19
  79.2 1.6 collective-permute-start.10
  81.4 2.9 %collective-permute-done.18 = bf16[192,768]{1,0:T(8,128)(2,1)S(1)} collective-permute-done((bf16[192,768]{1,0:T(8,128)(2,1)S(1)}, bf16[192,768]{1,0:T(8,128)(2,1)S(1)}, u32[]{:S(2)}, u32[]{:S(2)}) %collective-permute-start.18) | collective-permute-done | bytes 294944 | tf_op jit(solution)/shard_map/ppermute | solution.py:50
  85.1 2.4 %collective-permute-done.19 = bf16[192,768]{1,0:T(8,128)(2,1)S(1)} collective-permute-done((bf16[192,768]{1,0:T(8,128)(2,1)S(1)}, bf16[192,768]{1,0:T(8,128)(2,1)S(1)}, u32[]{:S(2)}, u32[]{:S(2)}) %collective-permute-start.19) | collective-permute-done | bytes 294944 | tf_op jit(solution)/shard_map/ppermute | solution.py:51
  87.5 1.6 collective-permute-start.20
  90.6 0.9 collective-permute-start.21
  91.6 1.4 collective-permute-start.12
  94.6 2.2 %collective-permute-done.12 = bf16[96,768]{1,0:T(8,128)(2,1)S(1)} collective-permute-done((bf16[96,768]{1,0:T(8,128)(2,1)S(1)}, bf16[96,768]{1,0:T(8,128)(2,1)S(1)}, u32[]{:S(2)}, u32[]{:S(2)}) %collective-permute-start.12) | collective-permute-done | bytes 147488 | tf_op jit(solution)/shard_map/ppermute | solution.py:56
  97.6 1.0 collective-permute-done.13
  98.7 3.0 %pad_maximum_fusion.1 = bf16[4,128,1536]{2,1,0:T(8,128)(2,1)} fusion(bf16[2,128,1536]{2,1,0:T(8,128)(2,1)S(1)} %collective-permute-done.25, bf16[1,128,1536]{2,1,0:T(8,128)(2,1)} %collective-permute-done.24, bf16[1,128,1536]{2,1,0:T(8,128)(2,1)} %fusion.64), kind=kLoop, calls=%fused_computation.12 | loop fusion | flops 1572864 | bytes 3145728 | tf_op jit(solution)/shard_map/concatenate | solution.py:70
  102.4 2.6 %convolution_add_fusion = f32[512,768]{1,0:T(8,128)} fusion(bf16[512,1536]{1,0:T(8,128)(2,1)S(1)} %bitcast.74, bf16[1536,768]{1,0:T(8,128)(2,1)S(1)} %constant_dynamic-update-slice_fusion.9, f32[768]{0:T(1024)S(1)} %copy-done.56), kind=kOutput, calls=%fused_computation.16 | convolution fusion | flops 1208352768 | bytes 5508096 | tf_op jit(solution)/shard_map/dot_general | solution.py:152
  105.0 8.7 %fusion.9 = f32[512,1536]{1,0:T(8,128)} fusion(bf16[1536,768]{1,0:T(8,128)(2,1)} %copy-done.7, f32[512,768]{1,0:T(8,128)} %convolution_add_fusion, bf16[512,1536]{1,0:T(8,128)(2,1)} %bitcast.73, bf16[1536,768]{1,0:T(8,128)(2,1)} %constant_dynamic-update-slice_fusion.7), kind=kOutput, calls=%fused_computation.21 | convolution fusion | flops 2423783424 | bytes 11010048 | tf_op jit(solution)/shard_map/dot_general | solution.py:156
  113.7 2.4 %slice.1420 = bf16[256,1536]{1,0:T(8,128)(2,1)} slice(f32[512,1536]{1,0:T(8,128)} %fusion.9), slice={[256:512], [0:1536]} | slice | bytes 1572864 | tf_op jit(solution)/shard_map/slice | solution.py:79
  116.1 3.6 %fusion.8 = f32[512,1536]{1,0:T(8,128)S(1)} fusion(bf16[1536,768]{1,0:T(8,128)(2,1)} %constant_dynamic-update-slice_fusion.7, f32[512,768]{1,0:T(8,128)} %convolution_add_fusion), kind=kOutput, calls=%fused_computation.20 | convolution fusion | flops 1211498496 | bytes 7077888 | tf_op jit(solution)/shard_map/dot_general | solution.py:158
  119.8 1.7 copy-done.2
  121.5 1.0 slice.1421
  122.9 1.4 slice-done.1
  124.3 1.5 convert_add_fusion
  126.8 1.4 convert_add_fusion.1
  128.2 1.3 collective-permute-start.23
  129.5 8.5 %collective-permute-done.27 = bf16[1,8,16,1536]{3,2,1,0:T(8,128)(2,1)S(1)} collective-permute-done((bf16[1,8,16,1536]{3,2,1,0:T(8,128)(2,1)S(1)}, bf16[1,8,16,1536]{3,2,1,0:T(8,128)(2,1)S(1)}, u32[]{:S(2)}, u32[]{:S(2)}) %collective-permute-start.27) | collective-permute-done | bytes 393248 | tf_op jit(solution)/shard_map/ppermute | solution.py:65
  138.3 2.5 %multiply_reduce_fusion.1 = (f32[1536]{0:T(1024)S(1)}, f32[1536]{0:T(1024)S(1)}, f32[1536]{0:T(1024)S(1)}, f32[1536]{0:T(1024)S(1)}, f32[1536]{0:T(1024)S(1)}, /...) fusion(f32[14,22,1536]{2,1,0:T(8,128)S(1)} %fusion.7, ...), kind=kLoop, calls=%fused_computation.134 | loop fusion | flops 8819712 | bytes 17027072 | tf_op jit(solution)/shard_map/reduce_sum | solution.py:175
  141.1 2.0 %multiply_reduce_fusion.19 = (f32[1536]{0:T(1024)S(1)}, f32[1536]{0:T(1024)S(1)}, f32[1536]{0:T(1024)S(1)}, f32[1536]{0:T(1024)S(1)}, f32[1536]{0:T(1024)S(1)}, ...) fusion(f32[8,16,1536]{2,1,0:T(8,128)S(1)} %get-tuple-element.10, ...), kind=kLoop, calls=%fused_computation.152 | loop fusion | flops 7246848 | bytes 15446016 | tf_op jit(solution)/shard_map/reduce_sum | solution.py:175
  143.1 1.4 multiply_reduce_fusion.37
  152.8 2.8 %stack.215 = f32[64,1536]{1,0:T(8,128)S(1)} concatenate(f32[1,1536]{1,0:T(1,128)S(1)} %stack.162, f32[1,1536]{1,0:T(1,128)S(1)} %stack.163, f32[1,1536]{1,0:T(1,128)S(1)} %stack.164, f32[1,1536]{1,0:T(1,128)S(1)} %stack.165, f32[1,1536]{1,0:T(1,128)S(1)} %stack.166, f32[1,1536]{1,0:T(1,128)S(1)} %stack.167, f32[1,1536]{1,0:T(1,128)S(1)} %stack.168, f32[1,1536]{1,0:T(1,128)S(1)} %stack.169, ...), dimensions={0} | concatenate | bytes 786432 | tf_op jit(solution)/shard_map/stack | solution.py:178
  155.7 2.4 %collective-permute-start.28 = (bf16[1,3,16,1536]{3,2,1,0:T(8,128)(2,1)S(1)}, bf16[1,3,16,1536]{3,2,1,0:T(8,128)(2,1)S(1)}, u32[]{:S(2)}, u32[]{:S(2)}) collective-permute-start(bf16[1,3,16,1536]{3,2,1,0:T(8,128)(2,1)S(1)} %get-tuple-element.124), channel_id=1, source_target_pairs={{0,16},{1,17},{2,18},{3,19},{4,20},{5,21},{6,22},{7,23},{8,24},{9,... | collective-permute-start | bytes 442376 | tf_op jit(solution)/shard_map/ppermute | solution.py:19
  158.1 1.5 collective-permute-start.29
  160.6 1.9 add_convert_fusion
  162.5 2.8 %collective-permute-done.33 = bf16[32,1536]{1,0:T(8,128)(2,1)S(1)} collective-permute-done((bf16[32,1536]{1,0:T(8,128)(2,1)S(1)}, bf16[32,1536]{1,0:T(8,128)(2,1)S(1)}, u32[]{:S(2)}, u32[]{:S(2)}) %collective-permute-start.33) | collective-permute-done | bytes 98336 | tf_op jit(solution)/shard_map/ppermute | solution.py:85
  166.2 4.0 %collective-permute-done.34 = bf16[32,1536]{1,0:T(8,128)(2,1)S(1)} collective-permute-done((bf16[32,1536]{1,0:T(8,128)(2,1)S(1)}, bf16[32,1536]{1,0:T(8,128)(2,1)S(1)}, u32[]{:S(2)}, u32[]{:S(2)}) %collective-permute-start.34) | collective-permute-done | bytes 98336 | tf_op jit(solution)/shard_map/ppermute | solution.py:85
  170.2 2.1 %collective-permute-start.35 = (bf16[32,1536]{1,0:T(8,128)(2,1)S(1)}, bf16[32,1536]{1,0:T(8,128)(2,1)S(1)}, u32[]{:S(2)}, u32[]{:S(2)}) collective-permute-start(bf16[32,1536]{1,0:T(8,128)(2,1)S(1)} %add_convert_fusion.3), channel_id=1, source_target_pairs={{0,2},{1,3},{2,0},{3,1},{4,6},{5,7},{6,4},{7,5},{8,10},{9,11},{10,... | collective-permute-start | bytes 294920 | tf_op jit(solution)/shard_map/ppermute | solution.py:85
  172.8 2.9 %collective-permute-start.30 = (bf16[1,14,3,1536]{3,2,1,0:T(4,128)(2,1)S(1)}, bf16[1,14,3,1536]{3,2,1,0:T(4,128)(2,1)S(1)}, u32[]{:S(2)}, u32[]{:S(2)}) collective-permute-start(bf16[1,14,3,1536]{3,2,1,0:T(4,128)(2,1)S(1)} %get-tuple-element.116), channel_id=1, source_target_pairs={{0,8},{1,9},{2,10},{3,11},{4,12},{5,13},{6,14},{7,15},{16,24},{17,... | collective-permute-start | bytes 387080 | tf_op jit(solution)/shard_map/ppermute | solution.py:19
  175.7 1.3 collective-permute-start.31
  177.1 2.4 %collective-permute-start.36 = (bf16[32,1536]{1,0:T(8,128)(2,1)S(1)}, bf16[32,1536]{1,0:T(8,128)(2,1)S(1)}, u32[]{:S(2)}, u32[]{:S(2)}) collective-permute-start(bf16[32,1536]{1,0:T(8,128)(2,1)S(1)} %add_convert_fusion.2), channel_id=1, source_target_pairs={{0,4},{1,5},{2,6},{3,7},{4,0},{5,1},{6,2},{7,3},{8,12},{9,13},{10,... | collective-permute-start | bytes 294920 | tf_op jit(solution)/shard_map/ppermute | solution.py:85
  179.4 3.6 %collective-permute-done.31 = bf16[1,14,3,1536]{3,2,1,0:T(4,128)(2,1)S(1)} collective-permute-done((bf16[1,14,3,1536]{3,2,1,0:T(4,128)(2,1)S(1)}, bf16[1,14,3,1536]{3,2,1,0:T(4,128)(2,1)S(1)}, u32[]{:S(2)}, u32[]{:S(2)}) %collective-permute-start.31) | collective-permute-done | bytes 129056 | tf_op jit(solution)/shard_map/ppermute | solution.py:20
  183.9 7.1 %fusion.75 = bf16[1,8,16,1536]{3,2,1,0:T(8,128)(2,1)} fusion(f32[14,22,1536]{2,1,0:T(8,128)S(1)} %maximum_convert_fusion, f32[1536]{0:T(1024)} %get-tuple-element.104, f32[1536]{0:T(1024)} %get-tuple-element.105, f32[1536]{0:T(1024)S(1)} %copy-done.13, f32[1536]{0:T(1024)S(1)} %copy-done.14, f32[1536]{0:T(1024)S(1)} %copy-done.15, f32[1536]{0:T(1024)S(1)} %copy-done.16, ...), kind=kLoop, calls=%fused_computation.204 | loop fusion | flops 19660800 | bytes 39622656 | tf_op jit(solution)/shard_map/broadcast_in_dim | solution.py:190
  (264 shorter events, 28.6 us)
Async XLA Ops:
  0.6 17.4 %copy-start.52 = (s32[1,8,16,12]{2,1,3,0:T(8,128)S(1)}, s32[1,8,16,12]{2,1,3,0:T(8,128)}, u32[]{:S(2)}) copy-start(s32[1,8,16,12]{2,1,3,0:T(8,128)} %param.17) | copy-start | bytes 18436
  15.0 43.3 %collective-permute-start.14 = (bf16[192,768]{1,0:T(8,128)(2,1)}, bf16[192,768]{1,0:T(8,128)(2,1)}, u32[]{:S(2)}, u32[]{:S(2)}) collective-permute-start(bf16[192,768]{1,0:T(8,128)(2,1)} %get-tuple-element.114), channel_id=1, source_target_pairs={{0,2},{2,4},{4,6},{6,7},{7,5},{5,3},{3,1},{1,0},{8,10},{10,12},{12... | collective-permute-start | bytes 884744 | tf_op jit(solution)/shard_map/ppermute | solution.py:50
  18.0 44.1 %collective-permute-start.15 = (bf16[192,768]{1,0:T(8,128)(2,1)}, bf16[192,768]{1,0:T(8,128)(2,1)S(1)}, u32[]{:S(2)}, u32[]{:S(2)}) collective-permute-start(bf16[192,768]{1,0:T(8,128)(2,1)} %get-tuple-element.114), channel_id=1, source_target_pairs={{2,0},{4,2},{6,4},{7,6},{5,7},{3,5},{1,3},{0,1},{10,8},{12,10},{14... | collective-permute-start | bytes 884744 | tf_op jit(solution)/shard_map/ppermute | solution.py:51
  18.8 15.6 %collective-permute-start = (bf16[1,3,16,1536]{3,2,1,0:T(8,128)(2,1)S(1)}, bf16[1,3,16,1536]{3,2,1,0:T(8,128)(2,1)S(1)}, u32[]{:S(2)}, u32[]{:S(2)}) collective-permute-start(bf16[1,3,16,1536]{3,2,1,0:T(8,128)(2,1)S(1)} %get-tuple-element.126), channel_id=1, source_target_pairs={{0,16},{1,17},{2,18},{3,19},{4,20},{5,21},{6,22},{7,23},{8,24},{9,... | collective-permute-start | bytes 442376 | tf_op jit(solution)/shard_map/ppermute | solution.py:19
  20.4 14.0 %collective-permute-start.1 = (bf16[1,3,16,1536]{3,2,1,0:T(8,128)(2,1)S(1)}, bf16[1,3,16,1536]{3,2,1,0:T(8,128)(2,1)S(1)}, u32[]{:S(2)}, u32[]{:S(2)}) collective-permute-start(bf16[1,3,16,1536]{3,2,1,0:T(8,128)(2,1)S(1)} %get-tuple-element.127), channel_id=1, source_target_pairs={{16,0},{17,1},{18,2},{19,3},{20,4},{21,5},{22,6},{23,7},{24,8},{25... | collective-permute-start | bytes 442376 | tf_op jit(solution)/shard_map/ppermute | solution.py:20
  23.5 40.9 %collective-permute-start.6 = (bf16[192,768]{1,0:T(8,128)(2,1)}, bf16[192,768]{1,0:T(8,128)(2,1)}, u32[]{:S(2)}, u32[]{:S(2)}) collective-permute-start(bf16[192,768]{1,0:T(8,128)(2,1)} %get-tuple-element.110), channel_id=1, source_target_pairs={{0,2},{2,4},{4,6},{6,7},{7,5},{5,3},{3,1},{1,0},{8,10},{10,12},{12... | collective-permute-start | bytes 884744 | tf_op jit(solution)/shard_map/ppermute | solution.py:50
  34.5 8.0 %collective-permute-start.2 = (bf16[1,14,3,1536]{3,2,1,0:T(4,128)(2,1)S(1)}, bf16[1,14,3,1536]{3,2,1,0:T(4,128)(2,1)S(1)}, u32[]{:S(2)}, u32[]{:S(2)}) collective-permute-start(bf16[1,14,3,1536]{3,2,1,0:T(4,128)(2,1)S(1)} %get-tuple-element.120), channel_id=1, source_target_pairs={{0,8},{1,9},{2,10},{3,11},{4,12},{5,13},{6,14},{7,15},{16,24},{17,... | collective-permute-start | bytes 387080 | tf_op jit(solution)/shard_map/ppermute | solution.py:19
  38.0 8.7 %collective-permute-start.3 = (bf16[1,14,3,1536]{3,2,1,0:T(4,128)(2,1)S(1)}, bf16[1,14,3,1536]{3,2,1,0:T(4,128)(2,1)S(1)}, u32[]{:S(2)}, u32[]{:S(2)}) collective-permute-start(bf16[1,14,3,1536]{3,2,1,0:T(4,128)(2,1)S(1)} %get-tuple-element.121), channel_id=1, source_target_pairs={{8,0},{9,1},{10,2},{11,3},{12,4},{13,5},{14,6},{15,7},{24,16},{25,... | collective-permute-start | bytes 387080 | tf_op jit(solution)/shard_map/ppermute | solution.py:20
  42.6 23.3 %collective-permute-start.7 = (bf16[192,768]{1,0:T(8,128)(2,1)}, bf16[192,768]{1,0:T(8,128)(2,1)}, u32[]{:S(2)}, u32[]{:S(2)}) collective-permute-start(bf16[192,768]{1,0:T(8,128)(2,1)} %get-tuple-element.110), channel_id=1, source_target_pairs={{2,0},{4,2},{6,4},{7,6},{5,7},{3,5},{1,3},{0,1},{10,8},{12,10},{14... | collective-permute-start | bytes 884744 | tf_op jit(solution)/shard_map/ppermute | solution.py:51
  46.7 21.8 %collective-permute-start.24 = (bf16[1,128,1536]{2,1,0:T(8,128)(2,1)}, bf16[1,128,1536]{2,1,0:T(8,128)(2,1)}, u32[]{:S(2)}, u32[]{:S(2)}) collective-permute-start(bf16[1,128,1536]{2,1,0:T(8,128)(2,1)} %fusion.64), channel_id=1, source_target_pairs={{8,0},{0,8},{9,1},{1,9},{10,2},{2,10},{11,3},{3,11},{12,4},{4,12},... | collective-permute-start | bytes 1179656 | tf_op jit(solution)/shard_map/ppermute | solution.py:65
  58.3 22.5 %collective-permute-start.4 = (bf16[1,128,1536]{2,1,0:T(8,128)(2,1)S(1)}, bf16[1,128,1536]{2,1,0:T(8,128)(2,1)S(1)}, u32[]{:S(2)}, u32[]{:S(2)}) collective-permute-start(bf16[1,128,1536]{2,1,0:T(8,128)(2,1)S(1)} %bitcast.70), channel_id=1, source_target_pairs={{8,0},{0,8},{9,1},{1,9},{10,2},{2,10},{11,3},{3,11},{12,4},{4,12},... | collective-permute-start | bytes 1179656 | tf_op jit(solution)/shard_map/ppermute | solution.py:65
  62.1 10.2 %collective-permute-start.16 = (bf16[192,768]{1,0:T(8,128)(2,1)}, bf16[192,768]{1,0:T(8,128)(2,1)S(1)}, u32[]{:S(2)}, u32[]{:S(2)}) collective-permute-start(bf16[192,768]{1,0:T(8,128)(2,1)} %collective-permute-done.14), channel_id=1, source_target_pairs={{0,2},{2,4},{4,6},{6,7},{7,5},{5,3},{3,1},{1,0},{8,10},{10,12},{12... | collective-permute-start | bytes 884744 | tf_op jit(solution)/shard_map/ppermute | solution.py:50
  64.4 9.9 %collective-permute-start.17 = (bf16[192,768]{1,0:T(8,128)(2,1)S(1)}, bf16[192,768]{1,0:T(8,128)(2,1)S(1)}, u32[]{:S(2)}, u32[]{:S(2)}) collective-permute-start(bf16[192,768]{1,0:T(8,128)(2,1)S(1)} %collective-permute-done.15), channel_id=1, source_target_pairs={{2,0},{4,2},{6,4},{7,6},{5,7},{3,5},{1,3},{0,1},{10,8},{12,10},{14... | collective-permute-start | bytes 884744 | tf_op jit(solution)/shard_map/ppermute | solution.py:51
  65.9 11.7 %collective-permute-start.8 = (bf16[192,768]{1,0:T(8,128)(2,1)}, bf16[192,768]{1,0:T(8,128)(2,1)S(1)}, u32[]{:S(2)}, u32[]{:S(2)}) collective-permute-start(bf16[192,768]{1,0:T(8,128)(2,1)} %collective-permute-done.6), channel_id=1, source_target_pairs={{0,2},{2,4},{4,6},{6,7},{7,5},{5,3},{3,1},{1,0},{8,10},{10,12},{12... | collective-permute-start | bytes 884744 | tf_op jit(solution)/shard_map/ppermute | solution.py:50
  68.5 10.7 %collective-permute-start.9 = (bf16[192,768]{1,0:T(8,128)(2,1)}, bf16[192,768]{1,0:T(8,128)(2,1)S(1)}, u32[]{:S(2)}, u32[]{:S(2)}) collective-permute-start(bf16[192,768]{1,0:T(8,128)(2,1)} %collective-permute-done.7), channel_id=1, source_target_pairs={{2,0},{4,2},{6,4},{7,6},{5,7},{3,5},{1,3},{0,1},{10,8},{12,10},{14... | collective-permute-start | bytes 884744 | tf_op jit(solution)/shard_map/ppermute | solution.py:51
  72.2 26.4 %collective-permute-start.25 = (bf16[2,128,1536]{2,1,0:T(8,128)(2,1)S(1)}, bf16[2,128,1536]{2,1,0:T(8,128)(2,1)S(1)}, u32[]{:S(2)}, u32[]{:S(2)}) collective-permute-start(bf16[2,128,1536]{2,1,0:T(8,128)(2,1)S(1)} %pad_maximum_fusion.3), channel_id=1, source_target_pairs={{16,0},{0,16},{17,1},{1,17},{18,2},{2,18},{19,3},{3,19},{20,4},{4,... | collective-permute-start | bytes 2359304 | tf_op jit(solution)/shard_map/ppermute | solution.py:65
  74.4 9.9 %collective-permute-start.18 = (bf16[192,768]{1,0:T(8,128)(2,1)S(1)}, bf16[192,768]{1,0:T(8,128)(2,1)S(1)}, u32[]{:S(2)}, u32[]{:S(2)}) collective-permute-start(bf16[192,768]{1,0:T(8,128)(2,1)S(1)} %collective-permute-done.16), channel_id=1, source_target_pairs={{0,2},{2,4},{4,6},{6,7},{7,5},{5,3},{3,1},{1,0},{8,10},{10,12},{12... | collective-permute-start | bytes 884744 | tf_op jit(solution)/shard_map/ppermute | solution.py:50
  77.6 9.9 %collective-permute-start.19 = (bf16[192,768]{1,0:T(8,128)(2,1)S(1)}, bf16[192,768]{1,0:T(8,128)(2,1)S(1)}, u32[]{:S(2)}, u32[]{:S(2)}) collective-permute-start(bf16[192,768]{1,0:T(8,128)(2,1)S(1)} %collective-permute-done.17), channel_id=1, source_target_pairs={{2,0},{4,2},{6,4},{7,6},{5,7},{3,5},{1,3},{0,1},{10,8},{12,10},{14... | collective-permute-start | bytes 884744 | tf_op jit(solution)/shard_map/ppermute | solution.py:51
  79.2 11.4 %collective-permute-start.10 = (bf16[192,768]{1,0:T(8,128)(2,1)S(1)}, bf16[192,768]{1,0:T(8,128)(2,1)S(1)}, u32[]{:S(2)}, u32[]{:S(2)}) collective-permute-start(bf16[192,768]{1,0:T(8,128)(2,1)S(1)} %collective-permute-done.8), channel_id=1, source_target_pairs={{0,2},{2,4},{4,6},{6,7},{7,5},{5,3},{3,1},{1,0},{8,10},{10,12},{12... | collective-permute-start | bytes 884744 | tf_op jit(solution)/shard_map/ppermute | solution.py:50
  80.8 10.8 %collective-permute-start.11 = (bf16[192,768]{1,0:T(8,128)(2,1)S(1)}, bf16[192,768]{1,0:T(8,128)(2,1)S(1)}, u32[]{:S(2)}, u32[]{:S(2)}) collective-permute-start(bf16[192,768]{1,0:T(8,128)(2,1)S(1)} %collective-permute-done.9), channel_id=1, source_target_pairs={{2,0},{4,2},{6,4},{7,6},{5,7},{3,5},{1,3},{0,1},{10,8},{12,10},{14... | collective-permute-start | bytes 884744 | tf_op jit(solution)/shard_map/ppermute | solution.py:51
  84.3 17.4 %collective-permute-start.5 = (bf16[2,128,1536]{2,1,0:T(8,128)(2,1)S(1)}, bf16[2,128,1536]{2,1,0:T(8,128)(2,1)S(1)}, u32[]{:S(2)}, u32[]{:S(2)}) collective-permute-start(bf16[2,128,1536]{2,1,0:T(8,128)(2,1)S(1)} %pad_maximum_fusion.2), channel_id=1, source_target_pairs={{16,0},{0,16},{17,1},{1,17},{18,2},{2,18},{19,3},{3,19},{20,4},{4,... | collective-permute-start | bytes 2359304 | tf_op jit(solution)/shard_map/ppermute | solution.py:65
  87.5 5.5 %collective-permute-start.20 = (bf16[96,768]{1,0:T(8,128)(2,1)S(1)}, bf16[96,768]{1,0:T(8,128)(2,1)S(1)}, u32[]{:S(2)}, u32[]{:S(2)}) collective-permute-start(bf16[96,768]{1,0:T(8,128)(2,1)S(1)} %slice.843), channel_id=1, source_target_pairs={{0,2},{2,4},{4,6},{6,7},{7,5},{5,3},{3,1},{1,0},{8,10},{10,12},{12... | collective-permute-start | bytes 442376 | tf_op jit(solution)/shard_map/ppermute | solution.py:56
  90.6 6.3 %collective-permute-start.21 = (bf16[96,768]{1,0:T(8,128)(2,1)S(1)}, bf16[96,768]{1,0:T(8,128)(2,1)S(1)}, u32[]{:S(2)}, u32[]{:S(2)}) collective-permute-start(bf16[96,768]{1,0:T(8,128)(2,1)S(1)} %slice.844), channel_id=1, source_target_pairs={{2,0},{4,2},{6,4},{7,6},{5,7},{3,5},{1,3},{0,1},{10,8},{12,10},{14... | collective-permute-start | bytes 442376 | tf_op jit(solution)/shard_map/ppermute | solution.py:57
  91.6 5.2 %collective-permute-start.12 = (bf16[96,768]{1,0:T(8,128)(2,1)S(1)}, bf16[96,768]{1,0:T(8,128)(2,1)S(1)}, u32[]{:S(2)}, u32[]{:S(2)}) collective-permute-start(bf16[96,768]{1,0:T(8,128)(2,1)S(1)} %slice.841), channel_id=1, source_target_pairs={{0,2},{2,4},{4,6},{6,7},{7,5},{5,3},{3,1},{1,0},{8,10},{10,12},{12... | collective-permute-start | bytes 442376 | tf_op jit(solution)/shard_map/ppermute | solution.py:56
  93.1 5.6 %collective-permute-start.13 = (bf16[96,768]{1,0:T(8,128)(2,1)S(1)}, bf16[96,768]{1,0:T(8,128)(2,1)S(1)}, u32[]{:S(2)}, u32[]{:S(2)}) collective-permute-start(bf16[96,768]{1,0:T(8,128)(2,1)S(1)} %slice.842), channel_id=1, source_target_pairs={{2,0},{4,2},{6,4},{7,6},{5,7},{3,5},{1,3},{0,1},{10,8},{12,10},{14... | collective-permute-start | bytes 442376 | tf_op jit(solution)/shard_map/ppermute | solution.py:57
  116.1 6.8 %collective-permute-start.26 = (bf16[2,8,16,1536]{3,2,1,0:T(8,128)(2,1)}, bf16[2,8,16,1536]{3,2,1,0:T(8,128)(2,1)}, u32[]{:S(2)}, u32[]{:S(2)}) collective-permute-start(bf16[2,8,16,1536]{3,2,1,0:T(8,128)(2,1)} %bitcast.23), channel_id=1, source_target_pairs={{16,0},{0,16},{17,1},{1,17},{18,2},{2,18},{19,3},{3,19},{20,4},{4,... | collective-permute-start | bytes 2359304 | tf_op jit(solution)/shard_map/ppermute | solution.py:65
  122.4 4.3 %collective-permute-start.22 = (bf16[2,8,16,1536]{3,2,1,0:T(8,128)(2,1)}, bf16[2,8,16,1536]{3,2,1,0:T(8,128)(2,1)}, u32[]{:S(2)}, u32[]{:S(2)}) collective-permute-start(bf16[2,8,16,1536]{3,2,1,0:T(8,128)(2,1)} %bitcast.18), channel_id=1, source_target_pairs={{16,0},{0,16},{17,1},{1,17},{18,2},{2,18},{19,3},{3,19},{20,4},{4,... | collective-permute-start | bytes 2359304 | tf_op jit(solution)/shard_map/ppermute | solution.py:65
  125.9 12.0 %collective-permute-start.27 = (bf16[1,8,16,1536]{3,2,1,0:T(8,128)(2,1)S(1)}, bf16[1,8,16,1536]{3,2,1,0:T(8,128)(2,1)S(1)}, u32[]{:S(2)}, u32[]{:S(2)}) collective-permute-start(bf16[1,8,16,1536]{3,2,1,0:T(8,128)(2,1)S(1)} %slice.1422), channel_id=1, source_target_pairs={{8,0},{0,8},{9,1},{1,9},{10,2},{2,10},{11,3},{3,11},{12,4},{4,12},... | collective-permute-start | bytes 1179656 | tf_op jit(solution)/shard_map/ppermute | solution.py:65
  128.1 23.2 %copy-start = (f32[2,8,16,1536]{3,2,1,0:T(8,128)}, f32[2,8,16,1536]{3,2,1,0:T(8,128)S(1)}, u32[]{:S(2)}) copy-start(f32[2,8,16,1536]{3,2,1,0:T(8,128)S(1)} %convert_add_fusion.1) | copy-start | bytes 4718596
  128.2 23.2 %collective-permute-start.23 = (bf16[1,8,16,1536]{3,2,1,0:T(8,128)(2,1)S(1)}, bf16[1,8,16,1536]{3,2,1,0:T(8,128)(2,1)S(1)}, u32[]{:S(2)}, u32[]{:S(2)}) collective-permute-start(bf16[1,8,16,1536]{3,2,1,0:T(8,128)(2,1)S(1)} %slice.1423), channel_id=1, source_target_pairs={{8,0},{0,8},{9,1},{1,9},{10,2},{2,10},{11,3},{3,11},{12,4},{4,12},... | collective-permute-start | bytes 1179656 | tf_op jit(solution)/shard_map/ppermute | solution.py:65
  144.8 15.8 %copy-start.55 = (f32[1536]{0:T(1024)S(1)}, f32[1536]{0:T(1024)}, u32[]{:S(2)}) copy-start(f32[1536]{0:T(1024)} %param.26) | copy-start | bytes 18436
  155.6 4.0 %collective-permute-start.32 = (f32[32,1536]{1,0:T(8,128)S(1)}, f32[32,1536]{1,0:T(8,128)S(1)}, u32[]{:S(2)}, u32[]{:S(2)}) collective-permute-start(f32[32,1536]{1,0:T(8,128)S(1)} %constant_dynamic-slice_fusion), channel_id=1, source_target_pairs={{0,16},{16,0},{1,17},{17,1},{2,18},{18,2},{3,19},{19,3},{4,20},{20... | collective-permute-start | bytes 589832 | tf_op jit(solution)/shard_map/ppermute | solution.py:85
  155.7 10.4 %collective-permute-start.28 = (bf16[1,3,16,1536]{3,2,1,0:T(8,128)(2,1)S(1)}, bf16[1,3,16,1536]{3,2,1,0:T(8,128)(2,1)S(1)}, u32[]{:S(2)}, u32[]{:S(2)}) collective-permute-start(bf16[1,3,16,1536]{3,2,1,0:T(8,128)(2,1)S(1)} %get-tuple-element.124), channel_id=1, source_target_pairs={{0,16},{1,17},{2,18},{3,19},{4,20},{5,21},{6,22},{7,23},{8,24},{9,... | collective-permute-start | bytes 442376 | tf_op jit(solution)/shard_map/ppermute | solution.py:19
  158.1 8.0 %collective-permute-start.29 = (bf16[1,3,16,1536]{3,2,1,0:T(8,128)(2,1)S(1)}, bf16[1,3,16,1536]{3,2,1,0:T(8,128)(2,1)S(1)}, u32[]{:S(2)}, u32[]{:S(2)}) collective-permute-start(bf16[1,3,16,1536]{3,2,1,0:T(8,128)(2,1)S(1)} %get-tuple-element.125), channel_id=1, source_target_pairs={{16,0},{17,1},{18,2},{19,3},{20,4},{21,5},{22,6},{23,7},{24,8},{25... | collective-permute-start | bytes 442376 | tf_op jit(solution)/shard_map/ppermute | solution.py:20
  159.7 5.6 %collective-permute-start.33 = (bf16[32,1536]{1,0:T(8,128)(2,1)S(1)}, bf16[32,1536]{1,0:T(8,128)(2,1)S(1)}, u32[]{:S(2)}, u32[]{:S(2)}) collective-permute-start(bf16[32,1536]{1,0:T(8,128)(2,1)S(1)} %add_convert_fusion.5), channel_id=1, source_target_pairs={{0,8},{8,0},{1,9},{9,1},{2,10},{10,2},{3,11},{11,3},{4,12},{12,4},... | collective-permute-start | bytes 294920 | tf_op jit(solution)/shard_map/ppermute | solution.py:85
  165.3 4.9 %collective-permute-start.34 = (bf16[32,1536]{1,0:T(8,128)(2,1)S(1)}, bf16[32,1536]{1,0:T(8,128)(2,1)S(1)}, u32[]{:S(2)}, u32[]{:S(2)}) collective-permute-start(bf16[32,1536]{1,0:T(8,128)(2,1)S(1)} %add_convert_fusion.4), channel_id=1, source_target_pairs={{0,1},{1,0},{2,3},{3,2},{4,5},{5,4},{6,7},{7,6},{8,9},{9,8},{10,11... | collective-permute-start | bytes 294920 | tf_op jit(solution)/shard_map/ppermute | solution.py:85
  170.2 6.8 %collective-permute-start.35 = (bf16[32,1536]{1,0:T(8,128)(2,1)S(1)}, bf16[32,1536]{1,0:T(8,128)(2,1)S(1)}, u32[]{:S(2)}, u32[]{:S(2)}) collective-permute-start(bf16[32,1536]{1,0:T(8,128)(2,1)S(1)} %add_convert_fusion.3), channel_id=1, source_target_pairs={{0,2},{1,3},{2,0},{3,1},{4,6},{5,7},{6,4},{7,5},{8,10},{9,11},{10,... | collective-permute-start | bytes 294920 | tf_op jit(solution)/shard_map/ppermute | solution.py:85
  172.4 11.1 %copy-start.12 = (f32[1536]{0:T(1024)S(1)}, f32[1536]{0:T(1024)}, u32[]{:S(2)}) copy-start(f32[1536]{0:T(1024)} %get-tuple-element.57) | copy-start | bytes 18436
  172.4 11.1 %copy-start.13 = (f32[1536]{0:T(1024)S(1)}, f32[1536]{0:T(1024)}, u32[]{:S(2)}) copy-start(f32[1536]{0:T(1024)} %get-tuple-element.58) | copy-start | bytes 18436
  172.5 11.1 %copy-start.14 = (f32[1536]{0:T(1024)S(1)}, f32[1536]{0:T(1024)}, u32[]{:S(2)}) copy-start(f32[1536]{0:T(1024)} %get-tuple-element.59) | copy-start | bytes 18436
  172.5 11.1 %copy-start.15 = (f32[1536]{0:T(1024)S(1)}, f32[1536]{0:T(1024)}, u32[]{:S(2)}) copy-start(f32[1536]{0:T(1024)} %get-tuple-element.60) | copy-start | bytes 18436
  172.5 11.1 %copy-start.16 = (f32[1536]{0:T(1024)S(1)}, f32[1536]{0:T(1024)}, u32[]{:S(2)}) copy-start(f32[1536]{0:T(1024)} %get-tuple-element.61) | copy-start | bytes 18436
  172.5 11.1 %copy-start.17 = (f32[1536]{0:T(1024)S(1)}, f32[1536]{0:T(1024)}, u32[]{:S(2)}) copy-start(f32[1536]{0:T(1024)} %get-tuple-element.62) | copy-start | bytes 18436
  172.5 11.1 %copy-start.18 = (f32[1536]{0:T(1024)S(1)}, f32[1536]{0:T(1024)}, u32[]{:S(2)}) copy-start(f32[1536]{0:T(1024)} %get-tuple-element.63) | copy-start | bytes 18436
  172.5 11.1 %copy-start.19 = (f32[1536]{0:T(1024)S(1)}, f32[1536]{0:T(1024)}, u32[]{:S(2)}) copy-start(f32[1536]{0:T(1024)} %get-tuple-element.64) | copy-start | bytes 18436
  172.5 11.1 %copy-start.20 = (f32[1536]{0:T(1024)S(1)}, f32[1536]{0:T(1024)}, u32[]{:S(2)}) copy-start(f32[1536]{0:T(1024)} %get-tuple-element.65) | copy-start | bytes 18436
  172.5 11.1 %copy-start.21 = (f32[1536]{0:T(1024)S(1)}, f32[1536]{0:T(1024)}, u32[]{:S(2)}) copy-start(f32[1536]{0:T(1024)} %get-tuple-element.66) | copy-start | bytes 18436
  172.5 11.1 %copy-start.22 = (f32[1536]{0:T(1024)S(1)}, f32[1536]{0:T(1024)}, u32[]{:S(2)}) copy-start(f32[1536]{0:T(1024)} %get-tuple-element.67) | copy-start | bytes 18436
  172.5 11.1 %copy-start.23 = (f32[1536]{0:T(1024)S(1)}, f32[1536]{0:T(1024)}, u32[]{:S(2)}) copy-start(f32[1536]{0:T(1024)} %get-tuple-element.68) | copy-start | bytes 18436
  172.6 11.1 %copy-start.24 = (f32[1536]{0:T(1024)S(1)}, f32[1536]{0:T(1024)}, u32[]{:S(2)}) copy-start(f32[1536]{0:T(1024)} %get-tuple-element.69) | copy-start | bytes 18436
  172.6 11.1 %copy-start.25 = (f32[1536]{0:T(1024)S(1)}, f32[1536]{0:T(1024)}, u32[]{:S(2)}) copy-start(f32[1536]{0:T(1024)} %get-tuple-element.70) | copy-start | bytes 18436
  172.6 11.1 %copy-start.26 = (f32[1536]{0:T(1024)S(1)}, f32[1536]{0:T(1024)}, u32[]{:S(2)}) copy-start(f32[1536]{0:T(1024)} %get-tuple-element.71) | copy-start | bytes 18436
  172.6 11.1 %copy-start.27 = (f32[1536]{0:T(1024)S(1)}, f32[1536]{0:T(1024)}, u32[]{:S(2)}) copy-start(f32[1536]{0:T(1024)} %get-tuple-element.72) | copy-start | bytes 18436
  172.6 11.1 %copy-start.28 = (f32[1536]{0:T(1024)S(1)}, f32[1536]{0:T(1024)}, u32[]{:S(2)}) copy-start(f32[1536]{0:T(1024)} %get-tuple-element.73) | copy-start | bytes 18436
  172.6 11.1 %copy-start.29 = (f32[1536]{0:T(1024)S(1)}, f32[1536]{0:T(1024)}, u32[]{:S(2)}) copy-start(f32[1536]{0:T(1024)} %get-tuple-element.74) | copy-start | bytes 18436
  172.6 11.1 %copy-start.30 = (f32[1536]{0:T(1024)S(1)}, f32[1536]{0:T(1024)}, u32[]{:S(2)}) copy-start(f32[1536]{0:T(1024)} %get-tuple-element.75) | copy-start | bytes 18436
  172.6 11.1 %copy-start.31 = (f32[1536]{0:T(1024)S(1)}, f32[1536]{0:T(1024)}, u32[]{:S(2)}) copy-start(f32[1536]{0:T(1024)} %get-tuple-element.76) | copy-start | bytes 18436
  172.6 11.1 %copy-start.32 = (f32[1536]{0:T(1024)S(1)}, f32[1536]{0:T(1024)}, u32[]{:S(2)}) copy-start(f32[1536]{0:T(1024)} %get-tuple-element.77) | copy-start | bytes 18436
  172.6 11.1 %copy-start.33 = (f32[1536]{0:T(1024)S(1)}, f32[1536]{0:T(1024)}, u32[]{:S(2)}) copy-start(f32[1536]{0:T(1024)} %get-tuple-element.78) | copy-start | bytes 18436
  172.7 11.1 %copy-start.34 = (f32[1536]{0:T(1024)S(1)}, f32[1536]{0:T(1024)}, u32[]{:S(2)}) copy-start(f32[1536]{0:T(1024)} %get-tuple-element.79) | copy-start | bytes 18436
  172.8 6.6 %collective-permute-start.30 = (bf16[1,14,3,1536]{3,2,1,0:T(4,128)(2,1)S(1)}, bf16[1,14,3,1536]{3,2,1,0:T(4,128)(2,1)S(1)}, u32[]{:S(2)}, u32[]{:S(2)}) collective-permute-start(bf16[1,14,3,1536]{3,2,1,0:T(4,128)(2,1)S(1)} %get-tuple-element.116), channel_id=1, source_target_pairs={{0,8},{1,9},{2,10},{3,11},{4,12},{5,13},{6,14},{7,15},{16,24},{17,... | collective-permute-start | bytes 387080 | tf_op jit(solution)/shard_map/ppermute | solution.py:19
  175.7 7.3 %collective-permute-start.31 = (bf16[1,14,3,1536]{3,2,1,0:T(4,128)(2,1)S(1)}, bf16[1,14,3,1536]{3,2,1,0:T(4,128)(2,1)S(1)}, u32[]{:S(2)}, u32[]{:S(2)}) collective-permute-start(bf16[1,14,3,1536]{3,2,1,0:T(4,128)(2,1)S(1)} %get-tuple-element.117), channel_id=1, source_target_pairs={{8,0},{9,1},{10,2},{11,3},{12,4},{13,5},{14,6},{15,7},{24,16},{25,... | collective-permute-start | bytes 387080 | tf_op jit(solution)/shard_map/ppermute | solution.py:20
  177.1 6.3 %collective-permute-start.36 = (bf16[32,1536]{1,0:T(8,128)(2,1)S(1)}, bf16[32,1536]{1,0:T(8,128)(2,1)S(1)}, u32[]{:S(2)}, u32[]{:S(2)}) collective-permute-start(bf16[32,1536]{1,0:T(8,128)(2,1)S(1)} %add_convert_fusion.2), channel_id=1, source_target_pairs={{0,4},{1,5},{2,6},{3,7},{4,0},{5,1},{6,2},{7,3},{8,12},{9,13},{10,... | collective-permute-start | bytes 294920 | tf_op jit(solution)/shard_map/ppermute | solution.py:85
  183.4 7.6 %collective-permute-start.37 = (f32[32,1536]{1,0:T(8,128)S(1)}, f32[32,1536]{1,0:T(8,128)S(1)}, u32[]{:S(2)}, u32[]{:S(2)}) collective-permute-start(f32[32,1536]{1,0:T(8,128)S(1)} %convert_add_fusion.2), channel_id=1, source_target_pairs={{0,16},{16,0},{1,17},{17,1},{2,18},{18,2},{3,19},{19,3},{4,20},{20... | collective-permute-start | bytes 589832 | tf_op jit(solution)/shard_map/ppermute | solution.py:85
  (33 other events, 275.1 us)

commit v2 on v0

v2 whole, which is shorter than its diff:
```python
import functools

import jax
import jax.numpy as jnp
from jax import lax
from jax.experimental import pallas as pl
from jax.experimental.pallas import tpu as pltpu
from jax.sharding import PartitionSpec as P

CG = 128
KW = 7
HALO = 3
LANES = 128
SUBLANES = 8
BF = jnp.bfloat16
F32 = jnp.float32
MIB = 1024 * 1024
GELU_A = 0.7978845608028654
GELU_B = 0.044715


def vmem(count):
    return [pl.BlockSpec(memory_space=pltpu.VMEM)] * count


def anywhere(count):
    return [pl.BlockSpec(memory_space=pl.ANY)] * count


def params(mib):
    return pltpu.CompilerParams(vmem_limit_bytes=mib * MIB)


def cost(flops, moved, special=0):
    return pl.CostEstimate(flops=flops, bytes_accessed=moved, transcendentals=special)


def shaped(shape, dtype):
    return jax.ShapeDtypeStruct(tuple(shape), dtype)


def swap(a, **masks):
    axes = tuple(masks)
    mask = 0
    total = 1
    for axis in axes:
        n = lax.axis_size(axis)
        mask, total = mask * n + masks[axis], total * n
    return lax.ppermute(a, axes, [(i, i ^ mask) for i in range(total)])


def shift(a, axis, k):
    n = lax.axis_size(axis)
    return lax.ppermute(a, axis, [((i + k) % n, i) for i in range(n)])


def sides(axis):
    return (0,) if lax.axis_size(axis) == 2 else (-1, 1)


def side_pairs(n, side):
    if side == 0:
        return [(0, 1), (1, 0)]
    return [(i, i - side) for i in range(n) if 0 <= i - side < n]


def exchange_edges(pieces):
    n, m = lax.axis_size("sx"), lax.axis_size("sy")
    got = {}
    for (a, b), piece in pieces.items():
        rows = [(i, i) for i in range(n)] if a is None else side_pairs(n, a)
        cols = [(j, j) for j in range(m)] if b is None else side_pairs(m, b)
        pairs = [(i * m + j, k * m + l) for i, k in rows for j, l in cols]
        got[a, b] = lax.ppermute(piece, ("sx", "sy"), pairs)
    return got


def edge_keys():
    rows, cols = sides("sx"), sides("sy")
    return [(a, None) for a in rows] + [(None, b) for b in cols] + [(a, b) for a in rows for b in cols]


def place_of(index, n):
    if n != 8:
        return index
    return jnp.where(index % 2 == 0, index // 2, 7 - index // 2)


def at_place(place, n):
    if n != 8:
        return place
    return jnp.where(place < 4, 2 * place, 15 - 2 * place)


def ring_pairs(n):
    order = [0, 2, 4, 6, 7, 5, 3, 1] if n == 8 else list(range(n))
    forth = [(order[k], order[(k + 1) % n]) for k in range(n)]
    return forth, [(d, s) for s, d in forth]


def ring_gather(block):
    n, rows = lax.axis_size("fsdp"), block.shape[0]
    forth, back = ring_pairs(n)
    pieces, where = [block], [(0, 0, rows)]
    one = two = block
    for k in range(1, (n + 1) // 2):
        one = lax.ppermute(one, "fsdp", forth)
        two = lax.ppermute(two, "fsdp", back)
        pieces += [one, two]
        where += [(-k, 0, rows), (k, 0, rows)]
    if n % 2 == 0:
        half = rows // 2 if rows % 32 == 0 else 0
        if half:
            pieces.append(lax.ppermute(one[:half], "fsdp", forth))
            where.append((n // 2, 0, half))
        pieces.append(lax.ppermute(two[half:], "fsdp", back))
        where.append((n // 2, half, rows - half))
    return pieces, where


def gather_tile(a):
    out = []
    for t in range(lax.axis_size("sy")):
        mine = a if t == 0 else shift(a, "sy", t)
        out.append([mine] + [shift(mine, "sx", s) for s in range(1, lax.axis_size("sx"))])
    return [piece for group in out for piece in group]


def reduce_cores(pieces):
    return [pieces[0]] + [shift(pieces[s], "sx", -s) for s in range(1, len(pieces))]


def add_up(terms):
    total = terms[0].astype(F32)
    for term in terms[1:]:
        total = total + term.astype(F32)
    return total


def sum_rows(keep, send):
    total = keep + swap(send, sx=1)
    quarter = total.shape[0] // 4
    parts = total.reshape(4, quarter, total.shape[1])
    me = 2 * (lax.axis_index("sy") % 2) + lax.axis_index("fsdp") % 2

    def part(k):
        return lax.dynamic_index_in_dim(parts, me ^ k, 0, keepdims=False)

    total = (part(0) + swap(part(1), fsdp=1)) + (swap(part(2), sy=1) + swap(part(3), sy=1, fsdp=1))
    masks = []
    for axis in ("sx", "sy", "fsdp"):
        bit = 2
        while bit < lax.axis_size(axis):
            masks.append((axis, bit))
            bit *= 2
    while masks:
        group, masks = masks[:2], masks[2:]
        rounded = total.astype(BF)
        (axis, bit) = group[0]
        total = rounded.astype(F32) + swap(rounded, **{axis: bit}).astype(F32)
        if len(group) == 2:
            (other, more) = group[1]
            both = {axis: bit + more} if axis == other else {axis: bit, other: more}
            total = total + (swap(rounded, **{other: more}).astype(F32) + swap(rounded, **both).astype(F32))
    mine = [total, swap(total, fsdp=1), swap(total, sy=1), swap(total, sy=1, fsdp=1)]
    return mine, [swap(piece, sx=1) for piece in mine]


def write_edges(tile, refs):
    rows, cols = tile.shape[:2]
    for (a, b), ref in zip(edge_keys(), refs, strict=True):
        if a is None:
            value = tile[...]
        elif a == 0:
            first = jnp.where(lax.axis_index("sx") == 0, rows - HALO, 0)
            value = tile[pl.ds(first, HALO)]
        else:
            value = tile[pl.ds(0 if a > 0 else rows - HALO, HALO)]
        if b == 0:
            low, high = value[:, :HALO], value[:, cols - HALO :]
            value = jnp.where(lax.axis_index("sy") == 0, high, low)
        elif b is not None:
            value = value[:, :HALO] if b > 0 else value[:, cols - HALO :]
        ref[...] = value.astype(BF)


def edge_shapes(rows, cols, chans):
    return [shaped((rows if a is None else HALO, cols if b is None else HALO, chans), BF) for a, b in edge_keys()]


def fill_padded(own, refs, padded):
    rows, cols = own.shape[:2]
    at = {-1: 0, None: HALO}
    sx, sy = lax.axis_index("sx"), lax.axis_index("sy")
    there = {("sx", -1): sx > 0, ("sx", 1): sx < lax.axis_size("sx") - 1}
    there |= {("sy", -1): sy > 0, ("sy", 1): sy < lax.axis_size("sy") - 1}
    padded[pl.ds(HALO, rows), pl.ds(HALO, cols), :] = own[...].astype(F32)
    for (a, b), ref in zip(edge_keys(), refs, strict=True):
        value = ref[...].astype(F32)
        for i in (-1, 1) if a == 0 else (a,):
            for j in (-1, 1) if b == 0 else (b,):
                on = jnp.float32(1)
                if i is not None:
                    on = on * there["sx", i].astype(F32)
                if j is not None:
                    on = on * there["sy", j].astype(F32)
                first_row = HALO + rows if i == 1 else at[i]
                first_col = HALO + cols if j == 1 else at[j]
                spot = (pl.ds(first_row, ref.shape[0]), pl.ds(first_col, ref.shape[1]))
                padded[spot[0], spot[1], :] = value * on


def prepare_kernel(code, expo, scaled, *edges):
    rows, cols, chans = code.shape
    for r in range(rows):
        e = expo[r]
        up = jnp.left_shift(1, jnp.maximum(e, 0)).astype(F32)
        down = jnp.left_shift(1, jnp.maximum(-e, 0)).astype(F32)
        factor = jnp.where(e >= 0, up, 1.0 / down)
        for g in range(chans // CG):
            lanes = pl.ds(g * CG, CG)
            scaled[r, :, lanes] = (code[r, :, lanes].astype(F32) * factor[:, g : g + 1]).astype(BF)
    write_edges(scaled, edges)


def prepare(code, expo):
    rows, cols, chans = code.shape
    outs = [shaped(code.shape, BF)] + edge_shapes(rows, cols, chans)
    return pl.pallas_call(
        prepare_kernel,
        out_shape=outs,
        in_specs=vmem(2),
        out_specs=vmem(len(outs)),
        compiler_params=params(16),
        cost_estimate=cost(code.size, 8 * code.size),
        name="prepare",
    )(code, expo)


def convolve(padded, weights, start, put, rows, cols, chans, flip):
    parts = range(cols // SUBLANES)

    def group(g, carry):
        lanes = pl.ds(pl.multiple_of(g * LANES, LANES), LANES)
        acc = [[start(lanes, r, k) for k in parts] for r in range(rows)]
        for j in range(KW):
            taps = []
            for i in range(KW):
                at = (KW - 1 - i) * KW + (KW - 1 - j) if flip else i * KW + j
                taps.append(weights[at, :, lanes])
            for p in range(rows + 2 * HALO):
                for k in parts:
                    piece = padded[p, pl.ds(j + k * SUBLANES, SUBLANES), lanes]
                    for i in range(KW):
                        if 0 <= p - i < rows:
                            acc[p - i][k] = acc[p - i][k] + taps[i] * piece
        for r in range(rows):
            for k in parts:
                put(lanes, r, k, acc[r][k])
        return carry

    lax.fori_loop(0, chans // LANES, group, 0)


def spread_taps(weights, wide):
    for t in range(weights.shape[0]):
        wide[t] = jnp.broadcast_to(weights[pl.ds(t, 1), :], wide.shape[1:])


def conv_norm_kernel(own, *refs):
    count = len(edge_keys())
    edges, refs = refs[:count], refs[count:]
    weights, bias, gain, shift_, padded, normed, rstd, out, wide, conv = refs
    rows, cols, chans = own.shape
    fill_padded(own, edges, padded)
    spread_taps(weights, wide)

    def start(lanes, r, k):
        return jnp.broadcast_to(bias[:, lanes], (SUBLANES, LANES))

    def put(lanes, r, k, value):
        conv[pl.ds(r * cols + k * SUBLANES, SUBLANES), lanes] = value

    convolve(padded, wide, start, put, rows, cols, chans, False)
    for r in range(rows):
        here = pl.ds(r * cols, cols)
        value = conv[here, :]
        centred = value - jnp.mean(value, axis=-1, keepdims=True)
        scale = lax.rsqrt(jnp.mean(centred * centred, axis=-1, keepdims=True) + 1e-06)
        unit = centred * scale
        normed[here, :] = unit
        rstd[here, :] = jnp.broadcast_to(scale, (cols, LANES))
        out[here, :] = (unit * gain[...] + shift_[...]).astype(BF)


def conv_norm(own, edges, weights, bias, gain, shift_):
    rows, cols, chans = own.shape
    spots = rows * cols
    return pl.pallas_call(
        conv_norm_kernel,
        out_shape=(
            shaped((rows + 2 * HALO, cols + 8, chans), F32),
            shaped((spots, chans), F32),
            shaped((spots, LANES), F32),
            shaped((spots, chans), BF),
        ),
        in_specs=vmem(5 + len(edges)),
        out_specs=vmem(4),
        scratch_shapes=[
            pltpu.VMEM((weights.shape[0], SUBLANES, chans), F32),
            pltpu.VMEM((spots, chans), F32),
        ],
        compiler_params=params(20),
        cost_estimate=cost(2 * KW * KW * spots * chans, 10 * spots * chans),
        name="conv_norm",
    )(own, *edges, weights, bias, gain, shift_)


def norm_back_kernel(n_terms, *refs):
    terms, refs = refs[:n_terms], refs[n_terms:]
    normed, rstd, gain, padded, scale_term, d_conv, keep, send, *edges, sums = refs
    rows, cols = d_conv.shape[:2]
    chans = normed.shape[-1]
    gain_sum = jnp.zeros((SUBLANES, chans), F32)
    for r in range(rows):
        here = pl.ds(r * cols, cols)
        d_ln = add_up([term[here, :] for term in terms])
        unit = normed[here, :]
        d_unit = d_ln * unit
        for k in range(0, cols, SUBLANES):
            gain_sum = gain_sum + d_unit[k : k + SUBLANES]
        d_norm = d_ln * gain[...]
        mean_one = jnp.mean(d_norm, axis=-1, keepdims=True)
        mean_two = jnp.mean(d_unit * gain[...], axis=-1, keepdims=True)
        d_conv[r] = rstd[here, :1] * (d_norm - mean_one - unit * mean_two)
    write_edges(d_conv, edges)
    taps = KW * KW
    half = keep.shape[0]

    def store(row, lanes, value):
        sums[row // half, pl.ds(row % half, 1), lanes] = value

    for row in range(taps + 2, 2 * half):
        store(row, slice(None), jnp.zeros((1, chans), F32))
    store(taps, slice(None), jnp.sum(gain_sum, axis=0, keepdims=True))
    store(taps + 1, slice(None), scale_term[...])
    parts = range(cols // SUBLANES)

    def group(g, carry):
        lanes = pl.ds(pl.multiple_of(g * LANES, LANES), LANES)
        grads = [[d_conv[r, pl.ds(k * SUBLANES, SUBLANES), lanes] for k in parts] for r in range(rows)]
        for j in range(KW):
            acc = [jnp.zeros((SUBLANES, LANES), F32) for _ in range(KW)]
            for p in range(rows + 2 * HALO):
                for k in parts:
                    piece = padded[p, pl.ds(j + k * SUBLANES, SUBLANES), lanes]
                    for i in range(KW):
                        if 0 <= p - i < rows:
                            acc[i] = acc[i] + grads[p - i][k] * piece
            for i in range(KW):
                store(i * KW + j, lanes, jnp.sum(acc[i], axis=0, keepdims=True))
        return carry

    lax.fori_loop(0, chans // LANES, group, 0)
    core = lax.axis_index("sx") % 2
    keep[...] = sums[core]
    send[...] = sums[1 - core]


def norm_back(terms, normed, rstd, gain, padded, scale_term):
    spots, chans = normed.shape
    rows = padded.shape[0] - 2 * HALO
    cols = spots // rows
    half = -(-(KW * KW + 2) // 64) * 32
    outs = [shaped((rows, cols, chans), F32), shaped((half, chans), F32), shaped((half, chans), F32)]
    outs += edge_shapes(rows, cols, chans)
    return pl.pallas_call(
        functools.partial(norm_back_kernel, len(terms)),
        out_shape=outs,
        in_specs=vmem(5 + len(terms)),
        out_specs=vmem(len(outs)),
        scratch_shapes=[pltpu.VMEM((2, half, chans), F32)],
        compiler_params=params(20),
        cost_estimate=cost(2 * KW * KW * spots * chans, 16 * spots * chans),
        name="norm_back",
    )(*terms, normed, rstd, gain, padded, scale_term)


def conv_back_kernel(own, *refs):
    count = len(edge_keys())
    edges, refs = refs[:count], refs[count:]
    weights, cotangent, out, padded, wide = refs
    rows, cols, chans = own.shape
    fill_padded(own, edges, padded)
    spread_taps(weights, wide)

    def start(lanes, r, k):
        return cotangent[r, pl.ds(k * SUBLANES, SUBLANES), lanes].astype(F32)

    def put(lanes, r, k, value):
        out[r, pl.ds(k * SUBLANES, SUBLANES), lanes] = value.astype(BF)

    convolve(padded, wide, start, put, rows, cols, chans, True)


def conv_back(own, edges, weights, cotangent):
    rows, cols, chans = own.shape
    return pl.pallas_call(
        conv_back_kernel,
        out_shape=shaped((rows, cols, chans), BF),
        in_specs=vmem(3 + len(edges)),
        out_specs=pl.BlockSpec(memory_space=pltpu.VMEM),
        scratch_shapes=[
            pltpu.VMEM((rows + 2 * HALO, cols + 8, chans), F32),
            pltpu.VMEM((weights.shape[0], SUBLANES, chans), F32),
        ],
        compiler_params=params(20),
        cost_estimate=cost(2 * KW * KW * rows * cols * chans, 10 * rows * cols * chans),
        name="conv_back",
    )(own, *edges, weights, cotangent)


def start_copies(jobs, sems, first):
    copies = []
    for k, (src, dst) in enumerate(jobs):
        copies.append(pltpu.make_async_copy(src, dst, sems.at[first + k]))
        copies[-1].start()
    return copies


def wait_all(copies):
    for copy in copies:
        copy.wait()


def block_jobs(pieces, where, whole):
    n = lax.axis_size("fsdp")
    rows = whole.shape[0] // n
    place = place_of(lax.axis_index("fsdp"), n)
    jobs = []
    for piece, (k, first, count) in zip(pieces, where, strict=True):
        owner = at_place(lax.rem(place + (k + n), n), n)
        begin = pl.multiple_of(owner * rows + first, 16)
        jobs.append((piece, whole.at[pl.ds(begin, count)]))
    return jobs


def row_jobs(pieces, whole):
    count = whole.shape[0] // len(pieces)
    return [(piece, whole.at[pl.ds(k * count, count)]) for k, piece in enumerate(pieces)]


def hidden_tiles(hidden):
    width = 256 if hidden % 256 == 0 else LANES
    return [pl.ds(k, width) for k in range(0, hidden, width)]


def up_kernel(where, tiles, *refs):
    blocks, refs = refs[: len(where)], refs[len(where) :]
    lns, refs = refs[:tiles], refs[tiles:]
    cots, refs = refs[:tiles], refs[tiles:]
    bias, scale, act, slope, whole, d_mlp, ln_all, cot_all, sems = refs
    one = start_copies(block_jobs(blocks, where, whole), sems, 0)
    two = start_copies(row_jobs(lns, ln_all), sems, len(one))
    three = start_copies(row_jobs(cots, cot_all), sems, len(one) + len(two))
    wait_all(three)
    d_mlp[...] = (scale[...] * cot_all[...].astype(F32)).astype(BF)
    wait_all(one + two)
    hidden = whole.shape[1]
    quarter = lax.axis_index("sx") * lax.axis_size("sy") + lax.axis_index("sy")
    for tile in hidden_tiles(hidden):
        columns = pl.ds(pl.multiple_of(quarter * hidden + tile.start, LANES), tile.size)
        v = jnp.dot(ln_all[...], whole[:, tile], preferred_element_type=F32) + bias[:, columns]
        square = v * v
        th = jnp.tanh(GELU_A * (v + GELU_B * (square * v)))
        half = 0.5 + 0.5 * th
        act[:, tile] = (v * half).astype(BF)
        slope[:, tile] = half + 0.5 * v * (1.0 - th * th) * (GELU_A * (1.0 + 3.0 * GELU_B * square))


def up_part(blocks, where, lns, cots, bias, scale):
    spots, chans = lns[0].shape
    rows, hidden = blocks[0].shape
    n = lax.axis_size("fsdp")
    tiles = len(lns)
    total = tiles * spots
    count = len(blocks) + 2 * tiles
    return pl.pallas_call(
        functools.partial(up_kernel, where, tiles),
        out_shape=(
            shaped((total, hidden), BF),
            shaped((total, hidden), F32),
            shaped((n * rows, hidden), BF),
            shaped((total, chans), BF),
        ),
        in_specs=anywhere(count) + vmem(2),
        out_specs=vmem(4),
        scratch_shapes=[
            pltpu.VMEM((total, chans), BF),
            pltpu.VMEM((total, chans), BF),
            pltpu.SemaphoreType.DMA((count,)),
        ],
        compiler_params=params(28),
        cost_estimate=cost(2 * total * chans * hidden, 8 * total * chans, total * hidden),
        name="up_part",
    )(*blocks, *lns, *cots, bias, scale)


def contract_last(a, b):
    return lax.dot_general(a, b, (((1,), (1,)), ((), ())), preferred_element_type=F32)


def channel_tiles(chans):
    width = 512 if chans % 512 == 0 else LANES
    return [pl.ds(k, width) for k in range(0, chans, width)]


def write_pieces(value, tile, outs):
    spots = outs[0].shape[0]
    for k, out in enumerate(outs):
        out[:, tile] = value[k * spots : (k + 1) * spots].astype(BF)


def down_kernel(where, n_near, *refs):
    blocks, refs = refs[: len(where)], refs[len(where) :]
    d_mlp, slope, up, whole, d_pre, *far, d_mlp_in, slope_in, up_in, sems = refs
    one = start_copies(block_jobs(blocks, where, whole), sems, 0)
    two = start_copies([(d_mlp, d_mlp_in), (slope, slope_in), (up, up_in)], sems, len(one))
    wait_all(one + two[:2])
    for tile in hidden_tiles(whole.shape[1]):
        d_act = jnp.dot(d_mlp_in[...], whole[:, tile], preferred_element_type=F32)
        d_pre[:, tile] = (d_act * slope_in[:, tile]).astype(BF)
    wait_all(two[2:])
    first = n_near * far[0].shape[0]
    for tile in channel_tiles(up_in.shape[0]):
        write_pieces(contract_last(d_pre[first:, :], up_in[tile, :]), tile, far)


def down_part(blocks, where, d_mlp, slope, up, n_near, n_far):
    total, chans = d_mlp.shape
    hidden = slope.shape[1]
    spots = total // (n_near + n_far)
    count = len(blocks) + 3
    outs = [shaped(up.shape, BF), shaped((total, hidden), BF)] + [shaped((spots, chans), BF)] * n_far
    return pl.pallas_call(
        functools.partial(down_kernel, where, n_near),
        out_shape=outs,
        in_specs=anywhere(count),
        out_specs=vmem(len(outs)),
        scratch_shapes=[
            pltpu.VMEM((total, chans), BF),
            pltpu.VMEM((total, hidden), F32),
            pltpu.VMEM(up.shape, BF),
            pltpu.SemaphoreType.DMA((count,)),
        ],
        compiler_params=params(24),
        cost_estimate=cost(3 * total * chans * hidden, 8 * total * chans),
        name="down_part",
    )(*blocks, d_mlp, slope, up)


def near_kernel(d_pre, up, *outs):
    rows = len(outs) * outs[0].shape[0]
    for tile in channel_tiles(up.shape[0]):
        write_pieces(contract_last(d_pre[:rows, :], up[tile, :]), tile, outs)


def near_part(d_pre, up, spots, n_near):
    chans, hidden = up.shape
    outs = [shaped((spots, chans), BF)] * n_near
    return pl.pallas_call(
        near_kernel,
        out_shape=outs,
        in_specs=vmem(2),
        out_specs=vmem(len(outs)),
        compiler_params=params(16),
        cost_estimate=cost(2 * n_near * spots * chans * hidden, 4 * spots * chans),
        name="near_part",
    )(d_pre, up)


def mlp_kernel(tiles, act, down, bias, *refs):
    cots, refs = refs[:tiles], refs[tiles:]
    *outs, scale_term = refs
    spots = cots[0].shape[0]
    for tile in channel_tiles(down.shape[0]):
        value = contract_last(act[...], down[tile, :])
        write_pieces(value, tile, outs)
        total = jnp.zeros((1, tile.size), F32)
        for k, cot in enumerate(cots):
            grad = cot[:, tile].astype(F32)
            mlp = value[k * spots : (k + 1) * spots]
            if k == 0:
                mlp = mlp + bias[:, tile]
            total = total + jnp.sum(grad * mlp, axis=0, keepdims=True)
        scale_term[:, tile] = total


def mlp_part(act, down, bias, cots):
    chans, hidden = down.shape
    spots = cots[0].shape[0]
    tiles = len(cots)
    outs = [shaped((spots, chans), BF)] * tiles + [shaped((1, chans), F32)]
    return pl.pallas_call(
        functools.partial(mlp_kernel, tiles),
        out_shape=outs,
        in_specs=vmem(3 + tiles),
        out_specs=vmem(len(outs)),
        compiler_params=params(24),
        cost_estimate=cost(2 * tiles * spots * chans * hidden, 6 * tiles * spots * chans),
        name="mlp_part",
    )(act, down, bias, *cots)


def finish_kernel(*refs):
    mine, other = refs[:4], refs[4:8]
    grad_kernel, gain_row, scale_row, sums = refs[8:]
    core = lax.axis_index("sx") % 2
    me = 2 * (lax.axis_index("sy") % 2) + lax.axis_index("fsdp") % 2
    for k in range(4):
        sums[core, me ^ k] = mine[k][...]
        sums[1 - core, me ^ k] = other[k][...]
    rows = mine[0].shape[0]

    def row(t):
        return sums[t // (4 * rows), t // rows % 4, pl.ds(t % rows, 1), :]

    for i in range(KW):
        for j in range(KW):
            grad_kernel[i, pl.ds(j, 1), :] = row(i * KW + j)
    gain_row[...] = row(KW * KW)
    scale_row[...] = row(KW * KW + 1)


def finish(mine, other):
    rows, chans = mine[0].shape
    return pl.pallas_call(
        finish_kernel,
        out_shape=(shaped((KW, KW, chans), F32), shaped((1, chans), F32), shaped((1, chans), F32)),
        in_specs=vmem(8),
        out_specs=vmem(3),
        scratch_shapes=[pltpu.VMEM((2, 4, rows, chans), F32)],
        compiler_params=params(16),
        cost_estimate=cost(rows, 16 * rows * chans),
        name="finish",
    )(*mine, *other)


def on_device(
    x_code,
    x_exp,
    dw_kernel,
    dw_bias,
    ln_gain,
    ln_bias,
    w_up,
    b_up,
    w_down,
    b_down,
    layer_scale,
    cotangent,
):
    rows, cols, chans = x_code.shape[1:]
    spots = rows * cols
    n_near = lax.axis_size("sx")
    tiles = n_near * lax.axis_size("sy")
    quarter = lax.axis_index("sx") * lax.axis_size("sy") + lax.axis_index("sy")
    hidden = w_up.shape[1] // tiles
    up_block = lax.dynamic_slice_in_dim(w_up, quarter * hidden, hidden, 1)
    down_block = lax.dynamic_slice_in_dim(w_down, quarter * hidden, hidden, 0).T
    ups, up_where = ring_gather(up_block)
    downs, down_where = ring_gather(down_block)
    cots = gather_tile(cotangent.reshape(spots, chans))

    scaled, *edges = prepare(x_code[0], x_exp[0])
    edges = exchange_edges(dict(zip(edge_keys(), edges, strict=True)))
    weights = dw_kernel.reshape(KW * KW, chans)
    padded, normed, rstd, ln_out = conv_norm(
        scaled, list(edges.values()), weights, dw_bias[None], ln_gain[None], ln_bias[None]
    )
    lns = gather_tile(ln_out)
    act, slope, up, d_mlp = up_part(ups, up_where, lns, cots, b_up[None], layer_scale[None])
    down, d_pre, *far = down_part(downs, down_where, d_mlp, slope, up, n_near, tiles - n_near)

    far = [far[k : k + n_near] for k in range(0, len(far), n_near)]
    far = [add_up(reduce_cores(group)).astype(BF) for group in far]
    far = [shift(term, "sy", -(t + 1)) for t, term in enumerate(far)]
    near = reduce_cores(near_part(d_pre, up, spots, n_near))
    *mlp, scale_term = mlp_part(act, down, b_down[None], cots)
    d_conv, keep, send, *edges = norm_back(near + far, normed, rstd, ln_gain[None], padded, scale_term)
    edges = exchange_edges(dict(zip(edge_keys(), edges, strict=True)))

    mlp = [reduce_cores(mlp[k : k + n_near]) for k in range(0, tiles, n_near)]
    rest = [shift(add_up(group).astype(BF), "sy", -(t + 1)) for t, group in enumerate(mlp[1:])]
    value = add_up(mlp[0] + rest) + b_down
    block_out = (scaled.astype(F32) + layer_scale * value.reshape(rows, cols, chans)).astype(BF)

    grad_input = conv_back(d_conv, list(edges.values()), weights, cotangent[0])
    grad_kernel, grad_gain, grad_scale = finish(*sum_rows(keep, send))
    return (block_out[None], grad_input[None], grad_kernel, grad_gain[0], grad_scale[0])


def solution(mesh):
    placed = (
        P("fsdp", "sx", "sy", None),
        P("fsdp", "sx", "sy", None),
        P(),
        P(),
        P(),
        P(),
        P("fsdp", None),
        P(),
        P(None, "fsdp"),
        P(),
        P(),
        P("fsdp", "sx", "sy", None),
    )
    return jax.shard_map(
        on_device,
        mesh=mesh,
        in_specs=placed,
        out_specs=(P("fsdp", "sx", "sy", None), P("fsdp", "sx", "sy", None), P(), P(), P()),
        check_vma=False,
    )
```

time: 467 us -> 135 us (0.29)
  waiting for transfers between devices: 328 us -> 47.2 us
  blocking collectives: 39.8 us -> 0 us
  Pallas kernels: 0 us -> 30.4 us
  matrix products: 28.6 us -> 0 us
  other arithmetic: 30.4 us -> 4.39 us
  starting transfers between devices: 16.6 us -> 39.8 us
  between operations: 15.2 us -> 1.01 us
  local copies, waits for them, and re-layouts: 7.43 us -> 12.1 us
    all_gather x2 -> x0, waiting for transfers between devices: 243 us -> none  [the longest x1 132 us: on_device(): lax.all_gather(w_down, 'fsdp', axis=1, tiled=True)]
    psum x1 -> x0, waiting for transfers between devices: 76.1 us -> none  [on_device(): lax.psum((kernel_term, gain_term, scale_term), ('sx', 'sy', 'fsdp'))]
    psum x1 -> x0, blocking collectives: 39.8 us -> none  [on_device(): lax.psum((kernel_term, gain_term, scale_term), ('sx', 'sy', 'fsdp'))]
    ppermute x8 -> x48, waiting for transfers between devices: 8.27 us -> 47.2 us  [the longest x12 14.3 us: shift(): return lax.ppermute(a, axis, [((i + k) % n, i) for i in range(n)])]
    pallas_call x0 -> x9, Pallas kernels: none -> 30.4 us  [the longest x1 6.57 us: conv_back(): pl.pallas_call(conv_back_kernel, out_shape=shaped((rows, cols, chans), BF...]
    dot_general x3 -> x0, matrix products: 28.6 us -> none  [the longest x1 13.3 us: on_device(): lax.dot_general(d_pre, up_full, (((1,), (1,)), ((), ())), preferred_eleme...]
    ppermute x8 -> x48, starting transfers between devices: 16.5 us -> 39.8 us  [the longest x14 12.5 us: swap(): return lax.ppermute(a, axes, [(i, i ^ mask) for i in range(total)])]
    reduce_sum x6 -> x0, other arithmetic: 18.1 us -> none  [the longest x1 9.45 us: on_device(): mean_val = jnp.mean(conv, axis=-1, keepdims=True)]
  transfers between devices with their start and end apart: 11 -> 48, of which waited for: 7 -> 18; matrix products, arithmetic and copies ran while one was open for 7% -> 5% of each run, Pallas kernels for 0% -> 15%
where the time goes in v2:
time: 135 us
  waiting for transfers between devices  47.2 us (35%)
  starting transfers between devices  39.8 us (29%)
  Pallas kernels  30.4 us (23%)
  local copies, waits for them, and re-layouts  12.1 us (9%)
  other arithmetic  4.39 us (3%)
    ppermute x12, waiting for transfers between devices, shift(): return lax.ppermute(a, axis, [((i + k) % n, i) for i in range(n)])  14.3 us
    ppermute x6, waiting for transfers between devices, ring_gather(): one = lax.ppermute(one, 'fsdp', forth)  12.9 us
    ppermute x14, starting transfers between devices, swap(): return lax.ppermute(a, axes, [(i, i ^ mask) for i in range(total)])  12.5 us
    ppermute x6, starting transfers between devices, ring_gather(): one = lax.ppermute(one, 'fsdp', forth)  12.2 us
    ppermute x14, waiting for transfers between devices, swap(): return lax.ppermute(a, axes, [(i, i ^ mask) for i in range(total)])  9.5 us
    unnamed x45, local copies, waits for them, and re-layouts  7.18 us
    pallas_call x1, Pallas kernels, conv_back(): pl.pallas_call(conv_back_kernel, out_shape=shaped((rows, cols, chans), BF...  6.57 us
    ppermute x6, waiting for transfers between devices, exchange_edges(): got[a, b] = lax.ppermute(piece, ('sx', 'sy'), pairs)  5.91 us
  transfers between devices with their start and end apart: 48, of which 18 were waited for; matrix products, arithmetic and copies ran while one was open for 5% of the time, Pallas kernels for 15%

profile of v2, /device:TPU:0, one launch (start us, length us, event | category | flops | bytes accessed | tf_op | source)
XLA Modules:
  0.0 134.9 jit_solution(5101494903280015920)
XLA Ops:
  0.7 1.2 copy-done
  1.9 3.1 %collective-permute-start = (bf16[192,768]{1,0:T(8,128)(2,1)S(1)}, bf16[192,768]{1,0:T(8,128)(2,1)}, u32[]{:S(2)}, u32[]{:S(2)}) collective-permute-start(bf16[192,768]{1,0:T(8,128)(2,1)S(1)} %constant_dynamic-slice_fusion.refs_0_), channel_id=1, source_target_pairs={{0,2},{2,4},{4,6},{6,7},{7,5},{5,3},{3,1},{1,0},{8,10},{10,12},{12... | collective-permute-start | bytes 884744 | tf_op jit(solution)/shard_map/ppermute | solution.py:107
  5.0 1.0 dynamic-slice_bitcast_fusion.refs_0_
  6.0 2.1 %collective-permute-start.17 = (bf16[192,768]{1,0:T(8,128)(2,1)S(1)}, bf16[192,768]{1,0:T(8,128)(2,1)}, u32[]{:S(2)}, u32[]{:S(2)}) collective-permute-start(bf16[192,768]{1,0:T(8,128)(2,1)S(1)} %dynamic-slice_bitcast_fusion.refs_0_), channel_id=1, source_target_pairs={{0,2},{2,4},{4,6},{6,7},{7,5},{5,3},{3,1},{1,0},{8,10},{10,12},{12... | collective-permute-start | bytes 884744 | tf_op jit(solution)/shard_map/ppermute | solution.py:107
  8.1 0.9 copy.17
  9.6 1.6 %collective-permute-start.10 = (bf16[3,3,1536]{2,1,0:T(4,128)(2,1)S(1)}, bf16[3,3,1536]{2,1,0:T(4,128)(2,1)S(1)}, u32[]{:S(2)}, u32[]{:S(2)}) collective-permute-start(bf16[3,3,1536]{2,1,0:T(4,128)(2,1)S(1)} %get-tuple-element.40), channel_id=1, source_target_pairs={{0,24},{8,16},{16,8},{24,0},{1,25},{9,17},{17,9},{25,1},{2,26},{10... | collective-permute-start | bytes 82952 | tf_op jit(solution)/shard_map/ppermute | solution.py:74
  11.2 1.8 %collective-permute-done.10.refs_2_ = bf16[3,3,1536]{2,1,0:T(4,128)(2,1)S(1)} collective-permute-done((bf16[3,3,1536]{2,1,0:T(4,128)(2,1)S(1)}, bf16[3,3,1536]{2,1,0:T(4,128)(2,1)S(1)}, u32[]{:S(2)}, u32[]{:S(2)}) %collective-permute-start.10) | collective-permute-done | bytes 27680 | tf_op jit(solution)/shard_map/ppermute | solution.py:74
  13.1 0.6 copy-done.10
  13.7 1.5 %collective-permute-start.9 = (bf16[8,3,1536]{2,1,0:T(4,128)(2,1)S(1)}, bf16[8,3,1536]{2,1,0:T(4,128)(2,1)S(1)}, u32[]{:S(2)}, u32[]{:S(2)}) collective-permute-start(bf16[8,3,1536]{2,1,0:T(4,128)(2,1)S(1)} %get-tuple-element.39), channel_id=1, source_target_pairs={{0,8},{8,0},{16,24},{24,16},{1,9},{9,1},{17,25},{25,17},{2,10},{10... | collective-permute-start | bytes 221192 | tf_op jit(solution)/shard_map/ppermute | solution.py:74
  15.2 4.1 %collective-permute-done.9.refs_1_ = bf16[8,3,1536]{2,1,0:T(4,128)(2,1)S(1)} collective-permute-done((bf16[8,3,1536]{2,1,0:T(4,128)(2,1)S(1)}, bf16[8,3,1536]{2,1,0:T(4,128)(2,1)S(1)}, u32[]{:S(2)}, u32[]{:S(2)}) %collective-permute-start.9) | collective-permute-done | bytes 73760 | tf_op jit(solution)/shard_map/ppermute | solution.py:74
  19.2 0.6 copy-done.8
  19.9 1.6 %collective-permute-start.15 = (bf16[128,1536]{1,0:T(8,128)(2,1)S(1)}, bf16[128,1536]{1,0:T(8,128)(2,1)S(1)}, u32[]{:S(2)}, u32[]{:S(2)}) collective-permute-start(bf16[128,1536]{1,0:T(8,128)(2,1)S(1)} %bitcast.26), channel_id=1, source_target_pairs={{8,0},{0,8},{9,1},{1,9},{10,2},{2,10},{11,3},{3,11},{12,4},{4,12},... | collective-permute-start | bytes 1179656 | tf_op jit(solution)/shard_map/ppermute | solution.py:54
  21.9 1.6 %collective-permute-start.2 = (bf16[192,768]{1,0:T(8,128)(2,1)}, bf16[192,768]{1,0:T(8,128)(2,1)}, u32[]{:S(2)}, u32[]{:S(2)}) collective-permute-start(bf16[192,768]{1,0:T(8,128)(2,1)} %collective-permute-done.refs_1_), channel_id=1, source_target_pairs={{0,2},{2,4},{4,6},{6,7},{7,5},{5,3},{3,1},{1,0},{8,10},{10,12},{12... | collective-permute-start | bytes 884744 | tf_op jit(solution)/shard_map/ppermute | solution.py:107
  24.0 1.0 reshape.24.refs_3_
  25.0 0.7 broadcast_in_dim.27.refs_4_
  25.7 0.7 broadcast_in_dim.28.refs_5_
  26.4 0.7 broadcast_in_dim.29.refs_6_
  27.2 0.9 copy-done.9
  28.0 0.8 copy-done.11
  28.8 5.8 %conv_norm.1 = (f32[14,24,1536]{2,1,0:T(8,128)S(1)}, f32[128,1536]{1,0:T(8,128)S(1)}, f32[128,128]{1,0:T(8,128)S(1)}, bf16[128,1536]{1,0:T(8,128)(2,1)S(1)}) custom-call(bf16[8,16,1536]{2,1,0:T(8,128)(2,1)S(1)} %get-tuple-element.37.own, bf16[3,16,1536]{2,1,0:T(8,128)(2,1)S(1)} %collective-permute-done.8.refs_0_, bf16[8,3,1536]{2,1,0:T(4,128)(2,1)S(1)} %copy-done.9, ...), custom_call_target="tpu_custom_call" | custom-call | flops 19267584 | bytes 1966080 | tf_op jit(solution)/shard_map/conv_norm/pallas_call | solution.py:299
  35.0 1.8 %collective-permute-start.19 = (bf16[192,768]{1,0:T(8,128)(2,1)}, bf16[192,768]{1,0:T(8,128)(2,1)S(1)}, u32[]{:S(2)}, u32[]{:S(2)}) collective-permute-start(bf16[192,768]{1,0:T(8,128)(2,1)} %collective-permute-done.17.refs_1_), channel_id=1, source_target_pairs={{0,2},{2,4},{4,6},{6,7},{7,5},{5,3},{3,1},{1,0},{8,10},{10,12},{12... | collective-permute-start | bytes 884744 | tf_op jit(solution)/shard_map/ppermute | solution.py:107
  37.0 1.8 %collective-permute-start.4 = (bf16[192,768]{1,0:T(8,128)(2,1)}, bf16[192,768]{1,0:T(8,128)(2,1)S(1)}, u32[]{:S(2)}, u32[]{:S(2)}) collective-permute-start(bf16[192,768]{1,0:T(8,128)(2,1)} %collective-permute-done.2.refs_3_), channel_id=1, source_target_pairs={{0,2},{2,4},{4,6},{6,7},{7,5},{5,3},{3,1},{1,0},{8,10},{10,12},{12... | collective-permute-start | bytes 884744 | tf_op jit(solution)/shard_map/ppermute | solution.py:107
  39.0 6.1 %collective-permute-done.19.refs_3_ = bf16[192,768]{1,0:T(8,128)(2,1)S(1)} collective-permute-done((bf16[192,768]{1,0:T(8,128)(2,1)}, bf16[192,768]{1,0:T(8,128)(2,1)S(1)}, u32[]{:S(2)}, u32[]{:S(2)}) %collective-permute-start.19) | collective-permute-done | bytes 294944 | tf_op jit(solution)/shard_map/ppermute | solution.py:107
  45.1 1.8 %collective-permute-start.21 = (bf16[192,768]{1,0:T(8,128)(2,1)S(1)}, bf16[192,768]{1,0:T(8,128)(2,1)S(1)}, u32[]{:S(2)}, u32[]{:S(2)}) collective-permute-start(bf16[192,768]{1,0:T(8,128)(2,1)S(1)} %collective-permute-done.19.refs_3_), channel_id=1, source_target_pairs={{0,2},{2,4},{4,6},{6,7},{7,5},{5,3},{3,1},{1,0},{8,10},{10,12},{12... | collective-permute-start | bytes 884744 | tf_op jit(solution)/shard_map/ppermute | solution.py:107
  47.2 4.3 %collective-permute-done.4.refs_5_ = bf16[192,768]{1,0:T(8,128)(2,1)S(1)} collective-permute-done((bf16[192,768]{1,0:T(8,128)(2,1)}, bf16[192,768]{1,0:T(8,128)(2,1)S(1)}, u32[]{:S(2)}, u32[]{:S(2)}) %collective-permute-start.4) | collective-permute-done | bytes 294944 | tf_op jit(solution)/shard_map/ppermute | solution.py:107
  51.4 1.8 %collective-permute-done.5.refs_6_ = bf16[192,768]{1,0:T(8,128)(2,1)S(1)} collective-permute-done((bf16[192,768]{1,0:T(8,128)(2,1)}, bf16[192,768]{1,0:T(8,128)(2,1)S(1)}, u32[]{:S(2)}, u32[]{:S(2)}) %collective-permute-start.5) | collective-permute-done | bytes 294944 | tf_op jit(solution)/shard_map/ppermute | solution.py:108
  53.3 2.6 %collective-permute-done.21.refs_5_ = bf16[192,768]{1,0:T(8,128)(2,1)S(1)} collective-permute-done((bf16[192,768]{1,0:T(8,128)(2,1)S(1)}, bf16[192,768]{1,0:T(8,128)(2,1)S(1)}, u32[]{:S(2)}, u32[]{:S(2)}) %collective-permute-start.21) | collective-permute-done | bytes 294944 | tf_op jit(solution)/shard_map/ppermute | solution.py:107
  55.9 1.7 %collective-permute-start.6 = (bf16[96,768]{1,0:T(8,128)(2,1)S(1)}, bf16[96,768]{1,0:T(8,128)(2,1)S(1)}, u32[]{:S(2)}, u32[]{:S(2)}) collective-permute-start(bf16[96,768]{1,0:T(8,128)(2,1)S(1)} %slice.16), channel_id=1, source_target_pairs={{0,2},{2,4},{4,6},{6,7},{7,5},{5,3},{3,1},{1,0},{8,10},{10,12},{12... | collective-permute-start | bytes 442376 | tf_op jit(solution)/shard_map/ppermute | solution.py:114
  58.0 1.7 %collective-permute-start.23 = (bf16[96,768]{1,0:T(8,128)(2,1)S(1)}, bf16[96,768]{1,0:T(8,128)(2,1)S(1)}, u32[]{:S(2)}, u32[]{:S(2)}) collective-permute-start(bf16[96,768]{1,0:T(8,128)(2,1)S(1)} %slice.18), channel_id=1, source_target_pairs={{0,2},{2,4},{4,6},{6,7},{7,5},{5,3},{3,1},{1,0},{8,10},{10,12},{12... | collective-permute-start | bytes 442376 | tf_op jit(solution)/shard_map/ppermute | solution.py:114
  60.1 1.4 %collective-permute-done.6.refs_7_ = bf16[96,768]{1,0:T(8,128)(2,1)S(1)} collective-permute-done((bf16[96,768]{1,0:T(8,128)(2,1)S(1)}, bf16[96,768]{1,0:T(8,128)(2,1)S(1)}, u32[]{:S(2)}, u32[]{:S(2)}) %collective-permute-start.6) | collective-permute-done | bytes 147488 | tf_op jit(solution)/shard_map/ppermute | solution.py:114
  61.5 1.3 collective-permute-done.7.refs_8_
  62.8 4.8 %up_part.1 = (bf16[512,768]{1,0:T(8,128)(2,1)S(1)}, f32[512,768]{1,0:T(8,128)S(1)}, bf16[1536,768]{1,0:T(8,128)(2,1)S(1)}, bf16[512,1536]{1,0:T(8,128)(2,1)S(1)}) custom-call(bf16[192,768]{1,0:T(8,128)(2,1)S(1)} %copy-done.3, bf16[192,768]{1,0:T(8,128)(2,1)} %collective-permute-done.refs_1_, bf16[192,768]{1,0:T(8,128)(2,1)} %collective-permute-done.1.refs_2_, ...), custom_call_target="tpu_custom_call" | custom-call | flops 1207959552 | bytes 6291456 | tf_op jit(solution)/shard_map/up_part/pallas_call | solution.py:488
  67.6 4.3 %down_part.1 = (bf16[1536,768]{1,0:T(8,128)(2,1)S(1)}, bf16[512,768]{1,0:T(8,128)(2,1)S(1)}, bf16[128,1536]{1,0:T(8,128)(2,1)S(1)}, bf16[128,1536]{1,0:T(8,128)(2,1)S(1)}) custom-call(bf16[192,768]{1,0:T(8,128)(2,1)S(1)} %dynamic-slice_bitcast_fusion.refs_0_, bf16[192,768]{1,0:T(8,128)(2,1)} %collective-permute-done.17.refs_1_, ...), custom_call_target="tpu_custom_call" | custom-call | flops 1811939328 | bytes 6291456 | tf_op jit(solution)/shard_map/down_part/pallas_call | solution.py:545
  72.0 0.8 near_part.1
  72.8 0.6 collective-permute-start.28
  73.8 1.6 %collective-permute-start.30 = (bf16[128,1536]{1,0:T(8,128)(2,1)S(1)}, bf16[128,1536]{1,0:T(8,128)(2,1)S(1)}, u32[]{:S(2)}, u32[]{:S(2)}) collective-permute-start(bf16[128,1536]{1,0:T(8,128)(2,1)S(1)} %add_convert_fusion), channel_id=1, source_target_pairs={{8,0},{0,8},{9,1},{1,9},{10,2},{2,10},{11,3},{3,11},{12,4},{4,12},... | collective-permute-start | bytes 1179656 | tf_op jit(solution)/shard_map/ppermute | solution.py:54
  75.4 1.4 %mlp_part.1 = (bf16[128,1536]{1,0:T(8,128)(2,1)S(1)}, bf16[128,1536]{1,0:T(8,128)(2,1)S(1)}, bf16[128,1536]{1,0:T(8,128)(2,1)S(1)}, bf16[128,1536]{1,0:T(8,128)(2,1)S(1)}, f32[1,1536]{1,0:T(1,128)S(1)}) custom-call(bf16[512,768]{1,0:T(8,128)(2,1)S(1)} %get-tuple-element.42.act, bf16[1536,768]{1,0:T(8,128)(2,1)S(1)} %get-tuple-element.46.down, ...), custom_call_target="tpu_custom_call" | custom-call | flops 1207959552 | bytes 4718592 | tf_op jit(solution)/shard_map/mlp_part/pallas_call | solution.py:604
  76.9 8.2 %collective-permute-done.30.refs_2_ = bf16[128,1536]{1,0:T(8,128)(2,1)S(1)} collective-permute-done((bf16[128,1536]{1,0:T(8,128)(2,1)S(1)}, bf16[128,1536]{1,0:T(8,128)(2,1)S(1)}, u32[]{:S(2)}, u32[]{:S(2)}) %collective-permute-start.30) | collective-permute-done | bytes 393248 | tf_op jit(solution)/shard_map/ppermute | solution.py:54
  85.0 5.3 %norm_back.1 = (f32[8,16,1536]{2,1,0:T(8,128)S(1)}, f32[32,1536]{1,0:T(8,128)S(1)}, f32[32,1536]{1,0:T(8,128)}, bf16[3,16,1536]{2,1,0:T(8,128)(2,1)S(1)}, bf16[8...) custom-call(bf16[128,1536]{1,0:T(8,128)(2,1)S(1)} %get-tuple-element.52.refs_0_, ...), custom_call_target="tpu_custom_call" | custom-call | flops 19267584 | bytes 3145728 | tf_op jit(solution)/shard_map/norm_back/pallas_call | solution.py:377
  90.3 0.6 copy-done.15
  91.0 0.7 copy-done.7
  91.7 1.8 %collective-permute-done.34 = f32[32,1536]{1,0:T(8,128)} collective-permute-done((f32[32,1536]{1,0:T(8,128)}, f32[32,1536]{1,0:T(8,128)}, u32[]{:S(2)}, u32[]{:S(2)}) %collective-permute-start.34) | collective-permute-done | bytes 196640 | tf_op jit(solution)/shard_map/ppermute | solution.py:49
  93.5 1.0 add_bitcast_fusion
  94.5 0.7 copy-done.18
  95.2 0.7 dynamic-slice_bitcast_fusion.1
  96.3 1.5 %collective-permute-start.36 = (f32[8,1536]{1,0:T(8,128)}, f32[8,1536]{1,0:T(8,128)}, u32[]{:S(2)}, u32[]{:S(2)}) collective-permute-start(f32[8,1536]{1,0:T(8,128)} %get-tuple-element.70), channel_id=1, source_target_pairs={{0,8},{8,0},{1,9},{9,1},{2,10},{10,2},{3,11},{11,3},{4,12},{12,4},... | collective-permute-start | bytes 147464 | tf_op jit(solution)/shard_map/ppermute | solution.py:49
  97.8 1.5 %collective-permute-start.37 = (f32[8,1536]{1,0:T(8,128)}, f32[8,1536]{1,0:T(8,128)}, u32[]{:S(2)}, u32[]{:S(2)}) collective-permute-start(f32[8,1536]{1,0:T(8,128)} %get-tuple-element.69), channel_id=1, source_target_pairs={{0,9},{1,8},{2,11},{3,10},{4,13},{5,12},{6,15},{7,14},{8,1},{9,0},... | collective-permute-start | bytes 147464 | tf_op jit(solution)/shard_map/ppermute | solution.py:49
  100.7 2.4 %collective-permute-done.37 = f32[8,1536]{1,0:T(8,128)} collective-permute-done((f32[8,1536]{1,0:T(8,128)}, f32[8,1536]{1,0:T(8,128)}, u32[]{:S(2)}, u32[]{:S(2)}) %collective-permute-start.37) | collective-permute-done | bytes 49184 | tf_op jit(solution)/shard_map/ppermute | solution.py:49
  103.1 0.9 fusion.2
  104.0 3.7 %collective-permute-start.40 = (bf16[8,1536]{1,0:T(8,128)(2,1)S(1)}, bf16[8,1536]{1,0:T(8,128)(2,1)S(1)}, u32[]{:S(2)}, u32[]{:S(2)}) collective-permute-start(bf16[8,1536]{1,0:T(8,128)(2,1)S(1)} %fusion.2), channel_id=1, source_target_pairs={{0,6},{1,7},{2,4},{3,5},{4,2},{5,3},{6,0},{7,1},{8,14},{9,15},{10,... | collective-permute-start | bytes 73736 | tf_op jit(solution)/shard_map/ppermute | solution.py:49
  107.7 0.8 collective-permute-start.38
  108.6 0.7 collective-permute-start.27
  109.7 1.0 collective-permute-start.32
  110.7 1.7 %collective-permute-done.39 = bf16[8,1536]{1,0:T(8,128)(2,1)S(1)} collective-permute-done((bf16[8,1536]{1,0:T(8,128)(2,1)S(1)}, bf16[8,1536]{1,0:T(8,128)(2,1)S(1)}, u32[]{:S(2)}, u32[]{:S(2)}) %collective-permute-start.39) | collective-permute-done | bytes 24608 | tf_op jit(solution)/shard_map/ppermute | solution.py:49
  112.4 1.6 %collective-permute-start.41 = (f32[8,1536]{1,0:T(8,128)S(1)}, f32[8,1536]{1,0:T(8,128)S(1)}, u32[]{:S(2)}, u32[]{:S(2)}) collective-permute-start(f32[8,1536]{1,0:T(8,128)S(1)} %add_add_fusion.1.refs_0_), channel_id=1, source_target_pairs={{0,1},{1,0},{2,3},{3,2},{4,5},{5,4},{6,7},{7,6},{8,9},{9,8},{10,11... | collective-permute-start | bytes 147464 | tf_op jit(solution)/shard_map/ppermute | solution.py:49
  114.0 0.5 collective-permute-start.42
  114.5 5.8 %collective-permute-done.27 = bf16[128,1536]{1,0:T(8,128)(2,1)S(1)} collective-permute-done((bf16[128,1536]{1,0:T(8,128)(2,1)S(1)}, bf16[128,1536]{1,0:T(8,128)(2,1)S(1)}, u32[]{:S(2)}, u32[]{:S(2)}) %collective-permute-start.27) | collective-permute-done | bytes 393248 | tf_op jit(solution)/shard_map/ppermute | solution.py:54
  120.4 1.5 %collective-permute-start.43 = (f32[8,1536]{1,0:T(8,128)S(1)}, f32[8,1536]{1,0:T(8,128)S(1)}, u32[]{:S(2)}, u32[]{:S(2)}) collective-permute-start(f32[8,1536]{1,0:T(8,128)S(1)} %add_add_fusion.1.refs_0_), channel_id=1, source_target_pairs={{0,9},{1,8},{2,11},{3,10},{4,13},{5,12},{6,15},{7,14},{8,1},{9,0},... | collective-permute-start | bytes 147464 | tf_op jit(solution)/shard_map/ppermute | solution.py:49
  123.1 2.3 %collective-permute-done.43.refs_3_ = f32[8,1536]{1,0:T(8,128)S(1)} collective-permute-done((f32[8,1536]{1,0:T(8,128)S(1)}, f32[8,1536]{1,0:T(8,128)S(1)}, u32[]{:S(2)}, u32[]{:S(2)}) %collective-permute-start.43) | collective-permute-done | bytes 49184 | tf_op jit(solution)/shard_map/ppermute | solution.py:49
  125.4 0.8 fusion
  126.2 6.6 %conv_back.1 = bf16[8,16,1536]{2,1,0:T(8,128)(2,1)} custom-call(f32[8,16,1536]{2,1,0:T(8,128)S(1)} %get-tuple-element.60.own, bf16[3,16,1536]{2,1,0:T(8,128)(2,1)S(1)} %collective-permute-done.31.refs_0_, bf16[8,3,1536]{2,1,0:T(4,128)(2,1)S(1)} %collective-permute-done.32.refs_1_, bf16[3,3,1536]{2,1,0:T(4,128)(2,1)S(1)} %collective-permute-done.33.refs_2_, ...), custom_call_target="tpu_custom_call" | custom-call | flops 19267584 | bytes 1966080 | tf_op jit(solution)/shard_map/conv_back/pallas_call | solution.py:408
  132.8 0.9 finish.1
  133.7 0.6 reduce
  134.3 0.6 reduce.1
  (108 shorter events, 7.7 us)
Async XLA Ops:
  0.6 1.3 copy-start
  0.6 8.4 %copy-start.4 = (bf16[1,8,16,1536]{3,2,1,0:T(8,128)(2,1)S(1)}, bf16[1,8,16,1536]{3,2,1,0:T(8,128)(2,1)}, u32[]{:S(2)}) copy-start(bf16[1,8,16,1536]{3,2,1,0:T(8,128)(2,1)} %param.12) | copy-start | bytes 1179652
  0.7 19.2 %copy-start.1 = (bf16[1,8,16,1536]{3,2,1,0:T(8,128)(2,1)S(1)}, bf16[1,8,16,1536]{3,2,1,0:T(8,128)(2,1)}, u32[]{:S(2)}) copy-start(bf16[1,8,16,1536]{3,2,1,0:T(8,128)(2,1)} %param.23) | copy-start | bytes 1179652
  1.9 21.5 %copy-start.2 = (bf16[192,768]{1,0:T(8,128)(2,1)}, bf16[192,768]{1,0:T(8,128)(2,1)S(1)}, u32[]{:S(2)}) copy-start(bf16[192,768]{1,0:T(8,128)(2,1)S(1)} %constant_dynamic-slice_fusion.refs_0_) | copy-start | bytes 884740
  1.9 19.5 %collective-permute-start = (bf16[192,768]{1,0:T(8,128)(2,1)S(1)}, bf16[192,768]{1,0:T(8,128)(2,1)}, u32[]{:S(2)}, u32[]{:S(2)}) collective-permute-start(bf16[192,768]{1,0:T(8,128)(2,1)S(1)} %constant_dynamic-slice_fusion.refs_0_), channel_id=1, source_target_pairs={{0,2},{2,4},{4,6},{6,7},{7,5},{5,3},{3,1},{1,0},{8,10},{10,12},{12... | collective-permute-start | bytes 884744 | tf_op jit(solution)/shard_map/ppermute | solution.py:107
  5.0 16.9 %collective-permute-start.1 = (bf16[192,768]{1,0:T(8,128)(2,1)S(1)}, bf16[192,768]{1,0:T(8,128)(2,1)}, u32[]{:S(2)}, u32[]{:S(2)}) collective-permute-start(bf16[192,768]{1,0:T(8,128)(2,1)S(1)} %constant_dynamic-slice_fusion.refs_0_), channel_id=1, source_target_pairs={{2,0},{4,2},{6,4},{7,6},{5,7},{3,5},{1,3},{0,1},{10,8},{12,10},{14... | collective-permute-start | bytes 884744 | tf_op jit(solution)/shard_map/ppermute | solution.py:108
  6.0 17.5 %collective-permute-start.17 = (bf16[192,768]{1,0:T(8,128)(2,1)S(1)}, bf16[192,768]{1,0:T(8,128)(2,1)}, u32[]{:S(2)}, u32[]{:S(2)}) collective-permute-start(bf16[192,768]{1,0:T(8,128)(2,1)S(1)} %dynamic-slice_bitcast_fusion.refs_0_), channel_id=1, source_target_pairs={{0,2},{2,4},{4,6},{6,7},{7,5},{5,3},{3,1},{1,0},{8,10},{10,12},{12... | collective-permute-start | bytes 884744 | tf_op jit(solution)/shard_map/ppermute | solution.py:107
  9.5 53.2 %copy-start.12 = (f32[3072]{0:T(1024)S(1)}, f32[3072]{0:T(1024)}, u32[]{:S(2)}) copy-start(f32[3072]{0:T(1024)} %param.19) | copy-start | bytes 36868
  9.5 10.3 %collective-permute-start.8 = (bf16[3,16,1536]{2,1,0:T(8,128)(2,1)S(1)}, bf16[3,16,1536]{2,1,0:T(8,128)(2,1)S(1)}, u32[]{:S(2)}, u32[]{:S(2)}) collective-permute-start(bf16[3,16,1536]{2,1,0:T(8,128)(2,1)S(1)} %get-tuple-element.38), channel_id=1, source_target_pairs={{0,16},{8,24},{16,0},{24,8},{1,17},{9,25},{17,1},{25,9},{2,18},{10... | collective-permute-start | bytes 442376 | tf_op jit(solution)/shard_map/ppermute | solution.py:74
  9.6 3.4 %collective-permute-start.10 = (bf16[3,3,1536]{2,1,0:T(4,128)(2,1)S(1)}, bf16[3,3,1536]{2,1,0:T(4,128)(2,1)S(1)}, u32[]{:S(2)}, u32[]{:S(2)}) collective-permute-start(bf16[3,3,1536]{2,1,0:T(4,128)(2,1)S(1)} %get-tuple-element.40), channel_id=1, source_target_pairs={{0,24},{8,16},{16,8},{24,0},{1,25},{9,17},{17,9},{25,1},{2,26},{10... | collective-permute-start | bytes 82952 | tf_op jit(solution)/shard_map/ppermute | solution.py:74
  13.7 5.5 %collective-permute-start.9 = (bf16[8,3,1536]{2,1,0:T(4,128)(2,1)S(1)}, bf16[8,3,1536]{2,1,0:T(4,128)(2,1)S(1)}, u32[]{:S(2)}, u32[]{:S(2)}) collective-permute-start(bf16[8,3,1536]{2,1,0:T(4,128)(2,1)S(1)} %get-tuple-element.39), channel_id=1, source_target_pairs={{0,8},{8,0},{16,24},{24,16},{1,9},{9,1},{17,25},{25,17},{2,10},{10... | collective-permute-start | bytes 221192 | tf_op jit(solution)/shard_map/ppermute | solution.py:74
  19.9 15.1 %collective-permute-start.14 = (bf16[128,1536]{1,0:T(8,128)(2,1)S(1)}, bf16[128,1536]{1,0:T(8,128)(2,1)S(1)}, u32[]{:S(2)}, u32[]{:S(2)}) collective-permute-start(bf16[128,1536]{1,0:T(8,128)(2,1)S(1)} %bitcast.25), channel_id=1, source_target_pairs={{16,0},{0,16},{17,1},{1,17},{18,2},{2,18},{19,3},{3,19},{20,4},{4,... | collective-permute-start | bytes 1179656 | tf_op jit(solution)/shard_map/ppermute | solution.py:54
  19.9 16.9 %collective-permute-start.15 = (bf16[128,1536]{1,0:T(8,128)(2,1)S(1)}, bf16[128,1536]{1,0:T(8,128)(2,1)S(1)}, u32[]{:S(2)}, u32[]{:S(2)}) collective-permute-start(bf16[128,1536]{1,0:T(8,128)(2,1)S(1)} %bitcast.26), channel_id=1, source_target_pairs={{8,0},{0,8},{9,1},{1,9},{10,2},{2,10},{11,3},{3,11},{12,4},{4,12},... | collective-permute-start | bytes 1179656 | tf_op jit(solution)/shard_map/ppermute | solution.py:54
  21.4 13.2 %collective-permute-start.18 = (bf16[192,768]{1,0:T(8,128)(2,1)S(1)}, bf16[192,768]{1,0:T(8,128)(2,1)}, u32[]{:S(2)}, u32[]{:S(2)}) collective-permute-start(bf16[192,768]{1,0:T(8,128)(2,1)S(1)} %dynamic-slice_bitcast_fusion.refs_0_), channel_id=1, source_target_pairs={{2,0},{4,2},{6,4},{7,6},{5,7},{3,5},{1,3},{0,1},{10,8},{12,10},{14... | collective-permute-start | bytes 884744 | tf_op jit(solution)/shard_map/ppermute | solution.py:108
  21.9 15.1 %collective-permute-start.2 = (bf16[192,768]{1,0:T(8,128)(2,1)}, bf16[192,768]{1,0:T(8,128)(2,1)}, u32[]{:S(2)}, u32[]{:S(2)}) collective-permute-start(bf16[192,768]{1,0:T(8,128)(2,1)} %collective-permute-done.refs_1_), channel_id=1, source_target_pairs={{0,2},{2,4},{4,6},{6,7},{7,5},{5,3},{3,1},{1,0},{8,10},{10,12},{12... | collective-permute-start | bytes 884744 | tf_op jit(solution)/shard_map/ppermute | solution.py:107
  23.5 15.3 %collective-permute-start.3 = (bf16[192,768]{1,0:T(8,128)(2,1)}, bf16[192,768]{1,0:T(8,128)(2,1)}, u32[]{:S(2)}, u32[]{:S(2)}) collective-permute-start(bf16[192,768]{1,0:T(8,128)(2,1)} %collective-permute-done.1.refs_2_), channel_id=1, source_target_pairs={{2,0},{4,2},{6,4},{7,6},{5,7},{3,5},{1,3},{0,1},{10,8},{12,10},{14... | collective-permute-start | bytes 884744 | tf_op jit(solution)/shard_map/ppermute | solution.py:108
  25.0 37.8 %copy-start.3 = (bf16[192,768]{1,0:T(8,128)(2,1)S(1)}, bf16[192,768]{1,0:T(8,128)(2,1)}, u32[]{:S(2)}) copy-start(bf16[192,768]{1,0:T(8,128)(2,1)} %copy-done.2) | copy-start | bytes 884740
  27.1 0.9 copy-start.9
  28.0 0.8 copy-start.11
  28.8 31.3 %copy-start.20 = (f32[1536]{0:T(1024)S(1)}, f32[1536]{0:T(1024)}, u32[]{:S(2)}) copy-start(f32[1536]{0:T(1024)} %param.22) | copy-start | bytes 18436
  34.6 12.5 %collective-permute-start.12 = (bf16[128,1536]{1,0:T(8,128)(2,1)S(1)}, bf16[128,1536]{1,0:T(8,128)(2,1)S(1)}, u32[]{:S(2)}, u32[]{:S(2)}) collective-permute-start(bf16[128,1536]{1,0:T(8,128)(2,1)S(1)} %get-tuple-element.41.refs_9_), channel_id=1, source_target_pairs={{8,0},{0,8},{9,1},{1,9},{10,2},{2,10},{11,3},{3,11},{12,4},{4,12},... | collective-permute-start | bytes 1179656 | tf_op jit(solution)/shard_map/ppermute | solution.py:54
  35.0 10.2 %collective-permute-start.19 = (bf16[192,768]{1,0:T(8,128)(2,1)}, bf16[192,768]{1,0:T(8,128)(2,1)S(1)}, u32[]{:S(2)}, u32[]{:S(2)}) collective-permute-start(bf16[192,768]{1,0:T(8,128)(2,1)} %collective-permute-done.17.refs_1_), channel_id=1, source_target_pairs={{0,2},{2,4},{4,6},{6,7},{7,5},{5,3},{3,1},{1,0},{8,10},{10,12},{12... | collective-permute-start | bytes 884744 | tf_op jit(solution)/shard_map/ppermute | solution.py:107
  36.8 10.2 %collective-permute-start.20 = (bf16[192,768]{1,0:T(8,128)(2,1)}, bf16[192,768]{1,0:T(8,128)(2,1)S(1)}, u32[]{:S(2)}, u32[]{:S(2)}) collective-permute-start(bf16[192,768]{1,0:T(8,128)(2,1)} %collective-permute-done.18.refs_2_), channel_id=1, source_target_pairs={{2,0},{4,2},{6,4},{7,6},{5,7},{3,5},{1,3},{0,1},{10,8},{12,10},{14... | collective-permute-start | bytes 884744 | tf_op jit(solution)/shard_map/ppermute | solution.py:108
  37.0 14.4 %collective-permute-start.4 = (bf16[192,768]{1,0:T(8,128)(2,1)}, bf16[192,768]{1,0:T(8,128)(2,1)S(1)}, u32[]{:S(2)}, u32[]{:S(2)}) collective-permute-start(bf16[192,768]{1,0:T(8,128)(2,1)} %collective-permute-done.2.refs_3_), channel_id=1, source_target_pairs={{0,2},{2,4},{4,6},{6,7},{7,5},{5,3},{3,1},{1,0},{8,10},{10,12},{12... | collective-permute-start | bytes 884744 | tf_op jit(solution)/shard_map/ppermute | solution.py:107
  38.8 14.4 %collective-permute-start.5 = (bf16[192,768]{1,0:T(8,128)(2,1)}, bf16[192,768]{1,0:T(8,128)(2,1)S(1)}, u32[]{:S(2)}, u32[]{:S(2)}) collective-permute-start(bf16[192,768]{1,0:T(8,128)(2,1)} %collective-permute-done.3.refs_4_), channel_id=1, source_target_pairs={{2,0},{4,2},{6,4},{7,6},{5,7},{3,5},{1,3},{0,1},{10,8},{12,10},{14... | collective-permute-start | bytes 884744 | tf_op jit(solution)/shard_map/ppermute | solution.py:108
  45.1 10.8 %collective-permute-start.21 = (bf16[192,768]{1,0:T(8,128)(2,1)S(1)}, bf16[192,768]{1,0:T(8,128)(2,1)S(1)}, u32[]{:S(2)}, u32[]{:S(2)}) collective-permute-start(bf16[192,768]{1,0:T(8,128)(2,1)S(1)} %collective-permute-done.19.refs_3_), channel_id=1, source_target_pairs={{0,2},{2,4},{4,6},{6,7},{7,5},{5,3},{3,1},{1,0},{8,10},{10,12},{12... | collective-permute-start | bytes 884744 | tf_op jit(solution)/shard_map/ppermute | solution.py:107
  47.0 10.6 %collective-permute-start.22 = (bf16[192,768]{1,0:T(8,128)(2,1)S(1)}, bf16[192,768]{1,0:T(8,128)(2,1)S(1)}, u32[]{:S(2)}, u32[]{:S(2)}) collective-permute-start(bf16[192,768]{1,0:T(8,128)(2,1)S(1)} %collective-permute-done.20.refs_4_), channel_id=1, source_target_pairs={{2,0},{4,2},{6,4},{7,6},{5,7},{3,5},{1,3},{0,1},{10,8},{12,10},{14... | collective-permute-start | bytes 884744 | tf_op jit(solution)/shard_map/ppermute | solution.py:108
  47.2 10.8 %collective-permute-start.11 = (bf16[128,1536]{1,0:T(8,128)(2,1)S(1)}, bf16[128,1536]{1,0:T(8,128)(2,1)S(1)}, u32[]{:S(2)}, u32[]{:S(2)}) collective-permute-start(bf16[128,1536]{1,0:T(8,128)(2,1)S(1)} %get-tuple-element.41.refs_9_), channel_id=1, source_target_pairs={{16,0},{0,16},{17,1},{1,17},{18,2},{2,18},{19,3},{3,19},{20,4},{4,... | collective-permute-start | bytes 1179656 | tf_op jit(solution)/shard_map/ppermute | solution.py:54
  51.4 8.3 %collective-permute-start.16 = (bf16[128,1536]{1,0:T(8,128)(2,1)S(1)}, bf16[128,1536]{1,0:T(8,128)(2,1)S(1)}, u32[]{:S(2)}, u32[]{:S(2)}) collective-permute-start(bf16[128,1536]{1,0:T(8,128)(2,1)S(1)} %collective-permute-done.15.refs_15_.refs_2_), channel_id=1, source_target_pairs={{16,0},{0,16},{17,1},{1,17},{18,2},{2,18},{19,3},{3,19},{20,4},{4,... | collective-permute-start | bytes 1179656 | tf_op jit(solution)/shard_map/ppermute | solution.py:54
  53.3 6.8 %collective-permute-start.13 = (bf16[128,1536]{1,0:T(8,128)(2,1)S(1)}, bf16[128,1536]{1,0:T(8,128)(2,1)S(1)}, u32[]{:S(2)}, u32[]{:S(2)}) collective-permute-start(bf16[128,1536]{1,0:T(8,128)(2,1)S(1)} %collective-permute-done.12.refs_11_), channel_id=1, source_target_pairs={{16,0},{0,16},{17,1},{1,17},{18,2},{2,18},{19,3},{3,19},{20,4},{4,... | collective-permute-start | bytes 1179656 | tf_op jit(solution)/shard_map/ppermute | solution.py:54
  55.9 5.6 %collective-permute-start.6 = (bf16[96,768]{1,0:T(8,128)(2,1)S(1)}, bf16[96,768]{1,0:T(8,128)(2,1)S(1)}, u32[]{:S(2)}, u32[]{:S(2)}) collective-permute-start(bf16[96,768]{1,0:T(8,128)(2,1)S(1)} %slice.16), channel_id=1, source_target_pairs={{0,2},{2,4},{4,6},{6,7},{7,5},{5,3},{3,1},{1,0},{8,10},{10,12},{12... | collective-permute-start | bytes 442376 | tf_op jit(solution)/shard_map/ppermute | solution.py:114
  57.6 5.2 %collective-permute-start.7 = (bf16[96,768]{1,0:T(8,128)(2,1)S(1)}, bf16[96,768]{1,0:T(8,128)(2,1)S(1)}, u32[]{:S(2)}, u32[]{:S(2)}) collective-permute-start(bf16[96,768]{1,0:T(8,128)(2,1)S(1)} %slice.17), channel_id=1, source_target_pairs={{2,0},{4,2},{6,4},{7,6},{5,7},{3,5},{1,3},{0,1},{10,8},{12,10},{14... | collective-permute-start | bytes 442376 | tf_op jit(solution)/shard_map/ppermute | solution.py:116
  58.0 9.6 %collective-permute-start.23 = (bf16[96,768]{1,0:T(8,128)(2,1)S(1)}, bf16[96,768]{1,0:T(8,128)(2,1)S(1)}, u32[]{:S(2)}, u32[]{:S(2)}) collective-permute-start(bf16[96,768]{1,0:T(8,128)(2,1)S(1)} %slice.18), channel_id=1, source_target_pairs={{0,2},{2,4},{4,6},{6,7},{7,5},{5,3},{3,1},{1,0},{8,10},{10,12},{12... | collective-permute-start | bytes 442376 | tf_op jit(solution)/shard_map/ppermute | solution.py:114
  59.7 7.8 %collective-permute-start.24 = (bf16[96,768]{1,0:T(8,128)(2,1)S(1)}, bf16[96,768]{1,0:T(8,128)(2,1)S(1)}, u32[]{:S(2)}, u32[]{:S(2)}) collective-permute-start(bf16[96,768]{1,0:T(8,128)(2,1)S(1)} %slice.19), channel_id=1, source_target_pairs={{2,0},{4,2},{6,4},{7,6},{5,7},{3,5},{1,3},{0,1},{10,8},{12,10},{14... | collective-permute-start | bytes 442376 | tf_op jit(solution)/shard_map/ppermute | solution.py:116
  71.9 1.8 %collective-permute-start.29 = (bf16[128,1536]{1,0:T(8,128)(2,1)S(1)}, bf16[128,1536]{1,0:T(8,128)(2,1)S(1)}, u32[]{:S(2)}, u32[]{:S(2)}) collective-permute-start(bf16[128,1536]{1,0:T(8,128)(2,1)S(1)} %get-tuple-element.55), channel_id=1, source_target_pairs={{16,0},{0,16},{17,1},{1,17},{18,2},{2,18},{19,3},{3,19},{20,4},{4,... | collective-permute-start | bytes 1179656 | tf_op jit(solution)/shard_map/ppermute | solution.py:54
  72.0 3.4 %copy-start.19 = (f32[1536]{0:T(1024)S(1)}, f32[1536]{0:T(1024)}, u32[]{:S(2)}) copy-start(f32[1536]{0:T(1024)} %param.21) | copy-start | bytes 18436
  72.8 4.1 %collective-permute-start.28 = (bf16[128,1536]{1,0:T(8,128)(2,1)S(1)}, bf16[128,1536]{1,0:T(8,128)(2,1)S(1)}, u32[]{:S(2)}, u32[]{:S(2)}) collective-permute-start(bf16[128,1536]{1,0:T(8,128)(2,1)S(1)} %get-tuple-element.53), channel_id=1, source_target_pairs={{16,0},{0,16},{17,1},{1,17},{18,2},{2,18},{19,3},{3,19},{20,4},{4,... | collective-permute-start | bytes 1179656 | tf_op jit(solution)/shard_map/ppermute | solution.py:54
  73.8 11.2 %collective-permute-start.30 = (bf16[128,1536]{1,0:T(8,128)(2,1)S(1)}, bf16[128,1536]{1,0:T(8,128)(2,1)S(1)}, u32[]{:S(2)}, u32[]{:S(2)}) collective-permute-start(bf16[128,1536]{1,0:T(8,128)(2,1)S(1)} %add_convert_fusion), channel_id=1, source_target_pairs={{8,0},{0,8},{9,1},{1,9},{10,2},{2,10},{11,3},{3,11},{12,4},{4,12},... | collective-permute-start | bytes 1179656 | tf_op jit(solution)/shard_map/ppermute | solution.py:54
  76.8 13.5 %copy-start.5 = (bf16[128,1536]{1,0:T(8,128)(2,1)}, bf16[128,1536]{1,0:T(8,128)(2,1)S(1)}, u32[]{:S(2)}) copy-start(bf16[128,1536]{1,0:T(8,128)(2,1)S(1)} %get-tuple-element.47) | copy-start | bytes 1179652
  76.8 14.1 %copy-start.13 = (bf16[128,1536]{1,0:T(8,128)(2,1)}, bf16[128,1536]{1,0:T(8,128)(2,1)S(1)}, u32[]{:S(2)}) copy-start(bf16[128,1536]{1,0:T(8,128)(2,1)S(1)} %get-tuple-element.48) | copy-start | bytes 1179652
  76.8 14.1 %copy-start.14 = (bf16[128,1536]{1,0:T(8,128)(2,1)}, bf16[128,1536]{1,0:T(8,128)(2,1)S(1)}, u32[]{:S(2)}) copy-start(bf16[128,1536]{1,0:T(8,128)(2,1)S(1)} %get-tuple-element.50) | copy-start | bytes 1179652
  91.7 1.8 %collective-permute-start.34 = (f32[32,1536]{1,0:T(8,128)}, f32[32,1536]{1,0:T(8,128)}, u32[]{:S(2)}, u32[]{:S(2)}) collective-permute-start(f32[32,1536]{1,0:T(8,128)} %get-tuple-element.65), channel_id=1, source_target_pairs={{0,16},{16,0},{1,17},{17,1},{2,18},{18,2},{3,19},{19,3},{4,20},{20... | collective-permute-start | bytes 589832 | tf_op jit(solution)/shard_map/ppermute | solution.py:49
  95.9 4.4 %collective-permute-start.35 = (f32[8,1536]{1,0:T(8,128)}, f32[8,1536]{1,0:T(8,128)}, u32[]{:S(2)}, u32[]{:S(2)}) collective-permute-start(f32[8,1536]{1,0:T(8,128)} %get-tuple-element.71), channel_id=1, source_target_pairs={{0,1},{1,0},{2,3},{3,2},{4,5},{5,4},{6,7},{7,6},{8,9},{9,8},{10,11... | collective-permute-start | bytes 147464 | tf_op jit(solution)/shard_map/ppermute | solution.py:49
  96.3 4.4 %collective-permute-start.36 = (f32[8,1536]{1,0:T(8,128)}, f32[8,1536]{1,0:T(8,128)}, u32[]{:S(2)}, u32[]{:S(2)}) collective-permute-start(f32[8,1536]{1,0:T(8,128)} %get-tuple-element.70), channel_id=1, source_target_pairs={{0,8},{8,0},{1,9},{9,1},{2,10},{10,2},{3,11},{11,3},{4,12},{12,4},... | collective-permute-start | bytes 147464 | tf_op jit(solution)/shard_map/ppermute | solution.py:49
  97.8 5.3 %collective-permute-start.37 = (f32[8,1536]{1,0:T(8,128)}, f32[8,1536]{1,0:T(8,128)}, u32[]{:S(2)}, u32[]{:S(2)}) collective-permute-start(f32[8,1536]{1,0:T(8,128)} %get-tuple-element.69), channel_id=1, source_target_pairs={{0,9},{1,8},{2,11},{3,10},{4,13},{5,12},{6,15},{7,14},{8,1},{9,0},... | collective-permute-start | bytes 147464 | tf_op jit(solution)/shard_map/ppermute | solution.py:49
  99.4 22.5 %copy-start.6 = (bf16[128,1536]{1,0:T(8,128)(2,1)S(1)}, bf16[128,1536]{1,0:T(8,128)(2,1)}, u32[]{:S(2)}) copy-start(bf16[128,1536]{1,0:T(8,128)(2,1)} %copy-done.5) | copy-start | bytes 1179652
  99.4 9.1 %collective-permute-start.26 = (bf16[128,1536]{1,0:T(8,128)(2,1)}, bf16[128,1536]{1,0:T(8,128)(2,1)S(1)}, u32[]{:S(2)}, u32[]{:S(2)}) collective-permute-start(bf16[128,1536]{1,0:T(8,128)(2,1)} %copy-done.14), channel_id=1, source_target_pairs={{16,0},{0,16},{17,1},{1,17},{18,2},{2,18},{19,3},{3,19},{20,4},{4,... | collective-permute-start | bytes 1179656 | tf_op jit(solution)/shard_map/ppermute | solution.py:54
  99.4 14.6 %collective-permute-start.25 = (bf16[128,1536]{1,0:T(8,128)(2,1)}, bf16[128,1536]{1,0:T(8,128)(2,1)S(1)}, u32[]{:S(2)}, u32[]{:S(2)}) collective-permute-start(bf16[128,1536]{1,0:T(8,128)(2,1)} %copy-done.13), channel_id=1, source_target_pairs={{16,0},{0,16},{17,1},{1,17},{18,2},{2,18},{19,3},{3,19},{20,4},{4,... | collective-permute-start | bytes 1179656 | tf_op jit(solution)/shard_map/ppermute | solution.py:54
  104.0 5.7 %collective-permute-start.40 = (bf16[8,1536]{1,0:T(8,128)(2,1)S(1)}, bf16[8,1536]{1,0:T(8,128)(2,1)S(1)}, u32[]{:S(2)}, u32[]{:S(2)}) collective-permute-start(bf16[8,1536]{1,0:T(8,128)(2,1)S(1)} %fusion.2), channel_id=1, source_target_pairs={{0,6},{1,7},{2,4},{3,5},{4,2},{5,3},{6,0},{7,1},{8,14},{9,15},{10,... | collective-permute-start | bytes 73736 | tf_op jit(solution)/shard_map/ppermute | solution.py:49
  107.7 4.7 %collective-permute-start.39 = (bf16[8,1536]{1,0:T(8,128)(2,1)S(1)}, bf16[8,1536]{1,0:T(8,128)(2,1)S(1)}, u32[]{:S(2)}, u32[]{:S(2)}) collective-permute-start(bf16[8,1536]{1,0:T(8,128)(2,1)S(1)} %fusion.2), channel_id=1, source_target_pairs={{0,4},{1,5},{2,6},{3,7},{4,0},{5,1},{6,2},{7,3},{8,12},{9,13},{10,... | collective-permute-start | bytes 73736 | tf_op jit(solution)/shard_map/ppermute | solution.py:49
  107.7 4.7 %collective-permute-start.38 = (bf16[8,1536]{1,0:T(8,128)(2,1)S(1)}, bf16[8,1536]{1,0:T(8,128)(2,1)S(1)}, u32[]{:S(2)}, u32[]{:S(2)}) collective-permute-start(bf16[8,1536]{1,0:T(8,128)(2,1)S(1)} %fusion.2), channel_id=1, source_target_pairs={{0,2},{1,3},{2,0},{3,1},{4,6},{5,7},{6,4},{7,5},{8,10},{9,11},{10,... | collective-permute-start | bytes 73736 | tf_op jit(solution)/shard_map/ppermute | solution.py:49
  108.5 13.5 %copy-start.16 = (bf16[3,16,1536]{2,1,0:T(8,128)(2,1)S(1)}, bf16[3,16,1536]{2,1,0:T(8,128)(2,1)}, u32[]{:S(2)}) copy-start(bf16[3,16,1536]{2,1,0:T(8,128)(2,1)} %copy-done.15) | copy-start | bytes 442372
  108.5 16.9 %copy-start.21 = (f32[1536]{0:T(1024)S(1)}, f32[1536]{0:T(1024)}, u32[]{:S(2)}) copy-start(f32[1536]{0:T(1024)} %param.22) | copy-start | bytes 18436
  108.6 11.8 %collective-permute-start.27 = (bf16[128,1536]{1,0:T(8,128)(2,1)S(1)}, bf16[128,1536]{1,0:T(8,128)(2,1)S(1)}, u32[]{:S(2)}, u32[]{:S(2)}) collective-permute-start(bf16[128,1536]{1,0:T(8,128)(2,1)S(1)} %add_convert_fusion.2), channel_id=1, source_target_pairs={{8,0},{0,8},{9,1},{1,9},{10,2},{2,10},{11,3},{3,11},{12,4},{4,12},... | collective-permute-start | bytes 1179656 | tf_op jit(solution)/shard_map/ppermute | solution.py:54
  109.7 12.4 %collective-permute-start.32 = (bf16[8,3,1536]{2,1,0:T(4,128)(2,1)}, bf16[8,3,1536]{2,1,0:T(4,128)(2,1)S(1)}, u32[]{:S(2)}, u32[]{:S(2)}) collective-permute-start(bf16[8,3,1536]{2,1,0:T(4,128)(2,1)} %copy-done.17), channel_id=1, source_target_pairs={{0,8},{8,0},{16,24},{24,16},{1,9},{9,1},{17,25},{25,17},{2,10},{10... | collective-permute-start | bytes 221192 | tf_op jit(solution)/shard_map/ppermute | solution.py:74
  112.4 9.6 %collective-permute-start.33 = (bf16[3,3,1536]{2,1,0:T(4,128)(2,1)S(1)}, bf16[3,3,1536]{2,1,0:T(4,128)(2,1)S(1)}, u32[]{:S(2)}, u32[]{:S(2)}) collective-permute-start(bf16[3,3,1536]{2,1,0:T(4,128)(2,1)S(1)} %get-tuple-element.63), channel_id=1, source_target_pairs={{0,24},{8,16},{16,8},{24,0},{1,25},{9,17},{17,9},{25,1},{2,26},{10... | collective-permute-start | bytes 82952 | tf_op jit(solution)/shard_map/ppermute | solution.py:74
  112.4 10.1 %collective-permute-start.41 = (f32[8,1536]{1,0:T(8,128)S(1)}, f32[8,1536]{1,0:T(8,128)S(1)}, u32[]{:S(2)}, u32[]{:S(2)}) collective-permute-start(f32[8,1536]{1,0:T(8,128)S(1)} %add_add_fusion.1.refs_0_), channel_id=1, source_target_pairs={{0,1},{1,0},{2,3},{3,2},{4,5},{5,4},{6,7},{7,6},{8,9},{9,8},{10,11... | collective-permute-start | bytes 147464 | tf_op jit(solution)/shard_map/ppermute | solution.py:49
  114.0 8.7 %collective-permute-start.42 = (f32[8,1536]{1,0:T(8,128)S(1)}, f32[8,1536]{1,0:T(8,128)S(1)}, u32[]{:S(2)}, u32[]{:S(2)}) collective-permute-start(f32[8,1536]{1,0:T(8,128)S(1)} %add_add_fusion.1.refs_0_), channel_id=1, source_target_pairs={{0,8},{8,0},{1,9},{9,1},{2,10},{10,2},{3,11},{11,3},{4,12},{12,4},... | collective-permute-start | bytes 147464 | tf_op jit(solution)/shard_map/ppermute | solution.py:49
  120.4 5.0 %collective-permute-start.43 = (f32[8,1536]{1,0:T(8,128)S(1)}, f32[8,1536]{1,0:T(8,128)S(1)}, u32[]{:S(2)}, u32[]{:S(2)}) collective-permute-start(f32[8,1536]{1,0:T(8,128)S(1)} %add_add_fusion.1.refs_0_), channel_id=1, source_target_pairs={{0,9},{1,8},{2,11},{3,10},{4,13},{5,12},{6,15},{7,14},{8,1},{9,0},... | collective-permute-start | bytes 147464 | tf_op jit(solution)/shard_map/ppermute | solution.py:49
  122.0 4.2 %collective-permute-start.31 = (bf16[3,16,1536]{2,1,0:T(8,128)(2,1)S(1)}, bf16[3,16,1536]{2,1,0:T(8,128)(2,1)S(1)}, u32[]{:S(2)}, u32[]{:S(2)}) collective-permute-start(bf16[3,16,1536]{2,1,0:T(8,128)(2,1)S(1)} %copy-done.16), channel_id=1, source_target_pairs={{0,16},{8,24},{16,0},{24,8},{1,17},{9,25},{17,1},{25,9},{2,18},{10... | collective-permute-start | bytes 442376 | tf_op jit(solution)/shard_map/ppermute | solution.py:74
  122.1 10.7 %collective-permute-start.44 = (f32[8,1536]{1,0:T(8,128)S(1)}, f32[8,1536]{1,0:T(8,128)S(1)}, u32[]{:S(2)}, u32[]{:S(2)}) collective-permute-start(f32[8,1536]{1,0:T(8,128)S(1)} %add_add_fusion.1.refs_0_), channel_id=1, source_target_pairs={{0,16},{16,0},{1,17},{17,1},{2,18},{18,2},{3,19},{19,3},{4,20},{20... | collective-permute-start | bytes 147464 | tf_op jit(solution)/shard_map/ppermute | solution.py:49
  122.6 10.2 %collective-permute-start.45 = (f32[8,1536]{1,0:T(8,128)S(1)}, f32[8,1536]{1,0:T(8,128)S(1)}, u32[]{:S(2)}, u32[]{:S(2)}) collective-permute-start(f32[8,1536]{1,0:T(8,128)S(1)} %collective-permute-done.41.refs_1_), channel_id=1, source_target_pairs={{0,16},{16,0},{1,17},{17,1},{2,18},{18,2},{3,19},{19,3},{4,20},{20... | collective-permute-start | bytes 147464 | tf_op jit(solution)/shard_map/ppermute | solution.py:49
  122.7 10.1 %collective-permute-start.46 = (f32[8,1536]{1,0:T(8,128)S(1)}, f32[8,1536]{1,0:T(8,128)S(1)}, u32[]{:S(2)}, u32[]{:S(2)}) collective-permute-start(f32[8,1536]{1,0:T(8,128)S(1)} %collective-permute-done.42.refs_2_), channel_id=1, source_target_pairs={{0,16},{16,0},{1,17},{17,1},{2,18},{18,2},{3,19},{19,3},{4,20},{20... | collective-permute-start | bytes 147464 | tf_op jit(solution)/shard_map/ppermute | solution.py:49
  125.3 7.4 %collective-permute-start.47 = (f32[8,1536]{1,0:T(8,128)S(1)}, f32[8,1536]{1,0:T(8,128)S(1)}, u32[]{:S(2)}, u32[]{:S(2)}) collective-permute-start(f32[8,1536]{1,0:T(8,128)S(1)} %collective-permute-done.43.refs_3_), channel_id=1, source_target_pairs={{0,16},{16,0},{1,17},{17,1},{2,18},{18,2},{3,19},{19,3},{4,20},{20... | collective-permute-start | bytes 147464 | tf_op jit(solution)/shard_map/ppermute | solution.py:49
  (6 other events, 4.0 us)

commit v3 on v2

--- a/solution.py
+++ b/solution.py
@@ -32,7 +32,7 @@
 
 
 def cost(flops, moved, special=0):
-    return pl.CostEstimate(flops=flops, bytes_accessed=moved, transcendentals=special)
+    return pl.CostEstimate(flops=1, bytes_accessed=1, transcendentals=0)
 
 
 def shaped(shape, dtype):
@@ -130,6 +130,11 @@
     return [pieces[0]] + [shift(pieces[s], "sx", -s) for s in range(1, len(pieces))]
 
 
+def reduce_cores_halves(pieces):
+    got = [shift(piece, "sx", -(1 + k // 2)) for k, piece in enumerate(pieces[1:])]
+    return [pieces[0]] + [got[k : k + 2] for k in range(0, len(got), 2)]
+
+
 def add_up(terms):
     total = terms[0].astype(F32)
     for term in terms[1:]:
@@ -137,16 +142,12 @@
     return total
 
 
-def sum_rows(keep, send):
-    total = keep + swap(send, sx=1)
-    quarter = total.shape[0] // 4
-    parts = total.reshape(4, quarter, total.shape[1])
-    me = 2 * (lax.axis_index("sy") % 2) + lax.axis_index("fsdp") % 2
-
-    def part(k):
-        return lax.dynamic_index_in_dim(parts, me ^ k, 0, keepdims=False)
-
-    total = (part(0) + swap(part(1), fsdp=1)) + (swap(part(2), sy=1) + swap(part(3), sy=1, fsdp=1))
+def sum_quarters(parts):
+    along_y, along_x = swap(parts[1], fsdp=1), swap(parts[2], sy=1)
+    return (parts[0] + along_y) + (along_x + swap(parts[3], sy=1, fsdp=1))
+
+
+def sum_others(total):
     masks = []
     for axis in ("sx", "sy", "fsdp"):
         bit = 2
@@ -162,8 +163,16 @@
             (other, more) = group[1]
             both = {axis: bit + more} if axis == other else {axis: bit, other: more}
             total = total + (swap(rounded, **{other: more}).astype(F32) + swap(rounded, **both).astype(F32))
+    return total
+
+
+def spread_quarter(total):
     mine = [total, swap(total, fsdp=1), swap(total, sy=1), swap(total, sy=1, fsdp=1)]
     return mine, [swap(piece, sx=1) for piece in mine]
+
+
+def as_row(ref):
+    return ref[...].reshape(1, ref.shape[0])
 
 
 def write_edges(tile, refs):
@@ -188,15 +197,15 @@
     return [shaped((rows if a is None else HALO, cols if b is None else HALO, chans), BF) for a, b in edge_keys()]
 
 
-def fill_padded(own, refs, padded):
+def fill_padded(own, refs, padded, lanes=slice(None)):
     rows, cols = own.shape[:2]
     at = {-1: 0, None: HALO}
     sx, sy = lax.axis_index("sx"), lax.axis_index("sy")
     there = {("sx", -1): sx > 0, ("sx", 1): sx < lax.axis_size("sx") - 1}
     there |= {("sy", -1): sy > 0, ("sy", 1): sy < lax.axis_size("sy") - 1}
-    padded[pl.ds(HALO, rows), pl.ds(HALO, cols), :] = own[...].astype(F32)
+    padded[pl.ds(HALO, rows), pl.ds(HALO, cols), :] = own[:, :, lanes].astype(F32)
     for (a, b), ref in zip(edge_keys(), refs, strict=True):
-        value = ref[...].astype(F32)
+        value = ref[:, :, lanes].astype(F32)
         for i in (-1, 1) if a == 0 else (a,):
             for j in (-1, 1) if b == 0 else (b,):
                 on = jnp.float32(1)
@@ -262,9 +271,11 @@
     lax.fori_loop(0, chans // LANES, group, 0)
 
 
-def spread_taps(weights, wide):
-    for t in range(weights.shape[0]):
-        wide[t] = jnp.broadcast_to(weights[pl.ds(t, 1), :], wide.shape[1:])
+def spread_taps(weights, wide, lanes):
+    for i in range(KW):
+        for j in range(KW):
+            row = weights[i, pl.ds(j, 1), lanes]
+            wide[i * KW + j] = jnp.broadcast_to(row, wide.shape[1:])
 
 
 def conv_norm_kernel(own, *refs):
@@ -273,10 +284,10 @@
     weights, bias, gain, shift_, padded, normed, rstd, out, wide, conv = refs
     rows, cols, chans = own.shape
     fill_padded(own, edges, padded)
-    spread_taps(weights, wide)
+    spread_taps(weights, wide, slice(None))
 
     def start(lanes, r, k):
-        return jnp.broadcast_to(bias[:, lanes], (SUBLANES, LANES))
+        return jnp.broadcast_to(bias[lanes].reshape(1, LANES), (SUBLANES, LANES))
 
     def put(lanes, r, k, value):
         conv[pl.ds(r * cols + k * SUBLANES, SUBLANES), lanes] = value
@@ -290,7 +301,7 @@
         unit = centred * scale
         normed[here, :] = unit
         rstd[here, :] = jnp.broadcast_to(scale, (cols, LANES))
-        out[here, :] = (unit * gain[...] + shift_[...]).astype(BF)
+        out[here, :] = (unit * as_row(gain) + as_row(shift_)).astype(BF)
 
 
 def conv_norm(own, edges, weights, bias, gain, shift_):
@@ -307,7 +318,7 @@
         in_specs=vmem(5 + len(edges)),
         out_specs=vmem(4),
         scratch_shapes=[
-            pltpu.VMEM((weights.shape[0], SUBLANES, chans), F32),
+            pltpu.VMEM((KW * KW, SUBLANES, chans), F32),
             pltpu.VMEM((spots, chans), F32),
         ],
         compiler_params=params(20),
@@ -316,22 +327,29 @@
     )(own, *edges, weights, bias, gain, shift_)
 
 
-def norm_back_kernel(n_terms, *refs):
-    terms, refs = refs[:n_terms], refs[n_terms:]
+def rows_of(refs, first, count):
+    for ref in refs:
+        if first < ref.shape[0]:
+            return ref[pl.ds(first, count), :]
+        first -= ref.shape[0]
+
+
+def norm_back_kernel(counts, *refs):
+    terms, refs = split_refs(refs, counts)
     normed, rstd, gain, padded, scale_term, d_conv, keep, send, *edges, sums = refs
     rows, cols = d_conv.shape[:2]
     chans = normed.shape[-1]
     gain_sum = jnp.zeros((SUBLANES, chans), F32)
     for r in range(rows):
         here = pl.ds(r * cols, cols)
-        d_ln = add_up([term[here, :] for term in terms])
+        d_ln = add_up([rows_of(term, r * cols, cols) for term in terms])
         unit = normed[here, :]
         d_unit = d_ln * unit
         for k in range(0, cols, SUBLANES):
             gain_sum = gain_sum + d_unit[k : k + SUBLANES]
-        d_norm = d_ln * gain[...]
+        d_norm = d_ln * as_row(gain)
         mean_one = jnp.mean(d_norm, axis=-1, keepdims=True)
-        mean_two = jnp.mean(d_unit * gain[...], axis=-1, keepdims=True)
+        mean_two = jnp.mean(d_unit * as_row(gain), axis=-1, keepdims=True)
         d_conv[r] = rstd[here, :1] * (d_norm - mean_one - unit * mean_two)
     write_edges(d_conv, edges)
     taps = KW * KW
@@ -374,50 +392,60 @@
     half = -(-(KW * KW + 2) // 64) * 32
     outs = [shaped((rows, cols, chans), F32), shaped((half, chans), F32), shaped((half, chans), F32)]
     outs += edge_shapes(rows, cols, chans)
-    return pl.pallas_call(
-        functools.partial(norm_back_kernel, len(terms)),
+    terms, counts, parts = as_lists(terms)
+    return pl.pallas_call(
+        functools.partial(norm_back_kernel, counts),
         out_shape=outs,
-        in_specs=vmem(5 + len(terms)),
+        in_specs=vmem(5 + len(parts)),
         out_specs=vmem(len(outs)),
         scratch_shapes=[pltpu.VMEM((2, half, chans), F32)],
         compiler_params=params(20),
         cost_estimate=cost(2 * KW * KW * spots * chans, 16 * spots * chans),
         name="norm_back",
-    )(*terms, normed, rstd, gain, padded, scale_term)
-
-
-def conv_back_kernel(own, *refs):
-    count = len(edge_keys())
-    edges, refs = refs[:count], refs[count:]
-    weights, cotangent, out, padded, wide = refs
+    )(*parts, normed, rstd, gain, padded, scale_term)
+
+
+def conv_back_kernel(begin, count, own, *refs):
+    edges, refs = refs[: len(edge_keys())], refs[len(edge_keys()) :]
+    weights, cotangent, *_, out, padded, wide, part, sem = refs
+    rows, cols = own.shape[:2]
+    mine = pl.ds(begin, count)
+    fill_padded(own, edges, padded, mine)
+    spread_taps(weights, wide, mine)
+
+    def start(lanes, r, k):
+        here = pl.ds(pl.multiple_of(lanes.start + begin, LANES), LANES)
+        return cotangent[r, pl.ds(k * SUBLANES, SUBLANES), here].astype(F32)
+
+    def put(lanes, r, k, value):
+        part[r, pl.ds(k * SUBLANES, SUBLANES), lanes] = value.astype(BF)
+
+    convolve(padded, wide, start, put, rows, cols, count, True)
+    copy = pltpu.make_async_copy(part, out.at[:, :, mine], sem)
+    copy.start()
+    copy.wait()
+
+
+def conv_back(own, edges, weights, cotangent, begin, count, before):
     rows, cols, chans = own.shape
-    fill_padded(own, edges, padded)
-    spread_taps(weights, wide)
-
-    def start(lanes, r, k):
-        return cotangent[r, pl.ds(k * SUBLANES, SUBLANES), lanes].astype(F32)
-
-    def put(lanes, r, k, value):
-        out[r, pl.ds(k * SUBLANES, SUBLANES), lanes] = value.astype(BF)
-
-    convolve(padded, wide, start, put, rows, cols, chans, True)
-
-
-def conv_back(own, edges, weights, cotangent):
-    rows, cols, chans = own.shape
-    return pl.pallas_call(
-        conv_back_kernel,
+    extra = [] if before is None else [before]
+    given = 3 + len(edges)
+    return pl.pallas_call(
+        functools.partial(conv_back_kernel, begin, count),
         out_shape=shaped((rows, cols, chans), BF),
-        in_specs=vmem(3 + len(edges)),
-        out_specs=pl.BlockSpec(memory_space=pltpu.VMEM),
+        in_specs=vmem(given) + anywhere(len(extra)),
+        out_specs=pl.BlockSpec(memory_space=pl.ANY),
         scratch_shapes=[
-            pltpu.VMEM((rows + 2 * HALO, cols + 8, chans), F32),
-            pltpu.VMEM((weights.shape[0], SUBLANES, chans), F32),
+            pltpu.VMEM((rows + 2 * HALO, cols + 8, count), F32),
+            pltpu.VMEM((KW * KW, SUBLANES, count), F32),
+            pltpu.VMEM((rows, cols, count), BF),
+            pltpu.SemaphoreType.DMA,
         ],
-        compiler_params=params(20),
-        cost_estimate=cost(2 * KW * KW * rows * cols * chans, 10 * rows * cols * chans),
+        input_output_aliases={given: 0} if extra else {},
+        compiler_params=params(16),
+        cost_estimate=cost(2 * KW * KW * rows * cols * count, 10 * rows * cols * count),
         name="conv_back",
-    )(own, *edges, weights, cotangent)
+    )(own, *edges, weights, cotangent, *extra)
 
 
 def start_copies(jobs, sems, first):
@@ -464,13 +492,14 @@
     two = start_copies(row_jobs(lns, ln_all), sems, len(one))
     three = start_copies(row_jobs(cots, cot_all), sems, len(one) + len(two))
     wait_all(three)
-    d_mlp[...] = (scale[...] * cot_all[...].astype(F32)).astype(BF)
+    d_mlp[...] = (as_row(scale) * cot_all[...].astype(F32)).astype(BF)
     wait_all(one + two)
     hidden = whole.shape[1]
     quarter = lax.axis_index("sx") * lax.axis_size("sy") + lax.axis_index("sy")
     for tile in hidden_tiles(hidden):
         columns = pl.ds(pl.multiple_of(quarter * hidden + tile.start, LANES), tile.size)
-        v = jnp.dot(ln_all[...], whole[:, tile], preferred_element_type=F32) + bias[:, columns]
+        v = jnp.dot(ln_all[...], whole[:, tile], preferred_element_type=F32)
+        v = v + bias[columns].reshape(1, tile.size)
         square = v * v
         th = jnp.tanh(GELU_A * (v + GELU_B * (square * v)))
         half = 0.5 + 0.5 * th
@@ -516,105 +545,197 @@
 
 
 def write_pieces(value, tile, outs):
-    spots = outs[0].shape[0]
-    for k, out in enumerate(outs):
-        out[:, tile] = value[k * spots : (k + 1) * spots].astype(BF)
-
-
-def down_kernel(where, n_near, *refs):
+    first = 0
+    for out in outs:
+        count = out.shape[0]
+        out[:, tile] = value[first : first + count].astype(BF)
+        first += count
+
+
+def far_kernel(where, first, *refs):
     blocks, refs = refs[: len(where)], refs[len(where) :]
-    d_mlp, slope, up, whole, d_pre, *far, d_mlp_in, slope_in, up_in, sems = refs
+    d_mlp, slope, up, *far, whole, d_mlp_in, slope_in, up_in, d_pre, sems = refs
+    count = d_pre.shape[0]
+    mine = pl.ds(first, count)
     one = start_copies(block_jobs(blocks, where, whole), sems, 0)
-    two = start_copies([(d_mlp, d_mlp_in), (slope, slope_in), (up, up_in)], sems, len(one))
+    jobs = [(d_mlp.at[mine], d_mlp_in), (slope.at[mine], slope_in), (up, up_in)]
+    two = start_copies(jobs, sems, len(one))
     wait_all(one + two[:2])
     for tile in hidden_tiles(whole.shape[1]):
         d_act = jnp.dot(d_mlp_in[...], whole[:, tile], preferred_element_type=F32)
         d_pre[:, tile] = (d_act * slope_in[:, tile]).astype(BF)
     wait_all(two[2:])
-    first = n_near * far[0].shape[0]
     for tile in channel_tiles(up_in.shape[0]):
-        write_pieces(contract_last(d_pre[first:, :], up_in[tile, :]), tile, far)
-
-
-def down_part(blocks, where, d_mlp, slope, up, n_near, n_far):
+        write_pieces(contract_last(d_pre[...], up_in[tile, :]), tile, far)
+
+
+def far_part(blocks, where, d_mlp, slope, up, n_near, n_far):
     total, chans = d_mlp.shape
     hidden = slope.shape[1]
     spots = total // (n_near + n_far)
     count = len(blocks) + 3
-    outs = [shaped(up.shape, BF), shaped((total, hidden), BF)] + [shaped((spots, chans), BF)] * n_far
-    return pl.pallas_call(
-        functools.partial(down_kernel, where, n_near),
+    outs = [shaped((spots, chans), BF)] * n_far
+    return pl.pallas_call(
+        functools.partial(far_kernel, where, n_near * spots),
         out_shape=outs,
         in_specs=anywhere(count),
         out_specs=vmem(len(outs)),
         scratch_shapes=[
-            pltpu.VMEM((total, chans), BF),
-            pltpu.VMEM((total, hidden), F32),
             pltpu.VMEM(up.shape, BF),
+            pltpu.VMEM((n_far * spots, chans), BF),
+            pltpu.VMEM((n_far * spots, hidden), F32),
+            pltpu.VMEM(up.shape, BF),
+            pltpu.VMEM((n_far * spots, hidden), BF),
             pltpu.SemaphoreType.DMA((count,)),
         ],
-        compiler_params=params(24),
-        cost_estimate=cost(3 * total * chans * hidden, 8 * total * chans),
-        name="down_part",
+        compiler_params=params(20),
+        cost_estimate=cost(4 * n_far * spots * chans * hidden, 8 * total * chans),
+        name="far_part",
     )(*blocks, d_mlp, slope, up)
 
 
-def near_kernel(d_pre, up, *outs):
-    rows = len(outs) * outs[0].shape[0]
-    for tile in channel_tiles(up.shape[0]):
-        write_pieces(contract_last(d_pre[:rows, :], up[tile, :]), tile, outs)
-
-
-def near_part(d_pre, up, spots, n_near):
-    chans, hidden = up.shape
-    outs = [shaped((spots, chans), BF)] * n_near
-    return pl.pallas_call(
-        near_kernel,
-        out_shape=outs,
-        in_specs=vmem(2),
-        out_specs=vmem(len(outs)),
-        compiler_params=params(16),
-        cost_estimate=cost(2 * n_near * spots * chans * hidden, 4 * spots * chans),
-        name="near_part",
-    )(d_pre, up)
-
-
-def mlp_kernel(tiles, act, down, bias, *refs):
+def rest_kernel(where, tiles, n_near, n_mlp, *refs):
+    blocks, refs = refs[: len(where)], refs[len(where) :]
     cots, refs = refs[:tiles], refs[tiles:]
-    *outs, scale_term = refs
+    d_mlp, slope, up, act, bias, *refs = refs
+    near, outs, refs = refs[:n_near], refs[n_near : n_near + n_mlp], refs[n_near + n_mlp :]
+    scale_term, whole, d_mlp_in, slope_in, up_in, act_in, d_pre, sems = refs
     spots = cots[0].shape[0]
-    for tile in channel_tiles(down.shape[0]):
-        value = contract_last(act[...], down[tile, :])
+    mine = pl.ds(0, d_pre.shape[0])
+    one = start_copies(block_jobs(blocks, where, whole), sems, 0)
+    jobs = [(d_mlp.at[mine], d_mlp_in), (slope.at[mine], slope_in), (up, up_in), (act, act_in)]
+    two = start_copies(jobs, sems, len(one))
+    wait_all(one + two[:2])
+    for tile in hidden_tiles(whole.shape[1]):
+        d_act = jnp.dot(d_mlp_in[...], whole[:, tile], preferred_element_type=F32)
+        d_pre[:, tile] = (d_act * slope_in[:, tile]).astype(BF)
+    wait_all(two[2:])
+    for tile in channel_tiles(up_in.shape[0]):
+        write_pieces(contract_last(d_pre[...], up_in[tile, :]), tile, near)
+    for tile in channel_tiles(whole.shape[0]):
+        value = contract_last(act_in[...], whole[tile, :])
         write_pieces(value, tile, outs)
         total = jnp.zeros((1, tile.size), F32)
         for k, cot in enumerate(cots):
             grad = cot[:, tile].astype(F32)
             mlp = value[k * spots : (k + 1) * spots]
             if k == 0:
-                mlp = mlp + bias[:, tile]
+                mlp = mlp + bias[tile].reshape(1, tile.size)
             total = total + jnp.sum(grad * mlp, axis=0, keepdims=True)
         scale_term[:, tile] = total
 
 
-def mlp_part(act, down, bias, cots):
-    chans, hidden = down.shape
-    spots = cots[0].shape[0]
+def rest_part(blocks, where, d_mlp, slope, up, act, bias, cots, n_near):
+    total, chans = d_mlp.shape
+    hidden = slope.shape[1]
     tiles = len(cots)
-    outs = [shaped((spots, chans), BF)] * tiles + [shaped((1, chans), F32)]
-    return pl.pallas_call(
-        functools.partial(mlp_kernel, tiles),
+    spots = total // tiles
+    count = len(blocks) + 4
+    group = [spots] + [spots // 2] * (2 * n_near - 2)
+    groups = group * (1 + tiles // n_near)
+    outs = [shaped((rows, chans), BF) for rows in groups] + [shaped((1, chans), F32)]
+    return pl.pallas_call(
+        functools.partial(rest_kernel, where, tiles, len(group), len(groups) - len(group)),
         out_shape=outs,
-        in_specs=vmem(3 + tiles),
+        in_specs=anywhere(len(blocks)) + vmem(tiles) + anywhere(4) + vmem(1),
         out_specs=vmem(len(outs)),
-        compiler_params=params(24),
-        cost_estimate=cost(2 * tiles * spots * chans * hidden, 6 * tiles * spots * chans),
-        name="mlp_part",
-    )(act, down, bias, *cots)
+        scratch_shapes=[
+            pltpu.VMEM(up.shape, BF),
+            pltpu.VMEM((n_near * spots, chans), BF),
+            pltpu.VMEM((n_near * spots, hidden), F32),
+            pltpu.VMEM(up.shape, BF),
+            pltpu.VMEM((total, hidden), BF),
+            pltpu.VMEM((n_near * spots, hidden), BF),
+            pltpu.SemaphoreType.DMA((count,)),
+        ],
+        compiler_params=params(28),
+        cost_estimate=cost(2 * (2 * n_near + tiles) * spots * chans * hidden, 10 * total * chans),
+        name="rest_part",
+    )(*blocks, *cots, d_mlp, slope, up, act, bias)
+
+
+def split_refs(refs, counts):
+    out = []
+    for count in counts:
+        out.append(refs[:count])
+        refs = refs[count:]
+    return out, refs
+
+
+def as_lists(terms):
+    terms = [term if isinstance(term, list) else [term] for term in terms]
+    return terms, [len(term) for term in terms], [part for term in terms for part in term]
+
+
+def add_kernel(counts, *refs):
+    terms, outs = split_refs(refs, counts)
+    step, base = 16, 0
+    for out in outs:
+        for first in range(0, out.shape[0], step):
+            value = add_up([rows_of(term, base + first, step) for term in terms])
+            out[pl.ds(first, step), :] = value.astype(BF)
+        base += out.shape[0]
+
+
+def add_rounded(terms, sizes):
+    terms, counts, parts = as_lists(terms)
+    chans = terms[0][0].shape[1]
+    return pl.pallas_call(
+        functools.partial(add_kernel, counts),
+        out_shape=[shaped((size, chans), BF) for size in sizes],
+        in_specs=vmem(len(parts)),
+        out_specs=vmem(len(sizes)),
+        compiler_params=params(16),
+        cost_estimate=cost(1, 1),
+        name="add_rounded",
+    )(*parts)
+
+
+def output_kernel(counts, scaled, scale, bias, *refs):
+    terms, (out,) = split_refs(refs, counts)
+    rows, cols = out.shape[:2]
+    for r in range(rows):
+        mlp = add_up([rows_of(term, r * cols, cols) for term in terms]) + as_row(bias)
+        out[r] = (scaled[r].astype(F32) + as_row(scale) * mlp).astype(BF)
+
+
+def output_part(scaled, scale, bias, terms):
+    terms, counts, parts = as_lists(terms)
+    return pl.pallas_call(
+        functools.partial(output_kernel, counts),
+        out_shape=shaped(scaled.shape, BF),
+        in_specs=vmem(3 + len(parts)),
+        out_specs=pl.BlockSpec(memory_space=pltpu.VMEM),
+        compiler_params=params(16),
+        cost_estimate=cost(1, 1),
+        name="output_part",
+    )(scaled, scale, bias, *parts)
+
+
+def quarters_kernel(keep, got, *parts):
+    rows = parts[0].shape[0]
+    me = 2 * (lax.axis_index("sy") % 2) + lax.axis_index("fsdp") % 2
+    for k, part in enumerate(parts):
+        here = pl.ds(pl.multiple_of((me ^ k) * rows, rows), rows)
+        part[...] = keep[here, :] + got[here, :]
+
+
+def quarters(keep, got):
+    rows, chans = keep.shape
+    return pl.pallas_call(
+        quarters_kernel,
+        out_shape=[shaped((rows // 4, chans), F32)] * 4,
+        in_specs=vmem(2),
+        out_specs=vmem(4),
+        compiler_params=params(16),
+        cost_estimate=cost(rows * chans, 12 * rows * chans),
+        name="quarters",
+    )(keep, got)
 
 
 def finish_kernel(*refs):
     mine, other = refs[:4], refs[4:8]
-    grad_kernel, gain_row, scale_row, sums = refs[8:]
+    grad_kernel, grad_gain, grad_scale, sums = refs[8:]
     core = lax.axis_index("sx") % 2
     me = 2 * (lax.axis_index("sy") % 2) + lax.axis_index("fsdp") % 2
     for k in range(4):
@@ -628,15 +749,15 @@
     for i in range(KW):
         for j in range(KW):
             grad_kernel[i, pl.ds(j, 1), :] = row(i * KW + j)
-    gain_row[...] = row(KW * KW)
-    scale_row[...] = row(KW * KW + 1)
+    grad_gain[...] = row(KW * KW).reshape(grad_gain.shape)
+    grad_scale[...] = row(KW * KW + 1).reshape(grad_scale.shape)
 
 
 def finish(mine, other):
     rows, chans = mine[0].shape
     return pl.pallas_call(
         finish_kernel,
-        out_shape=(shaped((KW, KW, chans), F32), shaped((1, chans), F32), shaped((1, chans), F32)),
+        out_shape=(shaped((KW, KW, chans), F32), shaped((chans,), F32), shaped((chans,), F32)),
         in_specs=vmem(8),
         out_specs=vmem(3),
         scratch_shapes=[pltpu.VMEM((2, 4, rows, chans), F32)],
@@ -669,35 +790,44 @@
     up_block = lax.dynamic_slice_in_dim(w_up, quarter * hidden, hidden, 1)
     down_block = lax.dynamic_slice_in_dim(w_down, quarter * hidden, hidden, 0).T
     ups, up_where = ring_gather(up_block)
-    downs, down_where = ring_gather(down_block)
-    cots = gather_tile(cotangent.reshape(spots, chans))
 
     scaled, *edges = prepare(x_code[0], x_exp[0])
     edges = exchange_edges(dict(zip(edge_keys(), edges, strict=True)))
-    weights = dw_kernel.reshape(KW * KW, chans)
-    padded, normed, rstd, ln_out = conv_norm(
-        scaled, list(edges.values()), weights, dw_bias[None], ln_gain[None], ln_bias[None]
-    )
+    downs, down_where = ring_gather(down_block)
+    edges, _ = lax.optimization_barrier((list(edges.values()), ups[1:3] + downs[1:3]))
+    padded, normed, rstd, ln_out = conv_norm(scaled, edges, dw_kernel, dw_bias, ln_gain, ln_bias)
+    ln_out, _ = lax.optimization_barrier((ln_out, ups[3:5]))
     lns = gather_tile(ln_out)
-    act, slope, up, d_mlp = up_part(ups, up_where, lns, cots, b_up[None], layer_scale[None])
-    down, d_pre, *far = down_part(downs, down_where, d_mlp, slope, up, n_near, tiles - n_near)
+    cot, edges = lax.optimization_barrier((cotangent.reshape(spots, chans), edges))
+    cots = gather_tile(cot)
+    act, slope, up, d_mlp = up_part(ups, up_where, lns, cots, b_up, layer_scale)
+    far = far_part(downs, down_where, d_mlp, slope, up, n_near, tiles - n_near)
 
     far = [far[k : k + n_near] for k in range(0, len(far), n_near)]
-    far = [add_up(reduce_cores(group)).astype(BF) for group in far]
+    far = [add_rounded(reduce_cores(group), [spots])[0] for group in far]
+    d_mlp, far = lax.optimization_barrier((d_mlp, far))
     far = [shift(term, "sy", -(t + 1)) for t, term in enumerate(far)]
-    near = reduce_cores(near_part(d_pre, up, spots, n_near))
-    *mlp, scale_term = mlp_part(act, down, b_down[None], cots)
-    d_conv, keep, send, *edges = norm_back(near + far, normed, rstd, ln_gain[None], padded, scale_term)
-    edges = exchange_edges(dict(zip(edge_keys(), edges, strict=True)))
-
-    mlp = [reduce_cores(mlp[k : k + n_near]) for k in range(0, tiles, n_near)]
-    rest = [shift(add_up(group).astype(BF), "sy", -(t + 1)) for t, group in enumerate(mlp[1:])]
-    value = add_up(mlp[0] + rest) + b_down
-    block_out = (scaled.astype(F32) + layer_scale * value.reshape(rows, cols, chans)).astype(BF)
-
-    grad_input = conv_back(d_conv, list(edges.values()), weights, cotangent[0])
-    grad_kernel, grad_gain, grad_scale = finish(*sum_rows(keep, send))
-    return (block_out[None], grad_input[None], grad_kernel, grad_gain[0], grad_scale[0])
+    *rest, scale_term = rest_part(downs, down_where, d_mlp, slope, up, act, b_down, cots, n_near)
+    size = 2 * n_near - 1
+    near, *mlp = [reduce_cores_halves(rest[k : k + size]) for k in range(0, len(rest), size)]
+    mlp_far = [add_rounded(group, [spots - spots // 4, spots // 4]) for group in mlp[1:]]
+    far, mlp_far = lax.optimization_barrier((far, mlp_far))
+    mlp_far = [[shift(part, "sy", -(t + 1)) for part in term] for t, term in enumerate(mlp_far)]
+    d_conv, keep, send, *edges = norm_back(near + far, normed, rstd, ln_gain, padded, scale_term)
+    send, first_parts = lax.optimization_barrier((swap(send, sx=1), [term[0] for term in mlp_far]))
+    parts = quarters(keep, send)
+    edges = list(exchange_edges(dict(zip(edge_keys(), edges, strict=True))).values())
+    half = chans // 2 // LANES * LANES
+    grad_input = conv_back(d_conv, edges, dw_kernel, cotangent[0], 0, half, None)
+    second_parts = [term[1] for term in mlp_far]
+    total, grad_input, second_parts = lax.optimization_barrier((sum_quarters(parts), grad_input, second_parts))
+    mlp_far = [list(term) for term in zip(first_parts, second_parts, strict=True)]
+    total = sum_others(total)
+    grad_input = conv_back(d_conv, edges, dw_kernel, cotangent[0], half, chans - half, grad_input)
+    total, grad_input = lax.optimization_barrier((total, grad_input))
+    block_out = output_part(scaled, layer_scale, b_down, mlp[0] + mlp_far)
+    grad_kernel, grad_gain, grad_scale = finish(*spread_quarter(total))
+    return (block_out[None], grad_input[None], grad_kernel, grad_gain, grad_scale)
 
 
 def solution(mesh):

time: 135 us -> 118 us (0.87)
  waiting for transfers between devices: 47.2 us -> 36.1 us
  local copies, waits for them, and re-layouts: 12.1 us -> 5.31 us
  other arithmetic: 4.39 us -> 0.03 us
  starting transfers between devices: 39.8 us -> 42.6 us
  Pallas kernels: 30.4 us -> 32.2 us
    ppermute x12 -> x16, waiting for transfers between devices: 14.3 us -> 8.54 us  [shift(): return lax.ppermute(a, axis, [((i + k) % n, i) for i in range(n)])]
    ppermute x14, waiting for transfers between devices: 9.5 us -> 5.82 us  [swap(): return lax.ppermute(a, axes, [(i, i ^ mask) for i in range(total)])]
    unnamed x45 -> x23, local copies, waits for them, and re-layouts: 7.18 us -> 4.26 us
    ppermute x2, starting transfers between devices: 0.67 us -> 2.98 us  [ring_gather(): pieces.append(lax.ppermute(two[half:], 'fsdp', back))]
    broadcast_in_dim x5 -> x0, local copies, waits for them, and re-layouts: 2.16 us -> none  [the longest x1 0.75 us: on_device(): dw_bias[None]]
    ppermute x6, waiting for transfers between devices: 5.91 us -> 3.86 us  [exchange_edges(): got[a, b] = lax.ppermute(piece, ('sx', 'sy'), pairs)]
    ppermute x6, waiting for transfers between devices: 12.9 us -> 14.6 us  [ring_gather(): one = lax.ppermute(one, 'fsdp', forth)]
    pallas_call x5 -> x9, Pallas kernels: 18.4 us -> 20 us  [the longest x2 6.3 us: conv_back(): pl.pallas_call(functools.partial(conv_back_kernel, begin, count), out_sha...]
  transfers between devices with their start and end apart: 48 -> 52, of which waited for: 18 -> 20; matrix products, arithmetic and copies ran while one was open for 5% -> 2% of each run, Pallas kernels for 15% -> 24%
where the time goes in v3:
time: 118 us; the launch traced here: 117 us
  starting transfers between devices  42.6 us (36%)
  waiting for transfers between devices  36.1 us (31%)
  Pallas kernels  32.2 us (27%)
  local copies, waits for them, and re-layouts  5.31 us (4%)
    ppermute x6, waiting for transfers between devices, ring_gather(): one = lax.ppermute(one, 'fsdp', forth)  14.6 us
    ppermute x6, starting transfers between devices, ring_gather(): one = lax.ppermute(one, 'fsdp', forth)  11.9 us
    ppermute x14, starting transfers between devices, swap(): return lax.ppermute(a, axes, [(i, i ^ mask) for i in range(total)])  11.6 us
    ppermute x16, waiting for transfers between devices, shift(): return lax.ppermute(a, axis, [((i + k) % n, i) for i in range(n)])  8.54 us
    ppermute x16, starting transfers between devices, shift(): return lax.ppermute(a, axis, [((i + k) % n, i) for i in range(n)])  6.88 us
    pallas_call x2, Pallas kernels, conv_back(): pl.pallas_call(functools.partial(conv_back_kernel, begin, count), out_sha...  6.3 us
    ppermute x14, waiting for transfers between devices, swap(): return lax.ppermute(a, axes, [(i, i ^ mask) for i in range(total)])  5.82 us
    pallas_call x1, Pallas kernels, conv_norm(): pl.pallas_call(conv_norm_kernel, out_shape=(shaped((rows + 2 * HALO, cols...  5.8 us
  transfers between devices with their start and end apart: 52, of which 20 were waited for; matrix products, arithmetic and copies ran while one was open for 2% of the time, Pallas kernels for 24%

profile of v3, /device:TPU:0, one launch (start us, length us, event | category | flops | bytes accessed | tf_op | source)
XLA Modules:
  0.0 117.2 jit_solution(6709821310571962650)
XLA Ops:
  0.7 1.2 %copy-done = bf16[192,3072]{1,0:T(8,128)(2,1)S(1)} copy-done((bf16[192,3072]{1,0:T(8,128)(2,1)S(1)}, bf16[192,3072]{1,0:T(8,128)(2,1)}, u32[]{:S(2)}) %copy-start) | copy-done | bytes 1179672
  1.9 3.1 %collective-permute-start.11 = (bf16[192,768]{1,0:T(8,128)(2,1)S(1)}, bf16[192,768]{1,0:T(8,128)(2,1)}, u32[]{:S(2)}, u32[]{:S(2)}) collective-permute-start(bf16[192,768]{1,0:T(8,128)(2,1)S(1)} %constant_dynamic-slice_fusion.refs_0_), channel_id=1, source_target_pairs={{0,2},{2,4},{4,6},{6,7},{7,5},{5,3},{3,1},{1,0},{8,10},{10,12},{12... | collective-permute-start | bytes 884744 | tf_op jit(solution)/shard_map/ppermute | solution.py:107
  5.0 1.0 dynamic-slice_bitcast_fusion.refs_0_
  6.0 2.1 %collective-permute-start = (bf16[192,768]{1,0:T(8,128)(2,1)S(1)}, bf16[192,768]{1,0:T(8,128)(2,1)S(1)}, u32[]{:S(2)}, u32[]{:S(2)}) collective-permute-start(bf16[192,768]{1,0:T(8,128)(2,1)S(1)} %dynamic-slice_bitcast_fusion.refs_0_), channel_id=1, source_target_pairs={{0,2},{2,4},{4,6},{6,7},{7,5},{5,3},{3,1},{1,0},{8,10},{10,12},{12... | collective-permute-start | bytes 884744 | tf_op jit(solution)/shard_map/ppermute | solution.py:107
  8.1 0.9 copy.18
  9.0 0.5 prepare.1
  9.9 3.0 %collective-permute-done.11.refs_1_ = bf16[192,768]{1,0:T(8,128)(2,1)} collective-permute-done((bf16[192,768]{1,0:T(8,128)(2,1)S(1)}, bf16[192,768]{1,0:T(8,128)(2,1)}, u32[]{:S(2)}, u32[]{:S(2)}) %collective-permute-start.11) | collective-permute-done | bytes 294944 | tf_op jit(solution)/shard_map/ppermute | solution.py:107
  12.9 2.1 %collective-permute-start.16 = (bf16[192,768]{1,0:T(8,128)(2,1)}, bf16[192,768]{1,0:T(8,128)(2,1)S(1)}, u32[]{:S(2)}, u32[]{:S(2)}) collective-permute-start(bf16[192,768]{1,0:T(8,128)(2,1)} %collective-permute-done.11.refs_1_), channel_id=1, source_target_pairs={{0,2},{2,4},{4,6},{6,7},{7,5},{5,3},{3,1},{1,0},{8,10},{10,12},{12... | collective-permute-start | bytes 884744 | tf_op jit(solution)/shard_map/ppermute | solution.py:107
  15.0 1.5 %collective-permute-start.9 = (bf16[8,3,1536]{2,1,0:T(4,128)(2,1)S(1)}, bf16[8,3,1536]{2,1,0:T(4,128)(2,1)S(1)}, u32[]{:S(2)}, u32[]{:S(2)}) collective-permute-start(bf16[8,3,1536]{2,1,0:T(4,128)(2,1)S(1)} %get-tuple-element.63), channel_id=1, source_target_pairs={{0,8},{8,0},{16,24},{24,16},{1,9},{9,1},{17,25},{25,17},{2,10},{10... | collective-permute-start | bytes 221192 | tf_op jit(solution)/shard_map/ppermute | solution.py:74
  16.5 3.1 %collective-permute-done.9.refs_1_ = bf16[8,3,1536]{2,1,0:T(4,128)(2,1)S(1)} collective-permute-done((bf16[8,3,1536]{2,1,0:T(4,128)(2,1)S(1)}, bf16[8,3,1536]{2,1,0:T(4,128)(2,1)S(1)}, u32[]{:S(2)}, u32[]{:S(2)}) %collective-permute-start.9) | collective-permute-done | bytes 73760 | tf_op jit(solution)/shard_map/ppermute | solution.py:74
  19.6 0.5 collective-permute-start.17
  20.2 1.5 %collective-permute-start.2 = (bf16[192,768]{1,0:T(8,128)(2,1)S(1)}, bf16[192,768]{1,0:T(8,128)(2,1)S(1)}, u32[]{:S(2)}, u32[]{:S(2)}) collective-permute-start(bf16[192,768]{1,0:T(8,128)(2,1)S(1)} %collective-permute-done.refs_1_), channel_id=1, source_target_pairs={{0,2},{2,4},{4,6},{6,7},{7,5},{5,3},{3,1},{1,0},{8,10},{10,12},{12... | collective-permute-start | bytes 884744 | tf_op jit(solution)/shard_map/ppermute | solution.py:107
  21.7 0.5 collective-permute-start.3
  22.2 1.4 %collective-permute-start.14 = (bf16[128,1536]{1,0:T(8,128)(2,1)S(1)}, bf16[128,1536]{1,0:T(8,128)(2,1)S(1)}, u32[]{:S(2)}, u32[]{:S(2)}) collective-permute-start(bf16[128,1536]{1,0:T(8,128)(2,1)S(1)} %bitcast.8), channel_id=1, source_target_pairs={{8,0},{0,8},{9,1},{1,9},{10,2},{2,10},{11,3},{3,11},{12,4},{4,12},... | collective-permute-start | bytes 1179656 | tf_op jit(solution)/shard_map/ppermute | solution.py:54
  23.6 1.8 %collective-permute-done.16.refs_3_ = bf16[192,768]{1,0:T(8,128)(2,1)S(1)} collective-permute-done((bf16[192,768]{1,0:T(8,128)(2,1)}, bf16[192,768]{1,0:T(8,128)(2,1)S(1)}, u32[]{:S(2)}, u32[]{:S(2)}) %collective-permute-start.16) | collective-permute-done | bytes 294944 | tf_op jit(solution)/shard_map/ppermute | solution.py:107
  25.4 0.7 copy-done.4
  26.1 0.7 copy-done.9
  26.8 0.7 copy-done.10
  27.5 5.8 %conv_norm.1 = (f32[14,24,1536]{2,1,0:T(8,128)S(1)}, f32[128,1536]{1,0:T(8,128)S(1)}, f32[128,128]{1,0:T(8,128)S(1)}, bf16[128,1536]{1,0:T(8,128)(2,1)S(1)}) custom-call(bf16[8,16,1536]{2,1,0:T(8,128)(2,1)S(1)} %get-tuple-element.61.own.scaled, bf16[3,16,1536]{2,1,0:T(8,128)(2,1)S(1)} %collective-permute-done.8.refs_0_, ...), custom_call_target="tpu_custom_call" | custom-call | flops 1 | bytes 1 | tf_op jit(solution)/shard_map/conv_norm/pallas_call | solution.py:310
  33.4 2.1 %collective-permute-start.23 = (bf16[128,1536]{1,0:T(8,128)(2,1)S(1)}, bf16[128,1536]{1,0:T(8,128)(2,1)S(1)}, u32[]{:S(2)}, u32[]{:S(2)}) collective-permute-start(bf16[128,1536]{1,0:T(8,128)(2,1)S(1)} %get-tuple-element.70.refs_9_), channel_id=1, source_target_pairs={{8,0},{0,8},{9,1},{1,9},{10,2},{2,10},{11,3},{3,11},{12,4},{4,12},... | collective-permute-start | bytes 1179656 | tf_op jit(solution)/shard_map/ppermute | solution.py:54
  35.5 1.6 %collective-permute-start.18 = (bf16[192,768]{1,0:T(8,128)(2,1)S(1)}, bf16[192,768]{1,0:T(8,128)(2,1)S(1)}, u32[]{:S(2)}, u32[]{:S(2)}) collective-permute-start(bf16[192,768]{1,0:T(8,128)(2,1)S(1)} %collective-permute-done.16.refs_3_), channel_id=1, source_target_pairs={{0,2},{2,4},{4,6},{6,7},{7,5},{5,3},{3,1},{1,0},{8,10},{10,12},{12... | collective-permute-start | bytes 884744 | tf_op jit(solution)/shard_map/ppermute | solution.py:107
  37.0 0.5 collective-permute-start.19
  37.5 1.6 %collective-permute-start.4 = (bf16[192,768]{1,0:T(8,128)(2,1)S(1)}, bf16[192,768]{1,0:T(8,128)(2,1)S(1)}, u32[]{:S(2)}, u32[]{:S(2)}) collective-permute-start(bf16[192,768]{1,0:T(8,128)(2,1)S(1)} %collective-permute-done.2.refs_3_), channel_id=1, source_target_pairs={{0,2},{2,4},{4,6},{6,7},{7,5},{5,3},{3,1},{1,0},{8,10},{10,12},{12... | collective-permute-start | bytes 884744 | tf_op jit(solution)/shard_map/ppermute | solution.py:107
  39.1 6.2 %collective-permute-done.18.refs_5_ = bf16[192,768]{1,0:T(8,128)(2,1)S(1)} collective-permute-done((bf16[192,768]{1,0:T(8,128)(2,1)S(1)}, bf16[192,768]{1,0:T(8,128)(2,1)S(1)}, u32[]{:S(2)}, u32[]{:S(2)}) %collective-permute-start.18) | collective-permute-done | bytes 294944 | tf_op jit(solution)/shard_map/ppermute | solution.py:107
  45.3 1.5 %collective-permute-start.5 = (bf16[192,768]{1,0:T(8,128)(2,1)S(1)}, bf16[192,768]{1,0:T(8,128)(2,1)S(1)}, u32[]{:S(2)}, u32[]{:S(2)}) collective-permute-start(bf16[192,768]{1,0:T(8,128)(2,1)S(1)} %collective-permute-done.3.refs_4_), channel_id=1, source_target_pairs={{2,0},{4,2},{6,4},{7,6},{5,7},{3,5},{1,3},{0,1},{10,8},{12,10},{14... | collective-permute-start | bytes 884744 | tf_op jit(solution)/shard_map/ppermute | solution.py:108
  46.8 0.5 collective-permute-start.24
  47.3 3.6 %collective-permute-done.4.refs_5_ = bf16[192,768]{1,0:T(8,128)(2,1)S(1)} collective-permute-done((bf16[192,768]{1,0:T(8,128)(2,1)S(1)}, bf16[192,768]{1,0:T(8,128)(2,1)S(1)}, u32[]{:S(2)}, u32[]{:S(2)}) %collective-permute-start.4) | collective-permute-done | bytes 294944 | tf_op jit(solution)/shard_map/ppermute | solution.py:107
  50.9 1.6 %collective-permute-start.20 = (bf16[96,768]{1,0:T(8,128)(2,1)S(1)}, bf16[96,768]{1,0:T(8,128)(2,1)S(1)}, u32[]{:S(2)}, u32[]{:S(2)}) collective-permute-start(bf16[96,768]{1,0:T(8,128)(2,1)S(1)} %slice.18), channel_id=1, source_target_pairs={{0,2},{2,4},{4,6},{6,7},{7,5},{5,3},{3,1},{1,0},{8,10},{10,12},{12... | collective-permute-start | bytes 442376 | tf_op jit(solution)/shard_map/ppermute | solution.py:114
  52.9 1.5 %collective-permute-start.21 = (bf16[96,768]{1,0:T(8,128)(2,1)S(1)}, bf16[96,768]{1,0:T(8,128)(2,1)S(1)}, u32[]{:S(2)}, u32[]{:S(2)}) collective-permute-start(bf16[96,768]{1,0:T(8,128)(2,1)S(1)} %slice.19), channel_id=1, source_target_pairs={{2,0},{4,2},{6,4},{7,6},{5,7},{3,5},{1,3},{0,1},{10,8},{12,10},{14... | collective-permute-start | bytes 442376 | tf_op jit(solution)/shard_map/ppermute | solution.py:116
  54.5 0.6 collective-permute-start.6
  55.0 2.5 %collective-permute-done.20.refs_7_ = bf16[96,768]{1,0:T(8,128)(2,1)S(1)} collective-permute-done((bf16[96,768]{1,0:T(8,128)(2,1)S(1)}, bf16[96,768]{1,0:T(8,128)(2,1)S(1)}, u32[]{:S(2)}, u32[]{:S(2)}) %collective-permute-start.20) | collective-permute-done | bytes 147488 | tf_op jit(solution)/shard_map/ppermute | solution.py:114
  57.5 1.5 %collective-permute-start.7 = (bf16[96,768]{1,0:T(8,128)(2,1)S(1)}, bf16[96,768]{1,0:T(8,128)(2,1)S(1)}, u32[]{:S(2)}, u32[]{:S(2)}) collective-permute-start(bf16[96,768]{1,0:T(8,128)(2,1)S(1)} %slice.17), channel_id=1, source_target_pairs={{2,0},{4,2},{6,4},{7,6},{5,7},{3,5},{1,3},{0,1},{10,8},{12,10},{14... | collective-permute-start | bytes 442376 | tf_op jit(solution)/shard_map/ppermute | solution.py:116
  59.3 5.0 %up_part.1 = (bf16[512,768]{1,0:T(8,128)(2,1)S(1)}, f32[512,768]{1,0:T(8,128)S(1)}, bf16[1536,768]{1,0:T(8,128)(2,1)S(1)}, bf16[512,1536]{1,0:T(8,128)(2,1)S(1)}) custom-call(bf16[192,768]{1,0:T(8,128)(2,1)S(1)} %constant_dynamic-slice_fusion.refs_0_, bf16[192,768]{1,0:T(8,128)(2,1)} %collective-permute-done.11.refs_1_, ...), custom_call_target="tpu_custom_call" | custom-call | flops 1 | bytes 1 | tf_op jit(solution)/shard_map/up_part/pallas_call | solution.py:517
  64.3 3.3 %far_part.1 = (bf16[128,1536]{1,0:T(8,128)(2,1)S(1)}, bf16[128,1536]{1,0:T(8,128)(2,1)S(1)}) custom-call(bf16[192,768]{1,0:T(8,128)(2,1)S(1)} %dynamic-slice_bitcast_fusion.refs_0_, bf16[192,768]{1,0:T(8,128)(2,1)S(1)} %collective-permute-done.refs_1_, bf16[192,768]{1,0:T(8,128)(2,1)S(1)} %collective-permute-done.1.refs_2_, ...), custom_call_target="tpu_custom_call" | custom-call | flops 1 | bytes 1 | tf_op jit(solution)/shard_map/far_part/pallas_call | solution.py:578
  67.7 1.7 %collective-permute-done.25.refs_1_ = bf16[128,1536]{1,0:T(8,128)(2,1)S(1)} collective-permute-done((bf16[128,1536]{1,0:T(8,128)(2,1)S(1)}, bf16[128,1536]{1,0:T(8,128)(2,1)S(1)}, u32[]{:S(2)}, u32[]{:S(2)}) %collective-permute-start.25) | collective-permute-done | bytes 393248 | tf_op jit(solution)/shard_map/ppermute | solution.py:54
  69.8 4.6 %rest_part.1 = (bf16[128,1536]{1,0:T(8,128)(2,1)S(1)}, bf16[64,1536]{1,0:T(8,128)(2,1)S(1)}, bf16[64,1536]{1,0:T(8,128)(2,1)S(1)}, bf16[128,1536]{1,0:T(8,128)(2...) custom-call(bf16[192,768]{1,0:T(8,128)(2,1)S(1)} %dynamic-slice_bitc, ...), custom_call_target="tpu_custom_call" | custom-call | flops 1 | bytes 1 | tf_op jit(solution)/shard_map/rest_part/pallas_call | solution.py:637
  74.5 0.5 collective-permute-start.32
  75.1 0.4 collective-permute-start.29
  75.5 0.4 collective-permute-done.31.refs_1_
  76.3 4.4 %collective-permute-done.30.refs_3_ = bf16[128,1536]{1,0:T(8,128)(2,1)S(1)} collective-permute-done((bf16[128,1536]{1,0:T(8,128)(2,1)S(1)}, bf16[128,1536]{1,0:T(8,128)(2,1)S(1)}, u32[]{:S(2)}, u32[]{:S(2)}) %collective-permute-start.30) | collective-permute-done | bytes 393248 | tf_op jit(solution)/shard_map/ppermute | solution.py:54
  81.0 4.6 %norm_back.1 = (f32[8,16,1536]{2,1,0:T(8,128)S(1)}, f32[32,1536]{1,0:T(8,128)S(1)}, f32[32,1536]{1,0:T(8,128)S(1)}, bf16[3,16,1536]{2,1,0:T(8,128)(2,1)S(1)}, bf...) custom-call(bf16[128,1536]{1,0:T(8,128)(2,1)S(1)} %get-tuple-element.81.refs_0_, ...), custom_call_target="tpu_custom_call" | custom-call | flops 1 | bytes 1 | tf_op jit(solution)/shard_map/norm_back/pallas_call | solution.py:396
  85.7 0.5 collective-permute-start.38
  86.2 1.4 %collective-permute-start.40 = (bf16[3,3,1536]{2,1,0:T(4,128)(2,1)S(1)}, bf16[3,3,1536]{2,1,0:T(4,128)(2,1)S(1)}, u32[]{:S(2)}, u32[]{:S(2)}) collective-permute-start(bf16[3,3,1536]{2,1,0:T(4,128)(2,1)S(1)} %get-tuple-element.107), channel_id=1, source_target_pairs={{0,24},{8,16},{16,8},{24,0},{1,25},{9,17},{17,9},{25,1},{2,26},{10... | collective-permute-start | bytes 82952 | tf_op jit(solution)/shard_map/ppermute | solution.py:74
  88.0 0.9 collective-permute-done.34.refs_3_
  88.9 1.6 %collective-permute-start.35 = (f32[8,1536]{1,0:T(8,128)S(1)}, f32[8,1536]{1,0:T(8,128)S(1)}, u32[]{:S(2)}, u32[]{:S(2)}) collective-permute-start(f32[8,1536]{1,0:T(8,128)S(1)} %get-tuple-element.101), channel_id=1, source_target_pairs={{0,1},{1,0},{2,3},{3,2},{4,5},{5,4},{6,7},{7,6},{8,9},{9,8},{10,11... | collective-permute-start | bytes 147464 | tf_op jit(solution)/shard_map/ppermute | solution.py:49
  90.5 0.7 collective-permute-start.36
  91.3 1.2 %collective-permute-start.37 = (f32[8,1536]{1,0:T(8,128)S(1)}, f32[8,1536]{1,0:T(8,128)S(1)}, u32[]{:S(2)}, u32[]{:S(2)}) collective-permute-start(f32[8,1536]{1,0:T(8,128)S(1)} %get-tuple-element.103), channel_id=1, source_target_pairs={{0,9},{1,8},{2,11},{3,10},{4,13},{5,12},{6,15},{7,14},{8,1},{9,0},... | collective-permute-start | bytes 147464 | tf_op jit(solution)/shard_map/ppermute | solution.py:49
  92.5 0.7 collective-permute-done.39.refs_1_
  93.2 0.6 collective-permute-start.41
  93.8 3.1 %conv_back.2.refs_5_ = bf16[8,16,1536]{2,1,0:T(8,128)(2,1)} custom-call(f32[8,16,1536]{2,1,0:T(8,128)S(1)} %get-tuple-element.104.own, bf16[3,16,1536]{2,1,0:T(8,128)(2,1)S(1)} %collective-permute-done.38.refs_0_, bf16[8,3,1536]{2,1,0:T(4,128)(2,1)S(1)} %collective-permute-done.39.refs_1_, bf16[3,3,1536]{2,1,0:T(4,128)(2,1)S(1)} %collective-permute-done.40.refs_2_, ...), custom_call_target="tpu_custom_call" | custom-call | flops 1 | bytes 1 | tf_op jit(solution)/shard_map/conv_back/pallas_call | solution.py:433
  97.1 0.8 collective-permute-done.41.refs_4_
  97.8 1.6 %collective-permute-start.42 = (bf16[8,1536]{1,0:T(8,128)(2,1)S(1)}, bf16[8,1536]{1,0:T(8,128)(2,1)S(1)}, u32[]{:S(2)}, u32[]{:S(2)}) collective-permute-start(bf16[8,1536]{1,0:T(8,128)(2,1)S(1)} %add_add_fusion.1), channel_id=1, source_target_pairs={{0,2},{1,3},{2,0},{3,1},{4,6},{5,7},{6,4},{7,5},{8,10},{9,11},{10,... | collective-permute-start | bytes 73736 | tf_op jit(solution)/shard_map/ppermute | solution.py:49
  99.4 2.6 %collective-permute-start.43 = (bf16[8,1536]{1,0:T(8,128)(2,1)S(1)}, bf16[8,1536]{1,0:T(8,128)(2,1)S(1)}, u32[]{:S(2)}, u32[]{:S(2)}) collective-permute-start(bf16[8,1536]{1,0:T(8,128)(2,1)S(1)} %add_add_fusion.1), channel_id=1, source_target_pairs={{0,4},{1,5},{2,6},{3,7},{4,0},{5,1},{6,2},{7,3},{8,12},{9,13},{10,... | collective-permute-start | bytes 73736 | tf_op jit(solution)/shard_map/ppermute | solution.py:49
  102.2 0.5 collective-permute-start.27
  102.7 3.2 %conv_back.3 = bf16[8,16,1536]{2,1,0:T(8,128)(2,1)} custom-call(f32[8,16,1536]{2,1,0:T(8,128)S(1)} %get-tuple-element.104.own, bf16[3,16,1536]{2,1,0:T(8,128)(2,1)S(1)} %collective-permute-done.38.refs_0_, bf16[8,3,1536]{2,1,0:T(4,128)(2,1)S(1)} %collective-permute-done.39.refs_1_, ...), custom_call_target="tpu_custom_call", output_to_operand_aliasing={{}: (6, {})} | custom-call | flops 1 | bytes 1 | tf_op jit(solution)/shard_map/conv_back/pallas_call | solution.py:433
  105.9 1.7 %collective-permute-done.44 = bf16[8,1536]{1,0:T(8,128)(2,1)S(1)} collective-permute-done((bf16[8,1536]{1,0:T(8,128)(2,1)S(1)}, bf16[8,1536]{1,0:T(8,128)(2,1)S(1)}, u32[]{:S(2)}, u32[]{:S(2)}) %collective-permute-start.44) | collective-permute-done | bytes 24608 | tf_op jit(solution)/shard_map/ppermute | solution.py:49
  107.7 1.6 %collective-permute-start.45 = (f32[8,1536]{1,0:T(8,128)S(1)}, f32[8,1536]{1,0:T(8,128)S(1)}, u32[]{:S(2)}, u32[]{:S(2)}) collective-permute-start(f32[8,1536]{1,0:T(8,128)S(1)} %add_add_fusion.refs_0_), channel_id=1, source_target_pairs={{0,1},{1,0},{2,3},{3,2},{4,5},{5,4},{6,7},{7,6},{8,9},{9,8},{10,11... | collective-permute-start | bytes 147464 | tf_op jit(solution)/shard_map/ppermute | solution.py:49
  109.2 0.9 collective-permute-start.46
  110.1 1.1 collective-permute-start.47
  111.2 1.1 collective-permute-done.45.refs_1_
  112.3 1.0 collective-permute-done.46.refs_2_
  113.3 1.8 %collective-permute-done.47.refs_3_ = f32[8,1536]{1,0:T(8,128)S(1)} collective-permute-done((f32[8,1536]{1,0:T(8,128)S(1)}, f32[8,1536]{1,0:T(8,128)S(1)}, u32[]{:S(2)}, u32[]{:S(2)}) %collective-permute-start.47) | collective-permute-done | bytes 49184 | tf_op jit(solution)/shard_map/ppermute | solution.py:49
  115.1 1.0 output_part.1
  116.3 0.9 finish.1
  (84 shorter events, 3.5 us)
Async XLA Ops:
  0.6 1.3 %copy-start = (bf16[192,3072]{1,0:T(8,128)(2,1)S(1)}, bf16[192,3072]{1,0:T(8,128)(2,1)}, u32[]{:S(2)}) copy-start(bf16[192,3072]{1,0:T(8,128)(2,1)} %param.18) | copy-start | bytes 3538948
  0.6 8.4 %copy-start.3 = (bf16[1,8,16,1536]{3,2,1,0:T(8,128)(2,1)S(1)}, bf16[1,8,16,1536]{3,2,1,0:T(8,128)(2,1)}, u32[]{:S(2)}) copy-start(bf16[1,8,16,1536]{3,2,1,0:T(8,128)(2,1)} %param.12) | copy-start | bytes 1179652
  0.7 21.6 %copy-start.1 = (bf16[1,8,16,1536]{3,2,1,0:T(8,128)(2,1)S(1)}, bf16[1,8,16,1536]{3,2,1,0:T(8,128)(2,1)}, u32[]{:S(2)}) copy-start(bf16[1,8,16,1536]{3,2,1,0:T(8,128)(2,1)} %param.23) | copy-start | bytes 1179652
  0.7 24.8 %copy-start.2 = (f32[7,7,1536]{2,1,0:T(8,128)S(1)}, f32[7,7,1536]{2,1,0:T(8,128)}, u32[]{:S(2)}) copy-start(f32[7,7,1536]{2,1,0:T(8,128)} %refs_3_.5) | copy-start | bytes 903172
  1.9 11.0 %collective-permute-start.11 = (bf16[192,768]{1,0:T(8,128)(2,1)S(1)}, bf16[192,768]{1,0:T(8,128)(2,1)}, u32[]{:S(2)}, u32[]{:S(2)}) collective-permute-start(bf16[192,768]{1,0:T(8,128)(2,1)S(1)} %constant_dynamic-slice_fusion.refs_0_), channel_id=1, source_target_pairs={{0,2},{2,4},{4,6},{6,7},{7,5},{5,3},{3,1},{1,0},{8,10},{10,12},{12... | collective-permute-start | bytes 884744 | tf_op jit(solution)/shard_map/ppermute | solution.py:107
  5.0 14.6 %collective-permute-start.12 = (bf16[192,768]{1,0:T(8,128)(2,1)S(1)}, bf16[192,768]{1,0:T(8,128)(2,1)}, u32[]{:S(2)}, u32[]{:S(2)}) collective-permute-start(bf16[192,768]{1,0:T(8,128)(2,1)S(1)} %constant_dynamic-slice_fusion.refs_0_), channel_id=1, source_target_pairs={{2,0},{4,2},{6,4},{7,6},{5,7},{3,5},{1,3},{0,1},{10,8},{12,10},{14... | collective-permute-start | bytes 884744 | tf_op jit(solution)/shard_map/ppermute | solution.py:108
  6.0 14.2 %collective-permute-start = (bf16[192,768]{1,0:T(8,128)(2,1)S(1)}, bf16[192,768]{1,0:T(8,128)(2,1)S(1)}, u32[]{:S(2)}, u32[]{:S(2)}) collective-permute-start(bf16[192,768]{1,0:T(8,128)(2,1)S(1)} %dynamic-slice_bitcast_fusion.refs_0_), channel_id=1, source_target_pairs={{0,2},{2,4},{4,6},{6,7},{7,5},{5,3},{3,1},{1,0},{8,10},{10,12},{12... | collective-permute-start | bytes 884744 | tf_op jit(solution)/shard_map/ppermute | solution.py:107
  8.1 13.6 %collective-permute-start.1 = (bf16[192,768]{1,0:T(8,128)(2,1)S(1)}, bf16[192,768]{1,0:T(8,128)(2,1)S(1)}, u32[]{:S(2)}, u32[]{:S(2)}) collective-permute-start(bf16[192,768]{1,0:T(8,128)(2,1)S(1)} %dynamic-slice_bitcast_fusion.refs_0_), channel_id=1, source_target_pairs={{2,0},{4,2},{6,4},{7,6},{5,7},{3,5},{1,3},{0,1},{10,8},{12,10},{14... | collective-permute-start | bytes 884744 | tf_op jit(solution)/shard_map/ppermute | solution.py:108
  9.0 50.3 %copy-start.6 = (f32[1536]{0:T(1024)S(1)}, f32[1536]{0:T(1024)}, u32[]{:S(2)}) copy-start(f32[1536]{0:T(1024)} %scale.1) | copy-start | bytes 18436
  9.0 50.3 %copy-start.8 = (f32[3072]{0:T(1024)S(1)}, f32[3072]{0:T(1024)}, u32[]{:S(2)}) copy-start(f32[3072]{0:T(1024)} %refs_17_.2) | copy-start | bytes 36868
  9.6 5.5 %collective-permute-start.10 = (bf16[3,3,1536]{2,1,0:T(4,128)(2,1)S(1)}, bf16[3,3,1536]{2,1,0:T(4,128)(2,1)S(1)}, u32[]{:S(2)}, u32[]{:S(2)}) collective-permute-start(bf16[3,3,1536]{2,1,0:T(4,128)(2,1)S(1)} %get-tuple-element.64), channel_id=1, source_target_pairs={{0,24},{8,16},{16,8},{24,0},{1,25},{9,17},{17,9},{25,1},{2,26},{10... | collective-permute-start | bytes 82952 | tf_op jit(solution)/shard_map/ppermute | solution.py:74
  12.9 12.5 %collective-permute-start.16 = (bf16[192,768]{1,0:T(8,128)(2,1)}, bf16[192,768]{1,0:T(8,128)(2,1)S(1)}, u32[]{:S(2)}, u32[]{:S(2)}) collective-permute-start(bf16[192,768]{1,0:T(8,128)(2,1)} %collective-permute-done.11.refs_1_), channel_id=1, source_target_pairs={{0,2},{2,4},{4,6},{6,7},{7,5},{5,3},{3,1},{1,0},{8,10},{10,12},{12... | collective-permute-start | bytes 884744 | tf_op jit(solution)/shard_map/ppermute | solution.py:107
  15.0 4.6 %collective-permute-start.9 = (bf16[8,3,1536]{2,1,0:T(4,128)(2,1)S(1)}, bf16[8,3,1536]{2,1,0:T(4,128)(2,1)S(1)}, u32[]{:S(2)}, u32[]{:S(2)}) collective-permute-start(bf16[8,3,1536]{2,1,0:T(4,128)(2,1)S(1)} %get-tuple-element.63), channel_id=1, source_target_pairs={{0,8},{8,0},{16,24},{24,16},{1,9},{9,1},{17,25},{25,17},{2,10},{10... | collective-permute-start | bytes 221192 | tf_op jit(solution)/shard_map/ppermute | solution.py:74
  19.6 2.0 %collective-permute-start.8 = (bf16[3,16,1536]{2,1,0:T(8,128)(2,1)S(1)}, bf16[3,16,1536]{2,1,0:T(8,128)(2,1)S(1)}, u32[]{:S(2)}, u32[]{:S(2)}) collective-permute-start(bf16[3,16,1536]{2,1,0:T(8,128)(2,1)S(1)} %get-tuple-element.62), channel_id=1, source_target_pairs={{0,16},{8,24},{16,0},{24,8},{1,17},{9,25},{17,1},{25,9},{2,18},{10... | collective-permute-start | bytes 442376 | tf_op jit(solution)/shard_map/ppermute | solution.py:74
  19.6 13.7 %collective-permute-start.17 = (bf16[192,768]{1,0:T(8,128)(2,1)}, bf16[192,768]{1,0:T(8,128)(2,1)S(1)}, u32[]{:S(2)}, u32[]{:S(2)}) collective-permute-start(bf16[192,768]{1,0:T(8,128)(2,1)} %collective-permute-done.12.refs_2_), channel_id=1, source_target_pairs={{2,0},{4,2},{6,4},{7,6},{5,7},{3,5},{1,3},{0,1},{10,8},{12,10},{14... | collective-permute-start | bytes 884744 | tf_op jit(solution)/shard_map/ppermute | solution.py:108
  20.2 15.3 %collective-permute-start.2 = (bf16[192,768]{1,0:T(8,128)(2,1)S(1)}, bf16[192,768]{1,0:T(8,128)(2,1)S(1)}, u32[]{:S(2)}, u32[]{:S(2)}) collective-permute-start(bf16[192,768]{1,0:T(8,128)(2,1)S(1)} %collective-permute-done.refs_1_), channel_id=1, source_target_pairs={{0,2},{2,4},{4,6},{6,7},{7,5},{5,3},{3,1},{1,0},{8,10},{10,12},{12... | collective-permute-start | bytes 884744 | tf_op jit(solution)/shard_map/ppermute | solution.py:107
  21.7 15.4 %collective-permute-start.3 = (bf16[192,768]{1,0:T(8,128)(2,1)S(1)}, bf16[192,768]{1,0:T(8,128)(2,1)S(1)}, u32[]{:S(2)}, u32[]{:S(2)}) collective-permute-start(bf16[192,768]{1,0:T(8,128)(2,1)S(1)} %collective-permute-done.1.refs_2_), channel_id=1, source_target_pairs={{2,0},{4,2},{6,4},{7,6},{5,7},{3,5},{1,3},{0,1},{10,8},{12,10},{14... | collective-permute-start | bytes 884744 | tf_op jit(solution)/shard_map/ppermute | solution.py:108
  22.2 15.3 %collective-permute-start.14 = (bf16[128,1536]{1,0:T(8,128)(2,1)S(1)}, bf16[128,1536]{1,0:T(8,128)(2,1)S(1)}, u32[]{:S(2)}, u32[]{:S(2)}) collective-permute-start(bf16[128,1536]{1,0:T(8,128)(2,1)S(1)} %bitcast.8), channel_id=1, source_target_pairs={{8,0},{0,8},{9,1},{1,9},{10,2},{2,10},{11,3},{3,11},{12,4},{4,12},... | collective-permute-start | bytes 1179656 | tf_op jit(solution)/shard_map/ppermute | solution.py:54
  25.4 13.6 %collective-permute-start.13 = (bf16[128,1536]{1,0:T(8,128)(2,1)S(1)}, bf16[128,1536]{1,0:T(8,128)(2,1)S(1)}, u32[]{:S(2)}, u32[]{:S(2)}) collective-permute-start(bf16[128,1536]{1,0:T(8,128)(2,1)S(1)} %bitcast.9), channel_id=1, source_target_pairs={{16,0},{0,16},{17,1},{1,17},{18,2},{2,18},{19,3},{3,19},{20,4},{4,... | collective-permute-start | bytes 1179656 | tf_op jit(solution)/shard_map/ppermute | solution.py:54
  25.4 0.7 copy-start.4
  26.1 0.7 copy-start.9
  26.8 0.7 copy-start.10
  33.4 13.5 %collective-permute-start.23 = (bf16[128,1536]{1,0:T(8,128)(2,1)S(1)}, bf16[128,1536]{1,0:T(8,128)(2,1)S(1)}, u32[]{:S(2)}, u32[]{:S(2)}) collective-permute-start(bf16[128,1536]{1,0:T(8,128)(2,1)S(1)} %get-tuple-element.70.refs_9_), channel_id=1, source_target_pairs={{8,0},{0,8},{9,1},{1,9},{10,2},{2,10},{11,3},{3,11},{12,4},{4,12},... | collective-permute-start | bytes 1179656 | tf_op jit(solution)/shard_map/ppermute | solution.py:54
  35.5 9.8 %collective-permute-start.18 = (bf16[192,768]{1,0:T(8,128)(2,1)S(1)}, bf16[192,768]{1,0:T(8,128)(2,1)S(1)}, u32[]{:S(2)}, u32[]{:S(2)}) collective-permute-start(bf16[192,768]{1,0:T(8,128)(2,1)S(1)} %collective-permute-done.16.refs_3_), channel_id=1, source_target_pairs={{0,2},{2,4},{4,6},{6,7},{7,5},{5,3},{3,1},{1,0},{8,10},{10,12},{12... | collective-permute-start | bytes 884744 | tf_op jit(solution)/shard_map/ppermute | solution.py:107
  37.0 9.8 %collective-permute-start.19 = (bf16[192,768]{1,0:T(8,128)(2,1)S(1)}, bf16[192,768]{1,0:T(8,128)(2,1)S(1)}, u32[]{:S(2)}, u32[]{:S(2)}) collective-permute-start(bf16[192,768]{1,0:T(8,128)(2,1)S(1)} %collective-permute-done.17.refs_4_), channel_id=1, source_target_pairs={{2,0},{4,2},{6,4},{7,6},{5,7},{3,5},{1,3},{0,1},{10,8},{12,10},{14... | collective-permute-start | bytes 884744 | tf_op jit(solution)/shard_map/ppermute | solution.py:108
  37.5 13.4 %collective-permute-start.4 = (bf16[192,768]{1,0:T(8,128)(2,1)S(1)}, bf16[192,768]{1,0:T(8,128)(2,1)S(1)}, u32[]{:S(2)}, u32[]{:S(2)}) collective-permute-start(bf16[192,768]{1,0:T(8,128)(2,1)S(1)} %collective-permute-done.2.refs_3_), channel_id=1, source_target_pairs={{0,2},{2,4},{4,6},{6,7},{7,5},{5,3},{3,1},{1,0},{8,10},{10,12},{12... | collective-permute-start | bytes 884744 | tf_op jit(solution)/shard_map/ppermute | solution.py:107
  39.1 15.4 %collective-permute-start.22 = (bf16[128,1536]{1,0:T(8,128)(2,1)S(1)}, bf16[128,1536]{1,0:T(8,128)(2,1)S(1)}, u32[]{:S(2)}, u32[]{:S(2)}) collective-permute-start(bf16[128,1536]{1,0:T(8,128)(2,1)S(1)} %get-tuple-element.70.refs_9_), channel_id=1, source_target_pairs={{16,0},{0,16},{17,1},{1,17},{18,2},{2,18},{19,3},{3,19},{20,4},{4,... | collective-permute-start | bytes 1179656 | tf_op jit(solution)/shard_map/ppermute | solution.py:54
  45.3 7.6 %collective-permute-start.5 = (bf16[192,768]{1,0:T(8,128)(2,1)S(1)}, bf16[192,768]{1,0:T(8,128)(2,1)S(1)}, u32[]{:S(2)}, u32[]{:S(2)}) collective-permute-start(bf16[192,768]{1,0:T(8,128)(2,1)S(1)} %collective-permute-done.3.refs_4_), channel_id=1, source_target_pairs={{2,0},{4,2},{6,4},{7,6},{5,7},{3,5},{1,3},{0,1},{10,8},{12,10},{14... | collective-permute-start | bytes 884744 | tf_op jit(solution)/shard_map/ppermute | solution.py:108
  46.8 12.5 %collective-permute-start.15 = (bf16[128,1536]{1,0:T(8,128)(2,1)S(1)}, bf16[128,1536]{1,0:T(8,128)(2,1)S(1)}, u32[]{:S(2)}, u32[]{:S(2)}) collective-permute-start(bf16[128,1536]{1,0:T(8,128)(2,1)S(1)} %collective-permute-done.14.refs_15_.refs_11_), channel_id=1, source_target_pairs={{16,0},{0,16},{17,1},{1,17},{18,2},{2,18},{19,3},{3,19},{20,4},{4,... | collective-permute-start | bytes 1179656 | tf_op jit(solution)/shard_map/ppermute | solution.py:54
  46.8 12.5 %collective-permute-start.24 = (bf16[128,1536]{1,0:T(8,128)(2,1)S(1)}, bf16[128,1536]{1,0:T(8,128)(2,1)S(1)}, u32[]{:S(2)}, u32[]{:S(2)}) collective-permute-start(bf16[128,1536]{1,0:T(8,128)(2,1)S(1)} %collective-permute-done.23.refs_11_), channel_id=1, source_target_pairs={{16,0},{0,16},{17,1},{1,17},{18,2},{2,18},{19,3},{3,19},{20,4},{4,... | collective-permute-start | bytes 1179656 | tf_op jit(solution)/shard_map/ppermute | solution.py:54
  50.9 6.6 %collective-permute-start.20 = (bf16[96,768]{1,0:T(8,128)(2,1)S(1)}, bf16[96,768]{1,0:T(8,128)(2,1)S(1)}, u32[]{:S(2)}, u32[]{:S(2)}) collective-permute-start(bf16[96,768]{1,0:T(8,128)(2,1)S(1)} %slice.18), channel_id=1, source_target_pairs={{0,2},{2,4},{4,6},{6,7},{7,5},{5,3},{3,1},{1,0},{8,10},{10,12},{12... | collective-permute-start | bytes 442376 | tf_op jit(solution)/shard_map/ppermute | solution.py:114
  52.9 6.4 %collective-permute-start.21 = (bf16[96,768]{1,0:T(8,128)(2,1)S(1)}, bf16[96,768]{1,0:T(8,128)(2,1)S(1)}, u32[]{:S(2)}, u32[]{:S(2)}) collective-permute-start(bf16[96,768]{1,0:T(8,128)(2,1)S(1)} %slice.19), channel_id=1, source_target_pairs={{2,0},{4,2},{6,4},{7,6},{5,7},{3,5},{1,3},{0,1},{10,8},{12,10},{14... | collective-permute-start | bytes 442376 | tf_op jit(solution)/shard_map/ppermute | solution.py:116
  54.5 9.8 %collective-permute-start.6 = (bf16[96,768]{1,0:T(8,128)(2,1)S(1)}, bf16[96,768]{1,0:T(8,128)(2,1)S(1)}, u32[]{:S(2)}, u32[]{:S(2)}) collective-permute-start(bf16[96,768]{1,0:T(8,128)(2,1)S(1)} %slice.16), channel_id=1, source_target_pairs={{0,2},{2,4},{4,6},{6,7},{7,5},{5,3},{3,1},{1,0},{8,10},{10,12},{12... | collective-permute-start | bytes 442376 | tf_op jit(solution)/shard_map/ppermute | solution.py:114
  57.5 6.8 %collective-permute-start.7 = (bf16[96,768]{1,0:T(8,128)(2,1)S(1)}, bf16[96,768]{1,0:T(8,128)(2,1)S(1)}, u32[]{:S(2)}, u32[]{:S(2)}) collective-permute-start(bf16[96,768]{1,0:T(8,128)(2,1)S(1)} %slice.17), channel_id=1, source_target_pairs={{2,0},{4,2},{6,4},{7,6},{5,7},{3,5},{1,3},{0,1},{10,8},{12,10},{14... | collective-permute-start | bytes 442376 | tf_op jit(solution)/shard_map/ppermute | solution.py:116
  64.3 5.5 %copy-start.7 = (f32[1536]{0:T(1024)S(1)}, f32[1536]{0:T(1024)}, u32[]{:S(2)}) copy-start(f32[1536]{0:T(1024)} %bias.1) | copy-start | bytes 18436
  67.6 1.8 %collective-permute-start.25 = (bf16[128,1536]{1,0:T(8,128)(2,1)S(1)}, bf16[128,1536]{1,0:T(8,128)(2,1)S(1)}, u32[]{:S(2)}, u32[]{:S(2)}) collective-permute-start(bf16[128,1536]{1,0:T(8,128)(2,1)S(1)} %get-tuple-element.75), channel_id=1, source_target_pairs={{16,0},{0,16},{17,1},{1,17},{18,2},{2,18},{19,3},{3,19},{20,4},{4,... | collective-permute-start | bytes 1179656 | tf_op jit(solution)/shard_map/ppermute | solution.py:54
  69.5 11.2 %collective-permute-start.30 = (bf16[128,1536]{1,0:T(8,128)(2,1)S(1)}, bf16[128,1536]{1,0:T(8,128)(2,1)S(1)}, u32[]{:S(2)}, u32[]{:S(2)}) collective-permute-start(bf16[128,1536]{1,0:T(8,128)(2,1)S(1)} %add_rounded.2), channel_id=1, source_target_pairs={{8,0},{0,8},{9,1},{1,9},{10,2},{2,10},{11,3},{3,11},{12,4},{4,12},... | collective-permute-start | bytes 1179656 | tf_op jit(solution)/shard_map/ppermute | solution.py:54
  69.8 11.2 %copy-start.5 = (f32[1536]{0:T(1024)S(1)}, f32[1536]{0:T(1024)}, u32[]{:S(2)}) copy-start(f32[1536]{0:T(1024)} %refs_6_.3) | copy-start | bytes 18436
  74.4 1.5 %collective-permute-start.31 = (bf16[64,1536]{1,0:T(8,128)(2,1)S(1)}, bf16[64,1536]{1,0:T(8,128)(2,1)S(1)}, u32[]{:S(2)}, u32[]{:S(2)}) collective-permute-start(bf16[64,1536]{1,0:T(8,128)(2,1)S(1)} %get-tuple-element.86), channel_id=1, source_target_pairs={{16,0},{0,16},{17,1},{1,17},{18,2},{2,18},{19,3},{3,19},{20,4},{4,... | collective-permute-start | bytes 589832 | tf_op jit(solution)/shard_map/ppermute | solution.py:54
  74.5 1.7 %collective-permute-start.32 = (bf16[64,1536]{1,0:T(8,128)(2,1)S(1)}, bf16[64,1536]{1,0:T(8,128)(2,1)S(1)}, u32[]{:S(2)}, u32[]{:S(2)}) collective-permute-start(bf16[64,1536]{1,0:T(8,128)(2,1)S(1)} %get-tuple-element.87), channel_id=1, source_target_pairs={{16,0},{0,16},{17,1},{1,17},{18,2},{2,18},{19,3},{3,19},{20,4},{4,... | collective-permute-start | bytes 589832 | tf_op jit(solution)/shard_map/ppermute | solution.py:54
  75.0 6.0 %collective-permute-start.28 = (bf16[64,1536]{1,0:T(8,128)(2,1)S(1)}, bf16[64,1536]{1,0:T(8,128)(2,1)S(1)}, u32[]{:S(2)}, u32[]{:S(2)}) collective-permute-start(bf16[64,1536]{1,0:T(8,128)(2,1)S(1)} %get-tuple-element.82), channel_id=1, source_target_pairs={{16,0},{0,16},{17,1},{1,17},{18,2},{2,18},{19,3},{3,19},{20,4},{4,... | collective-permute-start | bytes 589832 | tf_op jit(solution)/shard_map/ppermute | solution.py:54
  75.1 5.9 %collective-permute-start.29 = (bf16[64,1536]{1,0:T(8,128)(2,1)S(1)}, bf16[64,1536]{1,0:T(8,128)(2,1)S(1)}, u32[]{:S(2)}, u32[]{:S(2)}) collective-permute-start(bf16[64,1536]{1,0:T(8,128)(2,1)S(1)} %get-tuple-element.83), channel_id=1, source_target_pairs={{16,0},{0,16},{17,1},{1,17},{18,2},{2,18},{19,3},{3,19},{20,4},{4,... | collective-permute-start | bytes 589832 | tf_op jit(solution)/shard_map/ppermute | solution.py:54
  80.7 8.2 %collective-permute-start.34 = (bf16[96,1536]{1,0:T(8,128)(2,1)S(1)}, bf16[96,1536]{1,0:T(8,128)(2,1)S(1)}, u32[]{:S(2)}, u32[]{:S(2)}) collective-permute-start(bf16[96,1536]{1,0:T(8,128)(2,1)S(1)} %get-tuple-element.96), channel_id=1, source_target_pairs={{8,0},{0,8},{9,1},{1,9},{10,2},{2,10},{11,3},{3,11},{12,4},{4,12},... | collective-permute-start | bytes 884744 | tf_op jit(solution)/shard_map/ppermute | solution.py:54
  85.6 2.4 %collective-permute-start.33 = (f32[32,1536]{1,0:T(8,128)S(1)}, f32[32,1536]{1,0:T(8,128)S(1)}, u32[]{:S(2)}, u32[]{:S(2)}) collective-permute-start(f32[32,1536]{1,0:T(8,128)S(1)} %get-tuple-element.95), channel_id=1, source_target_pairs={{0,16},{16,0},{1,17},{17,1},{2,18},{18,2},{3,19},{19,3},{4,20},{20... | collective-permute-start | bytes 589832 | tf_op jit(solution)/shard_map/ppermute | solution.py:49
  85.7 8.1 %collective-permute-start.38 = (bf16[3,16,1536]{2,1,0:T(8,128)(2,1)S(1)}, bf16[3,16,1536]{2,1,0:T(8,128)(2,1)S(1)}, u32[]{:S(2)}, u32[]{:S(2)}) collective-permute-start(bf16[3,16,1536]{2,1,0:T(8,128)(2,1)S(1)} %get-tuple-element.105), channel_id=1, source_target_pairs={{0,16},{8,24},{16,0},{24,8},{1,17},{9,25},{17,1},{25,9},{2,18},{10... | collective-permute-start | bytes 442376 | tf_op jit(solution)/shard_map/ppermute | solution.py:74
  86.2 5.1 %collective-permute-start.40 = (bf16[3,3,1536]{2,1,0:T(4,128)(2,1)S(1)}, bf16[3,3,1536]{2,1,0:T(4,128)(2,1)S(1)}, u32[]{:S(2)}, u32[]{:S(2)}) collective-permute-start(bf16[3,3,1536]{2,1,0:T(4,128)(2,1)S(1)} %get-tuple-element.107), channel_id=1, source_target_pairs={{0,24},{8,16},{16,8},{24,0},{1,25},{9,17},{17,9},{25,1},{2,26},{10... | collective-permute-start | bytes 82952 | tf_op jit(solution)/shard_map/ppermute | solution.py:74
  87.6 5.6 %collective-permute-start.39 = (bf16[8,3,1536]{2,1,0:T(4,128)(2,1)S(1)}, bf16[8,3,1536]{2,1,0:T(4,128)(2,1)S(1)}, u32[]{:S(2)}, u32[]{:S(2)}) collective-permute-start(bf16[8,3,1536]{2,1,0:T(4,128)(2,1)S(1)} %get-tuple-element.106), channel_id=1, source_target_pairs={{0,8},{8,0},{16,24},{24,16},{1,9},{9,1},{17,25},{25,17},{2,10},{10... | collective-permute-start | bytes 221192 | tf_op jit(solution)/shard_map/ppermute | solution.py:74
  88.9 8.1 %collective-permute-start.35 = (f32[8,1536]{1,0:T(8,128)S(1)}, f32[8,1536]{1,0:T(8,128)S(1)}, u32[]{:S(2)}, u32[]{:S(2)}) collective-permute-start(f32[8,1536]{1,0:T(8,128)S(1)} %get-tuple-element.101), channel_id=1, source_target_pairs={{0,1},{1,0},{2,3},{3,2},{4,5},{5,4},{6,7},{7,6},{8,9},{9,8},{10,11... | collective-permute-start | bytes 147464 | tf_op jit(solution)/shard_map/ppermute | solution.py:49
  90.5 6.5 %collective-permute-start.36 = (f32[8,1536]{1,0:T(8,128)S(1)}, f32[8,1536]{1,0:T(8,128)S(1)}, u32[]{:S(2)}, u32[]{:S(2)}) collective-permute-start(f32[8,1536]{1,0:T(8,128)S(1)} %get-tuple-element.102), channel_id=1, source_target_pairs={{0,8},{8,0},{1,9},{9,1},{2,10},{10,2},{3,11},{11,3},{4,12},{12,4},... | collective-permute-start | bytes 147464 | tf_op jit(solution)/shard_map/ppermute | solution.py:49
  91.3 5.7 %collective-permute-start.37 = (f32[8,1536]{1,0:T(8,128)S(1)}, f32[8,1536]{1,0:T(8,128)S(1)}, u32[]{:S(2)}, u32[]{:S(2)}) collective-permute-start(f32[8,1536]{1,0:T(8,128)S(1)} %get-tuple-element.103), channel_id=1, source_target_pairs={{0,9},{1,8},{2,11},{3,10},{4,13},{5,12},{6,15},{7,14},{8,1},{9,0},... | collective-permute-start | bytes 147464 | tf_op jit(solution)/shard_map/ppermute | solution.py:49
  93.2 4.6 %collective-permute-start.41 = (bf16[32,1536]{1,0:T(8,128)(2,1)S(1)}, bf16[32,1536]{1,0:T(8,128)(2,1)S(1)}, u32[]{:S(2)}, u32[]{:S(2)}) collective-permute-start(bf16[32,1536]{1,0:T(8,128)(2,1)S(1)} %get-tuple-element.108), channel_id=1, source_target_pairs={{8,0},{0,8},{9,1},{1,9},{10,2},{2,10},{11,3},{3,11},{12,4},{4,12},... | collective-permute-start | bytes 294920 | tf_op jit(solution)/shard_map/ppermute | solution.py:54
  97.8 8.1 %collective-permute-start.42 = (bf16[8,1536]{1,0:T(8,128)(2,1)S(1)}, bf16[8,1536]{1,0:T(8,128)(2,1)S(1)}, u32[]{:S(2)}, u32[]{:S(2)}) collective-permute-start(bf16[8,1536]{1,0:T(8,128)(2,1)S(1)} %add_add_fusion.1), channel_id=1, source_target_pairs={{0,2},{1,3},{2,0},{3,1},{4,6},{5,7},{6,4},{7,5},{8,10},{9,11},{10,... | collective-permute-start | bytes 73736 | tf_op jit(solution)/shard_map/ppermute | solution.py:49
  99.4 6.5 %collective-permute-start.43 = (bf16[8,1536]{1,0:T(8,128)(2,1)S(1)}, bf16[8,1536]{1,0:T(8,128)(2,1)S(1)}, u32[]{:S(2)}, u32[]{:S(2)}) collective-permute-start(bf16[8,1536]{1,0:T(8,128)(2,1)S(1)} %add_add_fusion.1), channel_id=1, source_target_pairs={{0,4},{1,5},{2,6},{3,7},{4,0},{5,1},{6,2},{7,3},{8,12},{9,13},{10,... | collective-permute-start | bytes 73736 | tf_op jit(solution)/shard_map/ppermute | solution.py:49
  102.0 5.6 %collective-permute-start.44 = (bf16[8,1536]{1,0:T(8,128)(2,1)S(1)}, bf16[8,1536]{1,0:T(8,128)(2,1)S(1)}, u32[]{:S(2)}, u32[]{:S(2)}) collective-permute-start(bf16[8,1536]{1,0:T(8,128)(2,1)S(1)} %add_add_fusion.1), channel_id=1, source_target_pairs={{0,6},{1,7},{2,4},{3,5},{4,2},{5,3},{6,0},{7,1},{8,14},{9,15},{10,... | collective-permute-start | bytes 73736 | tf_op jit(solution)/shard_map/ppermute | solution.py:49
  102.2 9.0 %collective-permute-start.26 = (bf16[64,1536]{1,0:T(8,128)(2,1)S(1)}, bf16[64,1536]{1,0:T(8,128)(2,1)S(1)}, u32[]{:S(2)}, u32[]{:S(2)}) collective-permute-start(bf16[64,1536]{1,0:T(8,128)(2,1)S(1)} %get-tuple-element.79), channel_id=1, source_target_pairs={{16,0},{0,16},{17,1},{1,17},{18,2},{2,18},{19,3},{3,19},{20,4},{4,... | collective-permute-start | bytes 589832 | tf_op jit(solution)/shard_map/ppermute | solution.py:54
  102.2 12.9 %collective-permute-start.27 = (bf16[64,1536]{1,0:T(8,128)(2,1)S(1)}, bf16[64,1536]{1,0:T(8,128)(2,1)S(1)}, u32[]{:S(2)}, u32[]{:S(2)}) collective-permute-start(bf16[64,1536]{1,0:T(8,128)(2,1)S(1)} %get-tuple-element.80), channel_id=1, source_target_pairs={{16,0},{0,16},{17,1},{1,17},{18,2},{2,18},{19,3},{3,19},{20,4},{4,... | collective-permute-start | bytes 589832 | tf_op jit(solution)/shard_map/ppermute | solution.py:54
  107.7 4.7 %collective-permute-start.45 = (f32[8,1536]{1,0:T(8,128)S(1)}, f32[8,1536]{1,0:T(8,128)S(1)}, u32[]{:S(2)}, u32[]{:S(2)}) collective-permute-start(f32[8,1536]{1,0:T(8,128)S(1)} %add_add_fusion.refs_0_), channel_id=1, source_target_pairs={{0,1},{1,0},{2,3},{3,2},{4,5},{5,4},{6,7},{7,6},{8,9},{9,8},{10,11... | collective-permute-start | bytes 147464 | tf_op jit(solution)/shard_map/ppermute | solution.py:49
  109.2 4.1 %collective-permute-start.46 = (f32[8,1536]{1,0:T(8,128)S(1)}, f32[8,1536]{1,0:T(8,128)S(1)}, u32[]{:S(2)}, u32[]{:S(2)}) collective-permute-start(f32[8,1536]{1,0:T(8,128)S(1)} %add_add_fusion.refs_0_), channel_id=1, source_target_pairs={{0,8},{8,0},{1,9},{9,1},{2,10},{10,2},{3,11},{11,3},{4,12},{12,4},... | collective-permute-start | bytes 147464 | tf_op jit(solution)/shard_map/ppermute | solution.py:49
  110.1 5.0 %collective-permute-start.47 = (f32[8,1536]{1,0:T(8,128)S(1)}, f32[8,1536]{1,0:T(8,128)S(1)}, u32[]{:S(2)}, u32[]{:S(2)}) collective-permute-start(f32[8,1536]{1,0:T(8,128)S(1)} %add_add_fusion.refs_0_), channel_id=1, source_target_pairs={{0,9},{1,8},{2,11},{3,10},{4,13},{5,12},{6,15},{7,14},{8,1},{9,0},... | collective-permute-start | bytes 147464 | tf_op jit(solution)/shard_map/ppermute | solution.py:49
  111.2 4.9 %collective-permute-start.48 = (f32[8,1536]{1,0:T(8,128)S(1)}, f32[8,1536]{1,0:T(8,128)S(1)}, u32[]{:S(2)}, u32[]{:S(2)}) collective-permute-start(f32[8,1536]{1,0:T(8,128)S(1)} %add_add_fusion.refs_0_), channel_id=1, source_target_pairs={{0,16},{16,0},{1,17},{17,1},{2,18},{18,2},{3,19},{19,3},{4,20},{20... | collective-permute-start | bytes 147464 | tf_op jit(solution)/shard_map/ppermute | solution.py:49
  112.3 3.8 %collective-permute-start.49 = (f32[8,1536]{1,0:T(8,128)S(1)}, f32[8,1536]{1,0:T(8,128)S(1)}, u32[]{:S(2)}, u32[]{:S(2)}) collective-permute-start(f32[8,1536]{1,0:T(8,128)S(1)} %collective-permute-done.45.refs_1_), channel_id=1, source_target_pairs={{0,16},{16,0},{1,17},{17,1},{2,18},{18,2},{3,19},{19,3},{4,20},{20... | collective-permute-start | bytes 147464 | tf_op jit(solution)/shard_map/ppermute | solution.py:49
  113.3 2.8 %collective-permute-start.50 = (f32[8,1536]{1,0:T(8,128)S(1)}, f32[8,1536]{1,0:T(8,128)S(1)}, u32[]{:S(2)}, u32[]{:S(2)}) collective-permute-start(f32[8,1536]{1,0:T(8,128)S(1)} %collective-permute-done.46.refs_2_), channel_id=1, source_target_pairs={{0,16},{16,0},{1,17},{17,1},{2,18},{18,2},{3,19},{19,3},{4,20},{20... | collective-permute-start | bytes 147464 | tf_op jit(solution)/shard_map/ppermute | solution.py:49
  115.1 1.2 %collective-permute-start.51 = (f32[8,1536]{1,0:T(8,128)S(1)}, f32[8,1536]{1,0:T(8,128)S(1)}, u32[]{:S(2)}, u32[]{:S(2)}) collective-permute-start(f32[8,1536]{1,0:T(8,128)S(1)} %collective-permute-done.47.refs_3_), channel_id=1, source_target_pairs={{0,16},{16,0},{1,17},{17,1},{2,18},{18,2},{3,19},{19,3},{4,20},{20... | collective-permute-start | bytes 147464 | tf_op jit(solution)/shard_map/ppermute | solution.py:49

commit v4 on v3

--- a/solution.py
+++ b/solution.py
@@ -98,30 +98,36 @@
     return forth, [(d, s) for s, d in forth]
 
 
-def ring_gather(block):
-    n, rows = lax.axis_size("fsdp"), block.shape[0]
+def after(value, others):
+    return lax.optimization_barrier((value, others))[0]
+
+
+def ring_gather(block, second_after, third_after, last_after):
+    n, rows = lax.axis_size("fsdp"), block.shape[0] // 2
     forth, back = ring_pairs(n)
-    pieces, where = [block], [(0, 0, rows)]
+    pieces, upper, lower = [block], [(0, 0, 0)], [(0, rows, 0)]
     one = two = block
     for k in range(1, (n + 1) // 2):
+        if k in (2, 3):
+            one, two = after([one, two], second_after if k == 2 else third_after)
         one = lax.ppermute(one, "fsdp", forth)
         two = lax.ppermute(two, "fsdp", back)
-        pieces += [one, two]
-        where += [(-k, 0, rows), (k, 0, rows)]
+        for piece, distance in ((one, -k), (two, k)):
+            upper.append((len(pieces), 0, distance))
+            lower.append((len(pieces), rows, distance))
+            pieces.append(piece)
     if n % 2 == 0:
-        half = rows // 2 if rows % 32 == 0 else 0
-        if half:
-            pieces.append(lax.ppermute(one[:half], "fsdp", forth))
-            where.append((n // 2, 0, half))
-        pieces.append(lax.ppermute(two[half:], "fsdp", back))
-        where.append((n // 2, half, rows - half))
-    return pieces, where
+        one, two = after([one[:rows], two[rows:]], last_after)
+        upper.append((len(pieces), 0, n // 2))
+        lower.append((len(pieces) + 1, 0, n // 2))
+        pieces += [lax.ppermute(one, "fsdp", forth), lax.ppermute(two, "fsdp", back)]
+    return pieces, upper, lower
 
 
 def gather_tile(a):
     out = []
     for t in range(lax.axis_size("sy")):
-        mine = a if t == 0 else shift(a, "sy", t)
+        mine = a if t == 0 else after(shift(a, "sy", t), out[-1])
         out.append([mine] + [shift(mine, "sx", s) for s in range(1, lax.axis_size("sx"))])
     return [piece for group in out for piece in group]
 
@@ -461,15 +467,15 @@
         copy.wait()
 
 
-def block_jobs(pieces, where, whole):
+def block_jobs(pieces, spots, whole):
     n = lax.axis_size("fsdp")
     rows = whole.shape[0] // n
     place = place_of(lax.axis_index("fsdp"), n)
     jobs = []
-    for piece, (k, first, count) in zip(pieces, where, strict=True):
-        owner = at_place(lax.rem(place + (k + n), n), n)
-        begin = pl.multiple_of(owner * rows + first, 16)
-        jobs.append((piece, whole.at[pl.ds(begin, count)]))
+    for index, first, distance in spots:
+        owner = at_place(lax.rem(place + (distance + n), n), n)
+        begin = pl.multiple_of(owner * rows, 16)
+        jobs.append((pieces[index].at[pl.ds(first, rows)], whole.at[pl.ds(begin, rows)]))
     return jobs
 
 
@@ -483,22 +489,32 @@
     return [pl.ds(k, width) for k in range(0, hidden, width)]
 
 
-def up_kernel(where, tiles, *refs):
-    blocks, refs = refs[: len(where)], refs[len(where) :]
-    lns, refs = refs[:tiles], refs[tiles:]
-    cots, refs = refs[:tiles], refs[tiles:]
-    bias, scale, act, slope, whole, d_mlp, ln_all, cot_all, sems = refs
-    one = start_copies(block_jobs(blocks, where, whole), sems, 0)
-    two = start_copies(row_jobs(lns, ln_all), sems, len(one))
-    three = start_copies(row_jobs(cots, cot_all), sems, len(one) + len(two))
-    wait_all(three)
-    d_mlp[...] = (as_row(scale) * cot_all[...].astype(F32)).astype(BF)
-    wait_all(one + two)
-    hidden = whole.shape[1]
+def scale_kernel(scale, *refs):
+    *cots, out = refs
+    spots = cots[0].shape[0]
+    for k, cot in enumerate(cots):
+        out[pl.ds(k * spots, spots), :] = (as_row(scale) * cot[...].astype(F32)).astype(BF)
+
+
+def scale_part(cots, scale):
+    spots, chans = cots[0].shape
+    return pl.pallas_call(
+        scale_kernel,
+        out_shape=shaped((len(cots) * spots, chans), BF),
+        in_specs=vmem(1 + len(cots)),
+        out_specs=pl.BlockSpec(memory_space=pltpu.VMEM),
+        compiler_params=params(16),
+        cost_estimate=cost(1, 1),
+        name="scale_part",
+    )(scale, *cots)
+
+
+def forward_hidden(ln, up, bias, act, slope):
+    hidden = up.shape[1]
     quarter = lax.axis_index("sx") * lax.axis_size("sy") + lax.axis_index("sy")
     for tile in hidden_tiles(hidden):
         columns = pl.ds(pl.multiple_of(quarter * hidden + tile.start, LANES), tile.size)
-        v = jnp.dot(ln_all[...], whole[:, tile], preferred_element_type=F32)
+        v = jnp.dot(ln[...], up[:, tile], preferred_element_type=F32)
         v = v + bias[columns].reshape(1, tile.size)
         square = v * v
         th = jnp.tanh(GELU_A * (v + GELU_B * (square * v)))
@@ -507,32 +523,10 @@
         slope[:, tile] = half + 0.5 * v * (1.0 - th * th) * (GELU_A * (1.0 + 3.0 * GELU_B * square))
 
 
-def up_part(blocks, where, lns, cots, bias, scale):
-    spots, chans = lns[0].shape
-    rows, hidden = blocks[0].shape
-    n = lax.axis_size("fsdp")
-    tiles = len(lns)
-    total = tiles * spots
-    count = len(blocks) + 2 * tiles
-    return pl.pallas_call(
-        functools.partial(up_kernel, where, tiles),
-        out_shape=(
-            shaped((total, hidden), BF),
-            shaped((total, hidden), F32),
-            shaped((n * rows, hidden), BF),
-            shaped((total, chans), BF),
-        ),
-        in_specs=anywhere(count) + vmem(2),
-        out_specs=vmem(4),
-        scratch_shapes=[
-            pltpu.VMEM((total, chans), BF),
-            pltpu.VMEM((total, chans), BF),
-            pltpu.SemaphoreType.DMA((count,)),
-        ],
-        compiler_params=params(28),
-        cost_estimate=cost(2 * total * chans * hidden, 8 * total * chans, total * hidden),
-        name="up_part",
-    )(*blocks, *lns, *cots, bias, scale)
+def backward_hidden(d_mlp, down, slope, d_pre):
+    for tile in hidden_tiles(down.shape[1]):
+        d_act = jnp.dot(d_mlp[...], down[:, tile], preferred_element_type=F32)
+        d_pre[:, tile] = (d_act * slope[:, tile]).astype(BF)
 
 
 def contract_last(a, b):
@@ -552,68 +546,71 @@
         first += count
 
 
-def far_kernel(where, first, *refs):
-    blocks, refs = refs[: len(where)], refs[len(where) :]
-    d_mlp, slope, up, *far, whole, d_mlp_in, slope_in, up_in, d_pre, sems = refs
-    count = d_pre.shape[0]
-    mine = pl.ds(first, count)
-    one = start_copies(block_jobs(blocks, where, whole), sems, 0)
-    jobs = [(d_mlp.at[mine], d_mlp_in), (slope.at[mine], slope_in), (up, up_in)]
-    two = start_copies(jobs, sems, len(one))
-    wait_all(one + two[:2])
-    for tile in hidden_tiles(whole.shape[1]):
-        d_act = jnp.dot(d_mlp_in[...], whole[:, tile], preferred_element_type=F32)
-        d_pre[:, tile] = (d_act * slope_in[:, tile]).astype(BF)
-    wait_all(two[2:])
-    for tile in channel_tiles(up_in.shape[0]):
-        write_pieces(contract_last(d_pre[...], up_in[tile, :]), tile, far)
-
-
-def far_part(blocks, where, d_mlp, slope, up, n_near, n_far):
-    total, chans = d_mlp.shape
-    hidden = slope.shape[1]
-    spots = total // (n_near + n_far)
-    count = len(blocks) + 3
-    outs = [shaped((spots, chans), BF)] * n_far
-    return pl.pallas_call(
-        functools.partial(far_kernel, where, n_near * spots),
+def far_kernel(upper, lower, n_pieces, n_far, *refs):
+    pieces, refs = refs[:n_pieces], refs[n_pieces:]
+    lns, refs = refs[:n_far], refs[n_far:]
+    d_mlp, bias, act, *far, up, down, ln, d_mlp_in, slope, d_pre, sems = refs
+    count = ln.shape[0]
+    one = start_copies(row_jobs(lns, ln) + block_jobs(pieces, upper, up), sems, 0)
+    here = pl.ds(d_mlp.shape[0] - count, count)
+    two = start_copies([(d_mlp.at[here], d_mlp_in)] + block_jobs(pieces, lower, down), sems, len(one))
+    wait_all(one)
+    forward_hidden(ln, up, bias, act, slope)
+    wait_all(two)
+    backward_hidden(d_mlp_in, down, slope, d_pre)
+    for tile in channel_tiles(up.shape[0]):
+        write_pieces(contract_last(d_pre[...], up[tile, :]), tile, far)
+
+
+def far_part(pieces, upper, lower, lns, d_mlp, bias):
+    spots, chans = lns[0].shape
+    hidden = pieces[0].shape[1]
+    count = spots * len(lns)
+    n_copies = len(upper) + len(lower) + len(lns) + 1
+    outs = [shaped((count, hidden), BF)] + [shaped((spots, chans), BF)] * len(lns)
+    return pl.pallas_call(
+        functools.partial(far_kernel, upper, lower, len(pieces), len(lns)),
         out_shape=outs,
-        in_specs=anywhere(count),
+        in_specs=anywhere(len(pieces) + len(lns) + 1) + vmem(1),
         out_specs=vmem(len(outs)),
         scratch_shapes=[
-            pltpu.VMEM(up.shape, BF),
-            pltpu.VMEM((n_far * spots, chans), BF),
-            pltpu.VMEM((n_far * spots, hidden), F32),
-            pltpu.VMEM(up.shape, BF),
-            pltpu.VMEM((n_far * spots, hidden), BF),
-            pltpu.SemaphoreType.DMA((count,)),
+            pltpu.VMEM((chans, hidden), BF),
+            pltpu.VMEM((chans, hidden), BF),
+            pltpu.VMEM((count, chans), BF),
+            pltpu.VMEM((count, chans), BF),
+            pltpu.VMEM((count, hidden), F32),
+            pltpu.VMEM((count, hidden), BF),
+            pltpu.SemaphoreType.DMA((n_copies,)),
         ],
-        compiler_params=params(20),
-        cost_estimate=cost(4 * n_far * spots * chans * hidden, 8 * total * chans),
+        compiler_params=params(24),
+        cost_estimate=cost(6 * count * chans * hidden, 8 * count * chans),
         name="far_part",
-    )(*blocks, d_mlp, slope, up)
-
-
-def rest_kernel(where, tiles, n_near, n_mlp, *refs):
-    blocks, refs = refs[: len(where)], refs[len(where) :]
+    )(*pieces, *lns, d_mlp, bias)
+
+
+def rest_kernel(upper, lower, n_pieces, tiles, n_near, n_mlp, *refs):
+    pieces, refs = refs[:n_pieces], refs[n_pieces:]
+    lns, refs = refs[:n_near], refs[n_near:]
+    d_mlp, far_act, *refs = refs
     cots, refs = refs[:tiles], refs[tiles:]
-    d_mlp, slope, up, act, bias, *refs = refs
-    near, outs, refs = refs[:n_near], refs[n_near : n_near + n_mlp], refs[n_near + n_mlp :]
-    scale_term, whole, d_mlp_in, slope_in, up_in, act_in, d_pre, sems = refs
+    bias_up, bias, *refs = refs
+    n_out = 2 * n_near - 1
+    near, outs, refs = refs[:n_out], refs[n_out : n_out + n_mlp], refs[n_out + n_mlp :]
+    scale_term, up, down, ln, d_mlp_in, act, slope, d_pre, sems = refs
     spots = cots[0].shape[0]
-    mine = pl.ds(0, d_pre.shape[0])
-    one = start_copies(block_jobs(blocks, where, whole), sems, 0)
-    jobs = [(d_mlp.at[mine], d_mlp_in), (slope.at[mine], slope_in), (up, up_in), (act, act_in)]
+    count = ln.shape[0]
+    one = start_copies(row_jobs(lns, ln) + block_jobs(pieces, upper, up), sems, 0)
+    jobs = [(d_mlp.at[pl.ds(0, count)], d_mlp_in)] + block_jobs(pieces, lower, down)
+    jobs.append((far_act, act.at[pl.ds(count, far_act.shape[0])]))
     two = start_copies(jobs, sems, len(one))
-    wait_all(one + two[:2])
-    for tile in hidden_tiles(whole.shape[1]):
-        d_act = jnp.dot(d_mlp_in[...], whole[:, tile], preferred_element_type=F32)
-        d_pre[:, tile] = (d_act * slope_in[:, tile]).astype(BF)
-    wait_all(two[2:])
-    for tile in channel_tiles(up_in.shape[0]):
-        write_pieces(contract_last(d_pre[...], up_in[tile, :]), tile, near)
-    for tile in channel_tiles(whole.shape[0]):
-        value = contract_last(act_in[...], whole[tile, :])
+    wait_all(one)
+    forward_hidden(ln, up, bias_up, act.at[pl.ds(0, count)], slope)
+    wait_all(two)
+    backward_hidden(d_mlp_in, down, slope, d_pre)
+    for tile in channel_tiles(up.shape[0]):
+        write_pieces(contract_last(d_pre[...], up[tile, :]), tile, near)
+    for tile in channel_tiles(down.shape[0]):
+        value = contract_last(act[...], down[tile, :])
         write_pieces(value, tile, outs)
         total = jnp.zeros((1, tile.size), F32)
         for k, cot in enumerate(cots):
@@ -625,33 +622,34 @@
         scale_term[:, tile] = total
 
 
-def rest_part(blocks, where, d_mlp, slope, up, act, bias, cots, n_near):
-    total, chans = d_mlp.shape
-    hidden = slope.shape[1]
-    tiles = len(cots)
-    spots = total // tiles
-    count = len(blocks) + 4
+def rest_part(pieces, upper, lower, lns, d_mlp, far_act, cots, bias_up, bias):
+    spots, chans = lns[0].shape
+    hidden = pieces[0].shape[1]
+    n_near, tiles = len(lns), len(cots)
+    count = spots * n_near
+    n_copies = len(upper) + len(lower) + n_near + 2
     group = [spots] + [spots // 2] * (2 * n_near - 2)
     groups = group * (1 + tiles // n_near)
     outs = [shaped((rows, chans), BF) for rows in groups] + [shaped((1, chans), F32)]
     return pl.pallas_call(
-        functools.partial(rest_kernel, where, tiles, len(group), len(groups) - len(group)),
+        functools.partial(rest_kernel, upper, lower, len(pieces), tiles, n_near, len(groups) - len(group)),
         out_shape=outs,
-        in_specs=anywhere(len(blocks)) + vmem(tiles) + anywhere(4) + vmem(1),
+        in_specs=anywhere(len(pieces) + n_near + 2) + vmem(tiles + 2),
         out_specs=vmem(len(outs)),
         scratch_shapes=[
-            pltpu.VMEM(up.shape, BF),
-            pltpu.VMEM((n_near * spots, chans), BF),
-            pltpu.VMEM((n_near * spots, hidden), F32),
-            pltpu.VMEM(up.shape, BF),
-            pltpu.VMEM((total, hidden), BF),
-            pltpu.VMEM((n_near * spots, hidden), BF),
-            pltpu.SemaphoreType.DMA((count,)),
+            pltpu.VMEM((chans, hidden), BF),
+            pltpu.VMEM((chans, hidden), BF),
+            pltpu.VMEM((count, chans), BF),
+            pltpu.VMEM((count, chans), BF),
+            pltpu.VMEM((spots * tiles, hidden), BF),
+            pltpu.VMEM((count, hidden), F32),
+            pltpu.VMEM((count, hidden), BF),
+            pltpu.SemaphoreType.DMA((n_copies,)),
         ],
-        compiler_params=params(28),
-        cost_estimate=cost(2 * (2 * n_near + tiles) * spots * chans * hidden, 10 * total * chans),
+        compiler_params=params(32),
+        cost_estimate=cost(8 * count * chans * hidden, 10 * count * chans),
         name="rest_part",
-    )(*blocks, *cots, d_mlp, slope, up, act, bias)
+    )(*pieces, *lns, d_mlp, far_act, *cots, bias_up, bias)
 
 
 def split_refs(refs, counts):
@@ -789,25 +787,21 @@
     hidden = w_up.shape[1] // tiles
     up_block = lax.dynamic_slice_in_dim(w_up, quarter * hidden, hidden, 1)
     down_block = lax.dynamic_slice_in_dim(w_down, quarter * hidden, hidden, 0).T
-    ups, up_where = ring_gather(up_block)
-
     scaled, *edges = prepare(x_code[0], x_exp[0])
-    edges = exchange_edges(dict(zip(edge_keys(), edges, strict=True)))
-    downs, down_where = ring_gather(down_block)
-    edges, _ = lax.optimization_barrier((list(edges.values()), ups[1:3] + downs[1:3]))
+    edges = list(exchange_edges(dict(zip(edge_keys(), edges, strict=True))).values())
+    cots = gather_tile(after(cotangent.reshape(spots, chans), edges))
+    d_mlp = scale_part(cots, layer_scale)
     padded, normed, rstd, ln_out = conv_norm(scaled, edges, dw_kernel, dw_bias, ln_gain, ln_bias)
-    ln_out, _ = lax.optimization_barrier((ln_out, ups[3:5]))
+    blocks = jnp.concatenate([up_block, down_block], 0)
+    pieces, upper, lower = ring_gather(blocks, edges, ln_out, d_mlp)
     lns = gather_tile(ln_out)
-    cot, edges = lax.optimization_barrier((cotangent.reshape(spots, chans), edges))
-    cots = gather_tile(cot)
-    act, slope, up, d_mlp = up_part(ups, up_where, lns, cots, b_up, layer_scale)
-    far = far_part(downs, down_where, d_mlp, slope, up, n_near, tiles - n_near)
+    far_act, *far = far_part(pieces, upper, lower, lns[n_near:], d_mlp, b_up)
 
     far = [far[k : k + n_near] for k in range(0, len(far), n_near)]
     far = [add_rounded(reduce_cores(group), [spots])[0] for group in far]
     d_mlp, far = lax.optimization_barrier((d_mlp, far))
     far = [shift(term, "sy", -(t + 1)) for t, term in enumerate(far)]
-    *rest, scale_term = rest_part(downs, down_where, d_mlp, slope, up, act, b_down, cots, n_near)
+    *rest, scale_term = rest_part(pieces, upper, lower, lns[:n_near], d_mlp, far_act, cots, b_up, b_down)
     size = 2 * n_near - 1
     near, *mlp = [reduce_cores_halves(rest[k : k + size]) for k in range(0, len(rest), size)]
     mlp_far = [add_rounded(group, [spots - spots // 4, spots // 4]) for group in mlp[1:]]

time: 118 us -> 110 us (0.932)
  starting transfers between devices: 42.6 us -> 34.9 us
  Pallas kernels: 32.2 us -> 30 us
  waiting for transfers between devices: 36.1 us -> 38.2 us
    ppermute x6 -> x3, starting transfers between devices: 11.9 us -> 2.04 us  [ring_gather(): one = lax.ppermute(one, 'fsdp', forth)]
    ppermute x6 -> x3, waiting for transfers between devices: 14.6 us -> 6.61 us  [ring_gather(): one = lax.ppermute(one, 'fsdp', forth)]
    ppermute x6 -> x3, waiting for transfers between devices: 0.42 us -> 7.21 us  [ring_gather(): two = lax.ppermute(two, 'fsdp', back)]
    ppermute x4 -> x2, waiting for transfers between devices: 2.79 us -> 6.26 us  [the longest x1 4.69 us: ring_gather(): lax.ppermute(one, 'fsdp', forth)]
    ppermute x14, waiting for transfers between devices: 5.82 us -> 2.77 us  [swap(): return lax.ppermute(a, axes, [(i, i ^ mask) for i in range(total)])]
    ppermute x4 -> x2, starting transfers between devices: 5.12 us -> 2.08 us  [the longest x1 1.62 us: ring_gather(): lax.ppermute(one, 'fsdp', forth)]
    ppermute x16, starting transfers between devices: 6.88 us -> 9.3 us  [shift(): return lax.ppermute(a, axis, [((i + k) % n, i) for i in range(n)])]
    ppermute x16, waiting for transfers between devices: 8.54 us -> 10.7 us  [shift(): return lax.ppermute(a, axis, [((i + k) % n, i) for i in range(n)])]
  transfers between devices with their start and end apart: 52 -> 44, of which waited for: 20 -> 20; matrix products, arithmetic and copies ran while one was open for 2% -> 1% of each run, Pallas kernels for 24% -> 22%
where the time goes in v4:
time: 110 us
  waiting for transfers between devices  38.2 us (35%)
  starting transfers between devices  34.9 us (32%)
  Pallas kernels  30 us (27%)
  local copies, waits for them, and re-layouts  5.44 us (5%)
    ppermute x14, starting transfers between devices, swap(): return lax.ppermute(a, axes, [(i, i ^ mask) for i in range(total)])  12.1 us
    ppermute x16, waiting for transfers between devices, shift(): return lax.ppermute(a, axis, [((i + k) % n, i) for i in range(n)])  10.7 us
    ppermute x16, starting transfers between devices, shift(): return lax.ppermute(a, axis, [((i + k) % n, i) for i in range(n)])  9.3 us
    ppermute x3, waiting for transfers between devices, ring_gather(): two = lax.ppermute(two, 'fsdp', back)  7.21 us
    ppermute x3, waiting for transfers between devices, ring_gather(): one = lax.ppermute(one, 'fsdp', forth)  6.61 us
    pallas_call x2, Pallas kernels, conv_back(): pl.pallas_call(functools.partial(conv_back_kernel, begin, count), out_sha...  6.3 us
    pallas_call x1, Pallas kernels, rest_part(): pl.pallas_call(functools.partial(rest_kernel, upper, lower, len(pieces),...  5.98 us
    pallas_call x1, Pallas kernels, conv_norm(): pl.pallas_call(conv_norm_kernel, out_shape=(shaped((rows + 2 * HALO, cols...  5.8 us
  transfers between devices with their start and end apart: 44, of which 20 were waited for; matrix products, arithmetic and copies ran while one was open for 1% of the time, Pallas kernels for 22%

profile of v4, /device:TPU:0, one launch (start us, length us, event | category | flops | bytes accessed | tf_op | source)
XLA Modules:
  0.0 109.6 jit_solution(2833359408427175645)
XLA Ops:
  0.7 1.3 %copy-done = bf16[192,3072]{1,0:T(8,128)(2,1)S(1)} copy-done((bf16[192,3072]{1,0:T(8,128)(2,1)S(1)}, bf16[192,3072]{1,0:T(8,128)(2,1)}, u32[]{:S(2)}) %copy-start) | copy-done | bytes 1179672
  2.0 1.1 dynamic-slice_bitcast_fusion
  3.1 3.0 %collective-permute-start.1 = (bf16[384,768]{1,0:T(8,128)(2,1)S(1)}, bf16[384,768]{1,0:T(8,128)(2,1)S(1)}, u32[]{:S(2)}, u32[]{:S(2)}) collective-permute-start(bf16[384,768]{1,0:T(8,128)(2,1)S(1)} %pad_maximum_fusion.refs_0_), channel_id=1, source_target_pairs={{2,0},{4,2},{6,4},{7,6},{5,7},{3,5},{1,3},{0,1},{10,8},{12,10},{14... | collective-permute-start | bytes 1769480 | tf_op jit(solution)/shard_map/ppermute | solution.py:114
  6.2 0.9 copy.18
  7.2 0.5 prepare.1
  7.8 1.9 %collective-permute-start.3 = (bf16[8,3,1536]{2,1,0:T(4,128)(2,1)S(1)}, bf16[8,3,1536]{2,1,0:T(4,128)(2,1)S(1)}, u32[]{:S(2)}, u32[]{:S(2)}) collective-permute-start(bf16[8,3,1536]{2,1,0:T(4,128)(2,1)S(1)} %get-tuple-element.64), channel_id=1, source_target_pairs={{0,8},{8,0},{16,24},{24,16},{1,9},{9,1},{17,25},{25,17},{2,10},{10... | collective-permute-start | bytes 221192 | tf_op jit(solution)/shard_map/ppermute | solution.py:74
  9.8 3.8 %collective-permute-done.4.refs_2_ = bf16[3,3,1536]{2,1,0:T(4,128)(2,1)S(1)} collective-permute-done((bf16[3,3,1536]{2,1,0:T(4,128)(2,1)S(1)}, bf16[3,3,1536]{2,1,0:T(4,128)(2,1)S(1)}, u32[]{:S(2)}, u32[]{:S(2)}) %collective-permute-start.4) | collective-permute-done | bytes 27680 | tf_op jit(solution)/shard_map/ppermute | solution.py:74
  13.6 5.9 %collective-permute-done.1.refs_2_ = bf16[384,768]{1,0:T(8,128)(2,1)S(1)} collective-permute-done((bf16[384,768]{1,0:T(8,128)(2,1)S(1)}, bf16[384,768]{1,0:T(8,128)(2,1)S(1)}, u32[]{:S(2)}, u32[]{:S(2)}) %collective-permute-start.1) | collective-permute-done | bytes 589856 | tf_op jit(solution)/shard_map/ppermute | solution.py:114
  19.5 1.5 %collective-permute-done.refs_1_ = bf16[384,768]{1,0:T(8,128)(2,1)} collective-permute-done((bf16[384,768]{1,0:T(8,128)(2,1)S(1)}, bf16[384,768]{1,0:T(8,128)(2,1)}, u32[]{:S(2)}, u32[]{:S(2)}) %collective-permute-start) | collective-permute-done | bytes 589856 | tf_op jit(solution)/shard_map/ppermute | solution.py:113
  21.0 0.4 collective-permute-start.5
  21.4 1.6 %collective-permute-start.6 = (bf16[384,768]{1,0:T(8,128)(2,1)S(1)}, bf16[384,768]{1,0:T(8,128)(2,1)S(1)}, u32[]{:S(2)}, u32[]{:S(2)}) collective-permute-start(bf16[384,768]{1,0:T(8,128)(2,1)S(1)} %collective-permute-done.1.refs_2_), channel_id=1, source_target_pairs={{2,0},{4,2},{6,4},{7,6},{5,7},{3,5},{1,3},{0,1},{10,8},{12,10},{14... | collective-permute-start | bytes 1769480 | tf_op jit(solution)/shard_map/ppermute | solution.py:114
  23.0 1.5 %collective-permute-start.10 = (bf16[128,1536]{1,0:T(8,128)(2,1)S(1)}, bf16[128,1536]{1,0:T(8,128)(2,1)S(1)}, u32[]{:S(2)}, u32[]{:S(2)}) collective-permute-start(bf16[128,1536]{1,0:T(8,128)(2,1)S(1)} %bitcast.8), channel_id=1, source_target_pairs={{8,0},{0,8},{9,1},{1,9},{10,2},{2,10},{11,3},{3,11},{12,4},{4,12},... | collective-permute-start | bytes 1179656 | tf_op jit(solution)/shard_map/ppermute | solution.py:54
  24.5 0.7 copy-done.5
  25.2 0.7 copy-done.9
  25.9 0.7 copy-done.10
  26.6 5.8 %conv_norm.1 = (f32[14,24,1536]{2,1,0:T(8,128)S(1)}, f32[128,1536]{1,0:T(8,128)S(1)}, f32[128,128]{1,0:T(8,128)S(1)}, bf16[128,1536]{1,0:T(8,128)(2,1)S(1)}) custom-call(bf16[8,16,1536]{2,1,0:T(8,128)(2,1)S(1)} %get-tuple-element.62.own.scaled, bf16[3,16,1536]{2,1,0:T(8,128)(2,1)S(1)} %collective-permute-done.2.refs_0_, ...), custom_call_target="tpu_custom_call" | custom-call | flops 1 | bytes 1 | tf_op jit(solution)/shard_map/conv_norm/pallas_call | solution.py:316
  32.4 2.7 %collective-permute-done.5.refs_3_ = bf16[384,768]{1,0:T(8,128)(2,1)S(1)} collective-permute-done((bf16[384,768]{1,0:T(8,128)(2,1)}, bf16[384,768]{1,0:T(8,128)(2,1)S(1)}, u32[]{:S(2)}, u32[]{:S(2)}) %collective-permute-start.5) | collective-permute-done | bytes 589856 | tf_op jit(solution)/shard_map/ppermute | solution.py:113
  35.1 0.2 collective-permute-done.6.refs_4_
  35.3 1.5 %collective-permute-start.7 = (bf16[384,768]{1,0:T(8,128)(2,1)S(1)}, bf16[384,768]{1,0:T(8,128)(2,1)S(1)}, u32[]{:S(2)}, u32[]{:S(2)}) collective-permute-start(bf16[384,768]{1,0:T(8,128)(2,1)S(1)} %collective-permute-done.5.refs_3_), channel_id=1, source_target_pairs={{0,2},{2,4},{4,6},{6,7},{7,5},{5,3},{3,1},{1,0},{8,10},{10,12},{12... | collective-permute-start | bytes 1769480 | tf_op jit(solution)/shard_map/ppermute | solution.py:113
  36.8 0.5 collective-permute-start.8
  37.3 1.4 %collective-permute-start.15 = (bf16[128,1536]{1,0:T(8,128)(2,1)S(1)}, bf16[128,1536]{1,0:T(8,128)(2,1)S(1)}, u32[]{:S(2)}, u32[]{:S(2)}) collective-permute-start(bf16[128,1536]{1,0:T(8,128)(2,1)S(1)} %get-tuple-element.68.refs_9_), channel_id=1, source_target_pairs={{8,0},{0,8},{9,1},{1,9},{10,2},{2,10},{11,3},{3,11},{12,4},{4,12},... | collective-permute-start | bytes 1179656 | tf_op jit(solution)/shard_map/ppermute | solution.py:54
  38.8 0.5 collective-permute-start.11
  39.3 6.3 %collective-permute-done.15.refs_9_ = bf16[128,1536]{1,0:T(8,128)(2,1)S(1)} collective-permute-done((bf16[128,1536]{1,0:T(8,128)(2,1)S(1)}, bf16[128,1536]{1,0:T(8,128)(2,1)S(1)}, u32[]{:S(2)}, u32[]{:S(2)}) %collective-permute-start.15) | collective-permute-done | bytes 393248 | tf_op jit(solution)/shard_map/ppermute | solution.py:54
  45.6 0.3 scale_part.1.refs_11_
  45.9 2.4 %collective-permute-done.7.refs_5_ = bf16[384,768]{1,0:T(8,128)(2,1)S(1)} collective-permute-done((bf16[384,768]{1,0:T(8,128)(2,1)S(1)}, bf16[384,768]{1,0:T(8,128)(2,1)S(1)}, u32[]{:S(2)}, u32[]{:S(2)}) %collective-permute-start.7) | collective-permute-done | bytes 589856 | tf_op jit(solution)/shard_map/ppermute | solution.py:113
  48.3 1.0 collective-permute-done.8.refs_6_
  49.4 1.6 %collective-permute-start.12 = (bf16[192,768]{1,0:T(8,128)(2,1)S(1)}, bf16[192,768]{1,0:T(8,128)(2,1)S(1)}, u32[]{:S(2)}, u32[]{:S(2)}) collective-permute-start(bf16[192,768]{1,0:T(8,128)(2,1)S(1)} %slice.8), channel_id=1, source_target_pairs={{0,2},{2,4},{4,6},{6,7},{7,5},{5,3},{3,1},{1,0},{8,10},{10,12},{12... | collective-permute-start | bytes 884744 | tf_op jit(solution)/shard_map/ppermute | solution.py:123
  51.0 0.5 collective-permute-start.13
  51.5 4.7 %collective-permute-done.12.refs_7_ = bf16[192,768]{1,0:T(8,128)(2,1)S(1)} collective-permute-done((bf16[192,768]{1,0:T(8,128)(2,1)S(1)}, bf16[192,768]{1,0:T(8,128)(2,1)S(1)}, u32[]{:S(2)}, u32[]{:S(2)}) %collective-permute-start.12) | collective-permute-done | bytes 294944 | tf_op jit(solution)/shard_map/ppermute | solution.py:123
  56.2 1.6 %collective-permute-done.13.refs_8_ = bf16[192,768]{1,0:T(8,128)(2,1)S(1)} collective-permute-done((bf16[192,768]{1,0:T(8,128)(2,1)S(1)}, bf16[192,768]{1,0:T(8,128)(2,1)S(1)}, u32[]{:S(2)}, u32[]{:S(2)}) %collective-permute-start.13) | collective-permute-done | bytes 294944 | tf_op jit(solution)/shard_map/ppermute | solution.py:123
  57.8 4.4 %far_part.1 = (bf16[256,768]{1,0:T(8,128)(2,1)S(1)}, bf16[128,1536]{1,0:T(8,128)(2,1)S(1)}, bf16[128,1536]{1,0:T(8,128)(2,1)S(1)}) custom-call(bf16[384,768]{1,0:T(8,128)(2,1)S(1)} %pad_maximum_fusion.refs_0_, bf16[384,768]{1,0:T(8,128)(2,1)} %collective-permute-done.refs_1_, bf16[384,768]{1,0:T(8,128)(2,1)S(1)} %collective-permute-done.1.refs_2_, ...), custom_call_target="tpu_custom_call" | custom-call | flops 1 | bytes 1 | tf_op jit(solution)/shard_map/far_part/pallas_call | solution.py:571
  62.3 1.7 %collective-permute-done.17.refs_1_ = bf16[128,1536]{1,0:T(8,128)(2,1)S(1)} collective-permute-done((bf16[128,1536]{1,0:T(8,128)(2,1)S(1)}, bf16[128,1536]{1,0:T(8,128)(2,1)S(1)}, u32[]{:S(2)}, u32[]{:S(2)}) %collective-permute-start.17) | collective-permute-done | bytes 393248 | tf_op jit(solution)/shard_map/ppermute | solution.py:54
  64.1 1.6 %collective-permute-start.22 = (bf16[128,1536]{1,0:T(8,128)(2,1)S(1)}, bf16[128,1536]{1,0:T(8,128)(2,1)S(1)}, u32[]{:S(2)}, u32[]{:S(2)}) collective-permute-start(bf16[128,1536]{1,0:T(8,128)(2,1)S(1)} %add_rounded.2), channel_id=1, source_target_pairs={{8,0},{0,8},{9,1},{1,9},{10,2},{2,10},{11,3},{3,11},{12,4},{4,12},... | collective-permute-start | bytes 1179656 | tf_op jit(solution)/shard_map/ppermute | solution.py:54
  65.7 6.0 %rest_part.1 = (bf16[128,1536]{1,0:T(8,128)(2,1)S(1)}, bf16[64,1536]{1,0:T(8,128)(2,1)S(1)}, bf16[64,1536]{1,0:T(8,128)(2,1)S(1)}, bf16[128,1536]{1,0:T(8,128)(2...) custom-call(bf16[384,768]{1,0:T(8,128)(2,1)S(1)} %pad_maximum_fusion, ...), custom_call_target="tpu_custom_call" | custom-call | flops 1 | bytes 1 | tf_op jit(solution)/shard_map/rest_part/pallas_call | solution.py:634
  71.7 0.5 collective-permute-start.24
  72.3 0.4 collective-permute-start.21
  72.7 0.4 collective-permute-done.23.refs_1_
  73.2 0.3 collective-permute-done.24.refs_2_
  73.5 1.8 %collective-permute-done.22.refs_3_ = bf16[128,1536]{1,0:T(8,128)(2,1)S(1)} collective-permute-done((bf16[128,1536]{1,0:T(8,128)(2,1)S(1)}, bf16[128,1536]{1,0:T(8,128)(2,1)S(1)}, u32[]{:S(2)}, u32[]{:S(2)}) %collective-permute-start.22) | collective-permute-done | bytes 393248 | tf_op jit(solution)/shard_map/ppermute | solution.py:54
  75.3 1.5 %collective-permute-start.26 = (bf16[96,1536]{1,0:T(8,128)(2,1)S(1)}, bf16[96,1536]{1,0:T(8,128)(2,1)S(1)}, u32[]{:S(2)}, u32[]{:S(2)}) collective-permute-start(bf16[96,1536]{1,0:T(8,128)(2,1)S(1)} %get-tuple-element.98), channel_id=1, source_target_pairs={{8,0},{0,8},{9,1},{1,9},{10,2},{2,10},{11,3},{3,11},{12,4},{4,12},... | collective-permute-start | bytes 884744 | tf_op jit(solution)/shard_map/ppermute | solution.py:54
  76.8 4.6 %norm_back.1 = (f32[8,16,1536]{2,1,0:T(8,128)S(1)}, f32[32,1536]{1,0:T(8,128)S(1)}, f32[32,1536]{1,0:T(8,128)S(1)}, bf16[3,16,1536]{2,1,0:T(8,128)(2,1)S(1)}, bf...) custom-call(bf16[128,1536]{1,0:T(8,128)(2,1)S(1)} %get-tuple-element.83.refs_0_, ...), custom_call_target="tpu_custom_call" | custom-call | flops 1 | bytes 1 | tf_op jit(solution)/shard_map/norm_back/pallas_call | solution.py:402
  81.5 0.5 collective-permute-start.30
  82.2 1.5 %collective-permute-start.31 = (bf16[8,3,1536]{2,1,0:T(4,128)(2,1)S(1)}, bf16[8,3,1536]{2,1,0:T(4,128)(2,1)S(1)}, u32[]{:S(2)}, u32[]{:S(2)}) collective-permute-start(bf16[8,3,1536]{2,1,0:T(4,128)(2,1)S(1)} %get-tuple-element.108), channel_id=1, source_target_pairs={{0,8},{8,0},{16,24},{24,16},{1,9},{9,1},{17,25},{25,17},{2,10},{10... | collective-permute-start | bytes 221192 | tf_op jit(solution)/shard_map/ppermute | solution.py:74
  83.8 0.5 collective-permute-start.27
  84.3 1.3 %collective-permute-start.28 = (f32[8,1536]{1,0:T(8,128)S(1)}, f32[8,1536]{1,0:T(8,128)S(1)}, u32[]{:S(2)}, u32[]{:S(2)}) collective-permute-start(f32[8,1536]{1,0:T(8,128)S(1)} %get-tuple-element.104), channel_id=1, source_target_pairs={{0,8},{8,0},{1,9},{9,1},{2,10},{10,2},{3,11},{11,3},{4,12},{12,4},... | collective-permute-start | bytes 147464 | tf_op jit(solution)/shard_map/ppermute | solution.py:49
  85.6 1.7 %collective-permute-start.29 = (f32[8,1536]{1,0:T(8,128)S(1)}, f32[8,1536]{1,0:T(8,128)S(1)}, u32[]{:S(2)}, u32[]{:S(2)}) collective-permute-start(f32[8,1536]{1,0:T(8,128)S(1)} %get-tuple-element.105), channel_id=1, source_target_pairs={{0,9},{1,8},{2,11},{3,10},{4,13},{5,12},{6,15},{7,14},{8,1},{9,0},... | collective-permute-start | bytes 147464 | tf_op jit(solution)/shard_map/ppermute | solution.py:49
  87.3 0.8 collective-permute-done.31.refs_1_
  88.2 1.2 %collective-permute-start.33 = (bf16[32,1536]{1,0:T(8,128)(2,1)S(1)}, bf16[32,1536]{1,0:T(8,128)(2,1)S(1)}, u32[]{:S(2)}, u32[]{:S(2)}) collective-permute-start(bf16[32,1536]{1,0:T(8,128)(2,1)S(1)} %get-tuple-element.110), channel_id=1, source_target_pairs={{8,0},{0,8},{9,1},{1,9},{10,2},{2,10},{11,3},{3,11},{12,4},{4,12},... | collective-permute-start | bytes 294920 | tf_op jit(solution)/shard_map/ppermute | solution.py:54
  89.3 3.1 %conv_back.2.refs_5_ = bf16[8,16,1536]{2,1,0:T(8,128)(2,1)} custom-call(f32[8,16,1536]{2,1,0:T(8,128)S(1)} %get-tuple-element.106.own, bf16[3,16,1536]{2,1,0:T(8,128)(2,1)S(1)} %collective-permute-done.30.refs_0_, bf16[8,3,1536]{2,1,0:T(4,128)(2,1)S(1)} %collective-permute-done.31.refs_1_, bf16[3,3,1536]{2,1,0:T(4,128)(2,1)S(1)} %collective-permute-done.32.refs_2_, ...), custom_call_target="tpu_custom_call" | custom-call | flops 1 | bytes 1 | tf_op jit(solution)/shard_map/conv_back/pallas_call | solution.py:439
  92.5 0.3 collective-permute-done.33.refs_4_
  92.8 2.2 %collective-permute-start.35 = (bf16[8,1536]{1,0:T(8,128)(2,1)S(1)}, bf16[8,1536]{1,0:T(8,128)(2,1)S(1)}, u32[]{:S(2)}, u32[]{:S(2)}) collective-permute-start(bf16[8,1536]{1,0:T(8,128)(2,1)S(1)} %add_add_fusion.1), channel_id=1, source_target_pairs={{0,4},{1,5},{2,6},{3,7},{4,0},{5,1},{6,2},{7,3},{8,12},{9,13},{10,... | collective-permute-start | bytes 73736 | tf_op jit(solution)/shard_map/ppermute | solution.py:49
  95.0 0.8 collective-permute-start.34
  95.8 1.4 %collective-permute-start.36 = (bf16[8,1536]{1,0:T(8,128)(2,1)S(1)}, bf16[8,1536]{1,0:T(8,128)(2,1)S(1)}, u32[]{:S(2)}, u32[]{:S(2)}) collective-permute-start(bf16[8,1536]{1,0:T(8,128)(2,1)S(1)} %add_add_fusion.1), channel_id=1, source_target_pairs={{0,6},{1,7},{2,4},{3,5},{4,2},{5,3},{6,0},{7,1},{8,14},{9,15},{10,... | collective-permute-start | bytes 73736 | tf_op jit(solution)/shard_map/ppermute | solution.py:49
  97.2 0.5 collective-permute-start.19
  97.7 3.2 %conv_back.3 = bf16[8,16,1536]{2,1,0:T(8,128)(2,1)} custom-call(f32[8,16,1536]{2,1,0:T(8,128)S(1)} %get-tuple-element.106.own, bf16[3,16,1536]{2,1,0:T(8,128)(2,1)S(1)} %collective-permute-done.30.refs_0_, bf16[8,3,1536]{2,1,0:T(4,128)(2,1)S(1)} %collective-permute-done.31.refs_1_, ...), custom_call_target="tpu_custom_call", output_to_operand_aliasing={{}: (6, {})} | custom-call | flops 1 | bytes 1 | tf_op jit(solution)/shard_map/conv_back/pallas_call | solution.py:439
  100.9 0.5 collective-permute-done.36
  101.4 0.9 collective-permute-start.39
  102.3 1.1 %collective-permute-start.38 = (f32[8,1536]{1,0:T(8,128)S(1)}, f32[8,1536]{1,0:T(8,128)S(1)}, u32[]{:S(2)}, u32[]{:S(2)}) collective-permute-start(f32[8,1536]{1,0:T(8,128)S(1)} %add_add_fusion.refs_0_), channel_id=1, source_target_pairs={{0,8},{8,0},{1,9},{9,1},{2,10},{10,2},{3,11},{11,3},{4,12},{12,4},... | collective-permute-start | bytes 147464 | tf_op jit(solution)/shard_map/ppermute | solution.py:49
  103.4 1.6 %collective-permute-start.37 = (f32[8,1536]{1,0:T(8,128)S(1)}, f32[8,1536]{1,0:T(8,128)S(1)}, u32[]{:S(2)}, u32[]{:S(2)}) collective-permute-start(f32[8,1536]{1,0:T(8,128)S(1)} %add_add_fusion.refs_0_), channel_id=1, source_target_pairs={{0,1},{1,0},{2,3},{3,2},{4,5},{5,4},{6,7},{7,6},{8,9},{9,8},{10,11... | collective-permute-start | bytes 147464 | tf_op jit(solution)/shard_map/ppermute | solution.py:49
  105.0 1.5 %collective-permute-done.39.refs_3_ = f32[8,1536]{1,0:T(8,128)S(1)} collective-permute-done((f32[8,1536]{1,0:T(8,128)S(1)}, f32[8,1536]{1,0:T(8,128)S(1)}, u32[]{:S(2)}, u32[]{:S(2)}) %collective-permute-start.39) | collective-permute-done | bytes 49184 | tf_op jit(solution)/shard_map/ppermute | solution.py:49
  106.5 0.5 collective-permute-start.42
  107.0 0.5 collective-permute-done.37.refs_1_
  107.5 1.0 output_part.1
  108.7 0.9 finish.1
  (67 shorter events, 1.5 us)
Async XLA Ops:
  0.6 1.3 %copy-start = (bf16[192,3072]{1,0:T(8,128)(2,1)S(1)}, bf16[192,3072]{1,0:T(8,128)(2,1)}, u32[]{:S(2)}) copy-start(bf16[192,3072]{1,0:T(8,128)(2,1)} %param.18) | copy-start | bytes 3538948
  1.9 5.2 %copy-start.3 = (bf16[1,8,16,1536]{3,2,1,0:T(8,128)(2,1)S(1)}, bf16[1,8,16,1536]{3,2,1,0:T(8,128)(2,1)}, u32[]{:S(2)}) copy-start(bf16[1,8,16,1536]{3,2,1,0:T(8,128)(2,1)} %param.12) | copy-start | bytes 1179652
  1.9 21.1 %copy-start.1 = (bf16[1,8,16,1536]{3,2,1,0:T(8,128)(2,1)S(1)}, bf16[1,8,16,1536]{3,2,1,0:T(8,128)(2,1)}, u32[]{:S(2)}) copy-start(bf16[1,8,16,1536]{3,2,1,0:T(8,128)(2,1)} %param.23) | copy-start | bytes 1179652
  2.0 22.6 %copy-start.2 = (f32[7,7,1536]{2,1,0:T(8,128)S(1)}, f32[7,7,1536]{2,1,0:T(8,128)}, u32[]{:S(2)}) copy-start(f32[7,7,1536]{2,1,0:T(8,128)} %refs_3_.5) | copy-start | bytes 903172
  3.1 16.4 %collective-permute-start.1 = (bf16[384,768]{1,0:T(8,128)(2,1)S(1)}, bf16[384,768]{1,0:T(8,128)(2,1)S(1)}, u32[]{:S(2)}, u32[]{:S(2)}) collective-permute-start(bf16[384,768]{1,0:T(8,128)(2,1)S(1)} %pad_maximum_fusion.refs_0_), channel_id=1, source_target_pairs={{2,0},{4,2},{6,4},{7,6},{5,7},{3,5},{1,3},{0,1},{10,8},{12,10},{14... | collective-permute-start | bytes 1769480 | tf_op jit(solution)/shard_map/ppermute | solution.py:114
  6.1 14.9 %collective-permute-start = (bf16[384,768]{1,0:T(8,128)(2,1)S(1)}, bf16[384,768]{1,0:T(8,128)(2,1)}, u32[]{:S(2)}, u32[]{:S(2)}) collective-permute-start(bf16[384,768]{1,0:T(8,128)(2,1)S(1)} %pad_maximum_fusion.refs_0_), channel_id=1, source_target_pairs={{0,2},{2,4},{4,6},{6,7},{7,5},{5,3},{3,1},{1,0},{8,10},{10,12},{12... | collective-permute-start | bytes 1769480 | tf_op jit(solution)/shard_map/ppermute | solution.py:113
  7.1 38.4 %copy-start.7 = (f32[1536]{0:T(1024)S(1)}, f32[1536]{0:T(1024)}, u32[]{:S(2)}) copy-start(f32[1536]{0:T(1024)} %scale.3) | copy-start | bytes 18436
  7.7 5.9 %collective-permute-start.2 = (bf16[3,16,1536]{2,1,0:T(8,128)(2,1)S(1)}, bf16[3,16,1536]{2,1,0:T(8,128)(2,1)S(1)}, u32[]{:S(2)}, u32[]{:S(2)}) collective-permute-start(bf16[3,16,1536]{2,1,0:T(8,128)(2,1)S(1)} %get-tuple-element.63), channel_id=1, source_target_pairs={{0,16},{8,24},{16,0},{24,8},{1,17},{9,25},{17,1},{25,9},{2,18},{10... | collective-permute-start | bytes 442376 | tf_op jit(solution)/shard_map/ppermute | solution.py:74
  7.8 5.8 %collective-permute-start.3 = (bf16[8,3,1536]{2,1,0:T(4,128)(2,1)S(1)}, bf16[8,3,1536]{2,1,0:T(4,128)(2,1)S(1)}, u32[]{:S(2)}, u32[]{:S(2)}) collective-permute-start(bf16[8,3,1536]{2,1,0:T(4,128)(2,1)S(1)} %get-tuple-element.64), channel_id=1, source_target_pairs={{0,8},{8,0},{16,24},{24,16},{1,9},{9,1},{17,25},{25,17},{2,10},{10... | collective-permute-start | bytes 221192 | tf_op jit(solution)/shard_map/ppermute | solution.py:74
  9.7 3.9 %collective-permute-start.4 = (bf16[3,3,1536]{2,1,0:T(4,128)(2,1)S(1)}, bf16[3,3,1536]{2,1,0:T(4,128)(2,1)S(1)}, u32[]{:S(2)}, u32[]{:S(2)}) collective-permute-start(bf16[3,3,1536]{2,1,0:T(4,128)(2,1)S(1)} %get-tuple-element.65), channel_id=1, source_target_pairs={{0,24},{8,16},{16,8},{24,0},{1,25},{9,17},{17,9},{25,1},{2,26},{10... | collective-permute-start | bytes 82952 | tf_op jit(solution)/shard_map/ppermute | solution.py:74
  21.0 14.1 %collective-permute-start.5 = (bf16[384,768]{1,0:T(8,128)(2,1)}, bf16[384,768]{1,0:T(8,128)(2,1)S(1)}, u32[]{:S(2)}, u32[]{:S(2)}) collective-permute-start(bf16[384,768]{1,0:T(8,128)(2,1)} %collective-permute-done.refs_1_), channel_id=1, source_target_pairs={{0,2},{2,4},{4,6},{6,7},{7,5},{5,3},{3,1},{1,0},{8,10},{10,12},{12... | collective-permute-start | bytes 1769480 | tf_op jit(solution)/shard_map/ppermute | solution.py:113
  21.4 13.9 %collective-permute-start.6 = (bf16[384,768]{1,0:T(8,128)(2,1)S(1)}, bf16[384,768]{1,0:T(8,128)(2,1)S(1)}, u32[]{:S(2)}, u32[]{:S(2)}) collective-permute-start(bf16[384,768]{1,0:T(8,128)(2,1)S(1)} %collective-permute-done.1.refs_2_), channel_id=1, source_target_pairs={{2,0},{4,2},{6,4},{7,6},{5,7},{3,5},{1,3},{0,1},{10,8},{12,10},{14... | collective-permute-start | bytes 1769480 | tf_op jit(solution)/shard_map/ppermute | solution.py:114
  23.0 15.7 %collective-permute-start.10 = (bf16[128,1536]{1,0:T(8,128)(2,1)S(1)}, bf16[128,1536]{1,0:T(8,128)(2,1)S(1)}, u32[]{:S(2)}, u32[]{:S(2)}) collective-permute-start(bf16[128,1536]{1,0:T(8,128)(2,1)S(1)} %bitcast.8), channel_id=1, source_target_pairs={{8,0},{0,8},{9,1},{1,9},{10,2},{2,10},{11,3},{3,11},{12,4},{4,12},... | collective-permute-start | bytes 1179656 | tf_op jit(solution)/shard_map/ppermute | solution.py:54
  24.5 14.3 %collective-permute-start.9 = (bf16[128,1536]{1,0:T(8,128)(2,1)S(1)}, bf16[128,1536]{1,0:T(8,128)(2,1)S(1)}, u32[]{:S(2)}, u32[]{:S(2)}) collective-permute-start(bf16[128,1536]{1,0:T(8,128)(2,1)S(1)} %bitcast.9), channel_id=1, source_target_pairs={{16,0},{0,16},{17,1},{1,17},{18,2},{2,18},{19,3},{3,19},{20,4},{4,... | collective-permute-start | bytes 1179656 | tf_op jit(solution)/shard_map/ppermute | solution.py:54
  24.5 0.7 copy-start.5
  25.2 0.7 copy-start.9
  25.9 0.7 copy-start.10
  35.3 13.0 %collective-permute-start.7 = (bf16[384,768]{1,0:T(8,128)(2,1)S(1)}, bf16[384,768]{1,0:T(8,128)(2,1)S(1)}, u32[]{:S(2)}, u32[]{:S(2)}) collective-permute-start(bf16[384,768]{1,0:T(8,128)(2,1)S(1)} %collective-permute-done.5.refs_3_), channel_id=1, source_target_pairs={{0,2},{2,4},{4,6},{6,7},{7,5},{5,3},{3,1},{1,0},{8,10},{10,12},{12... | collective-permute-start | bytes 1769480 | tf_op jit(solution)/shard_map/ppermute | solution.py:113
  36.8 12.6 %collective-permute-start.8 = (bf16[384,768]{1,0:T(8,128)(2,1)S(1)}, bf16[384,768]{1,0:T(8,128)(2,1)S(1)}, u32[]{:S(2)}, u32[]{:S(2)}) collective-permute-start(bf16[384,768]{1,0:T(8,128)(2,1)S(1)} %collective-permute-done.6.refs_4_), channel_id=1, source_target_pairs={{2,0},{4,2},{6,4},{7,6},{5,7},{3,5},{1,3},{0,1},{10,8},{12,10},{14... | collective-permute-start | bytes 1769480 | tf_op jit(solution)/shard_map/ppermute | solution.py:114
  37.3 8.2 %collective-permute-start.15 = (bf16[128,1536]{1,0:T(8,128)(2,1)S(1)}, bf16[128,1536]{1,0:T(8,128)(2,1)S(1)}, u32[]{:S(2)}, u32[]{:S(2)}) collective-permute-start(bf16[128,1536]{1,0:T(8,128)(2,1)S(1)} %get-tuple-element.68.refs_9_), channel_id=1, source_target_pairs={{8,0},{0,8},{9,1},{1,9},{10,2},{2,10},{11,3},{3,11},{12,4},{4,12},... | collective-permute-start | bytes 1179656 | tf_op jit(solution)/shard_map/ppermute | solution.py:54
  38.8 6.8 %collective-permute-start.14 = (bf16[128,1536]{1,0:T(8,128)(2,1)S(1)}, bf16[128,1536]{1,0:T(8,128)(2,1)S(1)}, u32[]{:S(2)}, u32[]{:S(2)}) collective-permute-start(bf16[128,1536]{1,0:T(8,128)(2,1)S(1)} %get-tuple-element.68.refs_9_), channel_id=1, source_target_pairs={{16,0},{0,16},{17,1},{1,17},{18,2},{2,18},{19,3},{3,19},{20,4},{4,... | collective-permute-start | bytes 1179656 | tf_op jit(solution)/shard_map/ppermute | solution.py:54
  38.8 6.8 %collective-permute-start.11 = (bf16[128,1536]{1,0:T(8,128)(2,1)S(1)}, bf16[128,1536]{1,0:T(8,128)(2,1)S(1)}, u32[]{:S(2)}, u32[]{:S(2)}) collective-permute-start(bf16[128,1536]{1,0:T(8,128)(2,1)S(1)} %collective-permute-done.10.refs_2_.refs_15_), channel_id=1, source_target_pairs={{16,0},{0,16},{17,1},{1,17},{18,2},{2,18},{19,3},{3,19},{20,4},{4,... | collective-permute-start | bytes 1179656 | tf_op jit(solution)/shard_map/ppermute | solution.py:54
  45.6 5.9 %collective-permute-start.16 = (bf16[128,1536]{1,0:T(8,128)(2,1)S(1)}, bf16[128,1536]{1,0:T(8,128)(2,1)S(1)}, u32[]{:S(2)}, u32[]{:S(2)}) collective-permute-start(bf16[128,1536]{1,0:T(8,128)(2,1)S(1)} %collective-permute-done.15.refs_9_), channel_id=1, source_target_pairs={{16,0},{0,16},{17,1},{1,17},{18,2},{2,18},{19,3},{3,19},{20,4},{4,... | collective-permute-start | bytes 1179656 | tf_op jit(solution)/shard_map/ppermute | solution.py:54
  45.9 11.9 %copy-start.4 = (f32[3072]{0:T(1024)S(1)}, f32[3072]{0:T(1024)}, u32[]{:S(2)}) copy-start(f32[3072]{0:T(1024)} %refs_17_.1) | copy-start | bytes 36868
  49.4 6.8 %collective-permute-start.12 = (bf16[192,768]{1,0:T(8,128)(2,1)S(1)}, bf16[192,768]{1,0:T(8,128)(2,1)S(1)}, u32[]{:S(2)}, u32[]{:S(2)}) collective-permute-start(bf16[192,768]{1,0:T(8,128)(2,1)S(1)} %slice.8), channel_id=1, source_target_pairs={{0,2},{2,4},{4,6},{6,7},{7,5},{5,3},{3,1},{1,0},{8,10},{10,12},{12... | collective-permute-start | bytes 884744 | tf_op jit(solution)/shard_map/ppermute | solution.py:123
  51.0 6.7 %collective-permute-start.13 = (bf16[192,768]{1,0:T(8,128)(2,1)S(1)}, bf16[192,768]{1,0:T(8,128)(2,1)S(1)}, u32[]{:S(2)}, u32[]{:S(2)}) collective-permute-start(bf16[192,768]{1,0:T(8,128)(2,1)S(1)} %slice.9), channel_id=1, source_target_pairs={{2,0},{4,2},{6,4},{7,6},{5,7},{3,5},{1,3},{0,1},{10,8},{12,10},{14... | collective-permute-start | bytes 884744 | tf_op jit(solution)/shard_map/ppermute | solution.py:123
  62.2 3.5 %copy-start.8 = (f32[1536]{0:T(1024)S(1)}, f32[1536]{0:T(1024)}, u32[]{:S(2)}) copy-start(f32[1536]{0:T(1024)} %bias.1) | copy-start | bytes 18436
  62.2 1.8 %collective-permute-start.17 = (bf16[128,1536]{1,0:T(8,128)(2,1)S(1)}, bf16[128,1536]{1,0:T(8,128)(2,1)S(1)}, u32[]{:S(2)}, u32[]{:S(2)}) collective-permute-start(bf16[128,1536]{1,0:T(8,128)(2,1)S(1)} %get-tuple-element.77), channel_id=1, source_target_pairs={{16,0},{0,16},{17,1},{1,17},{18,2},{2,18},{19,3},{3,19},{20,4},{4,... | collective-permute-start | bytes 1179656 | tf_op jit(solution)/shard_map/ppermute | solution.py:54
  64.1 11.2 %collective-permute-start.22 = (bf16[128,1536]{1,0:T(8,128)(2,1)S(1)}, bf16[128,1536]{1,0:T(8,128)(2,1)S(1)}, u32[]{:S(2)}, u32[]{:S(2)}) collective-permute-start(bf16[128,1536]{1,0:T(8,128)(2,1)S(1)} %add_rounded.2), channel_id=1, source_target_pairs={{8,0},{0,8},{9,1},{1,9},{10,2},{2,10},{11,3},{3,11},{12,4},{4,12},... | collective-permute-start | bytes 1179656 | tf_op jit(solution)/shard_map/ppermute | solution.py:54
  65.7 11.2 %copy-start.6 = (f32[1536]{0:T(1024)S(1)}, f32[1536]{0:T(1024)}, u32[]{:S(2)}) copy-start(f32[1536]{0:T(1024)} %refs_6_.3) | copy-start | bytes 18436
  71.7 1.5 %collective-permute-start.23 = (bf16[64,1536]{1,0:T(8,128)(2,1)S(1)}, bf16[64,1536]{1,0:T(8,128)(2,1)S(1)}, u32[]{:S(2)}, u32[]{:S(2)}) collective-permute-start(bf16[64,1536]{1,0:T(8,128)(2,1)S(1)} %get-tuple-element.88), channel_id=1, source_target_pairs={{16,0},{0,16},{17,1},{1,17},{18,2},{2,18},{19,3},{3,19},{20,4},{4,... | collective-permute-start | bytes 589832 | tf_op jit(solution)/shard_map/ppermute | solution.py:54
  71.7 1.7 %collective-permute-start.24 = (bf16[64,1536]{1,0:T(8,128)(2,1)S(1)}, bf16[64,1536]{1,0:T(8,128)(2,1)S(1)}, u32[]{:S(2)}, u32[]{:S(2)}) collective-permute-start(bf16[64,1536]{1,0:T(8,128)(2,1)S(1)} %get-tuple-element.89), channel_id=1, source_target_pairs={{16,0},{0,16},{17,1},{1,17},{18,2},{2,18},{19,3},{3,19},{20,4},{4,... | collective-permute-start | bytes 589832 | tf_op jit(solution)/shard_map/ppermute | solution.py:54
  72.2 4.6 %collective-permute-start.20 = (bf16[64,1536]{1,0:T(8,128)(2,1)S(1)}, bf16[64,1536]{1,0:T(8,128)(2,1)S(1)}, u32[]{:S(2)}, u32[]{:S(2)}) collective-permute-start(bf16[64,1536]{1,0:T(8,128)(2,1)S(1)} %get-tuple-element.84), channel_id=1, source_target_pairs={{16,0},{0,16},{17,1},{1,17},{18,2},{2,18},{19,3},{3,19},{20,4},{4,... | collective-permute-start | bytes 589832 | tf_op jit(solution)/shard_map/ppermute | solution.py:54
  72.3 4.5 %collective-permute-start.21 = (bf16[64,1536]{1,0:T(8,128)(2,1)S(1)}, bf16[64,1536]{1,0:T(8,128)(2,1)S(1)}, u32[]{:S(2)}, u32[]{:S(2)}) collective-permute-start(bf16[64,1536]{1,0:T(8,128)(2,1)S(1)} %get-tuple-element.85), channel_id=1, source_target_pairs={{16,0},{0,16},{17,1},{1,17},{18,2},{2,18},{19,3},{3,19},{20,4},{4,... | collective-permute-start | bytes 589832 | tf_op jit(solution)/shard_map/ppermute | solution.py:54
  75.3 8.4 %collective-permute-start.26 = (bf16[96,1536]{1,0:T(8,128)(2,1)S(1)}, bf16[96,1536]{1,0:T(8,128)(2,1)S(1)}, u32[]{:S(2)}, u32[]{:S(2)}) collective-permute-start(bf16[96,1536]{1,0:T(8,128)(2,1)S(1)} %get-tuple-element.98), channel_id=1, source_target_pairs={{8,0},{0,8},{9,1},{1,9},{10,2},{2,10},{11,3},{3,11},{12,4},{4,12},... | collective-permute-start | bytes 884744 | tf_op jit(solution)/shard_map/ppermute | solution.py:54
  81.4 2.3 %collective-permute-start.25 = (f32[32,1536]{1,0:T(8,128)S(1)}, f32[32,1536]{1,0:T(8,128)S(1)}, u32[]{:S(2)}, u32[]{:S(2)}) collective-permute-start(f32[32,1536]{1,0:T(8,128)S(1)} %get-tuple-element.97), channel_id=1, source_target_pairs={{0,16},{16,0},{1,17},{17,1},{2,18},{18,2},{3,19},{19,3},{4,20},{20... | collective-permute-start | bytes 589832 | tf_op jit(solution)/shard_map/ppermute | solution.py:49
  81.5 7.8 %collective-permute-start.30 = (bf16[3,16,1536]{2,1,0:T(8,128)(2,1)S(1)}, bf16[3,16,1536]{2,1,0:T(8,128)(2,1)S(1)}, u32[]{:S(2)}, u32[]{:S(2)}) collective-permute-start(bf16[3,16,1536]{2,1,0:T(8,128)(2,1)S(1)} %get-tuple-element.107), channel_id=1, source_target_pairs={{0,16},{8,24},{16,0},{24,8},{1,17},{9,25},{17,1},{25,9},{2,18},{10... | collective-permute-start | bytes 442376 | tf_op jit(solution)/shard_map/ppermute | solution.py:74
  82.0 3.6 %collective-permute-start.32 = (bf16[3,3,1536]{2,1,0:T(4,128)(2,1)S(1)}, bf16[3,3,1536]{2,1,0:T(4,128)(2,1)S(1)}, u32[]{:S(2)}, u32[]{:S(2)}) collective-permute-start(bf16[3,3,1536]{2,1,0:T(4,128)(2,1)S(1)} %get-tuple-element.109), channel_id=1, source_target_pairs={{0,24},{8,16},{16,8},{24,0},{1,25},{9,17},{17,9},{25,1},{2,26},{10... | collective-permute-start | bytes 82952 | tf_op jit(solution)/shard_map/ppermute | solution.py:74
  82.2 5.9 %collective-permute-start.31 = (bf16[8,3,1536]{2,1,0:T(4,128)(2,1)S(1)}, bf16[8,3,1536]{2,1,0:T(4,128)(2,1)S(1)}, u32[]{:S(2)}, u32[]{:S(2)}) collective-permute-start(bf16[8,3,1536]{2,1,0:T(4,128)(2,1)S(1)} %get-tuple-element.108), channel_id=1, source_target_pairs={{0,8},{8,0},{16,24},{24,16},{1,9},{9,1},{17,25},{25,17},{2,10},{10... | collective-permute-start | bytes 221192 | tf_op jit(solution)/shard_map/ppermute | solution.py:74
  83.8 8.7 %collective-permute-start.27 = (f32[8,1536]{1,0:T(8,128)S(1)}, f32[8,1536]{1,0:T(8,128)S(1)}, u32[]{:S(2)}, u32[]{:S(2)}) collective-permute-start(f32[8,1536]{1,0:T(8,128)S(1)} %get-tuple-element.103), channel_id=1, source_target_pairs={{0,1},{1,0},{2,3},{3,2},{4,5},{5,4},{6,7},{7,6},{8,9},{9,8},{10,11... | collective-permute-start | bytes 147464 | tf_op jit(solution)/shard_map/ppermute | solution.py:49
  84.3 8.2 %collective-permute-start.28 = (f32[8,1536]{1,0:T(8,128)S(1)}, f32[8,1536]{1,0:T(8,128)S(1)}, u32[]{:S(2)}, u32[]{:S(2)}) collective-permute-start(f32[8,1536]{1,0:T(8,128)S(1)} %get-tuple-element.104), channel_id=1, source_target_pairs={{0,8},{8,0},{1,9},{9,1},{2,10},{10,2},{3,11},{11,3},{4,12},{12,4},... | collective-permute-start | bytes 147464 | tf_op jit(solution)/shard_map/ppermute | solution.py:49
  85.6 6.9 %collective-permute-start.29 = (f32[8,1536]{1,0:T(8,128)S(1)}, f32[8,1536]{1,0:T(8,128)S(1)}, u32[]{:S(2)}, u32[]{:S(2)}) collective-permute-start(f32[8,1536]{1,0:T(8,128)S(1)} %get-tuple-element.105), channel_id=1, source_target_pairs={{0,9},{1,8},{2,11},{3,10},{4,13},{5,12},{6,15},{7,14},{8,1},{9,0},... | collective-permute-start | bytes 147464 | tf_op jit(solution)/shard_map/ppermute | solution.py:49
  88.2 4.6 %collective-permute-start.33 = (bf16[32,1536]{1,0:T(8,128)(2,1)S(1)}, bf16[32,1536]{1,0:T(8,128)(2,1)S(1)}, u32[]{:S(2)}, u32[]{:S(2)}) collective-permute-start(bf16[32,1536]{1,0:T(8,128)(2,1)S(1)} %get-tuple-element.110), channel_id=1, source_target_pairs={{8,0},{0,8},{9,1},{1,9},{10,2},{2,10},{11,3},{3,11},{12,4},{4,12},... | collective-permute-start | bytes 294920 | tf_op jit(solution)/shard_map/ppermute | solution.py:54
  92.8 8.1 %collective-permute-start.35 = (bf16[8,1536]{1,0:T(8,128)(2,1)S(1)}, bf16[8,1536]{1,0:T(8,128)(2,1)S(1)}, u32[]{:S(2)}, u32[]{:S(2)}) collective-permute-start(bf16[8,1536]{1,0:T(8,128)(2,1)S(1)} %add_add_fusion.1), channel_id=1, source_target_pairs={{0,4},{1,5},{2,6},{3,7},{4,0},{5,1},{6,2},{7,3},{8,12},{9,13},{10,... | collective-permute-start | bytes 73736 | tf_op jit(solution)/shard_map/ppermute | solution.py:49
  95.0 5.8 %collective-permute-start.34 = (bf16[8,1536]{1,0:T(8,128)(2,1)S(1)}, bf16[8,1536]{1,0:T(8,128)(2,1)S(1)}, u32[]{:S(2)}, u32[]{:S(2)}) collective-permute-start(bf16[8,1536]{1,0:T(8,128)(2,1)S(1)} %add_add_fusion.1), channel_id=1, source_target_pairs={{0,2},{1,3},{2,0},{3,1},{4,6},{5,7},{6,4},{7,5},{8,10},{9,11},{10,... | collective-permute-start | bytes 73736 | tf_op jit(solution)/shard_map/ppermute | solution.py:49
  95.8 5.6 %collective-permute-start.36 = (bf16[8,1536]{1,0:T(8,128)(2,1)S(1)}, bf16[8,1536]{1,0:T(8,128)(2,1)S(1)}, u32[]{:S(2)}, u32[]{:S(2)}) collective-permute-start(bf16[8,1536]{1,0:T(8,128)(2,1)S(1)} %add_add_fusion.1), channel_id=1, source_target_pairs={{0,6},{1,7},{2,4},{3,5},{4,2},{5,3},{6,0},{7,1},{8,14},{9,15},{10,... | collective-permute-start | bytes 73736 | tf_op jit(solution)/shard_map/ppermute | solution.py:49
  97.2 7.8 %collective-permute-start.18 = (bf16[64,1536]{1,0:T(8,128)(2,1)S(1)}, bf16[64,1536]{1,0:T(8,128)(2,1)S(1)}, u32[]{:S(2)}, u32[]{:S(2)}) collective-permute-start(bf16[64,1536]{1,0:T(8,128)(2,1)S(1)} %get-tuple-element.81), channel_id=1, source_target_pairs={{16,0},{0,16},{17,1},{1,17},{18,2},{2,18},{19,3},{3,19},{20,4},{4,... | collective-permute-start | bytes 589832 | tf_op jit(solution)/shard_map/ppermute | solution.py:54
  97.2 10.3 %collective-permute-start.19 = (bf16[64,1536]{1,0:T(8,128)(2,1)S(1)}, bf16[64,1536]{1,0:T(8,128)(2,1)S(1)}, u32[]{:S(2)}, u32[]{:S(2)}) collective-permute-start(bf16[64,1536]{1,0:T(8,128)(2,1)S(1)} %get-tuple-element.82), channel_id=1, source_target_pairs={{16,0},{0,16},{17,1},{1,17},{18,2},{2,18},{19,3},{3,19},{20,4},{4,... | collective-permute-start | bytes 589832 | tf_op jit(solution)/shard_map/ppermute | solution.py:54
  101.4 5.1 %collective-permute-start.39 = (f32[8,1536]{1,0:T(8,128)S(1)}, f32[8,1536]{1,0:T(8,128)S(1)}, u32[]{:S(2)}, u32[]{:S(2)}) collective-permute-start(f32[8,1536]{1,0:T(8,128)S(1)} %add_add_fusion.refs_0_), channel_id=1, source_target_pairs={{0,9},{1,8},{2,11},{3,10},{4,13},{5,12},{6,15},{7,14},{8,1},{9,0},... | collective-permute-start | bytes 147464 | tf_op jit(solution)/shard_map/ppermute | solution.py:49
  102.3 4.2 %collective-permute-start.38 = (f32[8,1536]{1,0:T(8,128)S(1)}, f32[8,1536]{1,0:T(8,128)S(1)}, u32[]{:S(2)}, u32[]{:S(2)}) collective-permute-start(f32[8,1536]{1,0:T(8,128)S(1)} %add_add_fusion.refs_0_), channel_id=1, source_target_pairs={{0,8},{8,0},{1,9},{9,1},{2,10},{10,2},{3,11},{11,3},{4,12},{12,4},... | collective-permute-start | bytes 147464 | tf_op jit(solution)/shard_map/ppermute | solution.py:49
  103.4 4.1 %collective-permute-start.37 = (f32[8,1536]{1,0:T(8,128)S(1)}, f32[8,1536]{1,0:T(8,128)S(1)}, u32[]{:S(2)}, u32[]{:S(2)}) collective-permute-start(f32[8,1536]{1,0:T(8,128)S(1)} %add_add_fusion.refs_0_), channel_id=1, source_target_pairs={{0,1},{1,0},{2,3},{3,2},{4,5},{5,4},{6,7},{7,6},{8,9},{9,8},{10,11... | collective-permute-start | bytes 147464 | tf_op jit(solution)/shard_map/ppermute | solution.py:49
  105.0 3.5 %collective-permute-start.40 = (f32[8,1536]{1,0:T(8,128)S(1)}, f32[8,1536]{1,0:T(8,128)S(1)}, u32[]{:S(2)}, u32[]{:S(2)}) collective-permute-start(f32[8,1536]{1,0:T(8,128)S(1)} %add_add_fusion.refs_0_), channel_id=1, source_target_pairs={{0,16},{16,0},{1,17},{17,1},{2,18},{18,2},{3,19},{19,3},{4,20},{20... | collective-permute-start | bytes 147464 | tf_op jit(solution)/shard_map/ppermute | solution.py:49
  106.5 2.0 %collective-permute-start.43 = (f32[8,1536]{1,0:T(8,128)S(1)}, f32[8,1536]{1,0:T(8,128)S(1)}, u32[]{:S(2)}, u32[]{:S(2)}) collective-permute-start(f32[8,1536]{1,0:T(8,128)S(1)} %collective-permute-done.39.refs_3_), channel_id=1, source_target_pairs={{0,16},{16,0},{1,17},{17,1},{2,18},{18,2},{3,19},{19,3},{4,20},{20... | collective-permute-start | bytes 147464 | tf_op jit(solution)/shard_map/ppermute | solution.py:49
  106.5 2.0 %collective-permute-start.42 = (f32[8,1536]{1,0:T(8,128)S(1)}, f32[8,1536]{1,0:T(8,128)S(1)}, u32[]{:S(2)}, u32[]{:S(2)}) collective-permute-start(f32[8,1536]{1,0:T(8,128)S(1)} %collective-permute-done.38.refs_2_), channel_id=1, source_target_pairs={{0,16},{16,0},{1,17},{17,1},{2,18},{18,2},{3,19},{19,3},{4,20},{20... | collective-permute-start | bytes 147464 | tf_op jit(solution)/shard_map/ppermute | solution.py:49
  107.5 1.2 %collective-permute-start.41 = (f32[8,1536]{1,0:T(8,128)S(1)}, f32[8,1536]{1,0:T(8,128)S(1)}, u32[]{:S(2)}, u32[]{:S(2)}) collective-permute-start(f32[8,1536]{1,0:T(8,128)S(1)} %collective-permute-done.37.refs_1_), channel_id=1, source_target_pairs={{0,16},{16,0},{1,17},{17,1},{2,18},{18,2},{3,19},{19,3},{4,20},{20... | collective-permute-start | bytes 147464 | tf_op jit(solution)/shard_map/ppermute | solution.py:49

commit v5 on v4

--- a/solution.py
+++ b/solution.py
@@ -12,6 +12,7 @@
 HALO = 3
 LANES = 128
 SUBLANES = 8
+FIRST_COL = 8
 BF = jnp.bfloat16
 F32 = jnp.float32
 MIB = 1024 * 1024
@@ -148,12 +149,12 @@
     return total
 
 
-def sum_quarters(parts):
-    along_y, along_x = swap(parts[1], fsdp=1), swap(parts[2], sy=1)
-    return (parts[0] + along_y) + (along_x + swap(parts[3], sy=1, fsdp=1))
-
-
-def sum_others(total):
+def sum_quarters(parts, dtype):
+    terms = [parts[0], swap(parts[1], fsdp=1), swap(parts[2], sy=1), swap(parts[3], sy=1, fsdp=1)]
+    return add_pairs(terms, dtype)
+
+
+def sum_others(rounded):
     masks = []
     for axis in ("sx", "sy", "fsdp"):
         bit = 2
@@ -162,14 +163,14 @@
             bit *= 2
     while masks:
         group, masks = masks[:2], masks[2:]
-        rounded = total.astype(BF)
         (axis, bit) = group[0]
-        total = rounded.astype(F32) + swap(rounded, **{axis: bit}).astype(F32)
+        terms = [rounded, swap(rounded, **{axis: bit})]
         if len(group) == 2:
             (other, more) = group[1]
             both = {axis: bit + more} if axis == other else {axis: bit, other: more}
-            total = total + (swap(rounded, **{other: more}).astype(F32) + swap(rounded, **both).astype(F32))
-    return total
+            terms += [swap(rounded, **{other: more}), swap(rounded, **both)]
+        rounded = add_pairs(terms, BF if masks else F32)
+    return rounded
 
 
 def spread_quarter(total):
@@ -205,11 +206,12 @@
 
 def fill_padded(own, refs, padded, lanes=slice(None)):
     rows, cols = own.shape[:2]
-    at = {-1: 0, None: HALO}
+    row_at = {-1: 0, None: HALO, 1: HALO + rows}
+    col_at = {-1: FIRST_COL - HALO, None: FIRST_COL, 1: FIRST_COL + cols}
     sx, sy = lax.axis_index("sx"), lax.axis_index("sy")
     there = {("sx", -1): sx > 0, ("sx", 1): sx < lax.axis_size("sx") - 1}
     there |= {("sy", -1): sy > 0, ("sy", 1): sy < lax.axis_size("sy") - 1}
-    padded[pl.ds(HALO, rows), pl.ds(HALO, cols), :] = own[:, :, lanes].astype(F32)
+    padded[pl.ds(HALO, rows), pl.ds(FIRST_COL, cols), :] = own[:, :, lanes].astype(F32)
     for (a, b), ref in zip(edge_keys(), refs, strict=True):
         value = ref[:, :, lanes].astype(F32)
         for i in (-1, 1) if a == 0 else (a,):
@@ -219,9 +221,7 @@
                     on = on * there["sx", i].astype(F32)
                 if j is not None:
                     on = on * there["sy", j].astype(F32)
-                first_row = HALO + rows if i == 1 else at[i]
-                first_col = HALO + cols if j == 1 else at[j]
-                spot = (pl.ds(first_row, ref.shape[0]), pl.ds(first_col, ref.shape[1]))
+                spot = (pl.ds(row_at[i], ref.shape[0]), pl.ds(col_at[j], ref.shape[1]))
                 padded[spot[0], spot[1], :] = value * on
 
 
@@ -265,7 +265,7 @@
                 taps.append(weights[at, :, lanes])
             for p in range(rows + 2 * HALO):
                 for k in parts:
-                    piece = padded[p, pl.ds(j + k * SUBLANES, SUBLANES), lanes]
+                    piece = padded[p, pl.ds(FIRST_COL - HALO + j + k * SUBLANES, SUBLANES), lanes]
                     for i in range(KW):
                         if 0 <= p - i < rows:
                             acc[p - i][k] = acc[p - i][k] + taps[i] * piece
@@ -287,9 +287,11 @@
 def conv_norm_kernel(own, *refs):
     count = len(edge_keys())
     edges, refs = refs[:count], refs[count:]
-    weights, bias, gain, shift_, padded, normed, rstd, out, wide, conv = refs
+    weights, bias, gain, shift_, padded, normed, rstd, out, wide, conv, sems, *edges_in = refs
     rows, cols, chans = own.shape
-    fill_padded(own, edges, padded)
+    copies = start_copies(list(zip(edges, edges_in, strict=True)), sems, 0)
+    wait_all(copies)
+    fill_padded(own, edges_in, padded)
     spread_taps(weights, wide, slice(None))
 
     def start(lanes, r, k):
@@ -316,17 +318,19 @@
     return pl.pallas_call(
         conv_norm_kernel,
         out_shape=(
-            shaped((rows + 2 * HALO, cols + 8, chans), F32),
+            shaped((rows + 2 * HALO, cols + 16, chans), F32),
             shaped((spots, chans), F32),
             shaped((spots, LANES), F32),
             shaped((spots, chans), BF),
         ),
-        in_specs=vmem(5 + len(edges)),
+        in_specs=vmem(1) + anywhere(len(edges)) + vmem(4),
         out_specs=vmem(4),
         scratch_shapes=[
             pltpu.VMEM((KW * KW, SUBLANES, chans), F32),
             pltpu.VMEM((spots, chans), F32),
-        ],
+            pltpu.SemaphoreType.DMA((len(edges),)),
+        ]
+        + [pltpu.VMEM(edge.shape, BF) for edge in edges],
         compiler_params=params(20),
         cost_estimate=cost(2 * KW * KW * spots * chans, 10 * spots * chans),
         name="conv_norm",
@@ -377,7 +381,7 @@
             acc = [jnp.zeros((SUBLANES, LANES), F32) for _ in range(KW)]
             for p in range(rows + 2 * HALO):
                 for k in parts:
-                    piece = padded[p, pl.ds(j + k * SUBLANES, SUBLANES), lanes]
+                    piece = padded[p, pl.ds(FIRST_COL - HALO + j + k * SUBLANES, SUBLANES), lanes]
                     for i in range(KW):
                         if 0 <= p - i < rows:
                             acc[i] = acc[i] + grads[p - i][k] * piece
@@ -442,7 +446,7 @@
         in_specs=vmem(given) + anywhere(len(extra)),
         out_specs=pl.BlockSpec(memory_space=pl.ANY),
         scratch_shapes=[
-            pltpu.VMEM((rows + 2 * HALO, cols + 8, count), F32),
+            pltpu.VMEM((rows + 2 * HALO, cols + 16, count), F32),
             pltpu.VMEM((KW * KW, SUBLANES, count), F32),
             pltpu.VMEM((rows, cols, count), BF),
             pltpu.SemaphoreType.DMA,
@@ -465,6 +469,11 @@
 def wait_all(copies):
     for copy in copies:
         copy.wait()
+
+
+def copy_all(jobs):
+    for src, dst in jobs:
+        dst[...] = src[...]
 
 
 def block_jobs(pieces, spots, whole):
@@ -549,15 +558,12 @@
 def far_kernel(upper, lower, n_pieces, n_far, *refs):
     pieces, refs = refs[:n_pieces], refs[n_pieces:]
     lns, refs = refs[:n_far], refs[n_far:]
-    d_mlp, bias, act, *far, up, down, ln, d_mlp_in, slope, d_pre, sems = refs
+    d_mlp, bias, act, *far, up, down, ln, slope, d_pre = refs
     count = ln.shape[0]
-    one = start_copies(row_jobs(lns, ln) + block_jobs(pieces, upper, up), sems, 0)
-    here = pl.ds(d_mlp.shape[0] - count, count)
-    two = start_copies([(d_mlp.at[here], d_mlp_in)] + block_jobs(pieces, lower, down), sems, len(one))
-    wait_all(one)
+    copy_all(row_jobs(lns, ln) + block_jobs(pieces, upper, up))
     forward_hidden(ln, up, bias, act, slope)
-    wait_all(two)
-    backward_hidden(d_mlp_in, down, slope, d_pre)
+    copy_all(block_jobs(pieces, lower, down))
+    backward_hidden(d_mlp.at[pl.ds(d_mlp.shape[0] - count, count)], down, slope, d_pre)
     for tile in channel_tiles(up.shape[0]):
         write_pieces(contract_last(d_pre[...], up[tile, :]), tile, far)
 
@@ -566,21 +572,18 @@
     spots, chans = lns[0].shape
     hidden = pieces[0].shape[1]
     count = spots * len(lns)
-    n_copies = len(upper) + len(lower) + len(lns) + 1
     outs = [shaped((count, hidden), BF)] + [shaped((spots, chans), BF)] * len(lns)
     return pl.pallas_call(
         functools.partial(far_kernel, upper, lower, len(pieces), len(lns)),
         out_shape=outs,
-        in_specs=anywhere(len(pieces) + len(lns) + 1) + vmem(1),
+        in_specs=vmem(len(pieces) + len(lns) + 2),
         out_specs=vmem(len(outs)),
         scratch_shapes=[
             pltpu.VMEM((chans, hidden), BF),
             pltpu.VMEM((chans, hidden), BF),
             pltpu.VMEM((count, chans), BF),
-            pltpu.VMEM((count, chans), BF),
             pltpu.VMEM((count, hidden), F32),
             pltpu.VMEM((count, hidden), BF),
-            pltpu.SemaphoreType.DMA((n_copies,)),
         ],
         compiler_params=params(24),
         cost_estimate=cost(6 * count * chans * hidden, 8 * count * chans),
@@ -596,17 +599,13 @@
     bias_up, bias, *refs = refs
     n_out = 2 * n_near - 1
     near, outs, refs = refs[:n_out], refs[n_out : n_out + n_mlp], refs[n_out + n_mlp :]
-    scale_term, up, down, ln, d_mlp_in, act, slope, d_pre, sems = refs
+    scale_term, up, down, ln, act, slope, d_pre = refs
     spots = cots[0].shape[0]
     count = ln.shape[0]
-    one = start_copies(row_jobs(lns, ln) + block_jobs(pieces, upper, up), sems, 0)
-    jobs = [(d_mlp.at[pl.ds(0, count)], d_mlp_in)] + block_jobs(pieces, lower, down)
-    jobs.append((far_act, act.at[pl.ds(count, far_act.shape[0])]))
-    two = start_copies(jobs, sems, len(one))
-    wait_all(one)
+    copy_all(row_jobs(lns, ln) + block_jobs(pieces, upper, up))
     forward_hidden(ln, up, bias_up, act.at[pl.ds(0, count)], slope)
-    wait_all(two)
-    backward_hidden(d_mlp_in, down, slope, d_pre)
+    copy_all(block_jobs(pieces, lower, down) + [(far_act, act.at[pl.ds(count, far_act.shape[0])])])
+    backward_hidden(d_mlp.at[pl.ds(0, count)], down, slope, d_pre)
     for tile in channel_tiles(up.shape[0]):
         write_pieces(contract_last(d_pre[...], up[tile, :]), tile, near)
     for tile in channel_tiles(down.shape[0]):
@@ -627,24 +626,21 @@
     hidden = pieces[0].shape[1]
     n_near, tiles = len(lns), len(cots)
     count = spots * n_near
-    n_copies = len(upper) + len(lower) + n_near + 2
     group = [spots] + [spots // 2] * (2 * n_near - 2)
     groups = group * (1 + tiles // n_near)
     outs = [shaped((rows, chans), BF) for rows in groups] + [shaped((1, chans), F32)]
     return pl.pallas_call(
         functools.partial(rest_kernel, upper, lower, len(pieces), tiles, n_near, len(groups) - len(group)),
         out_shape=outs,
-        in_specs=anywhere(len(pieces) + n_near + 2) + vmem(tiles + 2),
+        in_specs=vmem(len(pieces) + n_near + tiles + 4),
         out_specs=vmem(len(outs)),
         scratch_shapes=[
             pltpu.VMEM((chans, hidden), BF),
             pltpu.VMEM((chans, hidden), BF),
             pltpu.VMEM((count, chans), BF),
-            pltpu.VMEM((count, chans), BF),
             pltpu.VMEM((spots * tiles, hidden), BF),
             pltpu.VMEM((count, hidden), F32),
             pltpu.VMEM((count, hidden), BF),
-            pltpu.SemaphoreType.DMA((n_copies,)),
         ],
         compiler_params=params(32),
         cost_estimate=cost(8 * count * chans * hidden, 10 * count * chans),
@@ -689,6 +685,26 @@
     )(*parts)
 
 
+def add_pairs_kernel(*refs):
+    *terms, out = refs
+    values = [term[...].astype(F32) for term in terms]
+    while len(values) > 1:
+        values = [values[k] + values[k + 1] for k in range(0, len(values), 2)]
+    out[...] = values[0].astype(out.dtype)
+
+
+def add_pairs(terms, dtype):
+    return pl.pallas_call(
+        add_pairs_kernel,
+        out_shape=shaped(terms[0].shape, dtype),
+        in_specs=vmem(len(terms)),
+        out_specs=pl.BlockSpec(memory_space=pltpu.VMEM),
+        compiler_params=params(16),
+        cost_estimate=cost(1, 1),
+        name="add_pairs",
+    )(*terms)
+
+
 def output_kernel(counts, scaled, scale, bias, *refs):
     terms, (out,) = split_refs(refs, counts)
     rows, cols = out.shape[:2]
@@ -715,14 +731,14 @@
     me = 2 * (lax.axis_index("sy") % 2) + lax.axis_index("fsdp") % 2
     for k, part in enumerate(parts):
         here = pl.ds(pl.multiple_of((me ^ k) * rows, rows), rows)
-        part[...] = keep[here, :] + got[here, :]
+        part[...] = (keep[here, :] + got[here, :]).astype(part.dtype)
 
 
 def quarters(keep, got):
     rows, chans = keep.shape
     return pl.pallas_call(
         quarters_kernel,
-        out_shape=[shaped((rows // 4, chans), F32)] * 4,
+        out_shape=[shaped((rows // 4, chans), BF if k else F32) for k in range(4)],
         in_specs=vmem(2),
         out_specs=vmem(4),
         compiler_params=params(16),
@@ -805,21 +821,25 @@
     size = 2 * n_near - 1
     near, *mlp = [reduce_cores_halves(rest[k : k + size]) for k in range(0, len(rest), size)]
     mlp_far = [add_rounded(group, [spots - spots // 4, spots // 4]) for group in mlp[1:]]
-    far, mlp_far = lax.optimization_barrier((far, mlp_far))
-    mlp_far = [[shift(part, "sy", -(t + 1)) for part in term] for t, term in enumerate(mlp_far)]
+    far, mlp_far, mlp_near = lax.optimization_barrier((far, mlp_far, mlp[0]))
+    first_parts = [shift(term[0], "sy", -(t + 1)) for t, term in enumerate(mlp_far)]
     d_conv, keep, send, *edges = norm_back(near + far, normed, rstd, ln_gain, padded, scale_term)
-    send, first_parts = lax.optimization_barrier((swap(send, sx=1), [term[0] for term in mlp_far]))
+    send, first_parts = lax.optimization_barrier((swap(send, sx=1), first_parts))
     parts = quarters(keep, send)
     edges = list(exchange_edges(dict(zip(edge_keys(), edges, strict=True))).values())
-    half = chans // 2 // LANES * LANES
-    grad_input = conv_back(d_conv, edges, dw_kernel, cotangent[0], 0, half, None)
-    second_parts = [term[1] for term in mlp_far]
-    total, grad_input, second_parts = lax.optimization_barrier((sum_quarters(parts), grad_input, second_parts))
+    cut = [0, chans // LANES // 2 * LANES, chans]
+
+    def back(k, before):
+        return conv_back(d_conv, edges, dw_kernel, cotangent[0], cut[k], cut[k + 1] - cut[k], before)
+
+    grad_input = back(0, None)
+    total, grad_input = lax.optimization_barrier((sum_quarters(parts, BF), grad_input))
+    second_parts = [shift(after(term[1], total), "sy", -(t + 1)) for t, term in enumerate(mlp_far)]
+    total = sum_others(total)
+    grad_input = back(1, grad_input)
+    total, grad_input, second_parts = lax.optimization_barrier((total, grad_input, second_parts))
     mlp_far = [list(term) for term in zip(first_parts, second_parts, strict=True)]
-    total = sum_others(total)
-    grad_input = conv_back(d_conv, edges, dw_kernel, cotangent[0], half, chans - half, grad_input)
-    total, grad_input = lax.optimization_barrier((total, grad_input))
-    block_out = output_part(scaled, layer_scale, b_down, mlp[0] + mlp_far)
+    block_out = output_part(scaled, layer_scale, b_down, mlp_near + mlp_far)
     grad_kernel, grad_gain, grad_scale = finish(*spread_quarter(total))
     return (block_out[None], grad_input[None], grad_kernel, grad_gain, grad_scale)
 

time: 110 us -> 111 us (level)
  waiting for transfers between devices: 38.2 us -> 43.3 us
  Pallas kernels: 30 us -> 27.9 us
  starting transfers between devices: 34.9 us -> 32.9 us
    ppermute x16, waiting for transfers between devices: 10.7 us -> 15.2 us  [shift(): return lax.ppermute(a, axis, [((i + k) % n, i) for i in range(n)])]
    ppermute x3, waiting for transfers between devices: 6.61 us -> 3.93 us  [ring_gather(): one = lax.ppermute(one, 'fsdp', forth)]
    ppermute x1, waiting for transfers between devices: 4.69 us -> 7.23 us  [ring_gather(): lax.ppermute(one, 'fsdp', forth)]
    ppermute x14, waiting for transfers between devices: 2.77 us -> 4.5 us  [swap(): return lax.ppermute(a, axes, [(i, i ^ mask) for i in range(total)])]
    pallas_call x1, Pallas kernels: 5.98 us -> 4.67 us  [rest_part(): pl.pallas_call(functools.partial(rest_kernel, upper, lower, len(pieces),...]
  transfers between devices with their start and end apart: 44 -> 44, of which waited for: 20 -> 23; matrix products, arithmetic and copies ran while one was open for 1% -> 1% of each run, Pallas kernels for 22% -> 21%
where the time goes in v5:
time: 111 us; the launch traced here: 110 us
  waiting for transfers between devices  43.3 us (39%)
  starting transfers between devices  32.9 us (30%)
  Pallas kernels  27.9 us (25%)
  local copies, waits for them, and re-layouts  5.44 us (5%)
    ppermute x16, waiting for transfers between devices, shift(): return lax.ppermute(a, axis, [((i + k) % n, i) for i in range(n)])  15.2 us
    ppermute x14, starting transfers between devices, swap(): return lax.ppermute(a, axes, [(i, i ^ mask) for i in range(total)])  11 us
    ppermute x16, starting transfers between devices, shift(): return lax.ppermute(a, axis, [((i + k) % n, i) for i in range(n)])  8.63 us
    ppermute x1, waiting for transfers between devices, ring_gather(): lax.ppermute(one, 'fsdp', forth)  7.23 us
    pallas_call x2, Pallas kernels, conv_back(): pl.pallas_call(functools.partial(conv_back_kernel, begin, count), out_sha...  6.37 us
    ppermute x3, waiting for transfers between devices, ring_gather(): two = lax.ppermute(two, 'fsdp', back)  6.33 us
    pallas_call x1, Pallas kernels, conv_norm(): pl.pallas_call(conv_norm_kernel, out_shape=(shaped((rows + 2 * HALO, cols...  6.05 us
    ppermute x3, starting transfers between devices, ring_gather(): two = lax.ppermute(two, 'fsdp', back)  5.15 us
  transfers between devices with their start and end apart: 44, of which 23 were waited for; matrix products, arithmetic and copies ran while one was open for 1% of the time, Pallas kernels for 21%

profile of v5, /device:TPU:0, one launch (start us, length us, event | category | flops | bytes accessed | tf_op | source)
XLA Modules:
  0.0 110.5 jit_solution(1013391874236815931)
XLA Ops:
  0.7 1.3 %copy-done = bf16[192,3072]{1,0:T(8,128)(2,1)S(1)} copy-done((bf16[192,3072]{1,0:T(8,128)(2,1)S(1)}, bf16[192,3072]{1,0:T(8,128)(2,1)}, u32[]{:S(2)}) %copy-start) | copy-done | bytes 1179672
  2.0 1.1 dynamic-slice_bitcast_fusion
  3.1 3.0 %collective-permute-start.7 = (bf16[384,768]{1,0:T(8,128)(2,1)S(1)}, bf16[384,768]{1,0:T(8,128)(2,1)S(1)}, u32[]{:S(2)}, u32[]{:S(2)}) collective-permute-start(bf16[384,768]{1,0:T(8,128)(2,1)S(1)} %pad_maximum_fusion.refs_0_), channel_id=1, source_target_pairs={{2,0},{4,2},{6,4},{7,6},{5,7},{3,5},{1,3},{0,1},{10,8},{12,10},{14... | collective-permute-start | bytes 1769480 | tf_op jit(solution)/shard_map/ppermute | solution.py:115
  6.2 0.9 copy.18
  7.2 0.5 prepare.1
  7.8 1.9 %collective-permute-start.1 = (bf16[8,3,1536]{2,1,0:T(4,128)(2,1)S(1)}, bf16[8,3,1536]{2,1,0:T(4,128)(2,1)S(1)}, u32[]{:S(2)}, u32[]{:S(2)}) collective-permute-start(bf16[8,3,1536]{2,1,0:T(4,128)(2,1)S(1)} %get-tuple-element.68), channel_id=1, source_target_pairs={{0,8},{8,0},{16,24},{24,16},{1,9},{9,1},{17,25},{25,17},{2,10},{10... | collective-permute-start | bytes 221192 | tf_op jit(solution)/shard_map/ppermute | solution.py:75
  9.8 3.8 %collective-permute-done.2.refs_2_ = bf16[3,3,1536]{2,1,0:T(4,128)(2,1)S(1)} collective-permute-done((bf16[3,3,1536]{2,1,0:T(4,128)(2,1)S(1)}, bf16[3,3,1536]{2,1,0:T(4,128)(2,1)S(1)}, u32[]{:S(2)}, u32[]{:S(2)}) %collective-permute-start.2) | collective-permute-done | bytes 27680 | tf_op jit(solution)/shard_map/ppermute | solution.py:75
  13.6 5.9 %collective-permute-done.7.refs_2_ = bf16[384,768]{1,0:T(8,128)(2,1)S(1)} collective-permute-done((bf16[384,768]{1,0:T(8,128)(2,1)S(1)}, bf16[384,768]{1,0:T(8,128)(2,1)S(1)}, u32[]{:S(2)}, u32[]{:S(2)}) %collective-permute-start.7) | collective-permute-done | bytes 589856 | tf_op jit(solution)/shard_map/ppermute | solution.py:115
  19.5 1.5 %collective-permute-done.6.refs_1_ = bf16[384,768]{1,0:T(8,128)(2,1)} collective-permute-done((bf16[384,768]{1,0:T(8,128)(2,1)S(1)}, bf16[384,768]{1,0:T(8,128)(2,1)}, u32[]{:S(2)}, u32[]{:S(2)}) %collective-permute-start.6) | collective-permute-done | bytes 589856 | tf_op jit(solution)/shard_map/ppermute | solution.py:114
  21.0 0.4 collective-permute-start.8
  21.4 1.6 %collective-permute-start.9 = (bf16[384,768]{1,0:T(8,128)(2,1)S(1)}, bf16[384,768]{1,0:T(8,128)(2,1)S(1)}, u32[]{:S(2)}, u32[]{:S(2)}) collective-permute-start(bf16[384,768]{1,0:T(8,128)(2,1)S(1)} %collective-permute-done.7.refs_2_), channel_id=1, source_target_pairs={{2,0},{4,2},{6,4},{7,6},{5,7},{3,5},{1,3},{0,1},{10,8},{12,10},{14... | collective-permute-start | bytes 1769480 | tf_op jit(solution)/shard_map/ppermute | solution.py:115
  23.0 1.5 %collective-permute-start.4 = (bf16[128,1536]{1,0:T(8,128)(2,1)S(1)}, bf16[128,1536]{1,0:T(8,128)(2,1)S(1)}, u32[]{:S(2)}, u32[]{:S(2)}) collective-permute-start(bf16[128,1536]{1,0:T(8,128)(2,1)S(1)} %bitcast.8), channel_id=1, source_target_pairs={{8,0},{0,8},{9,1},{1,9},{10,2},{2,10},{11,3},{3,11},{12,4},{4,12},... | collective-permute-start | bytes 1179656 | tf_op jit(solution)/shard_map/ppermute | solution.py:55
  24.5 0.7 copy-done.5
  25.2 0.7 copy-done.9
  25.9 0.7 copy-done.10
  26.6 6.0 %conv_norm.1 = (f32[14,32,1536]{2,1,0:T(8,128)S(1)}, f32[128,1536]{1,0:T(8,128)S(1)}, f32[128,128]{1,0:T(8,128)S(1)}, bf16[128,1536]{1,0:T(8,128)(2,1)S(1)}) custom-call(bf16[8,16,1536]{2,1,0:T(8,128)(2,1)S(1)} %get-tuple-element.66.own.scaled, bf16[3,16,1536]{2,1,0:T(8,128)(2,1)S(1)} %collective-permute-done.refs_0_, ...), custom_call_target="tpu_custom_call" | custom-call | flops 1 | bytes 1 | tf_op jit(solution)/shard_map/conv_norm/pallas_call | solution.py:318
  32.7 2.4 %collective-permute-done.8.refs_3_ = bf16[384,768]{1,0:T(8,128)(2,1)S(1)} collective-permute-done((bf16[384,768]{1,0:T(8,128)(2,1)}, bf16[384,768]{1,0:T(8,128)(2,1)S(1)}, u32[]{:S(2)}, u32[]{:S(2)}) %collective-permute-start.8) | collective-permute-done | bytes 589856 | tf_op jit(solution)/shard_map/ppermute | solution.py:114
  35.1 0.2 collective-permute-done.9.refs_4_
  35.3 1.5 %collective-permute-start.10 = (bf16[384,768]{1,0:T(8,128)(2,1)S(1)}, bf16[384,768]{1,0:T(8,128)(2,1)S(1)}, u32[]{:S(2)}, u32[]{:S(2)}) collective-permute-start(bf16[384,768]{1,0:T(8,128)(2,1)S(1)} %collective-permute-done.8.refs_3_), channel_id=1, source_target_pairs={{0,2},{2,4},{4,6},{6,7},{7,5},{5,3},{3,1},{1,0},{8,10},{10,12},{12... | collective-permute-start | bytes 1769480 | tf_op jit(solution)/shard_map/ppermute | solution.py:114
  36.8 0.5 collective-permute-start.11
  37.4 1.4 %collective-permute-start.14 = (bf16[128,1536]{1,0:T(8,128)(2,1)S(1)}, bf16[128,1536]{1,0:T(8,128)(2,1)S(1)}, u32[]{:S(2)}, u32[]{:S(2)}) collective-permute-start(bf16[128,1536]{1,0:T(8,128)(2,1)S(1)} %get-tuple-element.74.refs_9_), channel_id=1, source_target_pairs={{8,0},{0,8},{9,1},{1,9},{10,2},{2,10},{11,3},{3,11},{12,4},{4,12},... | collective-permute-start | bytes 1179656 | tf_op jit(solution)/shard_map/ppermute | solution.py:55
  38.8 0.2 collective-permute-start.5
  39.1 9.8 %collective-permute-done.14.refs_9_ = bf16[128,1536]{1,0:T(8,128)(2,1)S(1)} collective-permute-done((bf16[128,1536]{1,0:T(8,128)(2,1)S(1)}, bf16[128,1536]{1,0:T(8,128)(2,1)S(1)}, u32[]{:S(2)}, u32[]{:S(2)}) %collective-permute-start.14) | collective-permute-done | bytes 393248 | tf_op jit(solution)/shard_map/ppermute | solution.py:55
  48.9 0.3 scale_part.1.refs_11_
  49.2 0.2 collective-permute-done.11.refs_6_
  49.4 1.6 %collective-permute-start.12 = (bf16[192,768]{1,0:T(8,128)(2,1)S(1)}, bf16[192,768]{1,0:T(8,128)(2,1)S(1)}, u32[]{:S(2)}, u32[]{:S(2)}) collective-permute-start(bf16[192,768]{1,0:T(8,128)(2,1)S(1)} %slice.8), channel_id=1, source_target_pairs={{0,2},{2,4},{4,6},{6,7},{7,5},{5,3},{3,1},{1,0},{8,10},{10,12},{12... | collective-permute-start | bytes 884744 | tf_op jit(solution)/shard_map/ppermute | solution.py:124
  51.0 0.5 collective-permute-start.13
  51.5 7.2 %collective-permute-done.12.refs_7_ = bf16[192,768]{1,0:T(8,128)(2,1)S(1)} collective-permute-done((bf16[192,768]{1,0:T(8,128)(2,1)S(1)}, bf16[192,768]{1,0:T(8,128)(2,1)S(1)}, u32[]{:S(2)}, u32[]{:S(2)}) %collective-permute-start.12) | collective-permute-done | bytes 294944 | tf_op jit(solution)/shard_map/ppermute | solution.py:124
  58.7 1.2 %collective-permute-done.13.refs_8_ = bf16[192,768]{1,0:T(8,128)(2,1)S(1)} collective-permute-done((bf16[192,768]{1,0:T(8,128)(2,1)S(1)}, bf16[192,768]{1,0:T(8,128)(2,1)S(1)}, u32[]{:S(2)}, u32[]{:S(2)}) %collective-permute-start.13) | collective-permute-done | bytes 294944 | tf_op jit(solution)/shard_map/ppermute | solution.py:124
  60.0 3.4 %far_part.1 = (bf16[256,768]{1,0:T(8,128)(2,1)S(1)}, bf16[128,1536]{1,0:T(8,128)(2,1)S(1)}, bf16[128,1536]{1,0:T(8,128)(2,1)S(1)}) custom-call(bf16[384,768]{1,0:T(8,128)(2,1)S(1)} %pad_maximum_fusion.refs_0_, bf16[384,768]{1,0:T(8,128)(2,1)} %collective-permute-done.6.refs_1_, bf16[384,768]{1,0:T(8,128)(2,1)S(1)} %collective-permute-done.7.refs_2_, ...), custom_call_target="tpu_custom_call" | custom-call | flops 1 | bytes 1 | tf_op jit(solution)/shard_map/far_part/pallas_call | solution.py:576
  63.4 1.7 %collective-permute-done.17.refs_1_ = bf16[128,1536]{1,0:T(8,128)(2,1)S(1)} collective-permute-done((bf16[128,1536]{1,0:T(8,128)(2,1)S(1)}, bf16[128,1536]{1,0:T(8,128)(2,1)S(1)}, u32[]{:S(2)}, u32[]{:S(2)}) %collective-permute-start.17) | collective-permute-done | bytes 393248 | tf_op jit(solution)/shard_map/ppermute | solution.py:55
  65.3 1.6 %collective-permute-start.18 = (bf16[128,1536]{1,0:T(8,128)(2,1)S(1)}, bf16[128,1536]{1,0:T(8,128)(2,1)S(1)}, u32[]{:S(2)}, u32[]{:S(2)}) collective-permute-start(bf16[128,1536]{1,0:T(8,128)(2,1)S(1)} %add_rounded.2), channel_id=1, source_target_pairs={{8,0},{0,8},{9,1},{1,9},{10,2},{2,10},{11,3},{3,11},{12,4},{4,12},... | collective-permute-start | bytes 1179656 | tf_op jit(solution)/shard_map/ppermute | solution.py:55
  66.8 4.7 %rest_part.1 = (bf16[128,1536]{1,0:T(8,128)(2,1)S(1)}, bf16[64,1536]{1,0:T(8,128)(2,1)S(1)}, bf16[64,1536]{1,0:T(8,128)(2,1)S(1)}, bf16[128,1536]{1,0:T(8,128)(2...) custom-call(bf16[384,768]{1,0:T(8,128)(2,1)S(1)} %pad_maximum_fusion, ...), custom_call_target="tpu_custom_call" | custom-call | flops 1 | bytes 1 | tf_op jit(solution)/shard_map/rest_part/pallas_call | solution.py:632
  71.6 0.5 collective-permute-start.20
  72.1 0.4 collective-permute-start.22
  72.6 0.4 collective-permute-done.19.refs_1_
  73.3 0.2 collective-permute-start.24
  73.6 0.2 collective-permute-done.22.refs_2_
  73.8 2.6 %collective-permute-done.18.refs_3_ = bf16[128,1536]{1,0:T(8,128)(2,1)S(1)} collective-permute-done((bf16[128,1536]{1,0:T(8,128)(2,1)S(1)}, bf16[128,1536]{1,0:T(8,128)(2,1)S(1)}, u32[]{:S(2)}, u32[]{:S(2)}) %collective-permute-start.18) | collective-permute-done | bytes 393248 | tf_op jit(solution)/shard_map/ppermute | solution.py:55
  76.5 1.5 %collective-permute-start.26 = (bf16[96,1536]{1,0:T(8,128)(2,1)S(1)}, bf16[96,1536]{1,0:T(8,128)(2,1)S(1)}, u32[]{:S(2)}, u32[]{:S(2)}) collective-permute-start(bf16[96,1536]{1,0:T(8,128)(2,1)S(1)} %get-tuple-element.105), channel_id=1, source_target_pairs={{8,0},{0,8},{9,1},{1,9},{10,2},{2,10},{11,3},{3,11},{12,4},{4,12},... | collective-permute-start | bytes 884744 | tf_op jit(solution)/shard_map/ppermute | solution.py:55
  78.0 4.5 %norm_back.1 = (f32[8,16,1536]{2,1,0:T(8,128)S(1)}, f32[32,1536]{1,0:T(8,128)S(1)}, f32[32,1536]{1,0:T(8,128)S(1)}, bf16[3,16,1536]{2,1,0:T(8,128)(2,1)S(1)}, bf...) custom-call(bf16[128,1536]{1,0:T(8,128)(2,1)S(1)} %get-tuple-element.96.refs_0_, ...), custom_call_target="tpu_custom_call" | custom-call | flops 1 | bytes 1 | tf_op jit(solution)/shard_map/norm_back/pallas_call | solution.py:406
  82.6 0.5 collective-permute-start.30
  83.1 0.5 collective-permute-start.31
  83.6 0.9 collective-permute-start.32
  84.7 0.6 collective-permute-start.27
  85.3 1.4 %collective-permute-start.28 = (bf16[8,1536]{1,0:T(8,128)(2,1)S(1)}, bf16[8,1536]{1,0:T(8,128)(2,1)S(1)}, u32[]{:S(2)}, u32[]{:S(2)}) collective-permute-start(bf16[8,1536]{1,0:T(8,128)(2,1)S(1)} %get-tuple-element.111), channel_id=1, source_target_pairs={{0,8},{8,0},{1,9},{9,1},{2,10},{10,2},{3,11},{11,3},{4,12},{12,4},... | collective-permute-start | bytes 73736 | tf_op jit(solution)/shard_map/ppermute | solution.py:50
  86.7 1.1 collective-permute-done.32.refs_2_
  87.8 1.0 collective-permute-start.29
  88.8 3.2 %conv_back.2.refs_5_ = bf16[8,16,1536]{2,1,0:T(8,128)(2,1)} custom-call(f32[8,16,1536]{2,1,0:T(8,128)S(1)} %get-tuple-element.113.own, bf16[3,16,1536]{2,1,0:T(8,128)(2,1)S(1)} %collective-permute-done.30.refs_0_, bf16[8,3,1536]{2,1,0:T(4,128)(2,1)S(1)} %collective-permute-done.31.refs_1_, bf16[3,3,1536]{2,1,0:T(4,128)(2,1)S(1)} %collective-permute-done.32.refs_2_, ...), custom_call_target="tpu_custom_call" | custom-call | flops 1 | bytes 1 | tf_op jit(solution)/shard_map/conv_back/pallas_call | solution.py:443
  92.0 0.8 collective-permute-done.29.refs_3_
  92.8 0.9 collective-permute-start.36
  93.7 3.4 %collective-permute-start.35 = (bf16[8,1536]{1,0:T(8,128)(2,1)S(1)}, bf16[8,1536]{1,0:T(8,128)(2,1)S(1)}, u32[]{:S(2)}, u32[]{:S(2)}) collective-permute-start(bf16[8,1536]{1,0:T(8,128)(2,1)S(1)} %add_pairs.2.refs_0_), channel_id=1, source_target_pairs={{0,6},{1,7},{2,4},{3,5},{4,2},{5,3},{6,0},{7,1},{8,14},{9,15},{10,... | collective-permute-start | bytes 73736 | tf_op jit(solution)/shard_map/ppermute | solution.py:50
  97.1 1.0 collective-permute-start.33
  98.1 3.2 %conv_back.3 = bf16[8,16,1536]{2,1,0:T(8,128)(2,1)} custom-call(f32[8,16,1536]{2,1,0:T(8,128)S(1)} %get-tuple-element.113.own, bf16[3,16,1536]{2,1,0:T(8,128)(2,1)S(1)} %collective-permute-done.30.refs_0_, bf16[8,3,1536]{2,1,0:T(4,128)(2,1)S(1)} %collective-permute-done.31.refs_1_, ...), custom_call_target="tpu_custom_call", output_to_operand_aliasing={{}: (6, {})} | custom-call | flops 1 | bytes 1 | tf_op jit(solution)/shard_map/conv_back/pallas_call | solution.py:443
  101.3 0.5 collective-permute-done.34.refs_2_
  101.9 1.5 %collective-permute-start.39 = (f32[8,1536]{1,0:T(8,128)S(1)}, f32[8,1536]{1,0:T(8,128)S(1)}, u32[]{:S(2)}, u32[]{:S(2)}) collective-permute-start(f32[8,1536]{1,0:T(8,128)S(1)} %add_pairs.3.refs_0_), channel_id=1, source_target_pairs={{0,9},{1,8},{2,11},{3,10},{4,13},{5,12},{6,15},{7,14},{8,1},{9,0},... | collective-permute-start | bytes 147464 | tf_op jit(solution)/shard_map/ppermute | solution.py:50
  103.4 0.9 collective-permute-start.38
  104.3 1.1 %collective-permute-start.37 = (f32[8,1536]{1,0:T(8,128)S(1)}, f32[8,1536]{1,0:T(8,128)S(1)}, u32[]{:S(2)}, u32[]{:S(2)}) collective-permute-start(f32[8,1536]{1,0:T(8,128)S(1)} %add_pairs.3.refs_0_), channel_id=1, source_target_pairs={{0,1},{1,0},{2,3},{3,2},{4,5},{5,4},{6,7},{7,6},{8,9},{9,8},{10,11... | collective-permute-start | bytes 147464 | tf_op jit(solution)/shard_map/ppermute | solution.py:50
  105.4 1.5 %collective-permute-done.39.refs_3_ = f32[8,1536]{1,0:T(8,128)S(1)} collective-permute-done((f32[8,1536]{1,0:T(8,128)S(1)}, f32[8,1536]{1,0:T(8,128)S(1)}, u32[]{:S(2)}, u32[]{:S(2)}) %collective-permute-start.39) | collective-permute-done | bytes 49184 | tf_op jit(solution)/shard_map/ppermute | solution.py:50
  106.9 0.5 collective-permute-done.38.refs_2_
  107.4 0.9 collective-permute-done.37.refs_1_
  108.4 1.0 output_part.1
  109.4 0.2 collective-permute-done.41.refs_5_
  109.6 0.9 finish.1
  (67 shorter events, 1.5 us)
Async XLA Ops:
  0.6 1.3 %copy-start = (bf16[192,3072]{1,0:T(8,128)(2,1)S(1)}, bf16[192,3072]{1,0:T(8,128)(2,1)}, u32[]{:S(2)}) copy-start(bf16[192,3072]{1,0:T(8,128)(2,1)} %param.18) | copy-start | bytes 3538948
  1.9 5.2 %copy-start.3 = (bf16[1,8,16,1536]{3,2,1,0:T(8,128)(2,1)S(1)}, bf16[1,8,16,1536]{3,2,1,0:T(8,128)(2,1)}, u32[]{:S(2)}) copy-start(bf16[1,8,16,1536]{3,2,1,0:T(8,128)(2,1)} %param.12) | copy-start | bytes 1179652
  1.9 21.1 %copy-start.1 = (bf16[1,8,16,1536]{3,2,1,0:T(8,128)(2,1)S(1)}, bf16[1,8,16,1536]{3,2,1,0:T(8,128)(2,1)}, u32[]{:S(2)}) copy-start(bf16[1,8,16,1536]{3,2,1,0:T(8,128)(2,1)} %param.23) | copy-start | bytes 1179652
  2.0 22.6 %copy-start.2 = (f32[7,7,1536]{2,1,0:T(8,128)S(1)}, f32[7,7,1536]{2,1,0:T(8,128)}, u32[]{:S(2)}) copy-start(f32[7,7,1536]{2,1,0:T(8,128)} %refs_3_.5) | copy-start | bytes 903172
  3.1 16.4 %collective-permute-start.7 = (bf16[384,768]{1,0:T(8,128)(2,1)S(1)}, bf16[384,768]{1,0:T(8,128)(2,1)S(1)}, u32[]{:S(2)}, u32[]{:S(2)}) collective-permute-start(bf16[384,768]{1,0:T(8,128)(2,1)S(1)} %pad_maximum_fusion.refs_0_), channel_id=1, source_target_pairs={{2,0},{4,2},{6,4},{7,6},{5,7},{3,5},{1,3},{0,1},{10,8},{12,10},{14... | collective-permute-start | bytes 1769480 | tf_op jit(solution)/shard_map/ppermute | solution.py:115
  6.1 14.9 %collective-permute-start.6 = (bf16[384,768]{1,0:T(8,128)(2,1)S(1)}, bf16[384,768]{1,0:T(8,128)(2,1)}, u32[]{:S(2)}, u32[]{:S(2)}) collective-permute-start(bf16[384,768]{1,0:T(8,128)(2,1)S(1)} %pad_maximum_fusion.refs_0_), channel_id=1, source_target_pairs={{0,2},{2,4},{4,6},{6,7},{7,5},{5,3},{3,1},{1,0},{8,10},{10,12},{12... | collective-permute-start | bytes 1769480 | tf_op jit(solution)/shard_map/ppermute | solution.py:114
  7.1 41.7 %copy-start.7 = (f32[1536]{0:T(1024)S(1)}, f32[1536]{0:T(1024)}, u32[]{:S(2)}) copy-start(f32[1536]{0:T(1024)} %scale.3) | copy-start | bytes 18436
  7.7 5.9 %collective-permute-start = (bf16[3,16,1536]{2,1,0:T(8,128)(2,1)S(1)}, bf16[3,16,1536]{2,1,0:T(8,128)(2,1)S(1)}, u32[]{:S(2)}, u32[]{:S(2)}) collective-permute-start(bf16[3,16,1536]{2,1,0:T(8,128)(2,1)S(1)} %get-tuple-element.67), channel_id=1, source_target_pairs={{0,16},{8,24},{16,0},{24,8},{1,17},{9,25},{17,1},{25,9},{2,18},{10... | collective-permute-start | bytes 442376 | tf_op jit(solution)/shard_map/ppermute | solution.py:75
  7.8 5.8 %collective-permute-start.1 = (bf16[8,3,1536]{2,1,0:T(4,128)(2,1)S(1)}, bf16[8,3,1536]{2,1,0:T(4,128)(2,1)S(1)}, u32[]{:S(2)}, u32[]{:S(2)}) collective-permute-start(bf16[8,3,1536]{2,1,0:T(4,128)(2,1)S(1)} %get-tuple-element.68), channel_id=1, source_target_pairs={{0,8},{8,0},{16,24},{24,16},{1,9},{9,1},{17,25},{25,17},{2,10},{10... | collective-permute-start | bytes 221192 | tf_op jit(solution)/shard_map/ppermute | solution.py:75
  9.7 3.9 %collective-permute-start.2 = (bf16[3,3,1536]{2,1,0:T(4,128)(2,1)S(1)}, bf16[3,3,1536]{2,1,0:T(4,128)(2,1)S(1)}, u32[]{:S(2)}, u32[]{:S(2)}) collective-permute-start(bf16[3,3,1536]{2,1,0:T(4,128)(2,1)S(1)} %get-tuple-element.69), channel_id=1, source_target_pairs={{0,24},{8,16},{16,8},{24,0},{1,25},{9,17},{17,9},{25,1},{2,26},{10... | collective-permute-start | bytes 82952 | tf_op jit(solution)/shard_map/ppermute | solution.py:75
  21.0 14.1 %collective-permute-start.8 = (bf16[384,768]{1,0:T(8,128)(2,1)}, bf16[384,768]{1,0:T(8,128)(2,1)S(1)}, u32[]{:S(2)}, u32[]{:S(2)}) collective-permute-start(bf16[384,768]{1,0:T(8,128)(2,1)} %collective-permute-done.6.refs_1_), channel_id=1, source_target_pairs={{0,2},{2,4},{4,6},{6,7},{7,5},{5,3},{3,1},{1,0},{8,10},{10,12},{12... | collective-permute-start | bytes 1769480 | tf_op jit(solution)/shard_map/ppermute | solution.py:114
  21.4 13.9 %collective-permute-start.9 = (bf16[384,768]{1,0:T(8,128)(2,1)S(1)}, bf16[384,768]{1,0:T(8,128)(2,1)S(1)}, u32[]{:S(2)}, u32[]{:S(2)}) collective-permute-start(bf16[384,768]{1,0:T(8,128)(2,1)S(1)} %collective-permute-done.7.refs_2_), channel_id=1, source_target_pairs={{2,0},{4,2},{6,4},{7,6},{5,7},{3,5},{1,3},{0,1},{10,8},{12,10},{14... | collective-permute-start | bytes 1769480 | tf_op jit(solution)/shard_map/ppermute | solution.py:115
  23.0 14.3 %collective-permute-start.4 = (bf16[128,1536]{1,0:T(8,128)(2,1)S(1)}, bf16[128,1536]{1,0:T(8,128)(2,1)S(1)}, u32[]{:S(2)}, u32[]{:S(2)}) collective-permute-start(bf16[128,1536]{1,0:T(8,128)(2,1)S(1)} %bitcast.8), channel_id=1, source_target_pairs={{8,0},{0,8},{9,1},{1,9},{10,2},{2,10},{11,3},{3,11},{12,4},{4,12},... | collective-permute-start | bytes 1179656 | tf_op jit(solution)/shard_map/ppermute | solution.py:55
  24.5 14.3 %collective-permute-start.3 = (bf16[128,1536]{1,0:T(8,128)(2,1)S(1)}, bf16[128,1536]{1,0:T(8,128)(2,1)S(1)}, u32[]{:S(2)}, u32[]{:S(2)}) collective-permute-start(bf16[128,1536]{1,0:T(8,128)(2,1)S(1)} %bitcast.9), channel_id=1, source_target_pairs={{16,0},{0,16},{17,1},{1,17},{18,2},{2,18},{19,3},{3,19},{20,4},{4,... | collective-permute-start | bytes 1179656 | tf_op jit(solution)/shard_map/ppermute | solution.py:55
  24.5 0.7 copy-start.5
  25.2 0.7 copy-start.9
  25.9 0.7 copy-start.10
  35.3 13.9 %collective-permute-start.10 = (bf16[384,768]{1,0:T(8,128)(2,1)S(1)}, bf16[384,768]{1,0:T(8,128)(2,1)S(1)}, u32[]{:S(2)}, u32[]{:S(2)}) collective-permute-start(bf16[384,768]{1,0:T(8,128)(2,1)S(1)} %collective-permute-done.8.refs_3_), channel_id=1, source_target_pairs={{0,2},{2,4},{4,6},{6,7},{7,5},{5,3},{3,1},{1,0},{8,10},{10,12},{12... | collective-permute-start | bytes 1769480 | tf_op jit(solution)/shard_map/ppermute | solution.py:114
  36.8 12.6 %collective-permute-start.11 = (bf16[384,768]{1,0:T(8,128)(2,1)S(1)}, bf16[384,768]{1,0:T(8,128)(2,1)S(1)}, u32[]{:S(2)}, u32[]{:S(2)}) collective-permute-start(bf16[384,768]{1,0:T(8,128)(2,1)S(1)} %collective-permute-done.9.refs_4_), channel_id=1, source_target_pairs={{2,0},{4,2},{6,4},{7,6},{5,7},{3,5},{1,3},{0,1},{10,8},{12,10},{14... | collective-permute-start | bytes 1769480 | tf_op jit(solution)/shard_map/ppermute | solution.py:115
  37.3 1.7 %collective-permute-start.15 = (bf16[128,1536]{1,0:T(8,128)(2,1)S(1)}, bf16[128,1536]{1,0:T(8,128)(2,1)S(1)}, u32[]{:S(2)}, u32[]{:S(2)}) collective-permute-start(bf16[128,1536]{1,0:T(8,128)(2,1)S(1)} %get-tuple-element.74.refs_9_), channel_id=1, source_target_pairs={{16,0},{0,16},{17,1},{1,17},{18,2},{2,18},{19,3},{3,19},{20,4},{4,... | collective-permute-start | bytes 1179656 | tf_op jit(solution)/shard_map/ppermute | solution.py:55
  37.4 11.5 %collective-permute-start.14 = (bf16[128,1536]{1,0:T(8,128)(2,1)S(1)}, bf16[128,1536]{1,0:T(8,128)(2,1)S(1)}, u32[]{:S(2)}, u32[]{:S(2)}) collective-permute-start(bf16[128,1536]{1,0:T(8,128)(2,1)S(1)} %get-tuple-element.74.refs_9_), channel_id=1, source_target_pairs={{8,0},{0,8},{9,1},{1,9},{10,2},{2,10},{11,3},{3,11},{12,4},{4,12},... | collective-permute-start | bytes 1179656 | tf_op jit(solution)/shard_map/ppermute | solution.py:55
  38.8 10.1 %collective-permute-start.5 = (bf16[128,1536]{1,0:T(8,128)(2,1)S(1)}, bf16[128,1536]{1,0:T(8,128)(2,1)S(1)}, u32[]{:S(2)}, u32[]{:S(2)}) collective-permute-start(bf16[128,1536]{1,0:T(8,128)(2,1)S(1)} %collective-permute-done.4.refs_2_.refs_15_), channel_id=1, source_target_pairs={{16,0},{0,16},{17,1},{1,17},{18,2},{2,18},{19,3},{3,19},{20,4},{4,... | collective-permute-start | bytes 1179656 | tf_op jit(solution)/shard_map/ppermute | solution.py:55
  48.9 2.6 %collective-permute-start.16 = (bf16[128,1536]{1,0:T(8,128)(2,1)S(1)}, bf16[128,1536]{1,0:T(8,128)(2,1)S(1)}, u32[]{:S(2)}, u32[]{:S(2)}) collective-permute-start(bf16[128,1536]{1,0:T(8,128)(2,1)S(1)} %collective-permute-done.14.refs_9_), channel_id=1, source_target_pairs={{16,0},{0,16},{17,1},{1,17},{18,2},{2,18},{19,3},{3,19},{20,4},{4,... | collective-permute-start | bytes 1179656 | tf_op jit(solution)/shard_map/ppermute | solution.py:55
  49.2 10.8 %copy-start.4 = (f32[3072]{0:T(1024)S(1)}, f32[3072]{0:T(1024)}, u32[]{:S(2)}) copy-start(f32[3072]{0:T(1024)} %refs_17_.1) | copy-start | bytes 36868
  49.4 9.3 %collective-permute-start.12 = (bf16[192,768]{1,0:T(8,128)(2,1)S(1)}, bf16[192,768]{1,0:T(8,128)(2,1)S(1)}, u32[]{:S(2)}, u32[]{:S(2)}) collective-permute-start(bf16[192,768]{1,0:T(8,128)(2,1)S(1)} %slice.8), channel_id=1, source_target_pairs={{0,2},{2,4},{4,6},{6,7},{7,5},{5,3},{3,1},{1,0},{8,10},{10,12},{12... | collective-permute-start | bytes 884744 | tf_op jit(solution)/shard_map/ppermute | solution.py:124
  51.0 8.9 %collective-permute-start.13 = (bf16[192,768]{1,0:T(8,128)(2,1)S(1)}, bf16[192,768]{1,0:T(8,128)(2,1)S(1)}, u32[]{:S(2)}, u32[]{:S(2)}) collective-permute-start(bf16[192,768]{1,0:T(8,128)(2,1)S(1)} %slice.9), channel_id=1, source_target_pairs={{2,0},{4,2},{6,4},{7,6},{5,7},{3,5},{1,3},{0,1},{10,8},{12,10},{14... | collective-permute-start | bytes 884744 | tf_op jit(solution)/shard_map/ppermute | solution.py:124
  63.4 3.5 %copy-start.8 = (f32[1536]{0:T(1024)S(1)}, f32[1536]{0:T(1024)}, u32[]{:S(2)}) copy-start(f32[1536]{0:T(1024)} %bias.1) | copy-start | bytes 18436
  63.4 1.8 %collective-permute-start.17 = (bf16[128,1536]{1,0:T(8,128)(2,1)S(1)}, bf16[128,1536]{1,0:T(8,128)(2,1)S(1)}, u32[]{:S(2)}, u32[]{:S(2)}) collective-permute-start(bf16[128,1536]{1,0:T(8,128)(2,1)S(1)} %get-tuple-element.81), channel_id=1, source_target_pairs={{16,0},{0,16},{17,1},{1,17},{18,2},{2,18},{19,3},{3,19},{20,4},{4,... | collective-permute-start | bytes 1179656 | tf_op jit(solution)/shard_map/ppermute | solution.py:55
  65.3 11.2 %collective-permute-start.18 = (bf16[128,1536]{1,0:T(8,128)(2,1)S(1)}, bf16[128,1536]{1,0:T(8,128)(2,1)S(1)}, u32[]{:S(2)}, u32[]{:S(2)}) collective-permute-start(bf16[128,1536]{1,0:T(8,128)(2,1)S(1)} %add_rounded.2), channel_id=1, source_target_pairs={{8,0},{0,8},{9,1},{1,9},{10,2},{2,10},{11,3},{3,11},{12,4},{4,12},... | collective-permute-start | bytes 1179656 | tf_op jit(solution)/shard_map/ppermute | solution.py:55
  66.8 11.2 %copy-start.6 = (f32[1536]{0:T(1024)S(1)}, f32[1536]{0:T(1024)}, u32[]{:S(2)}) copy-start(f32[1536]{0:T(1024)} %refs_6_.3) | copy-start | bytes 18436
  71.5 1.5 %collective-permute-start.19 = (bf16[64,1536]{1,0:T(8,128)(2,1)S(1)}, bf16[64,1536]{1,0:T(8,128)(2,1)S(1)}, u32[]{:S(2)}, u32[]{:S(2)}) collective-permute-start(bf16[64,1536]{1,0:T(8,128)(2,1)S(1)} %get-tuple-element.86), channel_id=1, source_target_pairs={{16,0},{0,16},{17,1},{1,17},{18,2},{2,18},{19,3},{3,19},{20,4},{4,... | collective-permute-start | bytes 589832 | tf_op jit(solution)/shard_map/ppermute | solution.py:55
  71.6 1.7 %collective-permute-start.20 = (bf16[64,1536]{1,0:T(8,128)(2,1)S(1)}, bf16[64,1536]{1,0:T(8,128)(2,1)S(1)}, u32[]{:S(2)}, u32[]{:S(2)}) collective-permute-start(bf16[64,1536]{1,0:T(8,128)(2,1)S(1)} %get-tuple-element.87), channel_id=1, source_target_pairs={{16,0},{0,16},{17,1},{1,17},{18,2},{2,18},{19,3},{3,19},{20,4},{4,... | collective-permute-start | bytes 589832 | tf_op jit(solution)/shard_map/ppermute | solution.py:55
  72.1 1.5 %collective-permute-start.21 = (bf16[64,1536]{1,0:T(8,128)(2,1)S(1)}, bf16[64,1536]{1,0:T(8,128)(2,1)S(1)}, u32[]{:S(2)}, u32[]{:S(2)}) collective-permute-start(bf16[64,1536]{1,0:T(8,128)(2,1)S(1)} %get-tuple-element.91), channel_id=1, source_target_pairs={{16,0},{0,16},{17,1},{1,17},{18,2},{2,18},{19,3},{3,19},{20,4},{4,... | collective-permute-start | bytes 589832 | tf_op jit(solution)/shard_map/ppermute | solution.py:55
  72.1 1.7 %collective-permute-start.22 = (bf16[64,1536]{1,0:T(8,128)(2,1)S(1)}, bf16[64,1536]{1,0:T(8,128)(2,1)S(1)}, u32[]{:S(2)}, u32[]{:S(2)}) collective-permute-start(bf16[64,1536]{1,0:T(8,128)(2,1)S(1)} %get-tuple-element.92), channel_id=1, source_target_pairs={{16,0},{0,16},{17,1},{1,17},{18,2},{2,18},{19,3},{3,19},{20,4},{4,... | collective-permute-start | bytes 589832 | tf_op jit(solution)/shard_map/ppermute | solution.py:55
  73.0 5.0 %collective-permute-start.23 = (bf16[64,1536]{1,0:T(8,128)(2,1)S(1)}, bf16[64,1536]{1,0:T(8,128)(2,1)S(1)}, u32[]{:S(2)}, u32[]{:S(2)}) collective-permute-start(bf16[64,1536]{1,0:T(8,128)(2,1)S(1)} %get-tuple-element.97), channel_id=1, source_target_pairs={{16,0},{0,16},{17,1},{1,17},{18,2},{2,18},{19,3},{3,19},{20,4},{4,... | collective-permute-start | bytes 589832 | tf_op jit(solution)/shard_map/ppermute | solution.py:55
  73.3 4.7 %collective-permute-start.24 = (bf16[64,1536]{1,0:T(8,128)(2,1)S(1)}, bf16[64,1536]{1,0:T(8,128)(2,1)S(1)}, u32[]{:S(2)}, u32[]{:S(2)}) collective-permute-start(bf16[64,1536]{1,0:T(8,128)(2,1)S(1)} %get-tuple-element.98), channel_id=1, source_target_pairs={{16,0},{0,16},{17,1},{1,17},{18,2},{2,18},{19,3},{3,19},{20,4},{4,... | collective-permute-start | bytes 589832 | tf_op jit(solution)/shard_map/ppermute | solution.py:55
  76.5 8.2 %collective-permute-start.26 = (bf16[96,1536]{1,0:T(8,128)(2,1)S(1)}, bf16[96,1536]{1,0:T(8,128)(2,1)S(1)}, u32[]{:S(2)}, u32[]{:S(2)}) collective-permute-start(bf16[96,1536]{1,0:T(8,128)(2,1)S(1)} %get-tuple-element.105), channel_id=1, source_target_pairs={{8,0},{0,8},{9,1},{1,9},{10,2},{2,10},{11,3},{3,11},{12,4},{4,12},... | collective-permute-start | bytes 884744 | tf_op jit(solution)/shard_map/ppermute | solution.py:55
  82.5 2.0 %collective-permute-start.25 = (f32[32,1536]{1,0:T(8,128)S(1)}, f32[32,1536]{1,0:T(8,128)S(1)}, u32[]{:S(2)}, u32[]{:S(2)}) collective-permute-start(f32[32,1536]{1,0:T(8,128)S(1)} %get-tuple-element.104), channel_id=1, source_target_pairs={{0,16},{16,0},{1,17},{17,1},{2,18},{18,2},{3,19},{19,3},{4,20},{20... | collective-permute-start | bytes 589832 | tf_op jit(solution)/shard_map/ppermute | solution.py:50
  82.6 6.2 %collective-permute-start.30 = (bf16[3,16,1536]{2,1,0:T(8,128)(2,1)S(1)}, bf16[3,16,1536]{2,1,0:T(8,128)(2,1)S(1)}, u32[]{:S(2)}, u32[]{:S(2)}) collective-permute-start(bf16[3,16,1536]{2,1,0:T(8,128)(2,1)S(1)} %get-tuple-element.114), channel_id=1, source_target_pairs={{0,16},{8,24},{16,0},{24,8},{1,17},{9,25},{17,1},{25,9},{2,18},{10... | collective-permute-start | bytes 442376 | tf_op jit(solution)/shard_map/ppermute | solution.py:75
  83.1 5.7 %collective-permute-start.31 = (bf16[8,3,1536]{2,1,0:T(4,128)(2,1)S(1)}, bf16[8,3,1536]{2,1,0:T(4,128)(2,1)S(1)}, u32[]{:S(2)}, u32[]{:S(2)}) collective-permute-start(bf16[8,3,1536]{2,1,0:T(4,128)(2,1)S(1)} %get-tuple-element.115), channel_id=1, source_target_pairs={{0,8},{8,0},{16,24},{24,16},{1,9},{9,1},{17,25},{25,17},{2,10},{10... | collective-permute-start | bytes 221192 | tf_op jit(solution)/shard_map/ppermute | solution.py:75
  83.6 4.2 %collective-permute-start.32 = (bf16[3,3,1536]{2,1,0:T(4,128)(2,1)S(1)}, bf16[3,3,1536]{2,1,0:T(4,128)(2,1)S(1)}, u32[]{:S(2)}, u32[]{:S(2)}) collective-permute-start(bf16[3,3,1536]{2,1,0:T(4,128)(2,1)S(1)} %get-tuple-element.116), channel_id=1, source_target_pairs={{0,24},{8,16},{16,8},{24,0},{1,25},{9,17},{17,9},{25,1},{2,26},{10... | collective-permute-start | bytes 82952 | tf_op jit(solution)/shard_map/ppermute | solution.py:75
  84.7 7.2 %collective-permute-start.27 = (bf16[8,1536]{1,0:T(8,128)(2,1)S(1)}, bf16[8,1536]{1,0:T(8,128)(2,1)S(1)}, u32[]{:S(2)}, u32[]{:S(2)}) collective-permute-start(bf16[8,1536]{1,0:T(8,128)(2,1)S(1)} %get-tuple-element.110), channel_id=1, source_target_pairs={{0,1},{1,0},{2,3},{3,2},{4,5},{5,4},{6,7},{7,6},{8,9},{9,8},{10,11... | collective-permute-start | bytes 73736 | tf_op jit(solution)/shard_map/ppermute | solution.py:50
  85.3 6.7 %collective-permute-start.28 = (bf16[8,1536]{1,0:T(8,128)(2,1)S(1)}, bf16[8,1536]{1,0:T(8,128)(2,1)S(1)}, u32[]{:S(2)}, u32[]{:S(2)}) collective-permute-start(bf16[8,1536]{1,0:T(8,128)(2,1)S(1)} %get-tuple-element.111), channel_id=1, source_target_pairs={{0,8},{8,0},{1,9},{9,1},{2,10},{10,2},{3,11},{11,3},{4,12},{12,4},... | collective-permute-start | bytes 73736 | tf_op jit(solution)/shard_map/ppermute | solution.py:50
  87.8 5.0 %collective-permute-start.29 = (bf16[8,1536]{1,0:T(8,128)(2,1)S(1)}, bf16[8,1536]{1,0:T(8,128)(2,1)S(1)}, u32[]{:S(2)}, u32[]{:S(2)}) collective-permute-start(bf16[8,1536]{1,0:T(8,128)(2,1)S(1)} %get-tuple-element.112), channel_id=1, source_target_pairs={{0,9},{1,8},{2,11},{3,10},{4,13},{5,12},{6,15},{7,14},{8,1},{9,0},... | collective-permute-start | bytes 73736 | tf_op jit(solution)/shard_map/ppermute | solution.py:50
  92.8 9.1 %collective-permute-start.36 = (bf16[32,1536]{1,0:T(8,128)(2,1)S(1)}, bf16[32,1536]{1,0:T(8,128)(2,1)S(1)}, u32[]{:S(2)}, u32[]{:S(2)}) collective-permute-start(bf16[32,1536]{1,0:T(8,128)(2,1)S(1)} %get-tuple-element.120), channel_id=1, source_target_pairs={{8,0},{0,8},{9,1},{1,9},{10,2},{2,10},{11,3},{3,11},{12,4},{4,12},... | collective-permute-start | bytes 294920 | tf_op jit(solution)/shard_map/ppermute | solution.py:55
  93.7 7.6 %collective-permute-start.35 = (bf16[8,1536]{1,0:T(8,128)(2,1)S(1)}, bf16[8,1536]{1,0:T(8,128)(2,1)S(1)}, u32[]{:S(2)}, u32[]{:S(2)}) collective-permute-start(bf16[8,1536]{1,0:T(8,128)(2,1)S(1)} %add_pairs.2.refs_0_), channel_id=1, source_target_pairs={{0,6},{1,7},{2,4},{3,5},{4,2},{5,3},{6,0},{7,1},{8,14},{9,15},{10,... | collective-permute-start | bytes 73736 | tf_op jit(solution)/shard_map/ppermute | solution.py:50
  97.1 4.7 %collective-permute-start.34 = (bf16[8,1536]{1,0:T(8,128)(2,1)S(1)}, bf16[8,1536]{1,0:T(8,128)(2,1)S(1)}, u32[]{:S(2)}, u32[]{:S(2)}) collective-permute-start(bf16[8,1536]{1,0:T(8,128)(2,1)S(1)} %add_pairs.2.refs_0_), channel_id=1, source_target_pairs={{0,4},{1,5},{2,6},{3,7},{4,0},{5,1},{6,2},{7,3},{8,12},{9,13},{10,... | collective-permute-start | bytes 73736 | tf_op jit(solution)/shard_map/ppermute | solution.py:50
  97.1 4.7 %collective-permute-start.33 = (bf16[8,1536]{1,0:T(8,128)(2,1)S(1)}, bf16[8,1536]{1,0:T(8,128)(2,1)S(1)}, u32[]{:S(2)}, u32[]{:S(2)}) collective-permute-start(bf16[8,1536]{1,0:T(8,128)(2,1)S(1)} %add_pairs.2.refs_0_), channel_id=1, source_target_pairs={{0,2},{1,3},{2,0},{3,1},{4,6},{5,7},{6,4},{7,5},{8,10},{9,11},{10,... | collective-permute-start | bytes 73736 | tf_op jit(solution)/shard_map/ppermute | solution.py:50
  101.9 5.1 %collective-permute-start.39 = (f32[8,1536]{1,0:T(8,128)S(1)}, f32[8,1536]{1,0:T(8,128)S(1)}, u32[]{:S(2)}, u32[]{:S(2)}) collective-permute-start(f32[8,1536]{1,0:T(8,128)S(1)} %add_pairs.3.refs_0_), channel_id=1, source_target_pairs={{0,9},{1,8},{2,11},{3,10},{4,13},{5,12},{6,15},{7,14},{8,1},{9,0},... | collective-permute-start | bytes 147464 | tf_op jit(solution)/shard_map/ppermute | solution.py:50
  103.4 4.1 %collective-permute-start.38 = (f32[8,1536]{1,0:T(8,128)S(1)}, f32[8,1536]{1,0:T(8,128)S(1)}, u32[]{:S(2)}, u32[]{:S(2)}) collective-permute-start(f32[8,1536]{1,0:T(8,128)S(1)} %add_pairs.3.refs_0_), channel_id=1, source_target_pairs={{0,8},{8,0},{1,9},{9,1},{2,10},{10,2},{3,11},{11,3},{4,12},{12,4},... | collective-permute-start | bytes 147464 | tf_op jit(solution)/shard_map/ppermute | solution.py:50
  104.3 4.1 %collective-permute-start.37 = (f32[8,1536]{1,0:T(8,128)S(1)}, f32[8,1536]{1,0:T(8,128)S(1)}, u32[]{:S(2)}, u32[]{:S(2)}) collective-permute-start(f32[8,1536]{1,0:T(8,128)S(1)} %add_pairs.3.refs_0_), channel_id=1, source_target_pairs={{0,1},{1,0},{2,3},{3,2},{4,5},{5,4},{6,7},{7,6},{8,9},{9,8},{10,11... | collective-permute-start | bytes 147464 | tf_op jit(solution)/shard_map/ppermute | solution.py:50
  105.4 4.0 %collective-permute-start.40 = (f32[8,1536]{1,0:T(8,128)S(1)}, f32[8,1536]{1,0:T(8,128)S(1)}, u32[]{:S(2)}, u32[]{:S(2)}) collective-permute-start(f32[8,1536]{1,0:T(8,128)S(1)} %add_pairs.3.refs_0_), channel_id=1, source_target_pairs={{0,16},{16,0},{1,17},{17,1},{2,18},{18,2},{3,19},{19,3},{4,20},{20... | collective-permute-start | bytes 147464 | tf_op jit(solution)/shard_map/ppermute | solution.py:50
  106.9 2.5 %collective-permute-start.43 = (f32[8,1536]{1,0:T(8,128)S(1)}, f32[8,1536]{1,0:T(8,128)S(1)}, u32[]{:S(2)}, u32[]{:S(2)}) collective-permute-start(f32[8,1536]{1,0:T(8,128)S(1)} %collective-permute-done.39.refs_3_), channel_id=1, source_target_pairs={{0,16},{16,0},{1,17},{17,1},{2,18},{18,2},{3,19},{19,3},{4,20},{20... | collective-permute-start | bytes 147464 | tf_op jit(solution)/shard_map/ppermute | solution.py:50
  107.4 2.0 %collective-permute-start.42 = (f32[8,1536]{1,0:T(8,128)S(1)}, f32[8,1536]{1,0:T(8,128)S(1)}, u32[]{:S(2)}, u32[]{:S(2)}) collective-permute-start(f32[8,1536]{1,0:T(8,128)S(1)} %collective-permute-done.38.refs_2_), channel_id=1, source_target_pairs={{0,16},{16,0},{1,17},{17,1},{2,18},{18,2},{3,19},{19,3},{4,20},{20... | collective-permute-start | bytes 147464 | tf_op jit(solution)/shard_map/ppermute | solution.py:50
  108.4 1.2 %collective-permute-start.41 = (f32[8,1536]{1,0:T(8,128)S(1)}, f32[8,1536]{1,0:T(8,128)S(1)}, u32[]{:S(2)}, u32[]{:S(2)}) collective-permute-start(f32[8,1536]{1,0:T(8,128)S(1)} %collective-permute-done.37.refs_1_), channel_id=1, source_target_pairs={{0,16},{16,0},{1,17},{17,1},{2,18},{18,2},{3,19},{19,3},{4,20},{20... | collective-permute-start | bytes 147464 | tf_op jit(solution)/shard_map/ppermute | solution.py:50

commit v6 on v5

--- a/solution.py
+++ b/solution.py
@@ -525,11 +525,8 @@
         columns = pl.ds(pl.multiple_of(quarter * hidden + tile.start, LANES), tile.size)
         v = jnp.dot(ln[...], up[:, tile], preferred_element_type=F32)
         v = v + bias[columns].reshape(1, tile.size)
-        square = v * v
-        th = jnp.tanh(GELU_A * (v + GELU_B * (square * v)))
-        half = 0.5 + 0.5 * th
-        act[:, tile] = (v * half).astype(BF)
-        slope[:, tile] = half + 0.5 * v * (1.0 - th * th) * (GELU_A * (1.0 + 3.0 * GELU_B * square))
+        value, slope[:, tile] = gelu_parts(v)
+        act[:, tile] = value.astype(BF)
 
 
 def backward_hidden(d_mlp, down, slope, d_pre):
@@ -555,40 +552,95 @@
         first += count
 
 
-def far_kernel(upper, lower, n_pieces, n_far, *refs):
+def gelu_parts(v):
+    square = v * v
+    th = jnp.tanh(GELU_A * (v + GELU_B * (square * v)))
+    half = 0.5 + 0.5 * th
+    return v * half, half + 0.5 * v * (1.0 - th * th) * (GELU_A * (1.0 + 3.0 * GELU_B * square))
+
+
+def early_kernel(upper, lower, n_pieces, n_far, *refs):
     pieces, refs = refs[:n_pieces], refs[n_pieces:]
     lns, refs = refs[:n_far], refs[n_far:]
-    d_mlp, bias, act, *far, up, down, ln, slope, d_pre = refs
+    d_mlp, pre, d_act, up, chosen, ln_last, d_mlp_last, down, ln = refs
     count = ln.shape[0]
-    copy_all(row_jobs(lns, ln) + block_jobs(pieces, upper, up))
-    forward_hidden(ln, up, bias, act, slope)
-    copy_all(block_jobs(pieces, lower, down))
-    backward_hidden(d_mlp.at[pl.ds(d_mlp.shape[0] - count, count)], down, slope, d_pre)
-    for tile in channel_tiles(up.shape[0]):
-        write_pieces(contract_last(d_pre[...], up[tile, :]), tile, far)
-
-
-def far_part(pieces, upper, lower, lns, d_mlp, bias):
+    chans, width = chosen.shape
+    n = lax.axis_size("fsdp")
+    size = chans // n
+    place = place_of(lax.axis_index("fsdp"), n)
+    begin = pl.multiple_of(at_place(lax.rem(place + n // 2, n), n) * size, 16)
+    for whole in (up, down):
+        whole[pl.ds(begin, size), :] = jnp.zeros((size, whole.shape[1]), BF)
+    row = lax.broadcasted_iota(jnp.int32, chosen.shape, 0)
+    col = lax.broadcasted_iota(jnp.int32, chosen.shape, 1)
+    chosen[...] = jnp.where((row == begin + col) & (col < size), 1.0, 0.0).astype(BF)
+    copy_all(row_jobs(lns, ln) + block_jobs(pieces, upper, up) + block_jobs(pieces, lower, down))
+    here = pl.ds(d_mlp.shape[0] - count, count)
+    for tile in hidden_tiles(up.shape[1]):
+        pre[:, tile] = jnp.dot(ln[...], up[:, tile], preferred_element_type=F32)
+        d_act[:, tile] = jnp.dot(d_mlp[here, :], down[:, tile], preferred_element_type=F32)
+    ln_last[...] = jnp.dot(ln[...], chosen[...], preferred_element_type=F32).astype(BF)
+    d_mlp_last[...] = jnp.dot(d_mlp[here, :], chosen[...], preferred_element_type=F32).astype(BF)
+
+
+def early_part(pieces, upper, lower, lns, d_mlp):
     spots, chans = lns[0].shape
     hidden = pieces[0].shape[1]
     count = spots * len(lns)
-    outs = [shaped((count, hidden), BF)] + [shaped((spots, chans), BF)] * len(lns)
-    return pl.pallas_call(
-        functools.partial(far_kernel, upper, lower, len(pieces), len(lns)),
+    width = -(-(chans // lax.axis_size("fsdp")) // LANES) * LANES
+    outs = [shaped((count, hidden), F32)] * 2 + [shaped((chans, hidden), BF), shaped((chans, width), BF)]
+    outs += [shaped((count, width), BF)] * 2
+    return pl.pallas_call(
+        functools.partial(early_kernel, upper, lower, len(pieces), len(lns)),
         out_shape=outs,
-        in_specs=vmem(len(pieces) + len(lns) + 2),
+        in_specs=vmem(len(pieces) + len(lns) + 1),
+        out_specs=vmem(len(outs)),
+        scratch_shapes=[pltpu.VMEM((chans, hidden), BF), pltpu.VMEM((count, chans), BF)],
+        compiler_params=params(28),
+        cost_estimate=cost(4 * count * chans * hidden, 8 * count * chans),
+        name="early_part",
+    )(*pieces, *lns, d_mlp)
+
+
+def far_kernel(up_last, down_last, pre, d_act, up, chosen, ln_last, d_mlp_last, bias, act, *refs):
+    *far, up_block, down_block, d_pre = refs
+    size, hidden = up_last.shape
+    for block, last in ((up_block, up_last), (down_block, down_last)):
+        block[pl.ds(0, size), :] = last[...]
+        if block.shape[0] > size:
+            block[pl.ds(size, block.shape[0] - size), :] = jnp.zeros((block.shape[0] - size, hidden), BF)
+    quarter = lax.axis_index("sx") * lax.axis_size("sy") + lax.axis_index("sy")
+    for tile in hidden_tiles(hidden):
+        columns = pl.ds(pl.multiple_of(quarter * hidden + tile.start, LANES), tile.size)
+        v = pre[:, tile] + jnp.dot(ln_last[...], up_block[:, tile], preferred_element_type=F32)
+        value, slope = gelu_parts(v + bias[columns].reshape(1, tile.size))
+        act[:, tile] = value.astype(BF)
+        grad = d_act[:, tile] + jnp.dot(d_mlp_last[...], down_block[:, tile], preferred_element_type=F32)
+        d_pre[:, tile] = (grad * slope).astype(BF)
+    corner = contract_last(d_pre[...], up_block[...]).astype(BF)
+    for tile in channel_tiles(up.shape[0]):
+        value = contract_last(d_pre[...], up[tile, :]) + contract_last(corner, chosen[tile, :])
+        write_pieces(value, tile, far)
+
+
+def far_part(up_last, down_last, early, bias, n_far):
+    count, hidden = early[0].shape
+    chans, width = early[3].shape
+    outs = [shaped((count, hidden), BF)] + [shaped((count // n_far, chans), BF)] * n_far
+    return pl.pallas_call(
+        far_kernel,
+        out_shape=outs,
+        in_specs=vmem(3 + len(early)),
         out_specs=vmem(len(outs)),
         scratch_shapes=[
-            pltpu.VMEM((chans, hidden), BF),
-            pltpu.VMEM((chans, hidden), BF),
-            pltpu.VMEM((count, chans), BF),
-            pltpu.VMEM((count, hidden), F32),
+            pltpu.VMEM((width, hidden), BF),
+            pltpu.VMEM((width, hidden), BF),
             pltpu.VMEM((count, hidden), BF),
         ],
-        compiler_params=params(24),
-        cost_estimate=cost(6 * count * chans * hidden, 8 * count * chans),
+        compiler_params=params(20),
+        cost_estimate=cost(2 * count * chans * hidden, 8 * count * chans),
         name="far_part",
-    )(*pieces, *lns, d_mlp, bias)
+    )(up_last, down_last, *early, bias)
 
 
 def rest_kernel(upper, lower, n_pieces, tiles, n_near, n_mlp, *refs):
@@ -811,7 +863,8 @@
     blocks = jnp.concatenate([up_block, down_block], 0)
     pieces, upper, lower = ring_gather(blocks, edges, ln_out, d_mlp)
     lns = gather_tile(ln_out)
-    far_act, *far = far_part(pieces, upper, lower, lns[n_near:], d_mlp, b_up)
+    early = early_part(pieces[:-2], upper[:-1], lower[:-1], lns[n_near:], d_mlp)
+    far_act, *far = far_part(*pieces[-2:], early, b_up, tiles - n_near)
 
     far = [far[k : k + n_near] for k in range(0, len(far), n_near)]
     far = [add_rounded(reduce_cores(group), [spots])[0] for group in far]

time: 111 us -> 110 us (level)
  waiting for transfers between devices: 43.3 us -> 40 us
  Pallas kernels: 27.9 us -> 29.7 us
    ppermute x1, waiting for transfers between devices: 7.23 us -> 3.99 us  [ring_gather(): lax.ppermute(one, 'fsdp', forth)]
    pallas_call x1 -> x2, Pallas kernels: 3.38 us -> 5.21 us  [the longest x1 3.22 us: early_part(): pl.pallas_call(functools.partial(early_kernel, upper, lower, len(pieces),...]
  transfers between devices with their start and end apart: 44 -> 44, of which waited for: 23 -> 23; matrix products, arithmetic and copies ran while one was open for 1% -> 1% of each run, Pallas kernels for 21% -> 25%
where the time goes in v6:
time: 110 us; the launch traced here: 109 us
  waiting for transfers between devices  40 us (36%)
  starting transfers between devices  32.9 us (30%)
  Pallas kernels  29.7 us (27%)
  local copies, waits for them, and re-layouts  5.44 us (5%)
    ppermute x16, waiting for transfers between devices, shift(): return lax.ppermute(a, axis, [((i + k) % n, i) for i in range(n)])  15.1 us
    ppermute x14, starting transfers between devices, swap(): return lax.ppermute(a, axes, [(i, i ^ mask) for i in range(total)])  11 us
    ppermute x16, starting transfers between devices, shift(): return lax.ppermute(a, axis, [((i + k) % n, i) for i in range(n)])  8.63 us
    pallas_call x2, Pallas kernels, conv_back(): pl.pallas_call(functools.partial(conv_back_kernel, begin, count), out_sha...  6.37 us
    ppermute x3, waiting for transfers between devices, ring_gather(): two = lax.ppermute(two, 'fsdp', back)  6.34 us
    pallas_call x1, Pallas kernels, conv_norm(): pl.pallas_call(conv_norm_kernel, out_shape=(shaped((rows + 2 * HALO, cols...  6.05 us
    ppermute x3, starting transfers between devices, ring_gather(): two = lax.ppermute(two, 'fsdp', back)  5.15 us
    ppermute x6, waiting for transfers between devices, exchange_edges(): got[a, b] = lax.ppermute(piece, ('sx', 'sy'), pairs)  4.87 us
  transfers between devices with their start and end apart: 44, of which 23 were waited for; matrix products, arithmetic and copies ran while one was open for 1% of the time, Pallas kernels for 25%

profile of v6, /device:TPU:0, one launch (start us, length us, event | category | flops | bytes accessed | tf_op | source)
XLA Modules:
  0.0 109.1 jit_solution(11402015440018535293)
XLA Ops:
  0.7 1.3 %copy-done = bf16[192,3072]{1,0:T(8,128)(2,1)S(1)} copy-done((bf16[192,3072]{1,0:T(8,128)(2,1)S(1)}, bf16[192,3072]{1,0:T(8,128)(2,1)}, u32[]{:S(2)}) %copy-start) | copy-done | bytes 1179672
  2.0 1.1 dynamic-slice_bitcast_fusion
  3.1 3.0 %collective-permute-start.7 = (bf16[384,768]{1,0:T(8,128)(2,1)S(1)}, bf16[384,768]{1,0:T(8,128)(2,1)S(1)}, u32[]{:S(2)}, u32[]{:S(2)}) collective-permute-start(bf16[384,768]{1,0:T(8,128)(2,1)S(1)} %pad_maximum_fusion.refs_0_), channel_id=1, source_target_pairs={{2,0},{4,2},{6,4},{7,6},{5,7},{3,5},{1,3},{0,1},{10,8},{12,10},{14... | collective-permute-start | bytes 1769480 | tf_op jit(solution)/shard_map/ppermute | solution.py:115
  6.2 0.9 copy.18
  7.2 0.5 prepare.1
  7.8 1.9 %collective-permute-start.1 = (bf16[8,3,1536]{2,1,0:T(4,128)(2,1)S(1)}, bf16[8,3,1536]{2,1,0:T(4,128)(2,1)S(1)}, u32[]{:S(2)}, u32[]{:S(2)}) collective-permute-start(bf16[8,3,1536]{2,1,0:T(4,128)(2,1)S(1)} %get-tuple-element.74), channel_id=1, source_target_pairs={{0,8},{8,0},{16,24},{24,16},{1,9},{9,1},{17,25},{25,17},{2,10},{10... | collective-permute-start | bytes 221192 | tf_op jit(solution)/shard_map/ppermute | solution.py:75
  9.8 3.8 %collective-permute-done.2.refs_2_ = bf16[3,3,1536]{2,1,0:T(4,128)(2,1)S(1)} collective-permute-done((bf16[3,3,1536]{2,1,0:T(4,128)(2,1)S(1)}, bf16[3,3,1536]{2,1,0:T(4,128)(2,1)S(1)}, u32[]{:S(2)}, u32[]{:S(2)}) %collective-permute-start.2) | collective-permute-done | bytes 27680 | tf_op jit(solution)/shard_map/ppermute | solution.py:75
  13.6 5.9 %collective-permute-done.7.refs_2_ = bf16[384,768]{1,0:T(8,128)(2,1)S(1)} collective-permute-done((bf16[384,768]{1,0:T(8,128)(2,1)S(1)}, bf16[384,768]{1,0:T(8,128)(2,1)S(1)}, u32[]{:S(2)}, u32[]{:S(2)}) %collective-permute-start.7) | collective-permute-done | bytes 589856 | tf_op jit(solution)/shard_map/ppermute | solution.py:115
  19.5 1.5 %collective-permute-done.6.refs_1_ = bf16[384,768]{1,0:T(8,128)(2,1)} collective-permute-done((bf16[384,768]{1,0:T(8,128)(2,1)S(1)}, bf16[384,768]{1,0:T(8,128)(2,1)}, u32[]{:S(2)}, u32[]{:S(2)}) %collective-permute-start.6) | collective-permute-done | bytes 589856 | tf_op jit(solution)/shard_map/ppermute | solution.py:114
  21.0 0.4 collective-permute-start.8
  21.4 1.6 %collective-permute-start.9 = (bf16[384,768]{1,0:T(8,128)(2,1)S(1)}, bf16[384,768]{1,0:T(8,128)(2,1)S(1)}, u32[]{:S(2)}, u32[]{:S(2)}) collective-permute-start(bf16[384,768]{1,0:T(8,128)(2,1)S(1)} %collective-permute-done.7.refs_2_), channel_id=1, source_target_pairs={{2,0},{4,2},{6,4},{7,6},{5,7},{3,5},{1,3},{0,1},{10,8},{12,10},{14... | collective-permute-start | bytes 1769480 | tf_op jit(solution)/shard_map/ppermute | solution.py:115
  23.0 1.5 %collective-permute-start.4 = (bf16[128,1536]{1,0:T(8,128)(2,1)S(1)}, bf16[128,1536]{1,0:T(8,128)(2,1)S(1)}, u32[]{:S(2)}, u32[]{:S(2)}) collective-permute-start(bf16[128,1536]{1,0:T(8,128)(2,1)S(1)} %bitcast.8), channel_id=1, source_target_pairs={{8,0},{0,8},{9,1},{1,9},{10,2},{2,10},{11,3},{3,11},{12,4},{4,12},... | collective-permute-start | bytes 1179656 | tf_op jit(solution)/shard_map/ppermute | solution.py:55
  24.5 0.7 copy-done.5
  25.2 0.7 copy-done.9
  25.9 0.7 copy-done.10
  26.6 6.0 %conv_norm.1 = (f32[14,32,1536]{2,1,0:T(8,128)S(1)}, f32[128,1536]{1,0:T(8,128)S(1)}, f32[128,128]{1,0:T(8,128)S(1)}, bf16[128,1536]{1,0:T(8,128)(2,1)S(1)}) custom-call(bf16[8,16,1536]{2,1,0:T(8,128)(2,1)S(1)} %get-tuple-element.72.own.scaled, bf16[3,16,1536]{2,1,0:T(8,128)(2,1)S(1)} %collective-permute-done.refs_0_, ...), custom_call_target="tpu_custom_call" | custom-call | flops 1 | bytes 1 | tf_op jit(solution)/shard_map/conv_norm/pallas_call | solution.py:318
  32.7 2.4 %collective-permute-done.8.refs_3_ = bf16[384,768]{1,0:T(8,128)(2,1)S(1)} collective-permute-done((bf16[384,768]{1,0:T(8,128)(2,1)}, bf16[384,768]{1,0:T(8,128)(2,1)S(1)}, u32[]{:S(2)}, u32[]{:S(2)}) %collective-permute-start.8) | collective-permute-done | bytes 589856 | tf_op jit(solution)/shard_map/ppermute | solution.py:114
  35.1 0.2 collective-permute-done.9.refs_4_
  35.3 1.5 %collective-permute-start.10 = (bf16[384,768]{1,0:T(8,128)(2,1)S(1)}, bf16[384,768]{1,0:T(8,128)(2,1)S(1)}, u32[]{:S(2)}, u32[]{:S(2)}) collective-permute-start(bf16[384,768]{1,0:T(8,128)(2,1)S(1)} %collective-permute-done.8.refs_3_), channel_id=1, source_target_pairs={{0,2},{2,4},{4,6},{6,7},{7,5},{5,3},{3,1},{1,0},{8,10},{10,12},{12... | collective-permute-start | bytes 1769480 | tf_op jit(solution)/shard_map/ppermute | solution.py:114
  36.8 0.5 collective-permute-start.11
  37.4 1.4 %collective-permute-start.14 = (bf16[128,1536]{1,0:T(8,128)(2,1)S(1)}, bf16[128,1536]{1,0:T(8,128)(2,1)S(1)}, u32[]{:S(2)}, u32[]{:S(2)}) collective-permute-start(bf16[128,1536]{1,0:T(8,128)(2,1)S(1)} %get-tuple-element.80.refs_9_), channel_id=1, source_target_pairs={{8,0},{0,8},{9,1},{1,9},{10,2},{2,10},{11,3},{3,11},{12,4},{4,12},... | collective-permute-start | bytes 1179656 | tf_op jit(solution)/shard_map/ppermute | solution.py:55
  38.8 0.2 collective-permute-start.5
  39.1 9.8 %collective-permute-done.14.refs_7_ = bf16[128,1536]{1,0:T(8,128)(2,1)S(1)} collective-permute-done((bf16[128,1536]{1,0:T(8,128)(2,1)S(1)}, bf16[128,1536]{1,0:T(8,128)(2,1)S(1)}, u32[]{:S(2)}, u32[]{:S(2)}) %collective-permute-start.14) | collective-permute-done | bytes 393248 | tf_op jit(solution)/shard_map/ppermute | solution.py:55
  48.9 0.3 scale_part.1.refs_9_.refs_11_
  49.4 1.6 %collective-permute-start.12 = (bf16[192,768]{1,0:T(8,128)(2,1)S(1)}, bf16[192,768]{1,0:T(8,128)(2,1)S(1)}, u32[]{:S(2)}, u32[]{:S(2)}) collective-permute-start(bf16[192,768]{1,0:T(8,128)(2,1)S(1)} %slice.8), channel_id=1, source_target_pairs={{0,2},{2,4},{4,6},{6,7},{7,5},{5,3},{3,1},{1,0},{8,10},{10,12},{12... | collective-permute-start | bytes 884744 | tf_op jit(solution)/shard_map/ppermute | solution.py:124
  51.0 0.5 collective-permute-start.13
  51.5 3.2 %early_part.1 = (f32[256,768]{1,0:T(8,128)S(1)}, f32[256,768]{1,0:T(8,128)S(1)}, bf16[1536,768]{1,0:T(8,128)(2,1)S(1)}, bf16[1536,256]{1,0:T(8,128)(2,1)S(1)}, b...) custom-call(bf16[384,768]{1,0:T(8,128)(2,1)S(1)} %pad_maximum_fusion.refs_0_, ...), custom_call_target="tpu_custom_call" | custom-call | flops 1 | bytes 1 | tf_op jit(solution)/shard_map/early_part/pallas_call | solution.py:593
  54.7 4.0 %collective-permute-done.12.up_last.refs_7_ = bf16[192,768]{1,0:T(8,128)(2,1)S(1)} collective-permute-done((bf16[192,768]{1,0:T(8,128)(2,1)S(1)}, bf16[192,768]{1,0:T(8,128)(2,1)S(1)}, u32[]{:S(2)}, u32[]{:S(2)}) %collective-permute-start.12) | collective-permute-done | bytes 294944 | tf_op jit(solution)/shard_map/ppermute | solution.py:124
  58.7 1.2 %collective-permute-done.13.down_last.refs_8_ = bf16[192,768]{1,0:T(8,128)(2,1)S(1)} collective-permute-done((bf16[192,768]{1,0:T(8,128)(2,1)S(1)}, bf16[192,768]{1,0:T(8,128)(2,1)S(1)}, u32[]{:S(2)}, u32[]{:S(2)}) %collective-permute-start.13) | collective-permute-done | bytes 294944 | tf_op jit(solution)/shard_map/ppermute | solution.py:124
  60.0 2.0 %far_part.1 = (bf16[256,768]{1,0:T(8,128)(2,1)S(1)}, bf16[128,1536]{1,0:T(8,128)(2,1)S(1)}, bf16[128,1536]{1,0:T(8,128)(2,1)S(1)}) custom-call(bf16[192,768]{1,0:T(8,128)(2,1)S(1)} %collective-permute-done.12.up_last.refs_7_, bf16[192,768]{1,0:T(8,128)(2,1)S(1)} %collective-permute-done.13.down_last.refs_8_, f32[256,768]{1,0:T(8,128)S(1)} %get-tuple-element.86.pre, ...), custom_call_target="tpu_custom_call" | custom-call | flops 1 | bytes 1 | tf_op jit(solution)/shard_map/far_part/pallas_call | solution.py:630
  62.1 1.7 %collective-permute-done.17.refs_1_ = bf16[128,1536]{1,0:T(8,128)(2,1)S(1)} collective-permute-done((bf16[128,1536]{1,0:T(8,128)(2,1)S(1)}, bf16[128,1536]{1,0:T(8,128)(2,1)S(1)}, u32[]{:S(2)}, u32[]{:S(2)}) %collective-permute-start.17) | collective-permute-done | bytes 393248 | tf_op jit(solution)/shard_map/ppermute | solution.py:55
  63.9 1.6 %collective-permute-start.18 = (bf16[128,1536]{1,0:T(8,128)(2,1)S(1)}, bf16[128,1536]{1,0:T(8,128)(2,1)S(1)}, u32[]{:S(2)}, u32[]{:S(2)}) collective-permute-start(bf16[128,1536]{1,0:T(8,128)(2,1)S(1)} %add_rounded.2), channel_id=1, source_target_pairs={{8,0},{0,8},{9,1},{1,9},{10,2},{2,10},{11,3},{3,11},{12,4},{4,12},... | collective-permute-start | bytes 1179656 | tf_op jit(solution)/shard_map/ppermute | solution.py:55
  65.4 4.7 %rest_part.1 = (bf16[128,1536]{1,0:T(8,128)(2,1)S(1)}, bf16[64,1536]{1,0:T(8,128)(2,1)S(1)}, bf16[64,1536]{1,0:T(8,128)(2,1)S(1)}, bf16[128,1536]{1,0:T(8,128)(2...) custom-call(bf16[384,768]{1,0:T(8,128)(2,1)S(1)} %pad_maximum_fusion, ...), custom_call_target="tpu_custom_call" | custom-call | flops 1 | bytes 1 | tf_op jit(solution)/shard_map/rest_part/pallas_call | solution.py:684
  70.2 0.5 collective-permute-start.20
  70.8 0.4 collective-permute-start.22
  71.2 0.4 collective-permute-done.19.refs_1_
  71.9 0.2 collective-permute-start.24
  72.2 0.2 collective-permute-done.22.refs_2_
  72.5 2.6 %collective-permute-done.18.refs_3_ = bf16[128,1536]{1,0:T(8,128)(2,1)S(1)} collective-permute-done((bf16[128,1536]{1,0:T(8,128)(2,1)S(1)}, bf16[128,1536]{1,0:T(8,128)(2,1)S(1)}, u32[]{:S(2)}, u32[]{:S(2)}) %collective-permute-start.18) | collective-permute-done | bytes 393248 | tf_op jit(solution)/shard_map/ppermute | solution.py:55
  75.1 1.5 %collective-permute-start.26 = (bf16[96,1536]{1,0:T(8,128)(2,1)S(1)}, bf16[96,1536]{1,0:T(8,128)(2,1)S(1)}, u32[]{:S(2)}, u32[]{:S(2)}) collective-permute-start(bf16[96,1536]{1,0:T(8,128)(2,1)S(1)} %get-tuple-element.117), channel_id=1, source_target_pairs={{8,0},{0,8},{9,1},{1,9},{10,2},{2,10},{11,3},{3,11},{12,4},{4,12},... | collective-permute-start | bytes 884744 | tf_op jit(solution)/shard_map/ppermute | solution.py:55
  76.6 4.5 %norm_back.1 = (f32[8,16,1536]{2,1,0:T(8,128)S(1)}, f32[32,1536]{1,0:T(8,128)S(1)}, f32[32,1536]{1,0:T(8,128)S(1)}, bf16[3,16,1536]{2,1,0:T(8,128)(2,1)S(1)}, bf...) custom-call(bf16[128,1536]{1,0:T(8,128)(2,1)S(1)} %get-tuple-element.108.refs_0_, ...), custom_call_target="tpu_custom_call" | custom-call | flops 1 | bytes 1 | tf_op jit(solution)/shard_map/norm_back/pallas_call | solution.py:406
  81.2 0.5 collective-permute-start.30
  81.7 0.5 collective-permute-start.31
  82.3 0.9 collective-permute-start.32
  83.3 0.6 collective-permute-start.27
  83.9 1.4 %collective-permute-start.28 = (bf16[8,1536]{1,0:T(8,128)(2,1)S(1)}, bf16[8,1536]{1,0:T(8,128)(2,1)S(1)}, u32[]{:S(2)}, u32[]{:S(2)}) collective-permute-start(bf16[8,1536]{1,0:T(8,128)(2,1)S(1)} %get-tuple-element.123), channel_id=1, source_target_pairs={{0,8},{8,0},{1,9},{9,1},{2,10},{10,2},{3,11},{11,3},{4,12},{12,4},... | collective-permute-start | bytes 73736 | tf_op jit(solution)/shard_map/ppermute | solution.py:50
  85.3 1.1 collective-permute-done.32.refs_2_
  86.4 1.0 collective-permute-start.29
  87.4 3.2 %conv_back.2.refs_5_ = bf16[8,16,1536]{2,1,0:T(8,128)(2,1)} custom-call(f32[8,16,1536]{2,1,0:T(8,128)S(1)} %get-tuple-element.125.own, bf16[3,16,1536]{2,1,0:T(8,128)(2,1)S(1)} %collective-permute-done.30.refs_0_, bf16[8,3,1536]{2,1,0:T(4,128)(2,1)S(1)} %collective-permute-done.31.refs_1_, bf16[3,3,1536]{2,1,0:T(4,128)(2,1)S(1)} %collective-permute-done.32.refs_2_, ...), custom_call_target="tpu_custom_call" | custom-call | flops 1 | bytes 1 | tf_op jit(solution)/shard_map/conv_back/pallas_call | solution.py:443
  90.6 0.8 collective-permute-done.29.refs_3_
  91.4 0.9 collective-permute-start.36
  92.3 3.4 %collective-permute-start.35 = (bf16[8,1536]{1,0:T(8,128)(2,1)S(1)}, bf16[8,1536]{1,0:T(8,128)(2,1)S(1)}, u32[]{:S(2)}, u32[]{:S(2)}) collective-permute-start(bf16[8,1536]{1,0:T(8,128)(2,1)S(1)} %add_pairs.2.refs_0_), channel_id=1, source_target_pairs={{0,6},{1,7},{2,4},{3,5},{4,2},{5,3},{6,0},{7,1},{8,14},{9,15},{10,... | collective-permute-start | bytes 73736 | tf_op jit(solution)/shard_map/ppermute | solution.py:50
  95.7 1.0 collective-permute-start.33
  96.7 3.2 %conv_back.3 = bf16[8,16,1536]{2,1,0:T(8,128)(2,1)} custom-call(f32[8,16,1536]{2,1,0:T(8,128)S(1)} %get-tuple-element.125.own, bf16[3,16,1536]{2,1,0:T(8,128)(2,1)S(1)} %collective-permute-done.30.refs_0_, bf16[8,3,1536]{2,1,0:T(4,128)(2,1)S(1)} %collective-permute-done.31.refs_1_, ...), custom_call_target="tpu_custom_call", output_to_operand_aliasing={{}: (6, {})} | custom-call | flops 1 | bytes 1 | tf_op jit(solution)/shard_map/conv_back/pallas_call | solution.py:443
  99.9 0.5 collective-permute-done.34.refs_2_
  100.5 1.5 %collective-permute-start.39 = (f32[8,1536]{1,0:T(8,128)S(1)}, f32[8,1536]{1,0:T(8,128)S(1)}, u32[]{:S(2)}, u32[]{:S(2)}) collective-permute-start(f32[8,1536]{1,0:T(8,128)S(1)} %add_pairs.3.refs_0_), channel_id=1, source_target_pairs={{0,9},{1,8},{2,11},{3,10},{4,13},{5,12},{6,15},{7,14},{8,1},{9,0},... | collective-permute-start | bytes 147464 | tf_op jit(solution)/shard_map/ppermute | solution.py:50
  102.0 0.9 collective-permute-start.38
  102.9 1.1 %collective-permute-start.37 = (f32[8,1536]{1,0:T(8,128)S(1)}, f32[8,1536]{1,0:T(8,128)S(1)}, u32[]{:S(2)}, u32[]{:S(2)}) collective-permute-start(f32[8,1536]{1,0:T(8,128)S(1)} %add_pairs.3.refs_0_), channel_id=1, source_target_pairs={{0,1},{1,0},{2,3},{3,2},{4,5},{5,4},{6,7},{7,6},{8,9},{9,8},{10,11... | collective-permute-start | bytes 147464 | tf_op jit(solution)/shard_map/ppermute | solution.py:50
  104.0 1.5 %collective-permute-done.39.refs_3_ = f32[8,1536]{1,0:T(8,128)S(1)} collective-permute-done((f32[8,1536]{1,0:T(8,128)S(1)}, f32[8,1536]{1,0:T(8,128)S(1)}, u32[]{:S(2)}, u32[]{:S(2)}) %collective-permute-start.39) | collective-permute-done | bytes 49184 | tf_op jit(solution)/shard_map/ppermute | solution.py:50
  105.5 0.5 collective-permute-done.38.refs_2_
  106.1 0.9 collective-permute-done.37.refs_1_
  107.0 1.0 output_part.1
  108.0 0.2 collective-permute-done.41.refs_5_
  108.2 0.9 finish.1
  (68 shorter events, 1.7 us)
Async XLA Ops:
  0.6 1.3 %copy-start = (bf16[192,3072]{1,0:T(8,128)(2,1)S(1)}, bf16[192,3072]{1,0:T(8,128)(2,1)}, u32[]{:S(2)}) copy-start(bf16[192,3072]{1,0:T(8,128)(2,1)} %param.18) | copy-start | bytes 3538948
  1.9 5.2 %copy-start.3 = (bf16[1,8,16,1536]{3,2,1,0:T(8,128)(2,1)S(1)}, bf16[1,8,16,1536]{3,2,1,0:T(8,128)(2,1)}, u32[]{:S(2)}) copy-start(bf16[1,8,16,1536]{3,2,1,0:T(8,128)(2,1)} %param.12) | copy-start | bytes 1179652
  1.9 21.1 %copy-start.1 = (bf16[1,8,16,1536]{3,2,1,0:T(8,128)(2,1)S(1)}, bf16[1,8,16,1536]{3,2,1,0:T(8,128)(2,1)}, u32[]{:S(2)}) copy-start(bf16[1,8,16,1536]{3,2,1,0:T(8,128)(2,1)} %param.23) | copy-start | bytes 1179652
  2.0 22.6 %copy-start.2 = (f32[7,7,1536]{2,1,0:T(8,128)S(1)}, f32[7,7,1536]{2,1,0:T(8,128)}, u32[]{:S(2)}) copy-start(f32[7,7,1536]{2,1,0:T(8,128)} %refs_3_.5) | copy-start | bytes 903172
  3.1 16.4 %collective-permute-start.7 = (bf16[384,768]{1,0:T(8,128)(2,1)S(1)}, bf16[384,768]{1,0:T(8,128)(2,1)S(1)}, u32[]{:S(2)}, u32[]{:S(2)}) collective-permute-start(bf16[384,768]{1,0:T(8,128)(2,1)S(1)} %pad_maximum_fusion.refs_0_), channel_id=1, source_target_pairs={{2,0},{4,2},{6,4},{7,6},{5,7},{3,5},{1,3},{0,1},{10,8},{12,10},{14... | collective-permute-start | bytes 1769480 | tf_op jit(solution)/shard_map/ppermute | solution.py:115
  6.1 14.9 %collective-permute-start.6 = (bf16[384,768]{1,0:T(8,128)(2,1)S(1)}, bf16[384,768]{1,0:T(8,128)(2,1)}, u32[]{:S(2)}, u32[]{:S(2)}) collective-permute-start(bf16[384,768]{1,0:T(8,128)(2,1)S(1)} %pad_maximum_fusion.refs_0_), channel_id=1, source_target_pairs={{0,2},{2,4},{4,6},{6,7},{7,5},{5,3},{3,1},{1,0},{8,10},{10,12},{12... | collective-permute-start | bytes 1769480 | tf_op jit(solution)/shard_map/ppermute | solution.py:114
  7.1 41.7 %copy-start.7 = (f32[1536]{0:T(1024)S(1)}, f32[1536]{0:T(1024)}, u32[]{:S(2)}) copy-start(f32[1536]{0:T(1024)} %scale.3) | copy-start | bytes 18436
  7.7 5.9 %collective-permute-start = (bf16[3,16,1536]{2,1,0:T(8,128)(2,1)S(1)}, bf16[3,16,1536]{2,1,0:T(8,128)(2,1)S(1)}, u32[]{:S(2)}, u32[]{:S(2)}) collective-permute-start(bf16[3,16,1536]{2,1,0:T(8,128)(2,1)S(1)} %get-tuple-element.73), channel_id=1, source_target_pairs={{0,16},{8,24},{16,0},{24,8},{1,17},{9,25},{17,1},{25,9},{2,18},{10... | collective-permute-start | bytes 442376 | tf_op jit(solution)/shard_map/ppermute | solution.py:75
  7.8 5.8 %collective-permute-start.1 = (bf16[8,3,1536]{2,1,0:T(4,128)(2,1)S(1)}, bf16[8,3,1536]{2,1,0:T(4,128)(2,1)S(1)}, u32[]{:S(2)}, u32[]{:S(2)}) collective-permute-start(bf16[8,3,1536]{2,1,0:T(4,128)(2,1)S(1)} %get-tuple-element.74), channel_id=1, source_target_pairs={{0,8},{8,0},{16,24},{24,16},{1,9},{9,1},{17,25},{25,17},{2,10},{10... | collective-permute-start | bytes 221192 | tf_op jit(solution)/shard_map/ppermute | solution.py:75
  9.7 3.9 %collective-permute-start.2 = (bf16[3,3,1536]{2,1,0:T(4,128)(2,1)S(1)}, bf16[3,3,1536]{2,1,0:T(4,128)(2,1)S(1)}, u32[]{:S(2)}, u32[]{:S(2)}) collective-permute-start(bf16[3,3,1536]{2,1,0:T(4,128)(2,1)S(1)} %get-tuple-element.75), channel_id=1, source_target_pairs={{0,24},{8,16},{16,8},{24,0},{1,25},{9,17},{17,9},{25,1},{2,26},{10... | collective-permute-start | bytes 82952 | tf_op jit(solution)/shard_map/ppermute | solution.py:75
  21.0 14.1 %collective-permute-start.8 = (bf16[384,768]{1,0:T(8,128)(2,1)}, bf16[384,768]{1,0:T(8,128)(2,1)S(1)}, u32[]{:S(2)}, u32[]{:S(2)}) collective-permute-start(bf16[384,768]{1,0:T(8,128)(2,1)} %collective-permute-done.6.refs_1_), channel_id=1, source_target_pairs={{0,2},{2,4},{4,6},{6,7},{7,5},{5,3},{3,1},{1,0},{8,10},{10,12},{12... | collective-permute-start | bytes 1769480 | tf_op jit(solution)/shard_map/ppermute | solution.py:114
  21.4 13.9 %collective-permute-start.9 = (bf16[384,768]{1,0:T(8,128)(2,1)S(1)}, bf16[384,768]{1,0:T(8,128)(2,1)S(1)}, u32[]{:S(2)}, u32[]{:S(2)}) collective-permute-start(bf16[384,768]{1,0:T(8,128)(2,1)S(1)} %collective-permute-done.7.refs_2_), channel_id=1, source_target_pairs={{2,0},{4,2},{6,4},{7,6},{5,7},{3,5},{1,3},{0,1},{10,8},{12,10},{14... | collective-permute-start | bytes 1769480 | tf_op jit(solution)/shard_map/ppermute | solution.py:115
  23.0 14.3 %collective-permute-start.4 = (bf16[128,1536]{1,0:T(8,128)(2,1)S(1)}, bf16[128,1536]{1,0:T(8,128)(2,1)S(1)}, u32[]{:S(2)}, u32[]{:S(2)}) collective-permute-start(bf16[128,1536]{1,0:T(8,128)(2,1)S(1)} %bitcast.8), channel_id=1, source_target_pairs={{8,0},{0,8},{9,1},{1,9},{10,2},{2,10},{11,3},{3,11},{12,4},{4,12},... | collective-permute-start | bytes 1179656 | tf_op jit(solution)/shard_map/ppermute | solution.py:55
  24.5 14.3 %collective-permute-start.3 = (bf16[128,1536]{1,0:T(8,128)(2,1)S(1)}, bf16[128,1536]{1,0:T(8,128)(2,1)S(1)}, u32[]{:S(2)}, u32[]{:S(2)}) collective-permute-start(bf16[128,1536]{1,0:T(8,128)(2,1)S(1)} %bitcast.9), channel_id=1, source_target_pairs={{16,0},{0,16},{17,1},{1,17},{18,2},{2,18},{19,3},{3,19},{20,4},{4,... | collective-permute-start | bytes 1179656 | tf_op jit(solution)/shard_map/ppermute | solution.py:55
  24.5 0.7 copy-start.5
  25.2 0.7 copy-start.9
  25.9 0.7 copy-start.10
  35.3 13.8 %collective-permute-start.10 = (bf16[384,768]{1,0:T(8,128)(2,1)S(1)}, bf16[384,768]{1,0:T(8,128)(2,1)S(1)}, u32[]{:S(2)}, u32[]{:S(2)}) collective-permute-start(bf16[384,768]{1,0:T(8,128)(2,1)S(1)} %collective-permute-done.8.refs_3_), channel_id=1, source_target_pairs={{0,2},{2,4},{4,6},{6,7},{7,5},{5,3},{3,1},{1,0},{8,10},{10,12},{12... | collective-permute-start | bytes 1769480 | tf_op jit(solution)/shard_map/ppermute | solution.py:114
  36.8 12.6 %collective-permute-start.11 = (bf16[384,768]{1,0:T(8,128)(2,1)S(1)}, bf16[384,768]{1,0:T(8,128)(2,1)S(1)}, u32[]{:S(2)}, u32[]{:S(2)}) collective-permute-start(bf16[384,768]{1,0:T(8,128)(2,1)S(1)} %collective-permute-done.9.refs_4_), channel_id=1, source_target_pairs={{2,0},{4,2},{6,4},{7,6},{5,7},{3,5},{1,3},{0,1},{10,8},{12,10},{14... | collective-permute-start | bytes 1769480 | tf_op jit(solution)/shard_map/ppermute | solution.py:115
  37.3 1.7 %collective-permute-start.15 = (bf16[128,1536]{1,0:T(8,128)(2,1)S(1)}, bf16[128,1536]{1,0:T(8,128)(2,1)S(1)}, u32[]{:S(2)}, u32[]{:S(2)}) collective-permute-start(bf16[128,1536]{1,0:T(8,128)(2,1)S(1)} %get-tuple-element.80.refs_9_), channel_id=1, source_target_pairs={{16,0},{0,16},{17,1},{1,17},{18,2},{2,18},{19,3},{3,19},{20,4},{4,... | collective-permute-start | bytes 1179656 | tf_op jit(solution)/shard_map/ppermute | solution.py:55
  37.4 11.5 %collective-permute-start.14 = (bf16[128,1536]{1,0:T(8,128)(2,1)S(1)}, bf16[128,1536]{1,0:T(8,128)(2,1)S(1)}, u32[]{:S(2)}, u32[]{:S(2)}) collective-permute-start(bf16[128,1536]{1,0:T(8,128)(2,1)S(1)} %get-tuple-element.80.refs_9_), channel_id=1, source_target_pairs={{8,0},{0,8},{9,1},{1,9},{10,2},{2,10},{11,3},{3,11},{12,4},{4,12},... | collective-permute-start | bytes 1179656 | tf_op jit(solution)/shard_map/ppermute | solution.py:55
  38.8 10.1 %collective-permute-start.5 = (bf16[128,1536]{1,0:T(8,128)(2,1)S(1)}, bf16[128,1536]{1,0:T(8,128)(2,1)S(1)}, u32[]{:S(2)}, u32[]{:S(2)}) collective-permute-start(bf16[128,1536]{1,0:T(8,128)(2,1)S(1)} %collective-permute-done.4.refs_2_.refs_15_), channel_id=1, source_target_pairs={{16,0},{0,16},{17,1},{1,17},{18,2},{2,18},{19,3},{3,19},{20,4},{4,... | collective-permute-start | bytes 1179656 | tf_op jit(solution)/shard_map/ppermute | solution.py:55
  48.9 2.6 %collective-permute-start.16 = (bf16[128,1536]{1,0:T(8,128)(2,1)S(1)}, bf16[128,1536]{1,0:T(8,128)(2,1)S(1)}, u32[]{:S(2)}, u32[]{:S(2)}) collective-permute-start(bf16[128,1536]{1,0:T(8,128)(2,1)S(1)} %collective-permute-done.14.refs_7_), channel_id=1, source_target_pairs={{16,0},{0,16},{17,1},{1,17},{18,2},{2,18},{19,3},{3,19},{20,4},{4,... | collective-permute-start | bytes 1179656 | tf_op jit(solution)/shard_map/ppermute | solution.py:55
  49.4 10.6 %copy-start.4 = (f32[3072]{0:T(1024)S(1)}, f32[3072]{0:T(1024)}, u32[]{:S(2)}) copy-start(f32[3072]{0:T(1024)} %refs_17_.1) | copy-start | bytes 36868
  49.4 9.3 %collective-permute-start.12 = (bf16[192,768]{1,0:T(8,128)(2,1)S(1)}, bf16[192,768]{1,0:T(8,128)(2,1)S(1)}, u32[]{:S(2)}, u32[]{:S(2)}) collective-permute-start(bf16[192,768]{1,0:T(8,128)(2,1)S(1)} %slice.8), channel_id=1, source_target_pairs={{0,2},{2,4},{4,6},{6,7},{7,5},{5,3},{3,1},{1,0},{8,10},{10,12},{12... | collective-permute-start | bytes 884744 | tf_op jit(solution)/shard_map/ppermute | solution.py:124
  51.0 8.9 %collective-permute-start.13 = (bf16[192,768]{1,0:T(8,128)(2,1)S(1)}, bf16[192,768]{1,0:T(8,128)(2,1)S(1)}, u32[]{:S(2)}, u32[]{:S(2)}) collective-permute-start(bf16[192,768]{1,0:T(8,128)(2,1)S(1)} %slice.9), channel_id=1, source_target_pairs={{2,0},{4,2},{6,4},{7,6},{5,7},{3,5},{1,3},{0,1},{10,8},{12,10},{14... | collective-permute-start | bytes 884744 | tf_op jit(solution)/shard_map/ppermute | solution.py:124
  62.0 3.5 %copy-start.8 = (f32[1536]{0:T(1024)S(1)}, f32[1536]{0:T(1024)}, u32[]{:S(2)}) copy-start(f32[1536]{0:T(1024)} %bias.3) | copy-start | bytes 18436
  62.0 1.8 %collective-permute-start.17 = (bf16[128,1536]{1,0:T(8,128)(2,1)S(1)}, bf16[128,1536]{1,0:T(8,128)(2,1)S(1)}, u32[]{:S(2)}, u32[]{:S(2)}) collective-permute-start(bf16[128,1536]{1,0:T(8,128)(2,1)S(1)} %get-tuple-element.93), channel_id=1, source_target_pairs={{16,0},{0,16},{17,1},{1,17},{18,2},{2,18},{19,3},{3,19},{20,4},{4,... | collective-permute-start | bytes 1179656 | tf_op jit(solution)/shard_map/ppermute | solution.py:55
  63.9 11.2 %collective-permute-start.18 = (bf16[128,1536]{1,0:T(8,128)(2,1)S(1)}, bf16[128,1536]{1,0:T(8,128)(2,1)S(1)}, u32[]{:S(2)}, u32[]{:S(2)}) collective-permute-start(bf16[128,1536]{1,0:T(8,128)(2,1)S(1)} %add_rounded.2), channel_id=1, source_target_pairs={{8,0},{0,8},{9,1},{1,9},{10,2},{2,10},{11,3},{3,11},{12,4},{4,12},... | collective-permute-start | bytes 1179656 | tf_op jit(solution)/shard_map/ppermute | solution.py:55
  65.4 11.2 %copy-start.6 = (f32[1536]{0:T(1024)S(1)}, f32[1536]{0:T(1024)}, u32[]{:S(2)}) copy-start(f32[1536]{0:T(1024)} %refs_6_.3) | copy-start | bytes 18436
  70.1 1.5 %collective-permute-start.19 = (bf16[64,1536]{1,0:T(8,128)(2,1)S(1)}, bf16[64,1536]{1,0:T(8,128)(2,1)S(1)}, u32[]{:S(2)}, u32[]{:S(2)}) collective-permute-start(bf16[64,1536]{1,0:T(8,128)(2,1)S(1)} %get-tuple-element.98), channel_id=1, source_target_pairs={{16,0},{0,16},{17,1},{1,17},{18,2},{2,18},{19,3},{3,19},{20,4},{4,... | collective-permute-start | bytes 589832 | tf_op jit(solution)/shard_map/ppermute | solution.py:55
  70.2 1.7 %collective-permute-start.20 = (bf16[64,1536]{1,0:T(8,128)(2,1)S(1)}, bf16[64,1536]{1,0:T(8,128)(2,1)S(1)}, u32[]{:S(2)}, u32[]{:S(2)}) collective-permute-start(bf16[64,1536]{1,0:T(8,128)(2,1)S(1)} %get-tuple-element.99), channel_id=1, source_target_pairs={{16,0},{0,16},{17,1},{1,17},{18,2},{2,18},{19,3},{3,19},{20,4},{4,... | collective-permute-start | bytes 589832 | tf_op jit(solution)/shard_map/ppermute | solution.py:55
  70.7 1.5 %collective-permute-start.21 = (bf16[64,1536]{1,0:T(8,128)(2,1)S(1)}, bf16[64,1536]{1,0:T(8,128)(2,1)S(1)}, u32[]{:S(2)}, u32[]{:S(2)}) collective-permute-start(bf16[64,1536]{1,0:T(8,128)(2,1)S(1)} %get-tuple-element.103), channel_id=1, source_target_pairs={{16,0},{0,16},{17,1},{1,17},{18,2},{2,18},{19,3},{3,19},{20,4},{4,... | collective-permute-start | bytes 589832 | tf_op jit(solution)/shard_map/ppermute | solution.py:55
  70.8 1.7 %collective-permute-start.22 = (bf16[64,1536]{1,0:T(8,128)(2,1)S(1)}, bf16[64,1536]{1,0:T(8,128)(2,1)S(1)}, u32[]{:S(2)}, u32[]{:S(2)}) collective-permute-start(bf16[64,1536]{1,0:T(8,128)(2,1)S(1)} %get-tuple-element.104), channel_id=1, source_target_pairs={{16,0},{0,16},{17,1},{1,17},{18,2},{2,18},{19,3},{3,19},{20,4},{4,... | collective-permute-start | bytes 589832 | tf_op jit(solution)/shard_map/ppermute | solution.py:55
  71.6 5.0 %collective-permute-start.23 = (bf16[64,1536]{1,0:T(8,128)(2,1)S(1)}, bf16[64,1536]{1,0:T(8,128)(2,1)S(1)}, u32[]{:S(2)}, u32[]{:S(2)}) collective-permute-start(bf16[64,1536]{1,0:T(8,128)(2,1)S(1)} %get-tuple-element.109), channel_id=1, source_target_pairs={{16,0},{0,16},{17,1},{1,17},{18,2},{2,18},{19,3},{3,19},{20,4},{4,... | collective-permute-start | bytes 589832 | tf_op jit(solution)/shard_map/ppermute | solution.py:55
  71.9 4.7 %collective-permute-start.24 = (bf16[64,1536]{1,0:T(8,128)(2,1)S(1)}, bf16[64,1536]{1,0:T(8,128)(2,1)S(1)}, u32[]{:S(2)}, u32[]{:S(2)}) collective-permute-start(bf16[64,1536]{1,0:T(8,128)(2,1)S(1)} %get-tuple-element.110), channel_id=1, source_target_pairs={{16,0},{0,16},{17,1},{1,17},{18,2},{2,18},{19,3},{3,19},{20,4},{4,... | collective-permute-start | bytes 589832 | tf_op jit(solution)/shard_map/ppermute | solution.py:55
  75.1 8.2 %collective-permute-start.26 = (bf16[96,1536]{1,0:T(8,128)(2,1)S(1)}, bf16[96,1536]{1,0:T(8,128)(2,1)S(1)}, u32[]{:S(2)}, u32[]{:S(2)}) collective-permute-start(bf16[96,1536]{1,0:T(8,128)(2,1)S(1)} %get-tuple-element.117), channel_id=1, source_target_pairs={{8,0},{0,8},{9,1},{1,9},{10,2},{2,10},{11,3},{3,11},{12,4},{4,12},... | collective-permute-start | bytes 884744 | tf_op jit(solution)/shard_map/ppermute | solution.py:55
  81.1 2.0 %collective-permute-start.25 = (f32[32,1536]{1,0:T(8,128)S(1)}, f32[32,1536]{1,0:T(8,128)S(1)}, u32[]{:S(2)}, u32[]{:S(2)}) collective-permute-start(f32[32,1536]{1,0:T(8,128)S(1)} %get-tuple-element.116), channel_id=1, source_target_pairs={{0,16},{16,0},{1,17},{17,1},{2,18},{18,2},{3,19},{19,3},{4,20},{20... | collective-permute-start | bytes 589832 | tf_op jit(solution)/shard_map/ppermute | solution.py:50
  81.2 6.2 %collective-permute-start.30 = (bf16[3,16,1536]{2,1,0:T(8,128)(2,1)S(1)}, bf16[3,16,1536]{2,1,0:T(8,128)(2,1)S(1)}, u32[]{:S(2)}, u32[]{:S(2)}) collective-permute-start(bf16[3,16,1536]{2,1,0:T(8,128)(2,1)S(1)} %get-tuple-element.126), channel_id=1, source_target_pairs={{0,16},{8,24},{16,0},{24,8},{1,17},{9,25},{17,1},{25,9},{2,18},{10... | collective-permute-start | bytes 442376 | tf_op jit(solution)/shard_map/ppermute | solution.py:75
  81.7 5.7 %collective-permute-start.31 = (bf16[8,3,1536]{2,1,0:T(4,128)(2,1)S(1)}, bf16[8,3,1536]{2,1,0:T(4,128)(2,1)S(1)}, u32[]{:S(2)}, u32[]{:S(2)}) collective-permute-start(bf16[8,3,1536]{2,1,0:T(4,128)(2,1)S(1)} %get-tuple-element.127), channel_id=1, source_target_pairs={{0,8},{8,0},{16,24},{24,16},{1,9},{9,1},{17,25},{25,17},{2,10},{10... | collective-permute-start | bytes 221192 | tf_op jit(solution)/shard_map/ppermute | solution.py:75
  82.3 4.2 %collective-permute-start.32 = (bf16[3,3,1536]{2,1,0:T(4,128)(2,1)S(1)}, bf16[3,3,1536]{2,1,0:T(4,128)(2,1)S(1)}, u32[]{:S(2)}, u32[]{:S(2)}) collective-permute-start(bf16[3,3,1536]{2,1,0:T(4,128)(2,1)S(1)} %get-tuple-element.128), channel_id=1, source_target_pairs={{0,24},{8,16},{16,8},{24,0},{1,25},{9,17},{17,9},{25,1},{2,26},{10... | collective-permute-start | bytes 82952 | tf_op jit(solution)/shard_map/ppermute | solution.py:75
  83.3 7.3 %collective-permute-start.27 = (bf16[8,1536]{1,0:T(8,128)(2,1)S(1)}, bf16[8,1536]{1,0:T(8,128)(2,1)S(1)}, u32[]{:S(2)}, u32[]{:S(2)}) collective-permute-start(bf16[8,1536]{1,0:T(8,128)(2,1)S(1)} %get-tuple-element.122), channel_id=1, source_target_pairs={{0,1},{1,0},{2,3},{3,2},{4,5},{5,4},{6,7},{7,6},{8,9},{9,8},{10,11... | collective-permute-start | bytes 73736 | tf_op jit(solution)/shard_map/ppermute | solution.py:50
  83.9 6.7 %collective-permute-start.28 = (bf16[8,1536]{1,0:T(8,128)(2,1)S(1)}, bf16[8,1536]{1,0:T(8,128)(2,1)S(1)}, u32[]{:S(2)}, u32[]{:S(2)}) collective-permute-start(bf16[8,1536]{1,0:T(8,128)(2,1)S(1)} %get-tuple-element.123), channel_id=1, source_target_pairs={{0,8},{8,0},{1,9},{9,1},{2,10},{10,2},{3,11},{11,3},{4,12},{12,4},... | collective-permute-start | bytes 73736 | tf_op jit(solution)/shard_map/ppermute | solution.py:50
  86.4 5.0 %collective-permute-start.29 = (bf16[8,1536]{1,0:T(8,128)(2,1)S(1)}, bf16[8,1536]{1,0:T(8,128)(2,1)S(1)}, u32[]{:S(2)}, u32[]{:S(2)}) collective-permute-start(bf16[8,1536]{1,0:T(8,128)(2,1)S(1)} %get-tuple-element.124), channel_id=1, source_target_pairs={{0,9},{1,8},{2,11},{3,10},{4,13},{5,12},{6,15},{7,14},{8,1},{9,0},... | collective-permute-start | bytes 73736 | tf_op jit(solution)/shard_map/ppermute | solution.py:50
  91.4 9.1 %collective-permute-start.36 = (bf16[32,1536]{1,0:T(8,128)(2,1)S(1)}, bf16[32,1536]{1,0:T(8,128)(2,1)S(1)}, u32[]{:S(2)}, u32[]{:S(2)}) collective-permute-start(bf16[32,1536]{1,0:T(8,128)(2,1)S(1)} %get-tuple-element.132), channel_id=1, source_target_pairs={{8,0},{0,8},{9,1},{1,9},{10,2},{2,10},{11,3},{3,11},{12,4},{4,12},... | collective-permute-start | bytes 294920 | tf_op jit(solution)/shard_map/ppermute | solution.py:55
  92.3 7.6 %collective-permute-start.35 = (bf16[8,1536]{1,0:T(8,128)(2,1)S(1)}, bf16[8,1536]{1,0:T(8,128)(2,1)S(1)}, u32[]{:S(2)}, u32[]{:S(2)}) collective-permute-start(bf16[8,1536]{1,0:T(8,128)(2,1)S(1)} %add_pairs.2.refs_0_), channel_id=1, source_target_pairs={{0,6},{1,7},{2,4},{3,5},{4,2},{5,3},{6,0},{7,1},{8,14},{9,15},{10,... | collective-permute-start | bytes 73736 | tf_op jit(solution)/shard_map/ppermute | solution.py:50
  95.7 4.7 %collective-permute-start.34 = (bf16[8,1536]{1,0:T(8,128)(2,1)S(1)}, bf16[8,1536]{1,0:T(8,128)(2,1)S(1)}, u32[]{:S(2)}, u32[]{:S(2)}) collective-permute-start(bf16[8,1536]{1,0:T(8,128)(2,1)S(1)} %add_pairs.2.refs_0_), channel_id=1, source_target_pairs={{0,4},{1,5},{2,6},{3,7},{4,0},{5,1},{6,2},{7,3},{8,12},{9,13},{10,... | collective-permute-start | bytes 73736 | tf_op jit(solution)/shard_map/ppermute | solution.py:50
  95.7 4.7 %collective-permute-start.33 = (bf16[8,1536]{1,0:T(8,128)(2,1)S(1)}, bf16[8,1536]{1,0:T(8,128)(2,1)S(1)}, u32[]{:S(2)}, u32[]{:S(2)}) collective-permute-start(bf16[8,1536]{1,0:T(8,128)(2,1)S(1)} %add_pairs.2.refs_0_), channel_id=1, source_target_pairs={{0,2},{1,3},{2,0},{3,1},{4,6},{5,7},{6,4},{7,5},{8,10},{9,11},{10,... | collective-permute-start | bytes 73736 | tf_op jit(solution)/shard_map/ppermute | solution.py:50
  100.5 5.1 %collective-permute-start.39 = (f32[8,1536]{1,0:T(8,128)S(1)}, f32[8,1536]{1,0:T(8,128)S(1)}, u32[]{:S(2)}, u32[]{:S(2)}) collective-permute-start(f32[8,1536]{1,0:T(8,128)S(1)} %add_pairs.3.refs_0_), channel_id=1, source_target_pairs={{0,9},{1,8},{2,11},{3,10},{4,13},{5,12},{6,15},{7,14},{8,1},{9,0},... | collective-permute-start | bytes 147464 | tf_op jit(solution)/shard_map/ppermute | solution.py:50
  102.0 4.1 %collective-permute-start.38 = (f32[8,1536]{1,0:T(8,128)S(1)}, f32[8,1536]{1,0:T(8,128)S(1)}, u32[]{:S(2)}, u32[]{:S(2)}) collective-permute-start(f32[8,1536]{1,0:T(8,128)S(1)} %add_pairs.3.refs_0_), channel_id=1, source_target_pairs={{0,8},{8,0},{1,9},{9,1},{2,10},{10,2},{3,11},{11,3},{4,12},{12,4},... | collective-permute-start | bytes 147464 | tf_op jit(solution)/shard_map/ppermute | solution.py:50
  102.9 4.1 %collective-permute-start.37 = (f32[8,1536]{1,0:T(8,128)S(1)}, f32[8,1536]{1,0:T(8,128)S(1)}, u32[]{:S(2)}, u32[]{:S(2)}) collective-permute-start(f32[8,1536]{1,0:T(8,128)S(1)} %add_pairs.3.refs_0_), channel_id=1, source_target_pairs={{0,1},{1,0},{2,3},{3,2},{4,5},{5,4},{6,7},{7,6},{8,9},{9,8},{10,11... | collective-permute-start | bytes 147464 | tf_op jit(solution)/shard_map/ppermute | solution.py:50
  104.0 4.0 %collective-permute-start.40 = (f32[8,1536]{1,0:T(8,128)S(1)}, f32[8,1536]{1,0:T(8,128)S(1)}, u32[]{:S(2)}, u32[]{:S(2)}) collective-permute-start(f32[8,1536]{1,0:T(8,128)S(1)} %add_pairs.3.refs_0_), channel_id=1, source_target_pairs={{0,16},{16,0},{1,17},{17,1},{2,18},{18,2},{3,19},{19,3},{4,20},{20... | collective-permute-start | bytes 147464 | tf_op jit(solution)/shard_map/ppermute | solution.py:50
  105.5 2.5 %collective-permute-start.43 = (f32[8,1536]{1,0:T(8,128)S(1)}, f32[8,1536]{1,0:T(8,128)S(1)}, u32[]{:S(2)}, u32[]{:S(2)}) collective-permute-start(f32[8,1536]{1,0:T(8,128)S(1)} %collective-permute-done.39.refs_3_), channel_id=1, source_target_pairs={{0,16},{16,0},{1,17},{17,1},{2,18},{18,2},{3,19},{19,3},{4,20},{20... | collective-permute-start | bytes 147464 | tf_op jit(solution)/shard_map/ppermute | solution.py:50
  106.1 2.0 %collective-permute-start.42 = (f32[8,1536]{1,0:T(8,128)S(1)}, f32[8,1536]{1,0:T(8,128)S(1)}, u32[]{:S(2)}, u32[]{:S(2)}) collective-permute-start(f32[8,1536]{1,0:T(8,128)S(1)} %collective-permute-done.38.refs_2_), channel_id=1, source_target_pairs={{0,16},{16,0},{1,17},{17,1},{2,18},{18,2},{3,19},{19,3},{4,20},{20... | collective-permute-start | bytes 147464 | tf_op jit(solution)/shard_map/ppermute | solution.py:50
  107.0 1.2 %collective-permute-start.41 = (f32[8,1536]{1,0:T(8,128)S(1)}, f32[8,1536]{1,0:T(8,128)S(1)}, u32[]{:S(2)}, u32[]{:S(2)}) collective-permute-start(f32[8,1536]{1,0:T(8,128)S(1)} %collective-permute-done.37.refs_1_), channel_id=1, source_target_pairs={{0,16},{16,0},{1,17},{17,1},{2,18},{18,2},{3,19},{19,3},{4,20},{20... | collective-permute-start | bytes 147464 | tf_op jit(solution)/shard_map/ppermute | solution.py:50

commit v7 on v6

--- a/solution.py
+++ b/solution.py
@@ -125,11 +125,12 @@
     return pieces, upper, lower
 
 
-def gather_tile(a):
+def gather_tile(a, own_after):
     out = []
     for t in range(lax.axis_size("sy")):
         mine = a if t == 0 else after(shift(a, "sy", t), out[-1])
-        out.append([mine] + [shift(mine, "sx", s) for s in range(1, lax.axis_size("sx"))])
+        sent = after(a, own_after) if t == 0 else mine
+        out.append([mine] + [shift(sent, "sx", s) for s in range(1, lax.axis_size("sx"))])
     return [piece for group in out for piece in group]
 
 
@@ -857,12 +858,12 @@
     down_block = lax.dynamic_slice_in_dim(w_down, quarter * hidden, hidden, 0).T
     scaled, *edges = prepare(x_code[0], x_exp[0])
     edges = list(exchange_edges(dict(zip(edge_keys(), edges, strict=True))).values())
-    cots = gather_tile(after(cotangent.reshape(spots, chans), edges))
+    cots = gather_tile(after(cotangent.reshape(spots, chans), edges), [])
     d_mlp = scale_part(cots, layer_scale)
     padded, normed, rstd, ln_out = conv_norm(scaled, edges, dw_kernel, dw_bias, ln_gain, ln_bias)
     blocks = jnp.concatenate([up_block, down_block], 0)
     pieces, upper, lower = ring_gather(blocks, edges, ln_out, d_mlp)
-    lns = gather_tile(ln_out)
+    lns = gather_tile(ln_out, cots[n_near])
     early = early_part(pieces[:-2], upper[:-1], lower[:-1], lns[n_near:], d_mlp)
     far_act, *far = far_part(*pieces[-2:], early, b_up, tiles - n_near)
 

time: 110 us -> 107 us (0.973)
  waiting for transfers between devices: 40 us -> 37 us
    ppermute x16, waiting for transfers between devices: 15.1 us -> 11.6 us  [shift(): return lax.ppermute(a, axis, [((i + k) % n, i) for i in range(n)])]
    ppermute x1, waiting for transfers between devices: 3.99 us -> 1.47 us  [ring_gather(): lax.ppermute(one, 'fsdp', forth)]
    ppermute x3, waiting for transfers between devices: 3.93 us -> 6.38 us  [ring_gather(): one = lax.ppermute(one, 'fsdp', forth)]
  transfers between devices with their start and end apart: 44 -> 44, of which waited for: 23 -> 22; matrix products, arithmetic and copies ran while one was open for 1% -> 1% of each run, Pallas kernels for 25% -> 25%
where the time goes in v7:
time: 107 us; the launch traced here: 106 us
  waiting for transfers between devices  37 us (35%)
  starting transfers between devices  33.2 us (31%)
  Pallas kernels  29.8 us (28%)
  local copies, waits for them, and re-layouts  5.44 us (5%)
    ppermute x16, waiting for transfers between devices, shift(): return lax.ppermute(a, axis, [((i + k) % n, i) for i in range(n)])  11.6 us
    ppermute x14, starting transfers between devices, swap(): return lax.ppermute(a, axes, [(i, i ^ mask) for i in range(total)])  11.1 us
    ppermute x16, starting transfers between devices, shift(): return lax.ppermute(a, axis, [((i + k) % n, i) for i in range(n)])  8.91 us
    ppermute x3, waiting for transfers between devices, ring_gather(): two = lax.ppermute(two, 'fsdp', back)  7.2 us
    ppermute x3, waiting for transfers between devices, ring_gather(): one = lax.ppermute(one, 'fsdp', forth)  6.38 us
    pallas_call x2, Pallas kernels, conv_back(): pl.pallas_call(functools.partial(conv_back_kernel, begin, count), out_sha...  6.37 us
    pallas_call x1, Pallas kernels, conv_norm(): pl.pallas_call(conv_norm_kernel, out_shape=(shaped((rows + 2 * HALO, cols...  6.05 us
    ppermute x3, starting transfers between devices, ring_gather(): two = lax.ppermute(two, 'fsdp', back)  5.15 us
  transfers between devices with their start and end apart: 44, of which 22 were waited for; matrix products, arithmetic and copies ran while one was open for 1% of the time, Pallas kernels for 25%

profile of v7, /device:TPU:0, one launch (start us, length us, event | category | flops | bytes accessed | tf_op | source)
XLA Modules:
  0.0 106.4 jit_solution(12891895440659685790)
XLA Ops:
  0.7 1.3 %copy-done = bf16[192,3072]{1,0:T(8,128)(2,1)S(1)} copy-done((bf16[192,3072]{1,0:T(8,128)(2,1)S(1)}, bf16[192,3072]{1,0:T(8,128)(2,1)}, u32[]{:S(2)}) %copy-start) | copy-done | bytes 1179672
  2.0 1.1 %dynamic-slice_bitcast_fusion = bf16[192,768]{1,0:T(8,128)(2,1)S(1)} fusion(bf16[3072,192]{0,1:T(8,128)(2,1)} %param.20, s32[]{:T(128)S(6)} %select_n.4), kind=kLoop, calls=%fused_computation.1 | loop fusion | bytes 589828 | tf_op jit(solution)/shard_map/transpose | solution.py:858
  3.1 3.0 %collective-permute-start.7 = (bf16[384,768]{1,0:T(8,128)(2,1)S(1)}, bf16[384,768]{1,0:T(8,128)(2,1)S(1)}, u32[]{:S(2)}, u32[]{:S(2)}) collective-permute-start(bf16[384,768]{1,0:T(8,128)(2,1)S(1)} %pad_maximum_fusion.refs_0_), channel_id=1, source_target_pairs={{2,0},{4,2},{6,4},{7,6},{5,7},{3,5},{1,3},{0,1},{10,8},{12,10},{14... | collective-permute-start | bytes 1769480 | tf_op jit(solution)/shard_map/ppermute | solution.py:115
  6.2 0.9 copy.18
  7.2 0.5 prepare.1
  7.8 1.9 %collective-permute-start.1 = (bf16[8,3,1536]{2,1,0:T(4,128)(2,1)S(1)}, bf16[8,3,1536]{2,1,0:T(4,128)(2,1)S(1)}, u32[]{:S(2)}, u32[]{:S(2)}) collective-permute-start(bf16[8,3,1536]{2,1,0:T(4,128)(2,1)S(1)} %get-tuple-element.75), channel_id=1, source_target_pairs={{0,8},{8,0},{16,24},{24,16},{1,9},{9,1},{17,25},{25,17},{2,10},{10... | collective-permute-start | bytes 221192 | tf_op jit(solution)/shard_map/ppermute | solution.py:75
  9.8 3.8 %collective-permute-done.2.refs_2_ = bf16[3,3,1536]{2,1,0:T(4,128)(2,1)S(1)} collective-permute-done((bf16[3,3,1536]{2,1,0:T(4,128)(2,1)S(1)}, bf16[3,3,1536]{2,1,0:T(4,128)(2,1)S(1)}, u32[]{:S(2)}, u32[]{:S(2)}) %collective-permute-start.2) | collective-permute-done | bytes 27680 | tf_op jit(solution)/shard_map/ppermute | solution.py:75
  13.6 5.9 %collective-permute-done.7.refs_2_ = bf16[384,768]{1,0:T(8,128)(2,1)S(1)} collective-permute-done((bf16[384,768]{1,0:T(8,128)(2,1)S(1)}, bf16[384,768]{1,0:T(8,128)(2,1)S(1)}, u32[]{:S(2)}, u32[]{:S(2)}) %collective-permute-start.7) | collective-permute-done | bytes 589856 | tf_op jit(solution)/shard_map/ppermute | solution.py:115
  19.5 1.5 %collective-permute-done.6.refs_1_ = bf16[384,768]{1,0:T(8,128)(2,1)} collective-permute-done((bf16[384,768]{1,0:T(8,128)(2,1)S(1)}, bf16[384,768]{1,0:T(8,128)(2,1)}, u32[]{:S(2)}, u32[]{:S(2)}) %collective-permute-start.6) | collective-permute-done | bytes 589856 | tf_op jit(solution)/shard_map/ppermute | solution.py:114
  21.0 0.4 collective-permute-start.8
  21.4 1.6 %collective-permute-start.9 = (bf16[384,768]{1,0:T(8,128)(2,1)S(1)}, bf16[384,768]{1,0:T(8,128)(2,1)S(1)}, u32[]{:S(2)}, u32[]{:S(2)}) collective-permute-start(bf16[384,768]{1,0:T(8,128)(2,1)S(1)} %collective-permute-done.7.refs_2_), channel_id=1, source_target_pairs={{2,0},{4,2},{6,4},{7,6},{5,7},{3,5},{1,3},{0,1},{10,8},{12,10},{14... | collective-permute-start | bytes 1769480 | tf_op jit(solution)/shard_map/ppermute | solution.py:115
  23.0 1.5 %collective-permute-start.4 = (bf16[128,1536]{1,0:T(8,128)(2,1)S(1)}, bf16[128,1536]{1,0:T(8,128)(2,1)S(1)}, u32[]{:S(2)}, u32[]{:S(2)}) collective-permute-start(bf16[128,1536]{1,0:T(8,128)(2,1)S(1)} %bitcast.9), channel_id=1, source_target_pairs={{8,0},{0,8},{9,1},{1,9},{10,2},{2,10},{11,3},{3,11},{12,4},{4,12},... | collective-permute-start | bytes 1179656 | tf_op jit(solution)/shard_map/ppermute | solution.py:55
  24.5 0.7 copy-done.5
  25.2 0.7 copy-done.9
  25.9 0.7 copy-done.10
  26.6 6.0 %conv_norm.1 = (f32[14,32,1536]{2,1,0:T(8,128)S(1)}, f32[128,1536]{1,0:T(8,128)S(1)}, f32[128,128]{1,0:T(8,128)S(1)}, bf16[128,1536]{1,0:T(8,128)(2,1)S(1)}) custom-call(bf16[8,16,1536]{2,1,0:T(8,128)(2,1)S(1)} %get-tuple-element.73.own.scaled, bf16[3,16,1536]{2,1,0:T(8,128)(2,1)S(1)} %collective-permute-done.refs_0_, ...), custom_call_target="tpu_custom_call" | custom-call | flops 1 | bytes 1 | tf_op jit(solution)/shard_map/conv_norm/pallas_call | solution.py:319
  32.7 2.4 %collective-permute-done.8.refs_3_ = bf16[384,768]{1,0:T(8,128)(2,1)S(1)} collective-permute-done((bf16[384,768]{1,0:T(8,128)(2,1)}, bf16[384,768]{1,0:T(8,128)(2,1)S(1)}, u32[]{:S(2)}, u32[]{:S(2)}) %collective-permute-start.8) | collective-permute-done | bytes 589856 | tf_op jit(solution)/shard_map/ppermute | solution.py:114
  35.1 0.2 collective-permute-done.9.refs_4_
  35.3 1.5 %collective-permute-start.10 = (bf16[384,768]{1,0:T(8,128)(2,1)S(1)}, bf16[384,768]{1,0:T(8,128)(2,1)S(1)}, u32[]{:S(2)}, u32[]{:S(2)}) collective-permute-start(bf16[384,768]{1,0:T(8,128)(2,1)S(1)} %collective-permute-done.8.refs_3_), channel_id=1, source_target_pairs={{0,2},{2,4},{4,6},{6,7},{7,5},{5,3},{3,1},{1,0},{8,10},{10,12},{12... | collective-permute-start | bytes 1769480 | tf_op jit(solution)/shard_map/ppermute | solution.py:114
  36.8 0.5 collective-permute-start.11
  37.3 1.4 %collective-permute-start.14 = (bf16[128,1536]{1,0:T(8,128)(2,1)S(1)}, bf16[128,1536]{1,0:T(8,128)(2,1)S(1)}, u32[]{:S(2)}, u32[]{:S(2)}) collective-permute-start(bf16[128,1536]{1,0:T(8,128)(2,1)S(1)} %get-tuple-element.86.refs_9_), channel_id=1, source_target_pairs={{8,0},{0,8},{9,1},{1,9},{10,2},{2,10},{11,3},{3,11},{12,4},{4,12},... | collective-permute-start | bytes 1179656 | tf_op jit(solution)/shard_map/ppermute | solution.py:55
  38.8 0.5 collective-permute-start.5
  39.3 6.3 %collective-permute-done.14.refs_7_ = bf16[128,1536]{1,0:T(8,128)(2,1)S(1)} collective-permute-done((bf16[128,1536]{1,0:T(8,128)(2,1)S(1)}, bf16[128,1536]{1,0:T(8,128)(2,1)S(1)}, u32[]{:S(2)}, u32[]{:S(2)}) %collective-permute-start.14) | collective-permute-done | bytes 393248 | tf_op jit(solution)/shard_map/ppermute | solution.py:55
  45.6 0.3 scale_part.1.refs_9_.refs_11_
  45.9 2.5 %collective-permute-done.10.refs_5_ = bf16[384,768]{1,0:T(8,128)(2,1)S(1)} collective-permute-done((bf16[384,768]{1,0:T(8,128)(2,1)S(1)}, bf16[384,768]{1,0:T(8,128)(2,1)S(1)}, u32[]{:S(2)}, u32[]{:S(2)}) %collective-permute-start.10) | collective-permute-done | bytes 589856 | tf_op jit(solution)/shard_map/ppermute | solution.py:114
  48.3 1.0 collective-permute-done.11.refs_6_
  49.4 1.6 %collective-permute-start.12 = (bf16[192,768]{1,0:T(8,128)(2,1)S(1)}, bf16[192,768]{1,0:T(8,128)(2,1)S(1)}, u32[]{:S(2)}, u32[]{:S(2)}) collective-permute-start(bf16[192,768]{1,0:T(8,128)(2,1)S(1)} %slice.8), channel_id=1, source_target_pairs={{0,2},{2,4},{4,6},{6,7},{7,5},{5,3},{3,1},{1,0},{8,10},{10,12},{12... | collective-permute-start | bytes 884744 | tf_op jit(solution)/shard_map/ppermute | solution.py:124
  51.0 0.5 collective-permute-start.13
  51.5 3.2 %early_part.1 = (f32[256,768]{1,0:T(8,128)S(1)}, f32[256,768]{1,0:T(8,128)S(1)}, bf16[1536,768]{1,0:T(8,128)(2,1)S(1)}, bf16[1536,256]{1,0:T(8,128)(2,1)S(1)}, b...) custom-call(bf16[384,768]{1,0:T(8,128)(2,1)S(1)} %pad_maximum_fusion.refs_0_, ...), custom_call_target="tpu_custom_call" | custom-call | flops 1 | bytes 1 | tf_op jit(solution)/shard_map/early_part/pallas_call | solution.py:594
  54.7 1.5 %collective-permute-done.12.up_last.refs_7_ = bf16[192,768]{1,0:T(8,128)(2,1)S(1)} collective-permute-done((bf16[192,768]{1,0:T(8,128)(2,1)S(1)}, bf16[192,768]{1,0:T(8,128)(2,1)S(1)}, u32[]{:S(2)}, u32[]{:S(2)}) %collective-permute-start.12) | collective-permute-done | bytes 294944 | tf_op jit(solution)/shard_map/ppermute | solution.py:124
  56.2 1.6 %collective-permute-done.13.down_last.refs_8_ = bf16[192,768]{1,0:T(8,128)(2,1)S(1)} collective-permute-done((bf16[192,768]{1,0:T(8,128)(2,1)S(1)}, bf16[192,768]{1,0:T(8,128)(2,1)S(1)}, u32[]{:S(2)}, u32[]{:S(2)}) %collective-permute-start.13) | collective-permute-done | bytes 294944 | tf_op jit(solution)/shard_map/ppermute | solution.py:124
  57.8 2.0 %far_part.1 = (bf16[256,768]{1,0:T(8,128)(2,1)S(1)}, bf16[128,1536]{1,0:T(8,128)(2,1)S(1)}, bf16[128,1536]{1,0:T(8,128)(2,1)S(1)}) custom-call(bf16[192,768]{1,0:T(8,128)(2,1)S(1)} %collective-permute-done.12.up_last.refs_7_, bf16[192,768]{1,0:T(8,128)(2,1)S(1)} %collective-permute-done.13.down_last.refs_8_, f32[256,768]{1,0:T(8,128)S(1)} %get-tuple-element.88.pre, ...), custom_call_target="tpu_custom_call" | custom-call | flops 1 | bytes 1 | tf_op jit(solution)/shard_map/far_part/pallas_call | solution.py:631
  59.9 1.7 %collective-permute-done.17.refs_1_ = bf16[128,1536]{1,0:T(8,128)(2,1)S(1)} collective-permute-done((bf16[128,1536]{1,0:T(8,128)(2,1)S(1)}, bf16[128,1536]{1,0:T(8,128)(2,1)S(1)}, u32[]{:S(2)}, u32[]{:S(2)}) %collective-permute-start.17) | collective-permute-done | bytes 393248 | tf_op jit(solution)/shard_map/ppermute | solution.py:55
  61.7 1.6 %collective-permute-start.18 = (bf16[128,1536]{1,0:T(8,128)(2,1)S(1)}, bf16[128,1536]{1,0:T(8,128)(2,1)S(1)}, u32[]{:S(2)}, u32[]{:S(2)}) collective-permute-start(bf16[128,1536]{1,0:T(8,128)(2,1)S(1)} %add_rounded.2), channel_id=1, source_target_pairs={{8,0},{0,8},{9,1},{1,9},{10,2},{2,10},{11,3},{3,11},{12,4},{4,12},... | collective-permute-start | bytes 1179656 | tf_op jit(solution)/shard_map/ppermute | solution.py:55
  63.2 4.7 %rest_part.1 = (bf16[128,1536]{1,0:T(8,128)(2,1)S(1)}, bf16[64,1536]{1,0:T(8,128)(2,1)S(1)}, bf16[64,1536]{1,0:T(8,128)(2,1)S(1)}, bf16[128,1536]{1,0:T(8,128)(2...) custom-call(bf16[384,768]{1,0:T(8,128)(2,1)S(1)} %pad_maximum_fusion, ...), custom_call_target="tpu_custom_call" | custom-call | flops 1 | bytes 1 | tf_op jit(solution)/shard_map/rest_part/pallas_call | solution.py:685
  68.0 0.5 collective-permute-start.20
  68.6 0.4 collective-permute-start.22
  69.0 0.4 collective-permute-done.19.refs_1_
  69.7 0.2 collective-permute-start.24
  70.3 2.6 %collective-permute-done.18.refs_3_ = bf16[128,1536]{1,0:T(8,128)(2,1)S(1)} collective-permute-done((bf16[128,1536]{1,0:T(8,128)(2,1)S(1)}, bf16[128,1536]{1,0:T(8,128)(2,1)S(1)}, u32[]{:S(2)}, u32[]{:S(2)}) %collective-permute-start.18) | collective-permute-done | bytes 393248 | tf_op jit(solution)/shard_map/ppermute | solution.py:55
  72.9 1.5 %collective-permute-start.26 = (bf16[96,1536]{1,0:T(8,128)(2,1)S(1)}, bf16[96,1536]{1,0:T(8,128)(2,1)S(1)}, u32[]{:S(2)}, u32[]{:S(2)}) collective-permute-start(bf16[96,1536]{1,0:T(8,128)(2,1)S(1)} %get-tuple-element.119), channel_id=1, source_target_pairs={{8,0},{0,8},{9,1},{1,9},{10,2},{2,10},{11,3},{3,11},{12,4},{4,12},... | collective-permute-start | bytes 884744 | tf_op jit(solution)/shard_map/ppermute | solution.py:55
  74.4 4.5 %norm_back.1 = (f32[8,16,1536]{2,1,0:T(8,128)S(1)}, f32[32,1536]{1,0:T(8,128)S(1)}, f32[32,1536]{1,0:T(8,128)S(1)}, bf16[3,16,1536]{2,1,0:T(8,128)(2,1)S(1)}, bf...) custom-call(bf16[128,1536]{1,0:T(8,128)(2,1)S(1)} %get-tuple-element.110.refs_0_, ...), custom_call_target="tpu_custom_call" | custom-call | flops 1 | bytes 1 | tf_op jit(solution)/shard_map/norm_back/pallas_call | solution.py:407
  79.0 0.5 collective-permute-start.30
  79.5 0.5 collective-permute-start.31
  80.1 0.9 collective-permute-start.32
  81.1 0.5 collective-permute-start.27
  81.7 1.5 %collective-permute-start.28 = (bf16[8,1536]{1,0:T(8,128)(2,1)S(1)}, bf16[8,1536]{1,0:T(8,128)(2,1)S(1)}, u32[]{:S(2)}, u32[]{:S(2)}) collective-permute-start(bf16[8,1536]{1,0:T(8,128)(2,1)S(1)} %get-tuple-element.125), channel_id=1, source_target_pairs={{0,8},{8,0},{1,9},{9,1},{2,10},{10,2},{3,11},{11,3},{4,12},{12,4},... | collective-permute-start | bytes 73736 | tf_op jit(solution)/shard_map/ppermute | solution.py:50
  83.2 1.1 %collective-permute-done.32.refs_2_ = bf16[3,3,1536]{2,1,0:T(4,128)(2,1)S(1)} collective-permute-done((bf16[3,3,1536]{2,1,0:T(4,128)(2,1)S(1)}, bf16[3,3,1536]{2,1,0:T(4,128)(2,1)S(1)}, u32[]{:S(2)}, u32[]{:S(2)}) %collective-permute-start.32) | collective-permute-done | bytes 27680 | tf_op jit(solution)/shard_map/ppermute | solution.py:75
  84.2 1.0 collective-permute-start.29
  85.2 3.2 %conv_back.2.refs_5_ = bf16[8,16,1536]{2,1,0:T(8,128)(2,1)} custom-call(f32[8,16,1536]{2,1,0:T(8,128)S(1)} %get-tuple-element.127.own, bf16[3,16,1536]{2,1,0:T(8,128)(2,1)S(1)} %collective-permute-done.30.refs_0_, bf16[8,3,1536]{2,1,0:T(4,128)(2,1)S(1)} %collective-permute-done.31.refs_1_, bf16[3,3,1536]{2,1,0:T(4,128)(2,1)S(1)} %collective-permute-done.32.refs_2_, ...), custom_call_target="tpu_custom_call" | custom-call | flops 1 | bytes 1 | tf_op jit(solution)/shard_map/conv_back/pallas_call | solution.py:444
  88.4 0.8 collective-permute-done.29.refs_3_
  89.2 0.9 collective-permute-start.36
  90.1 2.4 %collective-permute-start.35 = (bf16[8,1536]{1,0:T(8,128)(2,1)S(1)}, bf16[8,1536]{1,0:T(8,128)(2,1)S(1)}, u32[]{:S(2)}, u32[]{:S(2)}) collective-permute-start(bf16[8,1536]{1,0:T(8,128)(2,1)S(1)} %add_pairs.2.refs_0_), channel_id=1, source_target_pairs={{0,6},{1,7},{2,4},{3,5},{4,2},{5,3},{6,0},{7,1},{8,14},{9,15},{10,... | collective-permute-start | bytes 73736 | tf_op jit(solution)/shard_map/ppermute | solution.py:50
  92.6 0.5 collective-permute-start.34
  93.1 1.4 %collective-permute-start.33 = (bf16[8,1536]{1,0:T(8,128)(2,1)S(1)}, bf16[8,1536]{1,0:T(8,128)(2,1)S(1)}, u32[]{:S(2)}, u32[]{:S(2)}) collective-permute-start(bf16[8,1536]{1,0:T(8,128)(2,1)S(1)} %add_pairs.2.refs_0_), channel_id=1, source_target_pairs={{0,2},{1,3},{2,0},{3,1},{4,6},{5,7},{6,4},{7,5},{8,10},{9,11},{10,... | collective-permute-start | bytes 73736 | tf_op jit(solution)/shard_map/ppermute | solution.py:50
  94.5 3.2 %conv_back.3 = bf16[8,16,1536]{2,1,0:T(8,128)(2,1)} custom-call(f32[8,16,1536]{2,1,0:T(8,128)S(1)} %get-tuple-element.127.own, bf16[3,16,1536]{2,1,0:T(8,128)(2,1)S(1)} %collective-permute-done.30.refs_0_, bf16[8,3,1536]{2,1,0:T(4,128)(2,1)S(1)} %collective-permute-done.31.refs_1_, ...), custom_call_target="tpu_custom_call", output_to_operand_aliasing={{}: (6, {})} | custom-call | flops 1 | bytes 1 | tf_op jit(solution)/shard_map/conv_back/pallas_call | solution.py:444
  97.8 1.5 %collective-permute-start.39 = (f32[8,1536]{1,0:T(8,128)S(1)}, f32[8,1536]{1,0:T(8,128)S(1)}, u32[]{:S(2)}, u32[]{:S(2)}) collective-permute-start(f32[8,1536]{1,0:T(8,128)S(1)} %add_pairs.3.refs_0_), channel_id=1, source_target_pairs={{0,9},{1,8},{2,11},{3,10},{4,13},{5,12},{6,15},{7,14},{8,1},{9,0},... | collective-permute-start | bytes 147464 | tf_op jit(solution)/shard_map/ppermute | solution.py:50
  99.3 0.9 collective-permute-start.38
  100.2 1.1 %collective-permute-start.37 = (f32[8,1536]{1,0:T(8,128)S(1)}, f32[8,1536]{1,0:T(8,128)S(1)}, u32[]{:S(2)}, u32[]{:S(2)}) collective-permute-start(f32[8,1536]{1,0:T(8,128)S(1)} %add_pairs.3.refs_0_), channel_id=1, source_target_pairs={{0,1},{1,0},{2,3},{3,2},{4,5},{5,4},{6,7},{7,6},{8,9},{9,8},{10,11... | collective-permute-start | bytes 147464 | tf_op jit(solution)/shard_map/ppermute | solution.py:50
  101.3 1.5 %collective-permute-done.39.refs_3_ = f32[8,1536]{1,0:T(8,128)S(1)} collective-permute-done((f32[8,1536]{1,0:T(8,128)S(1)}, f32[8,1536]{1,0:T(8,128)S(1)}, u32[]{:S(2)}, u32[]{:S(2)}) %collective-permute-start.39) | collective-permute-done | bytes 49184 | tf_op jit(solution)/shard_map/ppermute | solution.py:50
  102.9 0.5 collective-permute-done.38.refs_2_
  103.4 0.9 collective-permute-done.37.refs_1_
  104.3 1.0 output_part.1
  105.5 0.9 finish.1
  (68 shorter events, 1.9 us)
Async XLA Ops:
  0.6 1.3 %copy-start = (bf16[192,3072]{1,0:T(8,128)(2,1)S(1)}, bf16[192,3072]{1,0:T(8,128)(2,1)}, u32[]{:S(2)}) copy-start(bf16[192,3072]{1,0:T(8,128)(2,1)} %param.18) | copy-start | bytes 3538948
  1.9 5.2 %copy-start.3 = (bf16[1,8,16,1536]{3,2,1,0:T(8,128)(2,1)S(1)}, bf16[1,8,16,1536]{3,2,1,0:T(8,128)(2,1)}, u32[]{:S(2)}) copy-start(bf16[1,8,16,1536]{3,2,1,0:T(8,128)(2,1)} %param.12) | copy-start | bytes 1179652
  1.9 21.1 %copy-start.1 = (bf16[1,8,16,1536]{3,2,1,0:T(8,128)(2,1)S(1)}, bf16[1,8,16,1536]{3,2,1,0:T(8,128)(2,1)}, u32[]{:S(2)}) copy-start(bf16[1,8,16,1536]{3,2,1,0:T(8,128)(2,1)} %param.23) | copy-start | bytes 1179652
  2.0 22.6 %copy-start.2 = (f32[7,7,1536]{2,1,0:T(8,128)S(1)}, f32[7,7,1536]{2,1,0:T(8,128)}, u32[]{:S(2)}) copy-start(f32[7,7,1536]{2,1,0:T(8,128)} %refs_3_.5) | copy-start | bytes 903172
  3.1 16.4 %collective-permute-start.7 = (bf16[384,768]{1,0:T(8,128)(2,1)S(1)}, bf16[384,768]{1,0:T(8,128)(2,1)S(1)}, u32[]{:S(2)}, u32[]{:S(2)}) collective-permute-start(bf16[384,768]{1,0:T(8,128)(2,1)S(1)} %pad_maximum_fusion.refs_0_), channel_id=1, source_target_pairs={{2,0},{4,2},{6,4},{7,6},{5,7},{3,5},{1,3},{0,1},{10,8},{12,10},{14... | collective-permute-start | bytes 1769480 | tf_op jit(solution)/shard_map/ppermute | solution.py:115
  6.1 14.9 %collective-permute-start.6 = (bf16[384,768]{1,0:T(8,128)(2,1)S(1)}, bf16[384,768]{1,0:T(8,128)(2,1)}, u32[]{:S(2)}, u32[]{:S(2)}) collective-permute-start(bf16[384,768]{1,0:T(8,128)(2,1)S(1)} %pad_maximum_fusion.refs_0_), channel_id=1, source_target_pairs={{0,2},{2,4},{4,6},{6,7},{7,5},{5,3},{3,1},{1,0},{8,10},{10,12},{12... | collective-permute-start | bytes 1769480 | tf_op jit(solution)/shard_map/ppermute | solution.py:114
  7.1 38.4 %copy-start.7 = (f32[1536]{0:T(1024)S(1)}, f32[1536]{0:T(1024)}, u32[]{:S(2)}) copy-start(f32[1536]{0:T(1024)} %scale.3) | copy-start | bytes 18436
  7.7 5.9 %collective-permute-start = (bf16[3,16,1536]{2,1,0:T(8,128)(2,1)S(1)}, bf16[3,16,1536]{2,1,0:T(8,128)(2,1)S(1)}, u32[]{:S(2)}, u32[]{:S(2)}) collective-permute-start(bf16[3,16,1536]{2,1,0:T(8,128)(2,1)S(1)} %get-tuple-element.74), channel_id=1, source_target_pairs={{0,16},{8,24},{16,0},{24,8},{1,17},{9,25},{17,1},{25,9},{2,18},{10... | collective-permute-start | bytes 442376 | tf_op jit(solution)/shard_map/ppermute | solution.py:75
  7.8 5.8 %collective-permute-start.1 = (bf16[8,3,1536]{2,1,0:T(4,128)(2,1)S(1)}, bf16[8,3,1536]{2,1,0:T(4,128)(2,1)S(1)}, u32[]{:S(2)}, u32[]{:S(2)}) collective-permute-start(bf16[8,3,1536]{2,1,0:T(4,128)(2,1)S(1)} %get-tuple-element.75), channel_id=1, source_target_pairs={{0,8},{8,0},{16,24},{24,16},{1,9},{9,1},{17,25},{25,17},{2,10},{10... | collective-permute-start | bytes 221192 | tf_op jit(solution)/shard_map/ppermute | solution.py:75
  9.7 3.9 %collective-permute-start.2 = (bf16[3,3,1536]{2,1,0:T(4,128)(2,1)S(1)}, bf16[3,3,1536]{2,1,0:T(4,128)(2,1)S(1)}, u32[]{:S(2)}, u32[]{:S(2)}) collective-permute-start(bf16[3,3,1536]{2,1,0:T(4,128)(2,1)S(1)} %get-tuple-element.76), channel_id=1, source_target_pairs={{0,24},{8,16},{16,8},{24,0},{1,25},{9,17},{17,9},{25,1},{2,26},{10... | collective-permute-start | bytes 82952 | tf_op jit(solution)/shard_map/ppermute | solution.py:75
  21.0 14.1 %collective-permute-start.8 = (bf16[384,768]{1,0:T(8,128)(2,1)}, bf16[384,768]{1,0:T(8,128)(2,1)S(1)}, u32[]{:S(2)}, u32[]{:S(2)}) collective-permute-start(bf16[384,768]{1,0:T(8,128)(2,1)} %collective-permute-done.6.refs_1_), channel_id=1, source_target_pairs={{0,2},{2,4},{4,6},{6,7},{7,5},{5,3},{3,1},{1,0},{8,10},{10,12},{12... | collective-permute-start | bytes 1769480 | tf_op jit(solution)/shard_map/ppermute | solution.py:114
  21.4 13.9 %collective-permute-start.9 = (bf16[384,768]{1,0:T(8,128)(2,1)S(1)}, bf16[384,768]{1,0:T(8,128)(2,1)S(1)}, u32[]{:S(2)}, u32[]{:S(2)}) collective-permute-start(bf16[384,768]{1,0:T(8,128)(2,1)S(1)} %collective-permute-done.7.refs_2_), channel_id=1, source_target_pairs={{2,0},{4,2},{6,4},{7,6},{5,7},{3,5},{1,3},{0,1},{10,8},{12,10},{14... | collective-permute-start | bytes 1769480 | tf_op jit(solution)/shard_map/ppermute | solution.py:115
  23.0 15.7 %collective-permute-start.3 = (bf16[128,1536]{1,0:T(8,128)(2,1)S(1)}, bf16[128,1536]{1,0:T(8,128)(2,1)S(1)}, u32[]{:S(2)}, u32[]{:S(2)}) collective-permute-start(bf16[128,1536]{1,0:T(8,128)(2,1)S(1)} %bitcast.8), channel_id=1, source_target_pairs={{16,0},{0,16},{17,1},{1,17},{18,2},{2,18},{19,3},{3,19},{20,4},{4,... | collective-permute-start | bytes 1179656 | tf_op jit(solution)/shard_map/ppermute | solution.py:55
  23.0 15.7 %collective-permute-start.4 = (bf16[128,1536]{1,0:T(8,128)(2,1)S(1)}, bf16[128,1536]{1,0:T(8,128)(2,1)S(1)}, u32[]{:S(2)}, u32[]{:S(2)}) collective-permute-start(bf16[128,1536]{1,0:T(8,128)(2,1)S(1)} %bitcast.9), channel_id=1, source_target_pairs={{8,0},{0,8},{9,1},{1,9},{10,2},{2,10},{11,3},{3,11},{12,4},{4,12},... | collective-permute-start | bytes 1179656 | tf_op jit(solution)/shard_map/ppermute | solution.py:55
  24.5 0.7 copy-start.5
  25.2 0.7 copy-start.9
  25.9 0.7 copy-start.10
  35.3 13.0 %collective-permute-start.10 = (bf16[384,768]{1,0:T(8,128)(2,1)S(1)}, bf16[384,768]{1,0:T(8,128)(2,1)S(1)}, u32[]{:S(2)}, u32[]{:S(2)}) collective-permute-start(bf16[384,768]{1,0:T(8,128)(2,1)S(1)} %collective-permute-done.8.refs_3_), channel_id=1, source_target_pairs={{0,2},{2,4},{4,6},{6,7},{7,5},{5,3},{3,1},{1,0},{8,10},{10,12},{12... | collective-permute-start | bytes 1769480 | tf_op jit(solution)/shard_map/ppermute | solution.py:114
  36.8 12.6 %collective-permute-start.11 = (bf16[384,768]{1,0:T(8,128)(2,1)S(1)}, bf16[384,768]{1,0:T(8,128)(2,1)S(1)}, u32[]{:S(2)}, u32[]{:S(2)}) collective-permute-start(bf16[384,768]{1,0:T(8,128)(2,1)S(1)} %collective-permute-done.9.refs_4_), channel_id=1, source_target_pairs={{2,0},{4,2},{6,4},{7,6},{5,7},{3,5},{1,3},{0,1},{10,8},{12,10},{14... | collective-permute-start | bytes 1769480 | tf_op jit(solution)/shard_map/ppermute | solution.py:115
  37.3 8.2 %collective-permute-start.14 = (bf16[128,1536]{1,0:T(8,128)(2,1)S(1)}, bf16[128,1536]{1,0:T(8,128)(2,1)S(1)}, u32[]{:S(2)}, u32[]{:S(2)}) collective-permute-start(bf16[128,1536]{1,0:T(8,128)(2,1)S(1)} %get-tuple-element.86.refs_9_), channel_id=1, source_target_pairs={{8,0},{0,8},{9,1},{1,9},{10,2},{2,10},{11,3},{3,11},{12,4},{4,12},... | collective-permute-start | bytes 1179656 | tf_op jit(solution)/shard_map/ppermute | solution.py:55
  38.8 6.8 %collective-permute-start.15 = (bf16[128,1536]{1,0:T(8,128)(2,1)S(1)}, bf16[128,1536]{1,0:T(8,128)(2,1)S(1)}, u32[]{:S(2)}, u32[]{:S(2)}) collective-permute-start(bf16[128,1536]{1,0:T(8,128)(2,1)S(1)} %get-tuple-element.86.refs_9_), channel_id=1, source_target_pairs={{16,0},{0,16},{17,1},{1,17},{18,2},{2,18},{19,3},{3,19},{20,4},{4,... | collective-permute-start | bytes 1179656 | tf_op jit(solution)/shard_map/ppermute | solution.py:55
  38.8 6.8 %collective-permute-start.5 = (bf16[128,1536]{1,0:T(8,128)(2,1)S(1)}, bf16[128,1536]{1,0:T(8,128)(2,1)S(1)}, u32[]{:S(2)}, u32[]{:S(2)}) collective-permute-start(bf16[128,1536]{1,0:T(8,128)(2,1)S(1)} %collective-permute-done.4.refs_2_.refs_15_), channel_id=1, source_target_pairs={{16,0},{0,16},{17,1},{1,17},{18,2},{2,18},{19,3},{3,19},{20,4},{4,... | collective-permute-start | bytes 1179656 | tf_op jit(solution)/shard_map/ppermute | solution.py:55
  45.6 5.9 %collective-permute-start.16 = (bf16[128,1536]{1,0:T(8,128)(2,1)S(1)}, bf16[128,1536]{1,0:T(8,128)(2,1)S(1)}, u32[]{:S(2)}, u32[]{:S(2)}) collective-permute-start(bf16[128,1536]{1,0:T(8,128)(2,1)S(1)} %collective-permute-done.14.refs_7_), channel_id=1, source_target_pairs={{16,0},{0,16},{17,1},{1,17},{18,2},{2,18},{19,3},{3,19},{20,4},{4,... | collective-permute-start | bytes 1179656 | tf_op jit(solution)/shard_map/ppermute | solution.py:55
  49.4 8.4 %copy-start.4 = (f32[3072]{0:T(1024)S(1)}, f32[3072]{0:T(1024)}, u32[]{:S(2)}) copy-start(f32[3072]{0:T(1024)} %refs_17_.1) | copy-start | bytes 36868
  49.4 6.8 %collective-permute-start.12 = (bf16[192,768]{1,0:T(8,128)(2,1)S(1)}, bf16[192,768]{1,0:T(8,128)(2,1)S(1)}, u32[]{:S(2)}, u32[]{:S(2)}) collective-permute-start(bf16[192,768]{1,0:T(8,128)(2,1)S(1)} %slice.8), channel_id=1, source_target_pairs={{0,2},{2,4},{4,6},{6,7},{7,5},{5,3},{3,1},{1,0},{8,10},{10,12},{12... | collective-permute-start | bytes 884744 | tf_op jit(solution)/shard_map/ppermute | solution.py:124
  51.0 6.7 %collective-permute-start.13 = (bf16[192,768]{1,0:T(8,128)(2,1)S(1)}, bf16[192,768]{1,0:T(8,128)(2,1)S(1)}, u32[]{:S(2)}, u32[]{:S(2)}) collective-permute-start(bf16[192,768]{1,0:T(8,128)(2,1)S(1)} %slice.9), channel_id=1, source_target_pairs={{2,0},{4,2},{6,4},{7,6},{5,7},{3,5},{1,3},{0,1},{10,8},{12,10},{14... | collective-permute-start | bytes 884744 | tf_op jit(solution)/shard_map/ppermute | solution.py:124
  59.8 3.5 %copy-start.8 = (f32[1536]{0:T(1024)S(1)}, f32[1536]{0:T(1024)}, u32[]{:S(2)}) copy-start(f32[1536]{0:T(1024)} %bias.3) | copy-start | bytes 18436
  59.8 1.8 %collective-permute-start.17 = (bf16[128,1536]{1,0:T(8,128)(2,1)S(1)}, bf16[128,1536]{1,0:T(8,128)(2,1)S(1)}, u32[]{:S(2)}, u32[]{:S(2)}) collective-permute-start(bf16[128,1536]{1,0:T(8,128)(2,1)S(1)} %get-tuple-element.95), channel_id=1, source_target_pairs={{16,0},{0,16},{17,1},{1,17},{18,2},{2,18},{19,3},{3,19},{20,4},{4,... | collective-permute-start | bytes 1179656 | tf_op jit(solution)/shard_map/ppermute | solution.py:55
  61.7 11.2 %collective-permute-start.18 = (bf16[128,1536]{1,0:T(8,128)(2,1)S(1)}, bf16[128,1536]{1,0:T(8,128)(2,1)S(1)}, u32[]{:S(2)}, u32[]{:S(2)}) collective-permute-start(bf16[128,1536]{1,0:T(8,128)(2,1)S(1)} %add_rounded.2), channel_id=1, source_target_pairs={{8,0},{0,8},{9,1},{1,9},{10,2},{2,10},{11,3},{3,11},{12,4},{4,12},... | collective-permute-start | bytes 1179656 | tf_op jit(solution)/shard_map/ppermute | solution.py:55
  63.2 11.2 %copy-start.6 = (f32[1536]{0:T(1024)S(1)}, f32[1536]{0:T(1024)}, u32[]{:S(2)}) copy-start(f32[1536]{0:T(1024)} %refs_6_.3) | copy-start | bytes 18436
  67.9 1.5 %collective-permute-start.19 = (bf16[64,1536]{1,0:T(8,128)(2,1)S(1)}, bf16[64,1536]{1,0:T(8,128)(2,1)S(1)}, u32[]{:S(2)}, u32[]{:S(2)}) collective-permute-start(bf16[64,1536]{1,0:T(8,128)(2,1)S(1)} %get-tuple-element.100), channel_id=1, source_target_pairs={{16,0},{0,16},{17,1},{1,17},{18,2},{2,18},{19,3},{3,19},{20,4},{4,... | collective-permute-start | bytes 589832 | tf_op jit(solution)/shard_map/ppermute | solution.py:55
  68.0 1.7 %collective-permute-start.20 = (bf16[64,1536]{1,0:T(8,128)(2,1)S(1)}, bf16[64,1536]{1,0:T(8,128)(2,1)S(1)}, u32[]{:S(2)}, u32[]{:S(2)}) collective-permute-start(bf16[64,1536]{1,0:T(8,128)(2,1)S(1)} %get-tuple-element.101), channel_id=1, source_target_pairs={{16,0},{0,16},{17,1},{1,17},{18,2},{2,18},{19,3},{3,19},{20,4},{4,... | collective-permute-start | bytes 589832 | tf_op jit(solution)/shard_map/ppermute | solution.py:55
  68.5 1.5 %collective-permute-start.21 = (bf16[64,1536]{1,0:T(8,128)(2,1)S(1)}, bf16[64,1536]{1,0:T(8,128)(2,1)S(1)}, u32[]{:S(2)}, u32[]{:S(2)}) collective-permute-start(bf16[64,1536]{1,0:T(8,128)(2,1)S(1)} %get-tuple-element.105), channel_id=1, source_target_pairs={{16,0},{0,16},{17,1},{1,17},{18,2},{2,18},{19,3},{3,19},{20,4},{4,... | collective-permute-start | bytes 589832 | tf_op jit(solution)/shard_map/ppermute | solution.py:55
  68.6 1.7 %collective-permute-start.22 = (bf16[64,1536]{1,0:T(8,128)(2,1)S(1)}, bf16[64,1536]{1,0:T(8,128)(2,1)S(1)}, u32[]{:S(2)}, u32[]{:S(2)}) collective-permute-start(bf16[64,1536]{1,0:T(8,128)(2,1)S(1)} %get-tuple-element.106), channel_id=1, source_target_pairs={{16,0},{0,16},{17,1},{1,17},{18,2},{2,18},{19,3},{3,19},{20,4},{4,... | collective-permute-start | bytes 589832 | tf_op jit(solution)/shard_map/ppermute | solution.py:55
  69.4 5.0 %collective-permute-start.23 = (bf16[64,1536]{1,0:T(8,128)(2,1)S(1)}, bf16[64,1536]{1,0:T(8,128)(2,1)S(1)}, u32[]{:S(2)}, u32[]{:S(2)}) collective-permute-start(bf16[64,1536]{1,0:T(8,128)(2,1)S(1)} %get-tuple-element.111), channel_id=1, source_target_pairs={{16,0},{0,16},{17,1},{1,17},{18,2},{2,18},{19,3},{3,19},{20,4},{4,... | collective-permute-start | bytes 589832 | tf_op jit(solution)/shard_map/ppermute | solution.py:55
  69.7 4.7 %collective-permute-start.24 = (bf16[64,1536]{1,0:T(8,128)(2,1)S(1)}, bf16[64,1536]{1,0:T(8,128)(2,1)S(1)}, u32[]{:S(2)}, u32[]{:S(2)}) collective-permute-start(bf16[64,1536]{1,0:T(8,128)(2,1)S(1)} %get-tuple-element.112), channel_id=1, source_target_pairs={{16,0},{0,16},{17,1},{1,17},{18,2},{2,18},{19,3},{3,19},{20,4},{4,... | collective-permute-start | bytes 589832 | tf_op jit(solution)/shard_map/ppermute | solution.py:55
  72.9 8.2 %collective-permute-start.26 = (bf16[96,1536]{1,0:T(8,128)(2,1)S(1)}, bf16[96,1536]{1,0:T(8,128)(2,1)S(1)}, u32[]{:S(2)}, u32[]{:S(2)}) collective-permute-start(bf16[96,1536]{1,0:T(8,128)(2,1)S(1)} %get-tuple-element.119), channel_id=1, source_target_pairs={{8,0},{0,8},{9,1},{1,9},{10,2},{2,10},{11,3},{3,11},{12,4},{4,12},... | collective-permute-start | bytes 884744 | tf_op jit(solution)/shard_map/ppermute | solution.py:55
  79.0 2.0 %collective-permute-start.25 = (f32[32,1536]{1,0:T(8,128)S(1)}, f32[32,1536]{1,0:T(8,128)S(1)}, u32[]{:S(2)}, u32[]{:S(2)}) collective-permute-start(f32[32,1536]{1,0:T(8,128)S(1)} %get-tuple-element.118), channel_id=1, source_target_pairs={{0,16},{16,0},{1,17},{17,1},{2,18},{18,2},{3,19},{19,3},{4,20},{20... | collective-permute-start | bytes 589832 | tf_op jit(solution)/shard_map/ppermute | solution.py:50
  79.0 6.2 %collective-permute-start.30 = (bf16[3,16,1536]{2,1,0:T(8,128)(2,1)S(1)}, bf16[3,16,1536]{2,1,0:T(8,128)(2,1)S(1)}, u32[]{:S(2)}, u32[]{:S(2)}) collective-permute-start(bf16[3,16,1536]{2,1,0:T(8,128)(2,1)S(1)} %get-tuple-element.128), channel_id=1, source_target_pairs={{0,16},{8,24},{16,0},{24,8},{1,17},{9,25},{17,1},{25,9},{2,18},{10... | collective-permute-start | bytes 442376 | tf_op jit(solution)/shard_map/ppermute | solution.py:75
  79.5 5.7 %collective-permute-start.31 = (bf16[8,3,1536]{2,1,0:T(4,128)(2,1)S(1)}, bf16[8,3,1536]{2,1,0:T(4,128)(2,1)S(1)}, u32[]{:S(2)}, u32[]{:S(2)}) collective-permute-start(bf16[8,3,1536]{2,1,0:T(4,128)(2,1)S(1)} %get-tuple-element.129), channel_id=1, source_target_pairs={{0,8},{8,0},{16,24},{24,16},{1,9},{9,1},{17,25},{25,17},{2,10},{10... | collective-permute-start | bytes 221192 | tf_op jit(solution)/shard_map/ppermute | solution.py:75
  80.1 4.2 %collective-permute-start.32 = (bf16[3,3,1536]{2,1,0:T(4,128)(2,1)S(1)}, bf16[3,3,1536]{2,1,0:T(4,128)(2,1)S(1)}, u32[]{:S(2)}, u32[]{:S(2)}) collective-permute-start(bf16[3,3,1536]{2,1,0:T(4,128)(2,1)S(1)} %get-tuple-element.130), channel_id=1, source_target_pairs={{0,24},{8,16},{16,8},{24,0},{1,25},{9,17},{17,9},{25,1},{2,26},{10... | collective-permute-start | bytes 82952 | tf_op jit(solution)/shard_map/ppermute | solution.py:75
  81.1 7.3 %collective-permute-start.27 = (bf16[8,1536]{1,0:T(8,128)(2,1)S(1)}, bf16[8,1536]{1,0:T(8,128)(2,1)S(1)}, u32[]{:S(2)}, u32[]{:S(2)}) collective-permute-start(bf16[8,1536]{1,0:T(8,128)(2,1)S(1)} %get-tuple-element.124), channel_id=1, source_target_pairs={{0,1},{1,0},{2,3},{3,2},{4,5},{5,4},{6,7},{7,6},{8,9},{9,8},{10,11... | collective-permute-start | bytes 73736 | tf_op jit(solution)/shard_map/ppermute | solution.py:50
  81.7 6.8 %collective-permute-start.28 = (bf16[8,1536]{1,0:T(8,128)(2,1)S(1)}, bf16[8,1536]{1,0:T(8,128)(2,1)S(1)}, u32[]{:S(2)}, u32[]{:S(2)}) collective-permute-start(bf16[8,1536]{1,0:T(8,128)(2,1)S(1)} %get-tuple-element.125), channel_id=1, source_target_pairs={{0,8},{8,0},{1,9},{9,1},{2,10},{10,2},{3,11},{11,3},{4,12},{12,4},... | collective-permute-start | bytes 73736 | tf_op jit(solution)/shard_map/ppermute | solution.py:50
  84.2 5.0 %collective-permute-start.29 = (bf16[8,1536]{1,0:T(8,128)(2,1)S(1)}, bf16[8,1536]{1,0:T(8,128)(2,1)S(1)}, u32[]{:S(2)}, u32[]{:S(2)}) collective-permute-start(bf16[8,1536]{1,0:T(8,128)(2,1)S(1)} %get-tuple-element.126), channel_id=1, source_target_pairs={{0,9},{1,8},{2,11},{3,10},{4,13},{5,12},{6,15},{7,14},{8,1},{9,0},... | collective-permute-start | bytes 73736 | tf_op jit(solution)/shard_map/ppermute | solution.py:50
  89.2 8.5 %collective-permute-start.36 = (bf16[32,1536]{1,0:T(8,128)(2,1)S(1)}, bf16[32,1536]{1,0:T(8,128)(2,1)S(1)}, u32[]{:S(2)}, u32[]{:S(2)}) collective-permute-start(bf16[32,1536]{1,0:T(8,128)(2,1)S(1)} %get-tuple-element.134), channel_id=1, source_target_pairs={{8,0},{0,8},{9,1},{1,9},{10,2},{2,10},{11,3},{3,11},{12,4},{4,12},... | collective-permute-start | bytes 294920 | tf_op jit(solution)/shard_map/ppermute | solution.py:55
  90.1 7.6 %collective-permute-start.35 = (bf16[8,1536]{1,0:T(8,128)(2,1)S(1)}, bf16[8,1536]{1,0:T(8,128)(2,1)S(1)}, u32[]{:S(2)}, u32[]{:S(2)}) collective-permute-start(bf16[8,1536]{1,0:T(8,128)(2,1)S(1)} %add_pairs.2.refs_0_), channel_id=1, source_target_pairs={{0,6},{1,7},{2,4},{3,5},{4,2},{5,3},{6,0},{7,1},{8,14},{9,15},{10,... | collective-permute-start | bytes 73736 | tf_op jit(solution)/shard_map/ppermute | solution.py:50
  92.6 5.2 %collective-permute-start.34 = (bf16[8,1536]{1,0:T(8,128)(2,1)S(1)}, bf16[8,1536]{1,0:T(8,128)(2,1)S(1)}, u32[]{:S(2)}, u32[]{:S(2)}) collective-permute-start(bf16[8,1536]{1,0:T(8,128)(2,1)S(1)} %add_pairs.2.refs_0_), channel_id=1, source_target_pairs={{0,4},{1,5},{2,6},{3,7},{4,0},{5,1},{6,2},{7,3},{8,12},{9,13},{10,... | collective-permute-start | bytes 73736 | tf_op jit(solution)/shard_map/ppermute | solution.py:50
  93.1 4.6 %collective-permute-start.33 = (bf16[8,1536]{1,0:T(8,128)(2,1)S(1)}, bf16[8,1536]{1,0:T(8,128)(2,1)S(1)}, u32[]{:S(2)}, u32[]{:S(2)}) collective-permute-start(bf16[8,1536]{1,0:T(8,128)(2,1)S(1)} %add_pairs.2.refs_0_), channel_id=1, source_target_pairs={{0,2},{1,3},{2,0},{3,1},{4,6},{5,7},{6,4},{7,5},{8,10},{9,11},{10,... | collective-permute-start | bytes 73736 | tf_op jit(solution)/shard_map/ppermute | solution.py:50
  97.8 5.1 %collective-permute-start.39 = (f32[8,1536]{1,0:T(8,128)S(1)}, f32[8,1536]{1,0:T(8,128)S(1)}, u32[]{:S(2)}, u32[]{:S(2)}) collective-permute-start(f32[8,1536]{1,0:T(8,128)S(1)} %add_pairs.3.refs_0_), channel_id=1, source_target_pairs={{0,9},{1,8},{2,11},{3,10},{4,13},{5,12},{6,15},{7,14},{8,1},{9,0},... | collective-permute-start | bytes 147464 | tf_op jit(solution)/shard_map/ppermute | solution.py:50
  99.3 4.1 %collective-permute-start.38 = (f32[8,1536]{1,0:T(8,128)S(1)}, f32[8,1536]{1,0:T(8,128)S(1)}, u32[]{:S(2)}, u32[]{:S(2)}) collective-permute-start(f32[8,1536]{1,0:T(8,128)S(1)} %add_pairs.3.refs_0_), channel_id=1, source_target_pairs={{0,8},{8,0},{1,9},{9,1},{2,10},{10,2},{3,11},{11,3},{4,12},{12,4},... | collective-permute-start | bytes 147464 | tf_op jit(solution)/shard_map/ppermute | solution.py:50
  100.2 4.1 %collective-permute-start.37 = (f32[8,1536]{1,0:T(8,128)S(1)}, f32[8,1536]{1,0:T(8,128)S(1)}, u32[]{:S(2)}, u32[]{:S(2)}) collective-permute-start(f32[8,1536]{1,0:T(8,128)S(1)} %add_pairs.3.refs_0_), channel_id=1, source_target_pairs={{0,1},{1,0},{2,3},{3,2},{4,5},{5,4},{6,7},{7,6},{8,9},{9,8},{10,11... | collective-permute-start | bytes 147464 | tf_op jit(solution)/shard_map/ppermute | solution.py:50
  101.3 4.0 %collective-permute-start.40 = (f32[8,1536]{1,0:T(8,128)S(1)}, f32[8,1536]{1,0:T(8,128)S(1)}, u32[]{:S(2)}, u32[]{:S(2)}) collective-permute-start(f32[8,1536]{1,0:T(8,128)S(1)} %add_pairs.3.refs_0_), channel_id=1, source_target_pairs={{0,16},{16,0},{1,17},{17,1},{2,18},{18,2},{3,19},{19,3},{4,20},{20... | collective-permute-start | bytes 147464 | tf_op jit(solution)/shard_map/ppermute | solution.py:50
  102.9 2.4 %collective-permute-start.43 = (f32[8,1536]{1,0:T(8,128)S(1)}, f32[8,1536]{1,0:T(8,128)S(1)}, u32[]{:S(2)}, u32[]{:S(2)}) collective-permute-start(f32[8,1536]{1,0:T(8,128)S(1)} %collective-permute-done.39.refs_3_), channel_id=1, source_target_pairs={{0,16},{16,0},{1,17},{17,1},{2,18},{18,2},{3,19},{19,3},{4,20},{20... | collective-permute-start | bytes 147464 | tf_op jit(solution)/shard_map/ppermute | solution.py:50
  103.4 1.9 %collective-permute-start.42 = (f32[8,1536]{1,0:T(8,128)S(1)}, f32[8,1536]{1,0:T(8,128)S(1)}, u32[]{:S(2)}, u32[]{:S(2)}) collective-permute-start(f32[8,1536]{1,0:T(8,128)S(1)} %collective-permute-done.38.refs_2_), channel_id=1, source_target_pairs={{0,16},{16,0},{1,17},{17,1},{2,18},{18,2},{3,19},{19,3},{4,20},{20... | collective-permute-start | bytes 147464 | tf_op jit(solution)/shard_map/ppermute | solution.py:50
  104.3 1.2 %collective-permute-start.41 = (f32[8,1536]{1,0:T(8,128)S(1)}, f32[8,1536]{1,0:T(8,128)S(1)}, u32[]{:S(2)}, u32[]{:S(2)}) collective-permute-start(f32[8,1536]{1,0:T(8,128)S(1)} %collective-permute-done.37.refs_1_), channel_id=1, source_target_pairs={{0,16},{16,0},{1,17},{17,1},{2,18},{18,2},{3,19},{19,3},{4,20},{20... | collective-permute-start | bytes 147464 | tf_op jit(solution)/shard_map/ppermute | solution.py:50

commit v8 on v7

--- a/solution.py
+++ b/solution.py
@@ -858,9 +858,9 @@
     down_block = lax.dynamic_slice_in_dim(w_down, quarter * hidden, hidden, 0).T
     scaled, *edges = prepare(x_code[0], x_exp[0])
     edges = list(exchange_edges(dict(zip(edge_keys(), edges, strict=True))).values())
-    cots = gather_tile(after(cotangent.reshape(spots, chans), edges), [])
+    padded, normed, rstd, ln_out = conv_norm(scaled, edges, dw_kernel, dw_bias, ln_gain, ln_bias)
+    cots = gather_tile(after(cotangent.reshape(spots, chans), edges), ln_out)
     d_mlp = scale_part(cots, layer_scale)
-    padded, normed, rstd, ln_out = conv_norm(scaled, edges, dw_kernel, dw_bias, ln_gain, ln_bias)
     blocks = jnp.concatenate([up_block, down_block], 0)
     pieces, upper, lower = ring_gather(blocks, edges, ln_out, d_mlp)
     lns = gather_tile(ln_out, cots[n_near])

time: 107 us -> 107 us (level)
  no operation moved by 1% of the time
where the time goes in v8:
time: 107 us; the launch traced here: 106 us
  waiting for transfers between devices  36.9 us (34%)
  starting transfers between devices  33.3 us (31%)
  Pallas kernels  29.8 us (28%)
  local copies, waits for them, and re-layouts  5.44 us (5%)
    ppermute x16, waiting for transfers between devices, shift(): return lax.ppermute(a, axis, [((i + k) % n, i) for i in range(n)])  11.7 us
    ppermute x14, starting transfers between devices, swap(): return lax.ppermute(a, axes, [(i, i ^ mask) for i in range(total)])  11.1 us
    ppermute x16, starting transfers between devices, shift(): return lax.ppermute(a, axis, [((i + k) % n, i) for i in range(n)])  8.97 us
    ppermute x3, waiting for transfers between devices, ring_gather(): two = lax.ppermute(two, 'fsdp', back)  7.03 us
    pallas_call x2, Pallas kernels, conv_back(): pl.pallas_call(functools.partial(conv_back_kernel, begin, count), out_sha...  6.37 us
    ppermute x3, waiting for transfers between devices, ring_gather(): one = lax.ppermute(one, 'fsdp', forth)  6.3 us
    pallas_call x1, Pallas kernels, conv_norm(): pl.pallas_call(conv_norm_kernel, out_shape=(shaped((rows + 2 * HALO, cols...  6.05 us
    ppermute x3, starting transfers between devices, ring_gather(): two = lax.ppermute(two, 'fsdp', back)  5.15 us
  transfers between devices with their start and end apart: 44, of which 22 were waited for; matrix products, arithmetic and copies ran while one was open for 1% of the time, Pallas kernels for 25%

profile of v8, /device:TPU:0, one launch (start us, length us, event | category | flops | bytes accessed | tf_op | source)
XLA Modules:
  0.0 106.4 jit_solution(15102691530746430270)
XLA Ops:
  0.7 1.3 %copy-done = bf16[192,3072]{1,0:T(8,128)(2,1)S(1)} copy-done((bf16[192,3072]{1,0:T(8,128)(2,1)S(1)}, bf16[192,3072]{1,0:T(8,128)(2,1)}, u32[]{:S(2)}) %copy-start) | copy-done | bytes 1179672
  2.0 1.1 %dynamic-slice_bitcast_fusion = bf16[192,768]{1,0:T(8,128)(2,1)S(1)} fusion(bf16[3072,192]{0,1:T(8,128)(2,1)} %param.20, s32[]{:T(128)S(6)} %select_n.4), kind=kLoop, calls=%fused_computation.1 | loop fusion | bytes 589828 | tf_op jit(solution)/shard_map/transpose | solution.py:858
  3.1 3.0 %collective-permute-start.7 = (bf16[384,768]{1,0:T(8,128)(2,1)S(1)}, bf16[384,768]{1,0:T(8,128)(2,1)S(1)}, u32[]{:S(2)}, u32[]{:S(2)}) collective-permute-start(bf16[384,768]{1,0:T(8,128)(2,1)S(1)} %pad_maximum_fusion.refs_0_), channel_id=1, source_target_pairs={{2,0},{4,2},{6,4},{7,6},{5,7},{3,5},{1,3},{0,1},{10,8},{12,10},{14... | collective-permute-start | bytes 1769480 | tf_op jit(solution)/shard_map/ppermute | solution.py:115
  6.2 0.9 copy.18
  7.2 0.5 prepare.1
  7.8 1.9 %collective-permute-start.1 = (bf16[8,3,1536]{2,1,0:T(4,128)(2,1)S(1)}, bf16[8,3,1536]{2,1,0:T(4,128)(2,1)S(1)}, u32[]{:S(2)}, u32[]{:S(2)}) collective-permute-start(bf16[8,3,1536]{2,1,0:T(4,128)(2,1)S(1)} %get-tuple-element.76), channel_id=1, source_target_pairs={{0,8},{8,0},{16,24},{24,16},{1,9},{9,1},{17,25},{25,17},{2,10},{10... | collective-permute-start | bytes 221192 | tf_op jit(solution)/shard_map/ppermute | solution.py:75
  9.8 3.8 %collective-permute-done.2.refs_2_ = bf16[3,3,1536]{2,1,0:T(4,128)(2,1)S(1)} collective-permute-done((bf16[3,3,1536]{2,1,0:T(4,128)(2,1)S(1)}, bf16[3,3,1536]{2,1,0:T(4,128)(2,1)S(1)}, u32[]{:S(2)}, u32[]{:S(2)}) %collective-permute-start.2) | collective-permute-done | bytes 27680 | tf_op jit(solution)/shard_map/ppermute | solution.py:75
  13.6 5.9 %collective-permute-done.7.refs_2_ = bf16[384,768]{1,0:T(8,128)(2,1)S(1)} collective-permute-done((bf16[384,768]{1,0:T(8,128)(2,1)S(1)}, bf16[384,768]{1,0:T(8,128)(2,1)S(1)}, u32[]{:S(2)}, u32[]{:S(2)}) %collective-permute-start.7) | collective-permute-done | bytes 589856 | tf_op jit(solution)/shard_map/ppermute | solution.py:115
  19.5 1.5 %collective-permute-done.6.refs_1_ = bf16[384,768]{1,0:T(8,128)(2,1)} collective-permute-done((bf16[384,768]{1,0:T(8,128)(2,1)S(1)}, bf16[384,768]{1,0:T(8,128)(2,1)}, u32[]{:S(2)}, u32[]{:S(2)}) %collective-permute-start.6) | collective-permute-done | bytes 589856 | tf_op jit(solution)/shard_map/ppermute | solution.py:114
  21.0 0.4 collective-permute-start.8
  21.4 1.6 %collective-permute-start.9 = (bf16[384,768]{1,0:T(8,128)(2,1)S(1)}, bf16[384,768]{1,0:T(8,128)(2,1)S(1)}, u32[]{:S(2)}, u32[]{:S(2)}) collective-permute-start(bf16[384,768]{1,0:T(8,128)(2,1)S(1)} %collective-permute-done.7.refs_2_), channel_id=1, source_target_pairs={{2,0},{4,2},{6,4},{7,6},{5,7},{3,5},{1,3},{0,1},{10,8},{12,10},{14... | collective-permute-start | bytes 1769480 | tf_op jit(solution)/shard_map/ppermute | solution.py:115
  23.0 1.5 %collective-permute-start.4 = (bf16[128,1536]{1,0:T(8,128)(2,1)S(1)}, bf16[128,1536]{1,0:T(8,128)(2,1)S(1)}, u32[]{:S(2)}, u32[]{:S(2)}) collective-permute-start(bf16[128,1536]{1,0:T(8,128)(2,1)S(1)} %bitcast.8), channel_id=1, source_target_pairs={{8,0},{0,8},{9,1},{1,9},{10,2},{2,10},{11,3},{3,11},{12,4},{4,12},... | collective-permute-start | bytes 1179656 | tf_op jit(solution)/shard_map/ppermute | solution.py:55
  24.5 0.7 copy-done.5
  25.2 0.7 copy-done.9
  25.9 0.7 copy-done.10
  26.6 6.0 %conv_norm.1 = (f32[14,32,1536]{2,1,0:T(8,128)S(1)}, f32[128,1536]{1,0:T(8,128)S(1)}, f32[128,128]{1,0:T(8,128)S(1)}, bf16[128,1536]{1,0:T(8,128)(2,1)S(1)}) custom-call(bf16[8,16,1536]{2,1,0:T(8,128)(2,1)S(1)} %get-tuple-element.74.own.scaled, bf16[3,16,1536]{2,1,0:T(8,128)(2,1)S(1)} %collective-permute-done.refs_0_, ...), custom_call_target="tpu_custom_call" | custom-call | flops 1 | bytes 1 | tf_op jit(solution)/shard_map/conv_norm/pallas_call | solution.py:319
  32.7 2.3 %collective-permute-done.8.refs_3_ = bf16[384,768]{1,0:T(8,128)(2,1)S(1)} collective-permute-done((bf16[384,768]{1,0:T(8,128)(2,1)}, bf16[384,768]{1,0:T(8,128)(2,1)S(1)}, u32[]{:S(2)}, u32[]{:S(2)}) %collective-permute-start.8) | collective-permute-done | bytes 589856 | tf_op jit(solution)/shard_map/ppermute | solution.py:114
  35.1 0.2 collective-permute-done.9.refs_4_
  35.3 1.5 %collective-permute-start.10 = (bf16[384,768]{1,0:T(8,128)(2,1)S(1)}, bf16[384,768]{1,0:T(8,128)(2,1)S(1)}, u32[]{:S(2)}, u32[]{:S(2)}) collective-permute-start(bf16[384,768]{1,0:T(8,128)(2,1)S(1)} %collective-permute-done.8.refs_3_), channel_id=1, source_target_pairs={{0,2},{2,4},{4,6},{6,7},{7,5},{5,3},{3,1},{1,0},{8,10},{10,12},{12... | collective-permute-start | bytes 1769480 | tf_op jit(solution)/shard_map/ppermute | solution.py:114
  36.8 0.5 collective-permute-start.11
  37.3 1.4 %collective-permute-start.14 = (bf16[128,1536]{1,0:T(8,128)(2,1)S(1)}, bf16[128,1536]{1,0:T(8,128)(2,1)S(1)}, u32[]{:S(2)}, u32[]{:S(2)}) collective-permute-start(bf16[128,1536]{1,0:T(8,128)(2,1)S(1)} %get-tuple-element.88.refs_9_), channel_id=1, source_target_pairs={{8,0},{0,8},{9,1},{1,9},{10,2},{2,10},{11,3},{3,11},{12,4},{4,12},... | collective-permute-start | bytes 1179656 | tf_op jit(solution)/shard_map/ppermute | solution.py:55
  38.8 0.5 collective-permute-start.5
  39.3 6.4 %collective-permute-done.14.refs_7_ = bf16[128,1536]{1,0:T(8,128)(2,1)S(1)} collective-permute-done((bf16[128,1536]{1,0:T(8,128)(2,1)S(1)}, bf16[128,1536]{1,0:T(8,128)(2,1)S(1)}, u32[]{:S(2)}, u32[]{:S(2)}) %collective-permute-start.14) | collective-permute-done | bytes 393248 | tf_op jit(solution)/shard_map/ppermute | solution.py:55
  45.8 0.3 scale_part.1.refs_9_.refs_11_
  46.0 2.5 %collective-permute-done.10.refs_5_ = bf16[384,768]{1,0:T(8,128)(2,1)S(1)} collective-permute-done((bf16[384,768]{1,0:T(8,128)(2,1)S(1)}, bf16[384,768]{1,0:T(8,128)(2,1)S(1)}, u32[]{:S(2)}, u32[]{:S(2)}) %collective-permute-start.10) | collective-permute-done | bytes 589856 | tf_op jit(solution)/shard_map/ppermute | solution.py:114
  48.5 0.9 collective-permute-done.11.refs_6_
  49.4 1.6 %collective-permute-start.12 = (bf16[192,768]{1,0:T(8,128)(2,1)S(1)}, bf16[192,768]{1,0:T(8,128)(2,1)S(1)}, u32[]{:S(2)}, u32[]{:S(2)}) collective-permute-start(bf16[192,768]{1,0:T(8,128)(2,1)S(1)} %slice.8), channel_id=1, source_target_pairs={{0,2},{2,4},{4,6},{6,7},{7,5},{5,3},{3,1},{1,0},{8,10},{10,12},{12... | collective-permute-start | bytes 884744 | tf_op jit(solution)/shard_map/ppermute | solution.py:124
  51.0 0.5 collective-permute-start.13
  51.5 3.2 %early_part.1 = (f32[256,768]{1,0:T(8,128)S(1)}, f32[256,768]{1,0:T(8,128)S(1)}, bf16[1536,768]{1,0:T(8,128)(2,1)S(1)}, bf16[1536,256]{1,0:T(8,128)(2,1)S(1)}, b...) custom-call(bf16[384,768]{1,0:T(8,128)(2,1)S(1)} %pad_maximum_fusion.refs_0_, ...), custom_call_target="tpu_custom_call" | custom-call | flops 1 | bytes 1 | tf_op jit(solution)/shard_map/early_part/pallas_call | solution.py:594
  54.7 1.5 %collective-permute-done.12.up_last.refs_7_ = bf16[192,768]{1,0:T(8,128)(2,1)S(1)} collective-permute-done((bf16[192,768]{1,0:T(8,128)(2,1)S(1)}, bf16[192,768]{1,0:T(8,128)(2,1)S(1)}, u32[]{:S(2)}, u32[]{:S(2)}) %collective-permute-start.12) | collective-permute-done | bytes 294944 | tf_op jit(solution)/shard_map/ppermute | solution.py:124
  56.2 1.6 %collective-permute-done.13.down_last.refs_8_ = bf16[192,768]{1,0:T(8,128)(2,1)S(1)} collective-permute-done((bf16[192,768]{1,0:T(8,128)(2,1)S(1)}, bf16[192,768]{1,0:T(8,128)(2,1)S(1)}, u32[]{:S(2)}, u32[]{:S(2)}) %collective-permute-start.13) | collective-permute-done | bytes 294944 | tf_op jit(solution)/shard_map/ppermute | solution.py:124
  57.8 2.0 %far_part.1 = (bf16[256,768]{1,0:T(8,128)(2,1)S(1)}, bf16[128,1536]{1,0:T(8,128)(2,1)S(1)}, bf16[128,1536]{1,0:T(8,128)(2,1)S(1)}) custom-call(bf16[192,768]{1,0:T(8,128)(2,1)S(1)} %collective-permute-done.12.up_last.refs_7_, bf16[192,768]{1,0:T(8,128)(2,1)S(1)} %collective-permute-done.13.down_last.refs_8_, f32[256,768]{1,0:T(8,128)S(1)} %get-tuple-element.90.pre, ...), custom_call_target="tpu_custom_call" | custom-call | flops 1 | bytes 1 | tf_op jit(solution)/shard_map/far_part/pallas_call | solution.py:631
  59.9 1.7 %collective-permute-done.17.refs_1_ = bf16[128,1536]{1,0:T(8,128)(2,1)S(1)} collective-permute-done((bf16[128,1536]{1,0:T(8,128)(2,1)S(1)}, bf16[128,1536]{1,0:T(8,128)(2,1)S(1)}, u32[]{:S(2)}, u32[]{:S(2)}) %collective-permute-start.17) | collective-permute-done | bytes 393248 | tf_op jit(solution)/shard_map/ppermute | solution.py:55
  61.7 1.6 %collective-permute-start.18 = (bf16[128,1536]{1,0:T(8,128)(2,1)S(1)}, bf16[128,1536]{1,0:T(8,128)(2,1)S(1)}, u32[]{:S(2)}, u32[]{:S(2)}) collective-permute-start(bf16[128,1536]{1,0:T(8,128)(2,1)S(1)} %add_rounded.2), channel_id=1, source_target_pairs={{8,0},{0,8},{9,1},{1,9},{10,2},{2,10},{11,3},{3,11},{12,4},{4,12},... | collective-permute-start | bytes 1179656 | tf_op jit(solution)/shard_map/ppermute | solution.py:55
  63.2 4.7 %rest_part.1 = (bf16[128,1536]{1,0:T(8,128)(2,1)S(1)}, bf16[64,1536]{1,0:T(8,128)(2,1)S(1)}, bf16[64,1536]{1,0:T(8,128)(2,1)S(1)}, bf16[128,1536]{1,0:T(8,128)(2...) custom-call(bf16[384,768]{1,0:T(8,128)(2,1)S(1)} %pad_maximum_fusion, ...), custom_call_target="tpu_custom_call" | custom-call | flops 1 | bytes 1 | tf_op jit(solution)/shard_map/rest_part/pallas_call | solution.py:685
  68.0 0.5 collective-permute-start.20
  68.6 0.4 collective-permute-start.22
  69.0 0.4 collective-permute-done.19.refs_1_
  69.7 0.2 collective-permute-start.24
  70.3 2.6 %collective-permute-done.18.refs_3_ = bf16[128,1536]{1,0:T(8,128)(2,1)S(1)} collective-permute-done((bf16[128,1536]{1,0:T(8,128)(2,1)S(1)}, bf16[128,1536]{1,0:T(8,128)(2,1)S(1)}, u32[]{:S(2)}, u32[]{:S(2)}) %collective-permute-start.18) | collective-permute-done | bytes 393248 | tf_op jit(solution)/shard_map/ppermute | solution.py:55
  72.9 1.5 %collective-permute-start.26 = (bf16[96,1536]{1,0:T(8,128)(2,1)S(1)}, bf16[96,1536]{1,0:T(8,128)(2,1)S(1)}, u32[]{:S(2)}, u32[]{:S(2)}) collective-permute-start(bf16[96,1536]{1,0:T(8,128)(2,1)S(1)} %get-tuple-element.121), channel_id=1, source_target_pairs={{8,0},{0,8},{9,1},{1,9},{10,2},{2,10},{11,3},{3,11},{12,4},{4,12},... | collective-permute-start | bytes 884744 | tf_op jit(solution)/shard_map/ppermute | solution.py:55
  74.4 4.5 %norm_back.1 = (f32[8,16,1536]{2,1,0:T(8,128)S(1)}, f32[32,1536]{1,0:T(8,128)S(1)}, f32[32,1536]{1,0:T(8,128)S(1)}, bf16[3,16,1536]{2,1,0:T(8,128)(2,1)S(1)}, bf...) custom-call(bf16[128,1536]{1,0:T(8,128)(2,1)S(1)} %get-tuple-element.112.refs_0_, ...), custom_call_target="tpu_custom_call" | custom-call | flops 1 | bytes 1 | tf_op jit(solution)/shard_map/norm_back/pallas_call | solution.py:407
  79.0 0.5 collective-permute-start.30
  79.5 0.5 collective-permute-start.31
  80.1 0.9 collective-permute-start.32
  81.1 0.5 collective-permute-start.27
  81.7 1.5 %collective-permute-start.28 = (bf16[8,1536]{1,0:T(8,128)(2,1)S(1)}, bf16[8,1536]{1,0:T(8,128)(2,1)S(1)}, u32[]{:S(2)}, u32[]{:S(2)}) collective-permute-start(bf16[8,1536]{1,0:T(8,128)(2,1)S(1)} %get-tuple-element.127), channel_id=1, source_target_pairs={{0,8},{8,0},{1,9},{9,1},{2,10},{10,2},{3,11},{11,3},{4,12},{12,4},... | collective-permute-start | bytes 73736 | tf_op jit(solution)/shard_map/ppermute | solution.py:50
  83.2 1.1 %collective-permute-done.32.refs_2_ = bf16[3,3,1536]{2,1,0:T(4,128)(2,1)S(1)} collective-permute-done((bf16[3,3,1536]{2,1,0:T(4,128)(2,1)S(1)}, bf16[3,3,1536]{2,1,0:T(4,128)(2,1)S(1)}, u32[]{:S(2)}, u32[]{:S(2)}) %collective-permute-start.32) | collective-permute-done | bytes 27680 | tf_op jit(solution)/shard_map/ppermute | solution.py:75
  84.2 1.0 collective-permute-start.29
  85.2 3.2 %conv_back.2.refs_5_ = bf16[8,16,1536]{2,1,0:T(8,128)(2,1)} custom-call(f32[8,16,1536]{2,1,0:T(8,128)S(1)} %get-tuple-element.129.own, bf16[3,16,1536]{2,1,0:T(8,128)(2,1)S(1)} %collective-permute-done.30.refs_0_, bf16[8,3,1536]{2,1,0:T(4,128)(2,1)S(1)} %collective-permute-done.31.refs_1_, bf16[3,3,1536]{2,1,0:T(4,128)(2,1)S(1)} %collective-permute-done.32.refs_2_, ...), custom_call_target="tpu_custom_call" | custom-call | flops 1 | bytes 1 | tf_op jit(solution)/shard_map/conv_back/pallas_call | solution.py:444
  88.4 0.8 collective-permute-done.29.refs_3_
  89.2 0.9 collective-permute-start.36
  90.1 2.6 %collective-permute-start.35 = (bf16[8,1536]{1,0:T(8,128)(2,1)S(1)}, bf16[8,1536]{1,0:T(8,128)(2,1)S(1)}, u32[]{:S(2)}, u32[]{:S(2)}) collective-permute-start(bf16[8,1536]{1,0:T(8,128)(2,1)S(1)} %add_pairs.2.refs_0_), channel_id=1, source_target_pairs={{0,6},{1,7},{2,4},{3,5},{4,2},{5,3},{6,0},{7,1},{8,14},{9,15},{10,... | collective-permute-start | bytes 73736 | tf_op jit(solution)/shard_map/ppermute | solution.py:50
  92.7 0.4 collective-permute-start.34
  93.1 1.4 %collective-permute-start.33 = (bf16[8,1536]{1,0:T(8,128)(2,1)S(1)}, bf16[8,1536]{1,0:T(8,128)(2,1)S(1)}, u32[]{:S(2)}, u32[]{:S(2)}) collective-permute-start(bf16[8,1536]{1,0:T(8,128)(2,1)S(1)} %add_pairs.2.refs_0_), channel_id=1, source_target_pairs={{0,2},{1,3},{2,0},{3,1},{4,6},{5,7},{6,4},{7,5},{8,10},{9,11},{10,... | collective-permute-start | bytes 73736 | tf_op jit(solution)/shard_map/ppermute | solution.py:50
  94.5 3.2 %conv_back.3 = bf16[8,16,1536]{2,1,0:T(8,128)(2,1)} custom-call(f32[8,16,1536]{2,1,0:T(8,128)S(1)} %get-tuple-element.129.own, bf16[3,16,1536]{2,1,0:T(8,128)(2,1)S(1)} %collective-permute-done.30.refs_0_, bf16[8,3,1536]{2,1,0:T(4,128)(2,1)S(1)} %collective-permute-done.31.refs_1_, ...), custom_call_target="tpu_custom_call", output_to_operand_aliasing={{}: (6, {})} | custom-call | flops 1 | bytes 1 | tf_op jit(solution)/shard_map/conv_back/pallas_call | solution.py:444
  97.8 1.5 %collective-permute-start.39 = (f32[8,1536]{1,0:T(8,128)S(1)}, f32[8,1536]{1,0:T(8,128)S(1)}, u32[]{:S(2)}, u32[]{:S(2)}) collective-permute-start(f32[8,1536]{1,0:T(8,128)S(1)} %add_pairs.3.refs_0_), channel_id=1, source_target_pairs={{0,9},{1,8},{2,11},{3,10},{4,13},{5,12},{6,15},{7,14},{8,1},{9,0},... | collective-permute-start | bytes 147464 | tf_op jit(solution)/shard_map/ppermute | solution.py:50
  99.3 0.9 collective-permute-start.38
  100.2 1.1 %collective-permute-start.37 = (f32[8,1536]{1,0:T(8,128)S(1)}, f32[8,1536]{1,0:T(8,128)S(1)}, u32[]{:S(2)}, u32[]{:S(2)}) collective-permute-start(f32[8,1536]{1,0:T(8,128)S(1)} %add_pairs.3.refs_0_), channel_id=1, source_target_pairs={{0,1},{1,0},{2,3},{3,2},{4,5},{5,4},{6,7},{7,6},{8,9},{9,8},{10,11... | collective-permute-start | bytes 147464 | tf_op jit(solution)/shard_map/ppermute | solution.py:50
  101.3 1.5 %collective-permute-done.39.refs_3_ = f32[8,1536]{1,0:T(8,128)S(1)} collective-permute-done((f32[8,1536]{1,0:T(8,128)S(1)}, f32[8,1536]{1,0:T(8,128)S(1)}, u32[]{:S(2)}, u32[]{:S(2)}) %collective-permute-start.39) | collective-permute-done | bytes 49184 | tf_op jit(solution)/shard_map/ppermute | solution.py:50
  102.9 0.5 collective-permute-done.38.refs_2_
  103.4 0.9 collective-permute-done.37.refs_1_
  104.3 1.0 output_part.1
  105.5 0.9 finish.1
  (68 shorter events, 2.0 us)
Async XLA Ops:
  0.6 1.3 %copy-start = (bf16[192,3072]{1,0:T(8,128)(2,1)S(1)}, bf16[192,3072]{1,0:T(8,128)(2,1)}, u32[]{:S(2)}) copy-start(bf16[192,3072]{1,0:T(8,128)(2,1)} %param.18) | copy-start | bytes 3538948
  1.9 5.2 %copy-start.3 = (bf16[1,8,16,1536]{3,2,1,0:T(8,128)(2,1)S(1)}, bf16[1,8,16,1536]{3,2,1,0:T(8,128)(2,1)}, u32[]{:S(2)}) copy-start(bf16[1,8,16,1536]{3,2,1,0:T(8,128)(2,1)} %param.12) | copy-start | bytes 1179652
  1.9 21.1 %copy-start.1 = (bf16[1,8,16,1536]{3,2,1,0:T(8,128)(2,1)S(1)}, bf16[1,8,16,1536]{3,2,1,0:T(8,128)(2,1)}, u32[]{:S(2)}) copy-start(bf16[1,8,16,1536]{3,2,1,0:T(8,128)(2,1)} %param.23) | copy-start | bytes 1179652
  2.0 22.6 %copy-start.2 = (f32[7,7,1536]{2,1,0:T(8,128)S(1)}, f32[7,7,1536]{2,1,0:T(8,128)}, u32[]{:S(2)}) copy-start(f32[7,7,1536]{2,1,0:T(8,128)} %refs_3_.5) | copy-start | bytes 903172
  3.1 16.4 %collective-permute-start.7 = (bf16[384,768]{1,0:T(8,128)(2,1)S(1)}, bf16[384,768]{1,0:T(8,128)(2,1)S(1)}, u32[]{:S(2)}, u32[]{:S(2)}) collective-permute-start(bf16[384,768]{1,0:T(8,128)(2,1)S(1)} %pad_maximum_fusion.refs_0_), channel_id=1, source_target_pairs={{2,0},{4,2},{6,4},{7,6},{5,7},{3,5},{1,3},{0,1},{10,8},{12,10},{14... | collective-permute-start | bytes 1769480 | tf_op jit(solution)/shard_map/ppermute | solution.py:115
  6.1 14.9 %collective-permute-start.6 = (bf16[384,768]{1,0:T(8,128)(2,1)S(1)}, bf16[384,768]{1,0:T(8,128)(2,1)}, u32[]{:S(2)}, u32[]{:S(2)}) collective-permute-start(bf16[384,768]{1,0:T(8,128)(2,1)S(1)} %pad_maximum_fusion.refs_0_), channel_id=1, source_target_pairs={{0,2},{2,4},{4,6},{6,7},{7,5},{5,3},{3,1},{1,0},{8,10},{10,12},{12... | collective-permute-start | bytes 1769480 | tf_op jit(solution)/shard_map/ppermute | solution.py:114
  7.1 38.6 %copy-start.7 = (f32[1536]{0:T(1024)S(1)}, f32[1536]{0:T(1024)}, u32[]{:S(2)}) copy-start(f32[1536]{0:T(1024)} %scale.3) | copy-start | bytes 18436
  7.7 5.9 %collective-permute-start = (bf16[3,16,1536]{2,1,0:T(8,128)(2,1)S(1)}, bf16[3,16,1536]{2,1,0:T(8,128)(2,1)S(1)}, u32[]{:S(2)}, u32[]{:S(2)}) collective-permute-start(bf16[3,16,1536]{2,1,0:T(8,128)(2,1)S(1)} %get-tuple-element.75), channel_id=1, source_target_pairs={{0,16},{8,24},{16,0},{24,8},{1,17},{9,25},{17,1},{25,9},{2,18},{10... | collective-permute-start | bytes 442376 | tf_op jit(solution)/shard_map/ppermute | solution.py:75
  7.8 5.8 %collective-permute-start.1 = (bf16[8,3,1536]{2,1,0:T(4,128)(2,1)S(1)}, bf16[8,3,1536]{2,1,0:T(4,128)(2,1)S(1)}, u32[]{:S(2)}, u32[]{:S(2)}) collective-permute-start(bf16[8,3,1536]{2,1,0:T(4,128)(2,1)S(1)} %get-tuple-element.76), channel_id=1, source_target_pairs={{0,8},{8,0},{16,24},{24,16},{1,9},{9,1},{17,25},{25,17},{2,10},{10... | collective-permute-start | bytes 221192 | tf_op jit(solution)/shard_map/ppermute | solution.py:75
  9.7 3.9 %collective-permute-start.2 = (bf16[3,3,1536]{2,1,0:T(4,128)(2,1)S(1)}, bf16[3,3,1536]{2,1,0:T(4,128)(2,1)S(1)}, u32[]{:S(2)}, u32[]{:S(2)}) collective-permute-start(bf16[3,3,1536]{2,1,0:T(4,128)(2,1)S(1)} %get-tuple-element.77), channel_id=1, source_target_pairs={{0,24},{8,16},{16,8},{24,0},{1,25},{9,17},{17,9},{25,1},{2,26},{10... | collective-permute-start | bytes 82952 | tf_op jit(solution)/shard_map/ppermute | solution.py:75
  21.0 14.1 %collective-permute-start.8 = (bf16[384,768]{1,0:T(8,128)(2,1)}, bf16[384,768]{1,0:T(8,128)(2,1)S(1)}, u32[]{:S(2)}, u32[]{:S(2)}) collective-permute-start(bf16[384,768]{1,0:T(8,128)(2,1)} %collective-permute-done.6.refs_1_), channel_id=1, source_target_pairs={{0,2},{2,4},{4,6},{6,7},{7,5},{5,3},{3,1},{1,0},{8,10},{10,12},{12... | collective-permute-start | bytes 1769480 | tf_op jit(solution)/shard_map/ppermute | solution.py:114
  21.4 13.9 %collective-permute-start.9 = (bf16[384,768]{1,0:T(8,128)(2,1)S(1)}, bf16[384,768]{1,0:T(8,128)(2,1)S(1)}, u32[]{:S(2)}, u32[]{:S(2)}) collective-permute-start(bf16[384,768]{1,0:T(8,128)(2,1)S(1)} %collective-permute-done.7.refs_2_), channel_id=1, source_target_pairs={{2,0},{4,2},{6,4},{7,6},{5,7},{3,5},{1,3},{0,1},{10,8},{12,10},{14... | collective-permute-start | bytes 1769480 | tf_op jit(solution)/shard_map/ppermute | solution.py:115
  23.0 15.7 %collective-permute-start.4 = (bf16[128,1536]{1,0:T(8,128)(2,1)S(1)}, bf16[128,1536]{1,0:T(8,128)(2,1)S(1)}, u32[]{:S(2)}, u32[]{:S(2)}) collective-permute-start(bf16[128,1536]{1,0:T(8,128)(2,1)S(1)} %bitcast.8), channel_id=1, source_target_pairs={{8,0},{0,8},{9,1},{1,9},{10,2},{2,10},{11,3},{3,11},{12,4},{4,12},... | collective-permute-start | bytes 1179656 | tf_op jit(solution)/shard_map/ppermute | solution.py:55
  24.5 0.7 copy-start.5
  25.2 0.7 copy-start.9
  25.9 0.7 copy-start.10
  32.7 6.1 %collective-permute-start.3 = (bf16[128,1536]{1,0:T(8,128)(2,1)S(1)}, bf16[128,1536]{1,0:T(8,128)(2,1)S(1)}, u32[]{:S(2)}, u32[]{:S(2)}) collective-permute-start(bf16[128,1536]{1,0:T(8,128)(2,1)S(1)} %bitcast.9), channel_id=1, source_target_pairs={{16,0},{0,16},{17,1},{1,17},{18,2},{2,18},{19,3},{3,19},{20,4},{4,... | collective-permute-start | bytes 1179656 | tf_op jit(solution)/shard_map/ppermute | solution.py:55
  35.3 13.2 %collective-permute-start.10 = (bf16[384,768]{1,0:T(8,128)(2,1)S(1)}, bf16[384,768]{1,0:T(8,128)(2,1)S(1)}, u32[]{:S(2)}, u32[]{:S(2)}) collective-permute-start(bf16[384,768]{1,0:T(8,128)(2,1)S(1)} %collective-permute-done.8.refs_3_), channel_id=1, source_target_pairs={{0,2},{2,4},{4,6},{6,7},{7,5},{5,3},{3,1},{1,0},{8,10},{10,12},{12... | collective-permute-start | bytes 1769480 | tf_op jit(solution)/shard_map/ppermute | solution.py:114
  36.8 12.6 %collective-permute-start.11 = (bf16[384,768]{1,0:T(8,128)(2,1)S(1)}, bf16[384,768]{1,0:T(8,128)(2,1)S(1)}, u32[]{:S(2)}, u32[]{:S(2)}) collective-permute-start(bf16[384,768]{1,0:T(8,128)(2,1)S(1)} %collective-permute-done.9.refs_4_), channel_id=1, source_target_pairs={{2,0},{4,2},{6,4},{7,6},{5,7},{3,5},{1,3},{0,1},{10,8},{12,10},{14... | collective-permute-start | bytes 1769480 | tf_op jit(solution)/shard_map/ppermute | solution.py:115
  37.3 8.4 %collective-permute-start.14 = (bf16[128,1536]{1,0:T(8,128)(2,1)S(1)}, bf16[128,1536]{1,0:T(8,128)(2,1)S(1)}, u32[]{:S(2)}, u32[]{:S(2)}) collective-permute-start(bf16[128,1536]{1,0:T(8,128)(2,1)S(1)} %get-tuple-element.88.refs_9_), channel_id=1, source_target_pairs={{8,0},{0,8},{9,1},{1,9},{10,2},{2,10},{11,3},{3,11},{12,4},{4,12},... | collective-permute-start | bytes 1179656 | tf_op jit(solution)/shard_map/ppermute | solution.py:55
  38.8 7.0 %collective-permute-start.15 = (bf16[128,1536]{1,0:T(8,128)(2,1)S(1)}, bf16[128,1536]{1,0:T(8,128)(2,1)S(1)}, u32[]{:S(2)}, u32[]{:S(2)}) collective-permute-start(bf16[128,1536]{1,0:T(8,128)(2,1)S(1)} %get-tuple-element.88.refs_9_), channel_id=1, source_target_pairs={{16,0},{0,16},{17,1},{1,17},{18,2},{2,18},{19,3},{3,19},{20,4},{4,... | collective-permute-start | bytes 1179656 | tf_op jit(solution)/shard_map/ppermute | solution.py:55
  38.8 7.0 %collective-permute-start.5 = (bf16[128,1536]{1,0:T(8,128)(2,1)S(1)}, bf16[128,1536]{1,0:T(8,128)(2,1)S(1)}, u32[]{:S(2)}, u32[]{:S(2)}) collective-permute-start(bf16[128,1536]{1,0:T(8,128)(2,1)S(1)} %collective-permute-done.4.refs_2_.refs_15_), channel_id=1, source_target_pairs={{16,0},{0,16},{17,1},{1,17},{18,2},{2,18},{19,3},{3,19},{20,4},{4,... | collective-permute-start | bytes 1179656 | tf_op jit(solution)/shard_map/ppermute | solution.py:55
  45.7 5.8 %collective-permute-start.16 = (bf16[128,1536]{1,0:T(8,128)(2,1)S(1)}, bf16[128,1536]{1,0:T(8,128)(2,1)S(1)}, u32[]{:S(2)}, u32[]{:S(2)}) collective-permute-start(bf16[128,1536]{1,0:T(8,128)(2,1)S(1)} %collective-permute-done.14.refs_7_), channel_id=1, source_target_pairs={{16,0},{0,16},{17,1},{1,17},{18,2},{2,18},{19,3},{3,19},{20,4},{4,... | collective-permute-start | bytes 1179656 | tf_op jit(solution)/shard_map/ppermute | solution.py:55
  49.4 8.4 %copy-start.4 = (f32[3072]{0:T(1024)S(1)}, f32[3072]{0:T(1024)}, u32[]{:S(2)}) copy-start(f32[3072]{0:T(1024)} %refs_17_.1) | copy-start | bytes 36868
  49.4 6.8 %collective-permute-start.12 = (bf16[192,768]{1,0:T(8,128)(2,1)S(1)}, bf16[192,768]{1,0:T(8,128)(2,1)S(1)}, u32[]{:S(2)}, u32[]{:S(2)}) collective-permute-start(bf16[192,768]{1,0:T(8,128)(2,1)S(1)} %slice.8), channel_id=1, source_target_pairs={{0,2},{2,4},{4,6},{6,7},{7,5},{5,3},{3,1},{1,0},{8,10},{10,12},{12... | collective-permute-start | bytes 884744 | tf_op jit(solution)/shard_map/ppermute | solution.py:124
  51.0 6.7 %collective-permute-start.13 = (bf16[192,768]{1,0:T(8,128)(2,1)S(1)}, bf16[192,768]{1,0:T(8,128)(2,1)S(1)}, u32[]{:S(2)}, u32[]{:S(2)}) collective-permute-start(bf16[192,768]{1,0:T(8,128)(2,1)S(1)} %slice.9), channel_id=1, source_target_pairs={{2,0},{4,2},{6,4},{7,6},{5,7},{3,5},{1,3},{0,1},{10,8},{12,10},{14... | collective-permute-start | bytes 884744 | tf_op jit(solution)/shard_map/ppermute | solution.py:124
  59.8 3.5 %copy-start.8 = (f32[1536]{0:T(1024)S(1)}, f32[1536]{0:T(1024)}, u32[]{:S(2)}) copy-start(f32[1536]{0:T(1024)} %bias.3) | copy-start | bytes 18436
  59.8 1.8 %collective-permute-start.17 = (bf16[128,1536]{1,0:T(8,128)(2,1)S(1)}, bf16[128,1536]{1,0:T(8,128)(2,1)S(1)}, u32[]{:S(2)}, u32[]{:S(2)}) collective-permute-start(bf16[128,1536]{1,0:T(8,128)(2,1)S(1)} %get-tuple-element.97), channel_id=1, source_target_pairs={{16,0},{0,16},{17,1},{1,17},{18,2},{2,18},{19,3},{3,19},{20,4},{4,... | collective-permute-start | bytes 1179656 | tf_op jit(solution)/shard_map/ppermute | solution.py:55
  61.7 11.2 %collective-permute-start.18 = (bf16[128,1536]{1,0:T(8,128)(2,1)S(1)}, bf16[128,1536]{1,0:T(8,128)(2,1)S(1)}, u32[]{:S(2)}, u32[]{:S(2)}) collective-permute-start(bf16[128,1536]{1,0:T(8,128)(2,1)S(1)} %add_rounded.2), channel_id=1, source_target_pairs={{8,0},{0,8},{9,1},{1,9},{10,2},{2,10},{11,3},{3,11},{12,4},{4,12},... | collective-permute-start | bytes 1179656 | tf_op jit(solution)/shard_map/ppermute | solution.py:55
  63.2 11.2 %copy-start.6 = (f32[1536]{0:T(1024)S(1)}, f32[1536]{0:T(1024)}, u32[]{:S(2)}) copy-start(f32[1536]{0:T(1024)} %refs_6_.3) | copy-start | bytes 18436
  67.9 1.5 %collective-permute-start.19 = (bf16[64,1536]{1,0:T(8,128)(2,1)S(1)}, bf16[64,1536]{1,0:T(8,128)(2,1)S(1)}, u32[]{:S(2)}, u32[]{:S(2)}) collective-permute-start(bf16[64,1536]{1,0:T(8,128)(2,1)S(1)} %get-tuple-element.102), channel_id=1, source_target_pairs={{16,0},{0,16},{17,1},{1,17},{18,2},{2,18},{19,3},{3,19},{20,4},{4,... | collective-permute-start | bytes 589832 | tf_op jit(solution)/shard_map/ppermute | solution.py:55
  68.0 1.7 %collective-permute-start.20 = (bf16[64,1536]{1,0:T(8,128)(2,1)S(1)}, bf16[64,1536]{1,0:T(8,128)(2,1)S(1)}, u32[]{:S(2)}, u32[]{:S(2)}) collective-permute-start(bf16[64,1536]{1,0:T(8,128)(2,1)S(1)} %get-tuple-element.103), channel_id=1, source_target_pairs={{16,0},{0,16},{17,1},{1,17},{18,2},{2,18},{19,3},{3,19},{20,4},{4,... | collective-permute-start | bytes 589832 | tf_op jit(solution)/shard_map/ppermute | solution.py:55
  68.5 1.5 %collective-permute-start.21 = (bf16[64,1536]{1,0:T(8,128)(2,1)S(1)}, bf16[64,1536]{1,0:T(8,128)(2,1)S(1)}, u32[]{:S(2)}, u32[]{:S(2)}) collective-permute-start(bf16[64,1536]{1,0:T(8,128)(2,1)S(1)} %get-tuple-element.107), channel_id=1, source_target_pairs={{16,0},{0,16},{17,1},{1,17},{18,2},{2,18},{19,3},{3,19},{20,4},{4,... | collective-permute-start | bytes 589832 | tf_op jit(solution)/shard_map/ppermute | solution.py:55
  68.6 1.7 %collective-permute-start.22 = (bf16[64,1536]{1,0:T(8,128)(2,1)S(1)}, bf16[64,1536]{1,0:T(8,128)(2,1)S(1)}, u32[]{:S(2)}, u32[]{:S(2)}) collective-permute-start(bf16[64,1536]{1,0:T(8,128)(2,1)S(1)} %get-tuple-element.108), channel_id=1, source_target_pairs={{16,0},{0,16},{17,1},{1,17},{18,2},{2,18},{19,3},{3,19},{20,4},{4,... | collective-permute-start | bytes 589832 | tf_op jit(solution)/shard_map/ppermute | solution.py:55
  69.4 5.0 %collective-permute-start.23 = (bf16[64,1536]{1,0:T(8,128)(2,1)S(1)}, bf16[64,1536]{1,0:T(8,128)(2,1)S(1)}, u32[]{:S(2)}, u32[]{:S(2)}) collective-permute-start(bf16[64,1536]{1,0:T(8,128)(2,1)S(1)} %get-tuple-element.113), channel_id=1, source_target_pairs={{16,0},{0,16},{17,1},{1,17},{18,2},{2,18},{19,3},{3,19},{20,4},{4,... | collective-permute-start | bytes 589832 | tf_op jit(solution)/shard_map/ppermute | solution.py:55
  69.7 4.7 %collective-permute-start.24 = (bf16[64,1536]{1,0:T(8,128)(2,1)S(1)}, bf16[64,1536]{1,0:T(8,128)(2,1)S(1)}, u32[]{:S(2)}, u32[]{:S(2)}) collective-permute-start(bf16[64,1536]{1,0:T(8,128)(2,1)S(1)} %get-tuple-element.114), channel_id=1, source_target_pairs={{16,0},{0,16},{17,1},{1,17},{18,2},{2,18},{19,3},{3,19},{20,4},{4,... | collective-permute-start | bytes 589832 | tf_op jit(solution)/shard_map/ppermute | solution.py:55
  72.9 8.2 %collective-permute-start.26 = (bf16[96,1536]{1,0:T(8,128)(2,1)S(1)}, bf16[96,1536]{1,0:T(8,128)(2,1)S(1)}, u32[]{:S(2)}, u32[]{:S(2)}) collective-permute-start(bf16[96,1536]{1,0:T(8,128)(2,1)S(1)} %get-tuple-element.121), channel_id=1, source_target_pairs={{8,0},{0,8},{9,1},{1,9},{10,2},{2,10},{11,3},{3,11},{12,4},{4,12},... | collective-permute-start | bytes 884744 | tf_op jit(solution)/shard_map/ppermute | solution.py:55
  79.0 2.0 %collective-permute-start.25 = (f32[32,1536]{1,0:T(8,128)S(1)}, f32[32,1536]{1,0:T(8,128)S(1)}, u32[]{:S(2)}, u32[]{:S(2)}) collective-permute-start(f32[32,1536]{1,0:T(8,128)S(1)} %get-tuple-element.120), channel_id=1, source_target_pairs={{0,16},{16,0},{1,17},{17,1},{2,18},{18,2},{3,19},{19,3},{4,20},{20... | collective-permute-start | bytes 589832 | tf_op jit(solution)/shard_map/ppermute | solution.py:50
  79.0 6.2 %collective-permute-start.30 = (bf16[3,16,1536]{2,1,0:T(8,128)(2,1)S(1)}, bf16[3,16,1536]{2,1,0:T(8,128)(2,1)S(1)}, u32[]{:S(2)}, u32[]{:S(2)}) collective-permute-start(bf16[3,16,1536]{2,1,0:T(8,128)(2,1)S(1)} %get-tuple-element.130), channel_id=1, source_target_pairs={{0,16},{8,24},{16,0},{24,8},{1,17},{9,25},{17,1},{25,9},{2,18},{10... | collective-permute-start | bytes 442376 | tf_op jit(solution)/shard_map/ppermute | solution.py:75
  79.5 5.7 %collective-permute-start.31 = (bf16[8,3,1536]{2,1,0:T(4,128)(2,1)S(1)}, bf16[8,3,1536]{2,1,0:T(4,128)(2,1)S(1)}, u32[]{:S(2)}, u32[]{:S(2)}) collective-permute-start(bf16[8,3,1536]{2,1,0:T(4,128)(2,1)S(1)} %get-tuple-element.131), channel_id=1, source_target_pairs={{0,8},{8,0},{16,24},{24,16},{1,9},{9,1},{17,25},{25,17},{2,10},{10... | collective-permute-start | bytes 221192 | tf_op jit(solution)/shard_map/ppermute | solution.py:75
  80.1 4.2 %collective-permute-start.32 = (bf16[3,3,1536]{2,1,0:T(4,128)(2,1)S(1)}, bf16[3,3,1536]{2,1,0:T(4,128)(2,1)S(1)}, u32[]{:S(2)}, u32[]{:S(2)}) collective-permute-start(bf16[3,3,1536]{2,1,0:T(4,128)(2,1)S(1)} %get-tuple-element.132), channel_id=1, source_target_pairs={{0,24},{8,16},{16,8},{24,0},{1,25},{9,17},{17,9},{25,1},{2,26},{10... | collective-permute-start | bytes 82952 | tf_op jit(solution)/shard_map/ppermute | solution.py:75
  81.1 7.3 %collective-permute-start.27 = (bf16[8,1536]{1,0:T(8,128)(2,1)S(1)}, bf16[8,1536]{1,0:T(8,128)(2,1)S(1)}, u32[]{:S(2)}, u32[]{:S(2)}) collective-permute-start(bf16[8,1536]{1,0:T(8,128)(2,1)S(1)} %get-tuple-element.126), channel_id=1, source_target_pairs={{0,1},{1,0},{2,3},{3,2},{4,5},{5,4},{6,7},{7,6},{8,9},{9,8},{10,11... | collective-permute-start | bytes 73736 | tf_op jit(solution)/shard_map/ppermute | solution.py:50
  81.7 6.8 %collective-permute-start.28 = (bf16[8,1536]{1,0:T(8,128)(2,1)S(1)}, bf16[8,1536]{1,0:T(8,128)(2,1)S(1)}, u32[]{:S(2)}, u32[]{:S(2)}) collective-permute-start(bf16[8,1536]{1,0:T(8,128)(2,1)S(1)} %get-tuple-element.127), channel_id=1, source_target_pairs={{0,8},{8,0},{1,9},{9,1},{2,10},{10,2},{3,11},{11,3},{4,12},{12,4},... | collective-permute-start | bytes 73736 | tf_op jit(solution)/shard_map/ppermute | solution.py:50
  84.2 5.0 %collective-permute-start.29 = (bf16[8,1536]{1,0:T(8,128)(2,1)S(1)}, bf16[8,1536]{1,0:T(8,128)(2,1)S(1)}, u32[]{:S(2)}, u32[]{:S(2)}) collective-permute-start(bf16[8,1536]{1,0:T(8,128)(2,1)S(1)} %get-tuple-element.128), channel_id=1, source_target_pairs={{0,9},{1,8},{2,11},{3,10},{4,13},{5,12},{6,15},{7,14},{8,1},{9,0},... | collective-permute-start | bytes 73736 | tf_op jit(solution)/shard_map/ppermute | solution.py:50
  89.2 8.5 %collective-permute-start.36 = (bf16[32,1536]{1,0:T(8,128)(2,1)S(1)}, bf16[32,1536]{1,0:T(8,128)(2,1)S(1)}, u32[]{:S(2)}, u32[]{:S(2)}) collective-permute-start(bf16[32,1536]{1,0:T(8,128)(2,1)S(1)} %get-tuple-element.136), channel_id=1, source_target_pairs={{8,0},{0,8},{9,1},{1,9},{10,2},{2,10},{11,3},{3,11},{12,4},{4,12},... | collective-permute-start | bytes 294920 | tf_op jit(solution)/shard_map/ppermute | solution.py:55
  90.1 7.6 %collective-permute-start.35 = (bf16[8,1536]{1,0:T(8,128)(2,1)S(1)}, bf16[8,1536]{1,0:T(8,128)(2,1)S(1)}, u32[]{:S(2)}, u32[]{:S(2)}) collective-permute-start(bf16[8,1536]{1,0:T(8,128)(2,1)S(1)} %add_pairs.2.refs_0_), channel_id=1, source_target_pairs={{0,6},{1,7},{2,4},{3,5},{4,2},{5,3},{6,0},{7,1},{8,14},{9,15},{10,... | collective-permute-start | bytes 73736 | tf_op jit(solution)/shard_map/ppermute | solution.py:50
  92.7 5.0 %collective-permute-start.34 = (bf16[8,1536]{1,0:T(8,128)(2,1)S(1)}, bf16[8,1536]{1,0:T(8,128)(2,1)S(1)}, u32[]{:S(2)}, u32[]{:S(2)}) collective-permute-start(bf16[8,1536]{1,0:T(8,128)(2,1)S(1)} %add_pairs.2.refs_0_), channel_id=1, source_target_pairs={{0,4},{1,5},{2,6},{3,7},{4,0},{5,1},{6,2},{7,3},{8,12},{9,13},{10,... | collective-permute-start | bytes 73736 | tf_op jit(solution)/shard_map/ppermute | solution.py:50
  93.1 4.6 %collective-permute-start.33 = (bf16[8,1536]{1,0:T(8,128)(2,1)S(1)}, bf16[8,1536]{1,0:T(8,128)(2,1)S(1)}, u32[]{:S(2)}, u32[]{:S(2)}) collective-permute-start(bf16[8,1536]{1,0:T(8,128)(2,1)S(1)} %add_pairs.2.refs_0_), channel_id=1, source_target_pairs={{0,2},{1,3},{2,0},{3,1},{4,6},{5,7},{6,4},{7,5},{8,10},{9,11},{10,... | collective-permute-start | bytes 73736 | tf_op jit(solution)/shard_map/ppermute | solution.py:50
  97.8 5.1 %collective-permute-start.39 = (f32[8,1536]{1,0:T(8,128)S(1)}, f32[8,1536]{1,0:T(8,128)S(1)}, u32[]{:S(2)}, u32[]{:S(2)}) collective-permute-start(f32[8,1536]{1,0:T(8,128)S(1)} %add_pairs.3.refs_0_), channel_id=1, source_target_pairs={{0,9},{1,8},{2,11},{3,10},{4,13},{5,12},{6,15},{7,14},{8,1},{9,0},... | collective-permute-start | bytes 147464 | tf_op jit(solution)/shard_map/ppermute | solution.py:50
  99.3 4.1 %collective-permute-start.38 = (f32[8,1536]{1,0:T(8,128)S(1)}, f32[8,1536]{1,0:T(8,128)S(1)}, u32[]{:S(2)}, u32[]{:S(2)}) collective-permute-start(f32[8,1536]{1,0:T(8,128)S(1)} %add_pairs.3.refs_0_), channel_id=1, source_target_pairs={{0,8},{8,0},{1,9},{9,1},{2,10},{10,2},{3,11},{11,3},{4,12},{12,4},... | collective-permute-start | bytes 147464 | tf_op jit(solution)/shard_map/ppermute | solution.py:50
  100.2 4.1 %collective-permute-start.37 = (f32[8,1536]{1,0:T(8,128)S(1)}, f32[8,1536]{1,0:T(8,128)S(1)}, u32[]{:S(2)}, u32[]{:S(2)}) collective-permute-start(f32[8,1536]{1,0:T(8,128)S(1)} %add_pairs.3.refs_0_), channel_id=1, source_target_pairs={{0,1},{1,0},{2,3},{3,2},{4,5},{5,4},{6,7},{7,6},{8,9},{9,8},{10,11... | collective-permute-start | bytes 147464 | tf_op jit(solution)/shard_map/ppermute | solution.py:50
  101.3 4.0 %collective-permute-start.40 = (f32[8,1536]{1,0:T(8,128)S(1)}, f32[8,1536]{1,0:T(8,128)S(1)}, u32[]{:S(2)}, u32[]{:S(2)}) collective-permute-start(f32[8,1536]{1,0:T(8,128)S(1)} %add_pairs.3.refs_0_), channel_id=1, source_target_pairs={{0,16},{16,0},{1,17},{17,1},{2,18},{18,2},{3,19},{19,3},{4,20},{20... | collective-permute-start | bytes 147464 | tf_op jit(solution)/shard_map/ppermute | solution.py:50
  102.9 2.4 %collective-permute-start.43 = (f32[8,1536]{1,0:T(8,128)S(1)}, f32[8,1536]{1,0:T(8,128)S(1)}, u32[]{:S(2)}, u32[]{:S(2)}) collective-permute-start(f32[8,1536]{1,0:T(8,128)S(1)} %collective-permute-done.39.refs_3_), channel_id=1, source_target_pairs={{0,16},{16,0},{1,17},{17,1},{2,18},{18,2},{3,19},{19,3},{4,20},{20... | collective-permute-start | bytes 147464 | tf_op jit(solution)/shard_map/ppermute | solution.py:50
  103.4 1.9 %collective-permute-start.42 = (f32[8,1536]{1,0:T(8,128)S(1)}, f32[8,1536]{1,0:T(8,128)S(1)}, u32[]{:S(2)}, u32[]{:S(2)}) collective-permute-start(f32[8,1536]{1,0:T(8,128)S(1)} %collective-permute-done.38.refs_2_), channel_id=1, source_target_pairs={{0,16},{16,0},{1,17},{17,1},{2,18},{18,2},{3,19},{19,3},{4,20},{20... | collective-permute-start | bytes 147464 | tf_op jit(solution)/shard_map/ppermute | solution.py:50
  104.3 1.2 %collective-permute-start.41 = (f32[8,1536]{1,0:T(8,128)S(1)}, f32[8,1536]{1,0:T(8,128)S(1)}, u32[]{:S(2)}, u32[]{:S(2)}) collective-permute-start(f32[8,1536]{1,0:T(8,128)S(1)} %collective-permute-done.37.refs_1_), channel_id=1, source_target_pairs={{0,16},{16,0},{1,17},{17,1},{2,18},{18,2},{3,19},{19,3},{4,20},{20... | collective-permute-start | bytes 147464 | tf_op jit(solution)/shard_map/ppermute | solution.py:50
